TPU v7x, 32 devices: a whole 2x2x4 slice. The times are simulated.
32 devices in a mesh: dp: 4 (over y, core), vocab: 8 (over z, x).
Axes of the slice: x: 2, y: 2, z: 4, core: 2. Of those that a mesh axis runs over, the one named last changes fastest.
Arguments:
- token_ids: int32 [32, 512], P(('dp', 'vocab')), may hold values from 0 to 7679, as said below
- lengths: int32 [32], P(('dp', 'vocab')), may hold values from 16 to 512, as said below
- type_ids: int32 [32, 512], P(('dp', 'vocab')), may hold values from 0 to 1
- word_table: bfloat16 [7680, 768], P('vocab'), may hold values from -6 to 6
- pos_table: bfloat16 [512, 768], replicated, may hold values from -3 to 3
- type_table: bfloat16 [2, 768], replicated, may hold values from -3 to 3
- gains: bfloat16 [5, 768], replicated, may hold values from 0.25 to 1.75
- shifts: bfloat16 [13, 768], replicated, may hold values from -2 to 2
- w_qkv: bfloat16 [2, 768, 2304], replicated, may hold values from -0.21875 to 0.21875
- w_out: bfloat16 [2, 768, 768], replicated, may hold values from -0.625 to 0.625
- b_ff1: bfloat16 [2, 3072], replicated, may hold values from -2 to 2
- w_ff1: bfloat16 [2, 768, 3072], replicated, may hold values from -0.21875 to 0.21875
- w_ff2: bfloat16 [2, 3072, 768], replicated, may hold values from -0.109375 to 0.109375
- cotangent: bfloat16 [32, 512, 768], P(('dp', 'vocab')), may hold values from -6 to 6
Outputs:
- hidden_out: bfloat16 [32, 512, 768], P(('dp', 'vocab'))
- table_grad: float32 [7680, 768], P('vocab')
- pos_grad: float32 [512, 768], P('vocab')
- type_grad: float32 [2, 768], P(None, 'vocab')
- gains_grad: float32 [5, 768], P(None, 'vocab')
- shifts_grad: float32 [13, 768], P(None, 'vocab')
- w_qkv_grad: float32 [2, 768, 2304], P(None, 'vocab')
- w_out_grad: float32 [2, 768, 768], P(None, 'vocab')
- b_ff1_grad: float32 [2, 3072], P(None, 'vocab')
- w_ff1_grad: float32 [2, 768, 3072], P(None, 'vocab')
- w_ff2_grad: float32 [2, 3072, 768], P(None, 'vocab')
Inputs may be any that keep to these rules, and one draw needn't show every extreme that they name: `token_ids`: among the tokens of one device at most 128 ids lie in the 960 rows held by any one index of vocab, and in exactly 128 for one of them. `lengths`: the first sequence has 512 tokens; slots of a sequence beyond its length are padding that no query attends to.
All inputs are finite; a program needn't handle non-finite values.
Results may differ from a plain program's by a relative error of at most 0.02.
Values may be sent and summed in bfloat16 or wider, within the bound.
No kernel may reach another device: no remote copies, remote signals or barrier semaphores. Data moves between devices by JAX's collectives and lax.ppermute only.
A program may use at most 256 MiB of HBM per device.

v0:
```python
import jax
import jax.numpy as jnp
from jax import lax
from jax.sharding import PartitionSpec as P

HEADS = 12
HEAD_DIM = 64
NL = 2


norm_eps = 1e-12


def normalize(inputs):
    centered = inputs - jnp.mean(inputs, axis=-1, keepdims=True)
    spread = lax.rsqrt(jnp.mean(centered * centered, axis=-1, keepdims=True) + norm_eps)
    return (centered * spread, spread)


def norm_back(grad_out, normed, spread, gain_row):
    scaled = grad_out * gain_row
    return spread * (
        scaled
        - jnp.mean(scaled, axis=-1, keepdims=True)
        - normed * jnp.mean(scaled * normed, axis=-1, keepdims=True)
    )


def contract_rows(left_op, right_op):
    return lax.dot_general(
        left_op, right_op, (((0,), (0,)), ((), ())), preferred_element_type=jnp.float32
    )


def contract_cols(left_op, right_op):
    return lax.dot_general(
        left_op, right_op, (((1,), (1,)), ((), ())), preferred_element_type=jnp.float32
    )


def split_heads(matrix):
    return matrix.reshape(matrix.shape[0], HEADS, HEAD_DIM)


def activate(inputs):
    return jax.nn.gelu(inputs, approximate=False)


def score_block(queries, keys_in, length):
    scores = jnp.einsum(
        "qhd,khd->hqk",
        split_heads(queries),
        split_heads(keys_in),
        preferred_element_type=jnp.float32,
    ) * HEAD_DIM ** (-0.5)
    visible = jnp.arange(keys_in.shape[0])[None, None, :] < length
    return jnp.where(visible, scores, -1e30)


def attend(blocks):
    queries, keys_in, values, length = blocks
    scores = score_block(queries, keys_in, length)
    top_score = jnp.max(scores, axis=-1, keepdims=True)
    weights = jnp.exp(scores - top_score)
    row_total = jnp.sum(weights, axis=-1, keepdims=True)
    softened = (weights / row_total).astype(jnp.bfloat16)
    context = jnp.einsum(
        "hqk,khd->qhd", softened, split_heads(values), preferred_element_type=jnp.float32
    )
    return (
        context.reshape(queries.shape).astype(jnp.bfloat16),
        top_score[..., 0] + jnp.log(row_total[..., 0]),
    )


def attend_back(blocks):
    queries, keys_in, values, length, total_log, grad_context = blocks
    scores = score_block(queries, keys_in, length)
    softened = jnp.exp(scores - total_log[..., None])
    grad_split = split_heads(grad_context)
    grad_probs = jnp.einsum(
        "qhd,khd->hqk", grad_split, split_heads(values), preferred_element_type=jnp.float32
    )
    grad_values = jnp.einsum(
        "hqk,qhd->khd",
        softened.astype(jnp.bfloat16),
        grad_split,
        preferred_element_type=jnp.float32,
    )
    weighted = jnp.sum(softened * grad_probs, axis=-1, keepdims=True)
    grad_scores = (softened * (grad_probs - weighted)).astype(jnp.bfloat16)
    score_scale = HEAD_DIM ** (-0.5)
    grad_queries = (
        jnp.einsum(
            "hqk,khd->qhd", grad_scores, split_heads(keys_in), preferred_element_type=jnp.float32
        )
        * score_scale
    )
    grad_keys = (
        jnp.einsum(
            "hqk,qhd->khd", grad_scores, split_heads(queries), preferred_element_type=jnp.float32
        )
        * score_scale
    )
    return (
        grad_queries.reshape(queries.shape),
        grad_keys.reshape(queries.shape),
        grad_values.reshape(queries.shape),
    )


def on_device(
    token_ids,
    lengths,
    type_ids,
    word_table,
    pos_table,
    type_table,
    gains,
    shifts,
    w_qkv,
    w_out,
    b_ff1,
    w_ff1,
    w_ff2,
    cotangent,
):
    owners = lax.axis_size("vocab")
    local_rows = word_table.shape[0]
    seq_count = token_ids.shape[0]
    token_count = seq_count * token_ids.shape[1]
    model_width = word_table.shape[1]
    slot_count = 2 * token_count // owners
    gain_vals = gains.astype(jnp.float32)
    shift_vals = shifts.astype(jnp.float32)
    ffn_bias = b_ff1.astype(jnp.float32)
    flat_ids = token_ids.reshape(token_count)
    owner_of = flat_ids // local_rows
    wanted = flat_ids - owner_of * local_rows
    chosen = (owner_of[:, None] == jnp.arange(owners, dtype=jnp.int32)[None, :]).astype(jnp.int32)
    before = jnp.cumsum(chosen, axis=0) - chosen
    slot_of = owner_of * slot_count + jnp.sum(before * chosen, axis=1)
    requests = (
        jnp.zeros((owners * slot_count,), jnp.int32)
        .at[slot_of]
        .set(wanted)
        .reshape(owners, slot_count)
    )
    asked_rows = lax.all_to_all(requests, "vocab", split_axis=0, concat_axis=0, tiled=True)
    found_rows = word_table[asked_rows]
    replies = lax.all_to_all(found_rows, "vocab", split_axis=0, concat_axis=0, tiled=True)
    word_rows = replies.reshape(owners * slot_count, model_width)[slot_of].astype(jnp.float32)
    type_flat = type_ids.reshape(token_count)
    type_rows = jnp.where(
        type_flat[:, None] == 1,
        type_table[1].astype(jnp.float32)[None, :],
        type_table[0].astype(jnp.float32)[None, :],
    )
    position_rows = jnp.tile(pos_table.astype(jnp.float32), (seq_count, 1))
    embedded = word_rows + position_rows + type_rows
    normed_emb, spread_emb = normalize(embedded)
    states = normed_emb * gain_vals[0] + shift_vals[0]
    saved_acts = []
    for layer_num in range(NL):
        shift_base = 1 + 6 * layer_num
        states_low = states.astype(jnp.bfloat16)
        mixed_qkv = jnp.dot(states_low, w_qkv[layer_num], preferred_element_type=jnp.float32)
        queries = (mixed_qkv[:, :model_width] + shift_vals[shift_base]).astype(jnp.bfloat16)
        keys_in = mixed_qkv[:, model_width : 2 * model_width].astype(jnp.bfloat16)
        values = (mixed_qkv[:, 2 * model_width :] + shift_vals[shift_base + 1]).astype(jnp.bfloat16)
        per_seq = (
            queries.reshape(seq_count, -1, model_width),
            keys_in.reshape(seq_count, -1, model_width),
            values.reshape(seq_count, -1, model_width),
            lengths,
        )
        context, total_log = lax.map(attend, per_seq)
        context = context.reshape(token_count, model_width)
        attended = (
            jnp.dot(context, w_out[layer_num], preferred_element_type=jnp.float32)
            + shift_vals[shift_base + 2]
        )
        normed_one, spread_one = normalize(states + attended)
        middle = normed_one * gain_vals[1 + 2 * layer_num] + shift_vals[shift_base + 3]
        middle_low = middle.astype(jnp.bfloat16)
        hidden_pre = (
            jnp.dot(middle_low, w_ff1[layer_num], preferred_element_type=jnp.float32)
            + ffn_bias[layer_num]
        )
        active = activate(hidden_pre).astype(jnp.bfloat16)
        ffn_out = (
            jnp.dot(active, w_ff2[layer_num], preferred_element_type=jnp.float32)
            + shift_vals[shift_base + 4]
        )
        normed_two, spread_two = normalize(middle + ffn_out)
        saved_acts.append(
            (
                states_low,
                per_seq,
                total_log,
                context,
                normed_one,
                spread_one,
                middle_low,
                hidden_pre,
                active,
                normed_two,
                spread_two,
            )
        )
        states = normed_two * gain_vals[2 + 2 * layer_num] + shift_vals[shift_base + 5]
    hidden_out = states.reshape(seq_count, -1, model_width).astype(jnp.bfloat16)
    grad_states = cotangent.reshape(token_count, model_width).astype(jnp.float32)
    gain_grads = [None] * (2 * NL + 1)
    shift_grads = [None] * (6 * NL + 1)
    bias_grads = [None] * NL
    layer_grads = [None] * NL
    for layer_num in reversed(range(NL)):
        (
            states_low,
            per_seq,
            total_log,
            context,
            normed_one,
            spread_one,
            middle_low,
            hidden_pre,
            active,
            normed_two,
            spread_two,
        ) = saved_acts[layer_num]
        shift_base = 1 + 6 * layer_num
        gain_grads[2 + 2 * layer_num] = jnp.sum(grad_states * normed_two, axis=0)
        shift_grads[shift_base + 5] = jnp.sum(grad_states, axis=0)
        grad_second = norm_back(grad_states, normed_two, spread_two, gain_vals[2 + 2 * layer_num])
        shift_grads[shift_base + 4] = jnp.sum(grad_second, axis=0)
        second_low = grad_second.astype(jnp.bfloat16)
        grad_w_two = contract_rows(active, second_low)
        grad_active = contract_cols(second_low, w_ff2[layer_num])
        grad_pre = jax.vjp(activate, hidden_pre)[1](grad_active)[0]
        bias_grads[layer_num] = jnp.sum(grad_pre, axis=0)
        pre_low = grad_pre.astype(jnp.bfloat16)
        grad_w_one = contract_rows(middle_low, pre_low)
        grad_middle = grad_second + contract_cols(pre_low, w_ff1[layer_num])
        gain_grads[1 + 2 * layer_num] = jnp.sum(grad_middle * normed_one, axis=0)
        shift_grads[shift_base + 3] = jnp.sum(grad_middle, axis=0)
        grad_first = norm_back(grad_middle, normed_one, spread_one, gain_vals[1 + 2 * layer_num])
        shift_grads[shift_base + 2] = jnp.sum(grad_first, axis=0)
        first_low = grad_first.astype(jnp.bfloat16)
        grad_w_out = contract_rows(context, first_low)
        grad_context = contract_cols(first_low, w_out[layer_num]).astype(jnp.bfloat16)
        grad_queries, grad_keys, grad_values = lax.map(
            attend_back,
            (
                per_seq[0],
                per_seq[1],
                per_seq[2],
                per_seq[3],
                total_log,
                grad_context.reshape(seq_count, -1, model_width),
            ),
        )
        grad_queries = grad_queries.reshape(token_count, model_width)
        grad_keys = grad_keys.reshape(token_count, model_width)
        grad_values = grad_values.reshape(token_count, model_width)
        shift_grads[shift_base] = jnp.sum(grad_queries, axis=0)
        shift_grads[shift_base + 1] = jnp.sum(grad_values, axis=0)
        grad_mixed = jnp.concatenate([grad_queries, grad_keys, grad_values], axis=1).astype(
            jnp.bfloat16
        )
        grad_w_qkv = contract_rows(states_low, grad_mixed)
        grad_states = grad_first + contract_cols(grad_mixed, w_qkv[layer_num])
        layer_grads[layer_num] = (grad_w_qkv, grad_w_out, grad_w_one, grad_w_two)
    gain_grads[0] = jnp.sum(grad_states * normed_emb, axis=0)
    shift_grads[0] = jnp.sum(grad_states, axis=0)
    grad_embedded = norm_back(grad_states, normed_emb, spread_emb, gain_vals[0])
    position_grad = jnp.sum(grad_embedded.reshape(seq_count, -1, model_width), axis=0)
    type_zero = jnp.sum(jnp.where(type_flat[:, None] == 0, grad_embedded, 0.0), axis=0)
    type_one = jnp.sum(jnp.where(type_flat[:, None] == 1, grad_embedded, 0.0), axis=0)
    type_sums = jnp.stack([type_zero, type_one])
    gain_sums = jnp.stack(gain_grads)
    shift_sums = jnp.stack(shift_grads)
    bias_sums = jnp.stack(bias_grads)
    qkv_sums = jnp.stack([layer_grads[layer_num][0] for layer_num in range(NL)])
    out_sums = jnp.stack([layer_grads[layer_num][1] for layer_num in range(NL)])
    one_sums = jnp.stack([layer_grads[layer_num][2] for layer_num in range(NL)])
    two_sums = jnp.stack([layer_grads[layer_num][3] for layer_num in range(NL)])
    outgoing = (
        jnp.zeros((owners * slot_count, model_width), jnp.float32).at[slot_of].set(grad_embedded)
    )
    incoming = lax.all_to_all(
        outgoing.reshape(owners, slot_count, model_width).astype(jnp.bfloat16),
        "vocab",
        split_axis=0,
        concat_axis=0,
        tiled=True,
    ).astype(jnp.float32)
    table_part = (
        jnp.zeros((local_rows, model_width), jnp.float32)
        .at[asked_rows.reshape(-1)]
        .add(incoming.reshape(-1, model_width))
    )
    shares = (
        lax.psum_scatter(
            qkv_sums.astype(jnp.bfloat16), "vocab", scatter_dimension=1, tiled=True
        ).astype(jnp.float32),
        lax.psum_scatter(
            out_sums.astype(jnp.bfloat16), "vocab", scatter_dimension=1, tiled=True
        ).astype(jnp.float32),
        lax.psum_scatter(
            one_sums.astype(jnp.bfloat16), "vocab", scatter_dimension=1, tiled=True
        ).astype(jnp.float32),
        lax.psum_scatter(
            two_sums.astype(jnp.bfloat16), "vocab", scatter_dimension=1, tiled=True
        ).astype(jnp.float32),
        lax.psum_scatter(
            position_grad.astype(jnp.bfloat16), "vocab", scatter_dimension=0, tiled=True
        ).astype(jnp.float32),
        lax.psum_scatter(
            bias_sums.astype(jnp.bfloat16), "vocab", scatter_dimension=1, tiled=True
        ).astype(jnp.float32),
        lax.psum_scatter(
            gain_sums.astype(jnp.bfloat16), "vocab", scatter_dimension=1, tiled=True
        ).astype(jnp.float32),
        lax.psum_scatter(
            shift_sums.astype(jnp.bfloat16), "vocab", scatter_dimension=1, tiled=True
        ).astype(jnp.float32),
        lax.psum_scatter(
            type_sums.astype(jnp.bfloat16), "vocab", scatter_dimension=1, tiled=True
        ).astype(jnp.float32),
    )
    totals = (
        lax.psum(shares[0].astype(jnp.bfloat16), "dp").astype(jnp.float32),
        lax.psum(shares[1].astype(jnp.bfloat16), "dp").astype(jnp.float32),
        lax.psum(shares[2].astype(jnp.bfloat16), "dp").astype(jnp.float32),
        lax.psum(shares[3].astype(jnp.bfloat16), "dp").astype(jnp.float32),
        lax.psum(shares[4].astype(jnp.bfloat16), "dp").astype(jnp.float32),
        lax.psum(shares[5].astype(jnp.bfloat16), "dp").astype(jnp.float32),
        lax.psum(shares[6].astype(jnp.bfloat16), "dp").astype(jnp.float32),
        lax.psum(shares[7].astype(jnp.bfloat16), "dp").astype(jnp.float32),
        lax.psum(shares[8].astype(jnp.bfloat16), "dp").astype(jnp.float32),
        lax.psum(table_part.astype(jnp.bfloat16), "dp").astype(jnp.float32),
    )
    (
        qkv_out,
        wout_out,
        one_out,
        two_out,
        pos_out,
        bias_out,
        gain_out,
        shift_out,
        type_out,
        table_out,
    ) = totals
    return (
        hidden_out,
        table_out,
        pos_out,
        type_out,
        gain_out,
        shift_out,
        qkv_out,
        wout_out,
        bias_out,
        one_out,
        two_out,
    )


def solution(mesh):
    in_specs = (
        P(("dp", "vocab"), None),
        P(("dp", "vocab")),
        P(("dp", "vocab"), None),
        P("vocab", None),
        P(),
        P(),
        P(),
        P(),
        P(),
        P(),
        P(),
        P(),
        P(),
        P(("dp", "vocab"), None, None),
    )
    out_specs = (
        P(("dp", "vocab"), None, None),
        P("vocab", None),
        P("vocab", None),
        P(None, "vocab"),
        P(None, "vocab"),
        P(None, "vocab"),
        P(None, "vocab", None),
        P(None, "vocab", None),
        P(None, "vocab"),
        P(None, "vocab", None),
        P(None, "vocab", None),
    )
    return jax.shard_map(
        on_device, mesh=mesh, in_specs=in_specs, out_specs=out_specs, check_vma=False
    )
```

profile of v0, /device:TPU:0, one launch (start us, length us, event | category | flops | bytes accessed | tf_op | source)
XLA Modules:
  0.0 1287.9 jit_solution(16295583784691700822)
XLA Ops:
  14.1 13.5 %all_to_all.22 = s32[8,1,128]{2,1,0:T(1,128)S(1)} all-to-all(s32[8,1,128]{2,1,0:T(1,128)S(1)} %bitcast.274), channel_id=1, replica_groups=mesh['dp'=4,'vocab'=8] {'vocab'}, dimensions={0} | all-to-all | bytes 8192 | tf_op jit(solution)/shard_map/all_to_all | solution.py:149
  39.4 33.8 %all-to-all-done.1 = bf16[8,128,768]{2,1,0:T(8,128)(2,1)S(1)} async-done(((bf16[8,128,768]{2,1,0:T(8,128)(2,1)}), bf16[8,128,768]{2,1,0:T(8,128)(2,1)S(1)}, u32[]{:S(2)}, u32[]{:S(2)}) %all-to-all-start.1) | async-done | bytes 1572896 | tf_op jit(solution)/shard_map/all_to_all | solution.py:151
  103.3 21.3 %multiply_convert_fusion.3 = (bf16[512,3072]{1,0:T(8,128)(2,1)S(1)}, f32[512,3072]{1,0:T(8,128)}, f32[512,3072]{1,0:T(8,128)}) fusion(f32[3072]{0:T(1024)S(1)} %bitcast.275, bf16[2,768,3072]{2,1,0:T(8,128)(2,1)} %param.25, f32[512,768]{1,0:T(8,128)S(1)} %get-tuple-element.191, f32[768]{0:T(1024)S(1)} %get-tuple-element.142, ...), kind=kOutput, calls=%fused_computation.47 | convolution fusion | flops 2521694208 | bytes 22042624 | tf_op jit(solution)/shard_map/dot_general | solution.py:187
  139.7 7.4 fusion.112
  148.6 20.9 %multiply_convert_fusion.2 = (bf16[512,3072]{1,0:T(8,128)(2,1)S(1)}, f32[512,3072]{1,0:T(8,128)}, f32[512,3072]{1,0:T(8,128)}) fusion(f32[3072]{0:T(1024)S(1)} %bitcast.277, bf16[2,768,3072]{2,1,0:T(8,128)(2,1)} %param.25, f32[512,768]{1,0:T(8,128)S(1)} %get-tuple-element.198, f32[768]{0:T(1024)S(1)} %get-tuple-element.136, ...), kind=kOutput, calls=%fused_computation.34 | convolution fusion | flops 2521694208 | bytes 22042624 | tf_op jit(solution)/shard_map/dot_general | solution.py:187
  176.1 10.0 fusion.173
  197.0 10.6 multiply_reduce_fusion.1
  229.8 8.5 fusion.174
  250.1 10.8 multiply_reduce_fusion
  303.7 7.5 fusion.43
  315.5 8.3 pad_maximum_fusion.1
  324.4 7.6 fusion.40
  336.9 8.3 pad_maximum_fusion
  368.2 45.0 %all-to-all-done.2 = bf16[8,128,768]{2,1,0:T(8,128)(2,1)} async-done(((bf16[8,128,768]{2,1,0:T(8,128)(2,1)}), bf16[8,128,768]{2,1,0:T(8,128)(2,1)}, u32[]{:S(2)}, u32[]{:S(2)}) %all-to-all-start.2) | async-done | bytes 1572896 | tf_op jit(solution)/shard_map/all_to_all | solution.py:291
  413.2 9.8 scatter_custom_fusion.2
  426.2 19.9 %reduce-scatter.22.cloned.1.call-done = bf16[2,96,768]{2,1,0:T(8,128)(2,1)} async-done(((bf16[2,768,768]{2,1,0:T(8,128)(2,1)}), bf16[2,96,768]{2,1,0:T(8,128)(2,1)}) %reduce-scatter.22.cloned.1.call-update) | async-done | bytes 294928 | tf_op jit(solution)/shard_map/reduce_scatter | solution.py:307
  446.0 132.2 %reduce-scatter.20.cloned.1.call-done = bf16[2,96,2304]{2,1,0:T(8,128)(2,1)} async-done(((bf16[2,768,2304]{2,1,0:T(8,128)(2,1)}), bf16[2,96,2304]{2,1,0:T(8,128)(2,1)}) %reduce-scatter.20.cloned.1.call-update) | async-done | bytes 884752 | tf_op jit(solution)/shard_map/reduce_scatter | solution.py:304
  578.3 166.0 %reduce-scatter.26.cloned.1.call-done = bf16[2,384,768]{2,1,0:T(8,128)(2,1)} async-done(((bf16[2,3072,768]{2,1,0:T(8,128)(2,1)}), bf16[2,384,768]{2,1,0:T(8,128)(2,1)}) %reduce-scatter.26.cloned.1.call-update) | async-done | bytes 1179664 | tf_op jit(solution)/shard_map/reduce_scatter | solution.py:313
  744.3 166.0 %reduce-scatter.24.cloned.1.call-done = bf16[2,96,3072]{2,1,0:T(8,128)(2,1)} async-done(((bf16[2,768,3072]{2,1,0:T(8,128)(2,1)}), bf16[2,96,3072]{2,1,0:T(8,128)(2,1)}) %reduce-scatter.24.cloned.1.call-update) | async-done | bytes 1179664 | tf_op jit(solution)/shard_map/reduce_scatter | solution.py:310
  910.3 63.9 %reduce-scatter.28.cloned.1.call-done = bf16[96,2]{1,0:T(8,128)(2,1)} async-done(((bf16[768,2]{1,0:T(8,128)(2,1)}), bf16[96,2]{1,0:T(8,128)(2,1)}) %reduce-scatter.28.cloned.1.call-update) | async-done | bytes 400
  975.0 63.2 %reduce-scatter.30.cloned.1.call-done = bf16[96,5]{1,0:T(8,128)(2,1)} async-done(((bf16[768,5]{1,0:T(8,128)(2,1)}), bf16[96,5]{1,0:T(8,128)(2,1)}) %reduce-scatter.30.cloned.1.call-update) | async-done | bytes 976
  1039.0 64.6 %reduce-scatter.34.cloned.1.call-done = bf16[384,2]{1,0:T(8,128)(2,1)} async-done(((bf16[3072,2]{1,0:T(8,128)(2,1)}), bf16[384,2]{1,0:T(8,128)(2,1)}) %reduce-scatter.34.cloned.1.call-update) | async-done | bytes 1552
  1104.5 62.7 %reduce-scatter.32.cloned.1.call-done = bf16[96,13]{1,0:T(8,128)(2,1)} async-done(((bf16[768,13]{1,0:T(8,128)(2,1)}), bf16[96,13]{1,0:T(8,128)(2,1)}) %reduce-scatter.32.cloned.1.call-update) | async-done | bytes 2512
  1176.2 94.9 %all-reduce.4.cloned.1.call-done = (bf16[960,768]{1,0:T(8,128)(2,1)}, bf16[64,768]{1,0:T(8,128)(2,1)}, bf16[2,96,2304]{2,1,0:T(8,128)(2,1)}, bf16[2,96,768]{2,1,...) async-done(((bf16[960,768]{1,0:T(8,128)(2,1)}, bf16[64,768]{1,0:T(8,128)(2,1)}, bf16[2,96,2304]{2,1,0:T(8,128)(2,1)}, ...) | async-done | bytes 5111824 | tf_op jit(solution)/shard_map/psum | solution.py:342
  (449 shorter events, 213.8 us)
Async XLA Ops:
  11.6 26.3 %copy-start.84 = (s32[512,1]{0,1:T(1,128)}, s32[512,1]{0,1:T(1,128)S(1)}, u32[]{:S(2)}) copy-start(s32[512,1]{0,1:T(1,128)S(1)} %compare_select_fusion.1) | copy-start | bytes 6148
  33.4 39.7 %all-to-all-start.1 = ((bf16[8,128,768]{2,1,0:T(8,128)(2,1)}), bf16[8,128,768]{2,1,0:T(8,128)(2,1)S(1)}, u32[]{:S(2)}, u32[]{:S(2)}) async-start(bf16[8,128,768]{2,1,0:T(8,128)(2,1)} %bitcast.243), calls=%async_computation.1 | async-start | bytes 3145728 | tf_op jit(solution)/shard_map/all_to_all | solution.py:151
  37.2 389.0 %reduce-scatter.18.cloned.1.call-start = ((), (), s32[]{:S(2)}) async-start(), calls=%async_computation.12 | async-start | bytes 884736 | tf_op jit(solution)/shard_map/reduce_scatter | solution.py:316
  38.5 63.1 %copy-start.86 = (pred[512]{0:T(512)(128)(4,1)}, pred[512]{0:T(512)(128)(4,1)S(1)}, u32[]{:S(2)}) copy-start(pred[512]{0:T(512)(128)(4,1)S(1)} %get-tuple-element.155) | copy-start | bytes 1540
  38.5 63.1 %copy-start.58 = (f32[768]{0:T(1024)}, f32[768]{0:T(1024)S(1)}, u32[]{:S(2)}) copy-start(f32[768]{0:T(1024)S(1)} %get-tuple-element.152) | copy-start | bytes 9220
  38.5 63.1 %copy-start.60 = (f32[768]{0:T(1024)}, f32[768]{0:T(1024)S(1)}, u32[]{:S(2)}) copy-start(f32[768]{0:T(1024)S(1)} %get-tuple-element.153) | copy-start | bytes 9220
  39.3 62.4 %copy-start.73 = (f32[768]{0:T(1024)}, f32[768]{0:T(1024)S(1)}, u32[]{:S(2)}) copy-start(f32[768]{0:T(1024)S(1)} %get-tuple-element.222) | copy-start | bytes 9220
  39.3 62.4 %copy-start.93 = (f32[768]{0:T(1024)}, f32[768]{0:T(1024)S(1)}, u32[]{:S(2)}) copy-start(f32[768]{0:T(1024)S(1)} %get-tuple-element.146) | copy-start | bytes 9220
  39.3 85.3 %copy-start.71 = (f32[768]{0:T(1024)}, f32[768]{0:T(1024)S(1)}, u32[]{:S(2)}) copy-start(f32[768]{0:T(1024)S(1)} %get-tuple-element.223) | copy-start | bytes 9220
  39.3 85.3 %copy-start.91 = (f32[768]{0:T(1024)}, f32[768]{0:T(1024)S(1)}, u32[]{:S(2)}) copy-start(f32[768]{0:T(1024)S(1)} %get-tuple-element.142) | copy-start | bytes 9220
  39.3 107.7 %copy-start.95 = (f32[768]{0:T(1024)}, f32[768]{0:T(1024)S(1)}, u32[]{:S(2)}) copy-start(f32[768]{0:T(1024)S(1)} %get-tuple-element.140) | copy-start | bytes 9220
  39.3 130.1 %copy-start.89 = (f32[768]{0:T(1024)}, f32[768]{0:T(1024)S(1)}, u32[]{:S(2)}) copy-start(f32[768]{0:T(1024)S(1)} %get-tuple-element.136) | copy-start | bytes 9220
  75.2 26.5 %copy-start.4 = (bf16[512,768]{1,0:T(8,128)(2,1)}, bf16[512,768]{1,0:T(8,128)(2,1)S(1)}, u32[]{:S(2)}) copy-start(bf16[512,768]{1,0:T(8,128)(2,1)S(1)} %gather_fusion.1) | copy-start | bytes 2359300
  148.2 43.5 %copy-start.27 = (f32[512,768]{1,0:T(8,128)}, f32[512,768]{1,0:T(8,128)S(1)}, u32[]{:S(2)}) copy-start(f32[512,768]{1,0:T(8,128)S(1)} %get-tuple-element.198) | copy-start | bytes 4718596
  286.4 159.7 %reduce-scatter.22.cloned.1.call-start = ((), (), s32[]{:S(2)}) async-start(), calls=%async_computation.14 | async-start | bytes 2654208 | tf_op jit(solution)/shard_map/reduce_scatter | solution.py:307
  292.6 285.7 %reduce-scatter.20.cloned.1.call-start = ((), (), s32[]{:S(2)}) async-start(), calls=%async_computation.13 | async-start | bytes 7962624 | tf_op jit(solution)/shard_map/reduce_scatter | solution.py:304
  303.6 440.7 %reduce-scatter.26.cloned.1.call-start = ((), (), s32[]{:S(2)}) async-start(), calls=%async_computation.16 | async-start | bytes 10616832 | tf_op jit(solution)/shard_map/reduce_scatter | solution.py:313
  323.8 586.5 %reduce-scatter.24.cloned.1.call-start = ((), (), s32[]{:S(2)}) async-start(), calls=%async_computation.15 | async-start | bytes 10616832 | tf_op jit(solution)/shard_map/reduce_scatter | solution.py:310
  353.4 59.8 %all-to-all-start.2 = ((bf16[8,128,768]{2,1,0:T(8,128)(2,1)}), bf16[8,128,768]{2,1,0:T(8,128)(2,1)}, u32[]{:S(2)}, u32[]{:S(2)}) async-start(bf16[8,128,768]{2,1,0:T(8,128)(2,1)} %bitcast.242), calls=%async_computation.2 | async-start | bytes 3145728 | tf_op jit(solution)/shard_map/all_to_all | solution.py:291
  357.8 616.4 %reduce-scatter.28.cloned.1.call-start = ((), (), s32[]{:S(2)}) async-start(), calls=%async_computation.17 | async-start | bytes 221184
  358.8 679.4 %reduce-scatter.30.cloned.1.call-start = ((), (), s32[]{:S(2)}) async-start(), calls=%async_computation.18 | async-start | bytes 221184
  360.0 743.5 %reduce-scatter.34.cloned.1.call-start = ((), (), s32[]{:S(2)}) async-start(), calls=%async_computation.20 | async-start | bytes 884736
  361.4 805.9 %reduce-scatter.32.cloned.1.call-start = ((), (), s32[]{:S(2)}) async-start(), calls=%async_computation.19 | async-start | bytes 221184
  367.8 903.2 %all-reduce.4.cloned.1.call-start = ((), (), s32[]{:S(2)}) async-start(), calls=%async_computation.21 | async-start | bytes 10223616 | tf_op jit(solution)/shard_map/psum | solution.py:342
  (119 other events, 877.6 us)
Sparse Core Ops, SparseCore 0:
  286.5 61.2 reduce-scatter.17
  352.2 93.7 reduce-scatter.21
  450.2 128.0 reduce-scatter.19
  581.7 162.5 reduce-scatter.25
  747.7 162.5 reduce-scatter.23
  914.0 60.1 reduce-scatter.27
  978.0 60.1 reduce-scatter.29
  1042.0 61.4 reduce-scatter.33
  1107.1 60.0 reduce-scatter.31
  1170.7 100.3 all-reduce.3
where the time goes:
time: 1300 us; the launch traced here: 1290 us
  waiting for transfers between devices  912 us (70%)
  matrix products  189 us (15%)
  other arithmetic  92.1 us (7%)
  local copies, waits for them, and re-layouts  48.4 us (4%)
  blocking collectives  19.3 us (1%)
  between operations  17.4 us (1%)
    unnamed x14, waiting for transfers between devices  255 us
    reduce_scatter x1, waiting for transfers between devices, on_device(): lax.psum_scatter(two_sums.astype(jnp.bfloat16), 'vocab', scatter_dimensio...  166 us
    reduce_scatter x1, waiting for transfers between devices, on_device(): lax.psum_scatter(one_sums.astype(jnp.bfloat16), 'vocab', scatter_dimensio...  166 us
    reduce_scatter x1, waiting for transfers between devices, on_device(): lax.psum_scatter(qkv_sums.astype(jnp.bfloat16), 'vocab', scatter_dimensio...  132 us
    psum x1, waiting for transfers between devices, on_device(): lax.psum(table_part.astype(jnp.bfloat16), 'dp').astype(jnp.float32)  94.9 us
    all_to_all x1, waiting for transfers between devices, on_device(): lax.all_to_all(outgoing.reshape(owners, slot_count, model_width).astype(j...  45 us
    dot_general x8, matrix products, contract_cols(): lax.dot_general(left_op, right_op, (((1,), (1,)), ((), ())), preferred_el...  43.9 us
    dot_general x2, matrix products, on_device(): jnp.dot(middle_low, w_ff1[layer_num], preferred_element_type=jnp.float32)  42.1 us
  transfers between devices with their start and end apart: 12, of which 11 were waited for; matrix products, arithmetic and copies ran while one was open for 7% of the time, Pallas kernels for 0%

commit v1 on v0

v1 whole, which is shorter than its diff:
```python
import jax
import jax.numpy as jnp
from jax import lax
from jax.sharding import PartitionSpec as P

HEADS = 12
HEAD_DIM = 64
NL = 2

norm_eps = 1e-12
AXES = ("dp", "vocab")


def normalize(inputs):
    centered = inputs - jnp.mean(inputs, axis=-1, keepdims=True)
    spread = lax.rsqrt(jnp.mean(centered * centered, axis=-1, keepdims=True) + norm_eps)
    return (centered * spread, spread)


def norm_back(grad_out, normed, spread, gain_row):
    scaled = grad_out * gain_row
    return spread * (
        scaled
        - jnp.mean(scaled, axis=-1, keepdims=True)
        - normed * jnp.mean(scaled * normed, axis=-1, keepdims=True)
    )


def contract_rows(left_op, right_op):
    return lax.dot_general(
        left_op, right_op, (((0,), (0,)), ((), ())), preferred_element_type=jnp.float32
    )


def contract_cols(left_op, right_op):
    return lax.dot_general(
        left_op, right_op, (((1,), (1,)), ((), ())), preferred_element_type=jnp.float32
    )


def split_heads(matrix):
    return matrix.reshape(matrix.shape[0], HEADS, HEAD_DIM)


def activate(inputs):
    return jax.nn.gelu(inputs, approximate=False)


def score_block(queries, keys_in, length):
    scores = jnp.einsum(
        "qhd,khd->hqk",
        split_heads(queries),
        split_heads(keys_in),
        preferred_element_type=jnp.float32,
    ) * HEAD_DIM ** (-0.5)
    visible = jnp.arange(keys_in.shape[0])[None, None, :] < length
    return jnp.where(visible, scores, -1e30)


def attend(queries, keys_in, values, length):
    scores = score_block(queries, keys_in, length)
    top_score = jnp.max(scores, axis=-1, keepdims=True)
    weights = jnp.exp(scores - top_score)
    row_total = jnp.sum(weights, axis=-1, keepdims=True)
    softened = (weights / row_total).astype(jnp.bfloat16)
    context = jnp.einsum(
        "hqk,khd->qhd", softened, split_heads(values), preferred_element_type=jnp.float32
    )
    return (
        context.reshape(queries.shape).astype(jnp.bfloat16),
        top_score[..., 0] + jnp.log(row_total[..., 0]),
    )


def attend_back(queries, keys_in, values, length, total_log, grad_context):
    scores = score_block(queries, keys_in, length)
    softened = jnp.exp(scores - total_log[..., None])
    grad_split = split_heads(grad_context)
    grad_probs = jnp.einsum(
        "qhd,khd->hqk", grad_split, split_heads(values), preferred_element_type=jnp.float32
    )
    grad_values = jnp.einsum(
        "hqk,qhd->khd",
        softened.astype(jnp.bfloat16),
        grad_split,
        preferred_element_type=jnp.float32,
    )
    weighted = jnp.sum(softened * grad_probs, axis=-1, keepdims=True)
    grad_scores = (softened * (grad_probs - weighted)).astype(jnp.bfloat16)
    score_scale = HEAD_DIM ** (-0.5)
    grad_queries = (
        jnp.einsum(
            "hqk,khd->qhd", grad_scores, split_heads(keys_in), preferred_element_type=jnp.float32
        )
        * score_scale
    )
    grad_keys = (
        jnp.einsum(
            "hqk,qhd->khd", grad_scores, split_heads(queries), preferred_element_type=jnp.float32
        )
        * score_scale
    )
    return (
        grad_queries.reshape(queries.shape),
        grad_keys.reshape(queries.shape),
        grad_values.reshape(queries.shape),
    )


class Cube:
    def __init__(self, dp_size, vocab_size):
        self.dp_size = dp_size
        self.vocab_size = vocab_size
        self.dp_bits = dp_size.bit_length() - 1
        self.vocab_bits = vocab_size.bit_length() - 1
        assert 1 << self.dp_bits == dp_size and 1 << self.vocab_bits == vocab_size
        self.vocab_masks = [6 if bit == 2 else 1 << bit for bit in range(self.vocab_bits)]

    def permute(self, value, dp_mask, vocab_mask):
        count = self.vocab_size
        pairs = [
            (d * count + v, (d ^ dp_mask) * count + (v ^ vocab_mask))
            for d in range(self.dp_size)
            for v in range(count)
        ]
        return lax.ppermute(value, AXES, pairs)

    def core(self, value):
        return self.permute(value, 1, 0)

    def my_bit(self, bit):
        place = lax.axis_index("vocab")
        value = (place >> bit) & 1
        if bit == 1 and self.vocab_bits > 2:
            value = value ^ ((place >> 2) & 1)
        return value

    def to_blocks(self, matrix):
        rows, cols = matrix.shape
        part = rows // self.vocab_size
        if self.vocab_bits > 2:
            wide = matrix.reshape(self.vocab_size // 8, 2, 2, 2 * part, cols)
            wide = jnp.stack([wide[:, 0], wide[:, 1, ::-1]], axis=1)
        else:
            wide = matrix
        return wide.reshape((2,) * self.vocab_bits + (part, cols))

    def reduce(self, blocks, order):
        left = list(reversed(range(self.vocab_bits)))
        halved = False
        for dim in order:
            if dim == "y" and len(left) > 0 and self.dp_bits == 2:
                halved = True
                shape = blocks.shape
                rows = shape[-2] // 2
                blocks = blocks.reshape(shape[:-2] + (2, rows, shape[-1]))
                axis = len(shape) - 2
                mine = (lax.axis_index("dp") >> 1) & 1
                keep = lax.dynamic_index_in_dim(blocks, mine, axis, keepdims=False)
                send = lax.dynamic_index_in_dim(blocks, 1 - mine, axis, keepdims=False)
                blocks = self.add(keep, self.permute(send, 2, 0))
            elif dim == "y":
                for bit in range(1, self.dp_bits):
                    blocks = self.add(blocks, self.permute(blocks, 1 << bit, 0))
            else:
                axis = left.index(dim)
                left.pop(axis)
                mine = self.my_bit(dim)
                keep = lax.dynamic_index_in_dim(blocks, mine, axis, keepdims=False)
                send = lax.dynamic_index_in_dim(blocks, 1 - mine, axis, keepdims=False)
                blocks = self.add(keep, self.permute(send, 0, self.vocab_masks[dim]))
        if halved:
            other = self.permute(blocks, 2, 0)
            mine = ((lax.axis_index("dp") >> 1) & 1) == 0
            blocks = jnp.concatenate(
                [jnp.where(mine, blocks, other), jnp.where(mine, other, blocks)], axis=0
            )
        return blocks

    def add(self, left_op, right_op):
        return (left_op.astype(jnp.float32) + right_op.astype(jnp.float32)).astype(jnp.bfloat16)

    def halves(self, matrix):
        mine = lax.axis_index("dp") & 1
        width = matrix.shape[1] // 2
        keep = lax.dynamic_slice_in_dim(matrix, mine * width, width, 1)
        send = lax.dynamic_slice_in_dim(matrix, (1 - mine) * width, width, 1)
        return keep, send

    def join_core(self, share):
        other = self.core(share)
        mine = (lax.axis_index("dp") & 1) == 0
        return jnp.concatenate(
            [jnp.where(mine, share, other), jnp.where(mine, other, share)], axis=-1
        ).astype(jnp.float32)


def both(own, other):
    return jnp.concatenate([own, other], axis=0)


def on_device(
    cube,
    token_ids,
    lengths,
    type_ids,
    word_table,
    pos_table,
    type_table,
    gains,
    shifts,
    w_qkv,
    w_out,
    b_ff1,
    w_ff1,
    w_ff2,
    cotangent,
):
    owners = cube.vocab_size
    local_rows, model_width = word_table.shape
    assert token_ids.shape[0] == 1
    token_count = token_ids.shape[1]
    slot_count = 2 * token_count // owners
    slots = owners * slot_count
    gain_vals = gains.astype(jnp.float32)
    shift_vals = shifts.astype(jnp.float32)
    ffn_bias = b_ff1.astype(jnp.float32)
    flat_ids = token_ids.reshape(token_count)
    me = lax.axis_index("vocab")

    all_ids = lax.all_to_all(
        jnp.broadcast_to(flat_ids[None, :], (owners, token_count)),
        "vocab",
        split_axis=0,
        concat_axis=0,
        tiled=True,
    )
    local = all_ids - me * local_rows
    here = (local >= 0) & (local < local_rows)
    rank = jnp.cumsum(here.astype(jnp.int32), axis=1) - 1
    slot_hit = (
        jnp.where(here, rank, -1)[:, None, :]
        == jnp.arange(slot_count, dtype=jnp.int32)[None, :, None]
    )
    asked = jnp.sum(jnp.where(slot_hit, local[:, None, :] + 1, 0), axis=2).reshape(slots) - 1
    row_hit = (asked[:, None] == jnp.arange(local_rows, dtype=jnp.int32)[None, :]).astype(
        jnp.bfloat16
    )
    found_rows = jnp.dot(row_hit, word_table, preferred_element_type=jnp.float32).astype(
        jnp.bfloat16
    )
    replies = lax.all_to_all(
        found_rows.reshape(owners, slot_count, model_width),
        "vocab",
        split_axis=0,
        concat_axis=0,
        tiled=True,
    ).reshape(slots, model_width)
    owner_of = flat_ids // local_rows
    chosen = (owner_of[:, None] == jnp.arange(owners, dtype=jnp.int32)[None, :]).astype(jnp.int32)
    before = jnp.cumsum(chosen, axis=0) - chosen
    slot_of = owner_of * slot_count + jnp.sum(before * chosen, axis=1)
    dispatch = (slot_of[:, None] == jnp.arange(slots, dtype=jnp.int32)[None, :]).astype(
        jnp.bfloat16
    )
    word_rows = jnp.dot(dispatch, replies, preferred_element_type=jnp.float32)
    type_flat = type_ids.reshape(token_count)
    type_rows = jnp.where(
        type_flat[:, None] == 1,
        type_table[1].astype(jnp.float32)[None, :],
        type_table[0].astype(jnp.float32)[None, :],
    )
    embedded = word_rows + pos_table.astype(jnp.float32) + type_rows
    normed_emb, spread_emb = normalize(embedded)
    states = normed_emb * gain_vals[0] + shift_vals[0]
    saved_acts = []
    length = lengths[0]
    for layer_num in range(NL):
        shift_base = 1 + 6 * layer_num
        states_low = states.astype(jnp.bfloat16)
        states_other = cube.core(states_low)
        mixed_qkv = jnp.dot(states_low, w_qkv[layer_num], preferred_element_type=jnp.float32)
        queries = (mixed_qkv[:, :model_width] + shift_vals[shift_base]).astype(jnp.bfloat16)
        keys_in = mixed_qkv[:, model_width : 2 * model_width].astype(jnp.bfloat16)
        values = (mixed_qkv[:, 2 * model_width :] + shift_vals[shift_base + 1]).astype(jnp.bfloat16)
        context, total_log = attend(queries, keys_in, values, length)
        context_other = cube.core(context)
        attended = (
            jnp.dot(context, w_out[layer_num], preferred_element_type=jnp.float32)
            + shift_vals[shift_base + 2]
        )
        normed_one, spread_one = normalize(states + attended)
        middle = normed_one * gain_vals[1 + 2 * layer_num] + shift_vals[shift_base + 3]
        middle_low = middle.astype(jnp.bfloat16)
        middle_other = cube.core(middle_low)
        hidden_pre = (
            jnp.dot(middle_low, w_ff1[layer_num], preferred_element_type=jnp.float32)
            + ffn_bias[layer_num]
        )
        active = activate(hidden_pre).astype(jnp.bfloat16)
        active_other = cube.core(active)
        ffn_out = (
            jnp.dot(active, w_ff2[layer_num], preferred_element_type=jnp.float32)
            + shift_vals[shift_base + 4]
        )
        normed_two, spread_two = normalize(middle + ffn_out)
        saved_acts.append(
            (
                (states_low, states_other),
                (queries, keys_in, values),
                total_log,
                (context, context_other),
                normed_one,
                spread_one,
                (middle_low, middle_other),
                hidden_pre,
                (active, active_other),
                normed_two,
                spread_two,
            )
        )
        states = normed_two * gain_vals[2 + 2 * layer_num] + shift_vals[shift_base + 5]
    hidden_out = states.reshape(1, token_count, model_width).astype(jnp.bfloat16)
    grad_states = cotangent.reshape(token_count, model_width).astype(jnp.float32)
    gain_grads = [None] * (2 * NL + 1)
    shift_grads = [None] * (6 * NL + 1)
    bias_grads = [None] * NL
    layer_grads = [None] * NL
    bits = list(range(cube.vocab_bits))
    turn = lambda n: bits[n % len(bits) :] + bits[: n % len(bits)]
    for layer_num in reversed(range(NL)):
        (
            states_both,
            (queries, keys_in, values),
            total_log,
            context_both,
            normed_one,
            spread_one,
            middle_both,
            hidden_pre,
            active_both,
            normed_two,
            spread_two,
        ) = saved_acts[layer_num]
        shift_base = 1 + 6 * layer_num
        gain_grads[2 + 2 * layer_num] = jnp.sum(grad_states * normed_two, axis=0)
        shift_grads[shift_base + 5] = jnp.sum(grad_states, axis=0)
        grad_second = norm_back(grad_states, normed_two, spread_two, gain_vals[2 + 2 * layer_num])
        shift_grads[shift_base + 4] = jnp.sum(grad_second, axis=0)
        second_low = grad_second.astype(jnp.bfloat16)
        keep, send = cube.halves(second_low)
        grad_w_two = contract_rows(both(*active_both), both(keep, cube.core(send)))
        share_two = cube.reduce(
            cube.to_blocks(grad_w_two.astype(jnp.bfloat16)), ["y"] + turn(0)
        )
        grad_active = contract_cols(second_low, w_ff2[layer_num])
        grad_pre = jax.vjp(activate, hidden_pre)[1](grad_active)[0]
        bias_grads[layer_num] = jnp.sum(grad_pre, axis=0)
        pre_low = grad_pre.astype(jnp.bfloat16)
        keep, send = cube.halves(pre_low)
        grad_w_one = contract_rows(both(*middle_both), both(keep, cube.core(send)))
        share_one = cube.reduce(
            cube.to_blocks(grad_w_one.astype(jnp.bfloat16)), turn(1 + layer_num) + ["y"]
        )
        grad_middle = grad_second + contract_cols(pre_low, w_ff1[layer_num])
        gain_grads[1 + 2 * layer_num] = jnp.sum(grad_middle * normed_one, axis=0)
        shift_grads[shift_base + 3] = jnp.sum(grad_middle, axis=0)
        grad_first = norm_back(grad_middle, normed_one, spread_one, gain_vals[1 + 2 * layer_num])
        shift_grads[shift_base + 2] = jnp.sum(grad_first, axis=0)
        first_low = grad_first.astype(jnp.bfloat16)
        keep, send = cube.halves(first_low)
        grad_w_out = contract_rows(both(*context_both), both(keep, cube.core(send)))
        grad_context = contract_cols(first_low, w_out[layer_num]).astype(jnp.bfloat16)
        grad_queries, grad_keys, grad_values = attend_back(
            queries, keys_in, values, length, total_log, grad_context
        )
        shift_grads[shift_base] = jnp.sum(grad_queries, axis=0)
        shift_grads[shift_base + 1] = jnp.sum(grad_values, axis=0)
        grad_mixed = jnp.concatenate([grad_queries, grad_keys, grad_values], axis=1).astype(
            jnp.bfloat16
        )
        keep, send = cube.halves(grad_mixed)
        grad_w_qkv = contract_rows(both(*states_both), both(keep, cube.core(send)))
        share_mix = cube.reduce(
            cube.to_blocks(
                jnp.concatenate([grad_w_qkv, grad_w_out], axis=1).astype(jnp.bfloat16)
            ),
            turn(2 + 2 * layer_num) + ["y"],
        )
        grad_states = grad_first + contract_cols(grad_mixed, w_qkv[layer_num])
        layer_grads[layer_num] = (share_mix, share_one, share_two)
    gain_grads[0] = jnp.sum(grad_states * normed_emb, axis=0)
    shift_grads[0] = jnp.sum(grad_states, axis=0)
    grad_embedded = norm_back(grad_states, normed_emb, spread_emb, gain_vals[0])

    outgoing = lax.dot_general(
        dispatch,
        grad_embedded.astype(jnp.bfloat16),
        (((0,), (0,)), ((), ())),
        preferred_element_type=jnp.float32,
    ).astype(jnp.bfloat16)
    incoming = lax.all_to_all(
        outgoing.reshape(owners, slot_count, model_width),
        "vocab",
        split_axis=0,
        concat_axis=0,
        tiled=True,
    ).reshape(slots, model_width)
    table_part = contract_rows(row_hit, incoming).astype(jnp.bfloat16)
    keep, send = cube.halves(table_part)
    table_part = cube.add(keep, cube.core(send))
    for bit in range(1, cube.dp_bits):
        table_part = cube.add(table_part, cube.permute(table_part, 1 << bit, 0))
    table_out = cube.join_core(table_part)

    type_zero = jnp.sum(jnp.where(type_flat[:, None] == 0, grad_embedded, 0.0), axis=0)
    type_one = jnp.sum(jnp.where(type_flat[:, None] == 1, grad_embedded, 0.0), axis=0)
    small = jnp.concatenate(
        [
            jnp.stack([type_zero, type_one] + gain_grads + shift_grads).reshape(
                -1, owners, model_width // owners
            ),
            jnp.stack(bias_grads).reshape(NL, owners, -1, model_width // owners)
            .transpose(0, 2, 1, 3)
            .reshape(-1, owners, model_width // owners),
        ],
        axis=0,
    )
    small_rows = small.shape[0]
    small = small.transpose(1, 0, 2).reshape(owners, -1)
    packed_rows = -(-small.shape[1] // model_width)
    small = jnp.pad(small, ((0, 0), (0, packed_rows * model_width - small.shape[1])))
    pos_rows = token_count // owners
    packed = jnp.concatenate(
        [
            grad_embedded.reshape(owners, pos_rows, model_width),
            small.reshape(owners, packed_rows, model_width),
        ],
        axis=1,
    ).astype(jnp.bfloat16)
    keep, send = cube.halves(packed.reshape(-1, model_width))
    packed = cube.add(keep, cube.core(send))
    share_pack = cube.reduce(cube.to_blocks(packed), turn(1) + ["y"])

    mix_out, one_out, two_out = [], [], []
    for share_mix, share_one, share_two in layer_grads:
        wide = 3 * model_width // 2
        mix_out.append((share_mix[:, :wide], share_mix[:, wide:]))
        one_out.append(share_one)
        two_out.append(share_two)
    qkv_out = cube.join_core(jnp.stack([m[0] for m in mix_out]))
    wout_out = cube.join_core(jnp.stack([m[1] for m in mix_out]))
    one_out = cube.join_core(jnp.stack(one_out))
    two_out = cube.join_core(jnp.stack(two_out))
    pack_out = cube.join_core(share_pack)
    pos_out = pack_out[:pos_rows]
    small_out = pack_out[pos_rows:].reshape(-1)[: small_rows * (model_width // owners)].reshape(
        small_rows, model_width // owners
    )
    type_out = small_out[:2]
    gain_out = small_out[2 : 2 + 2 * NL + 1]
    shift_out = small_out[2 + 2 * NL + 1 : 2 + 2 * NL + 1 + 6 * NL + 1]
    bias_out = small_out[2 + 2 * NL + 1 + 6 * NL + 1 :].reshape(NL, -1)
    return (
        hidden_out,
        table_out,
        pos_out,
        type_out,
        gain_out,
        shift_out,
        qkv_out,
        wout_out,
        bias_out,
        one_out,
        two_out,
    )


def solution(mesh):
    cube = Cube(mesh.shape["dp"], mesh.shape["vocab"])
    in_specs = (
        P(("dp", "vocab"), None),
        P(("dp", "vocab")),
        P(("dp", "vocab"), None),
        P("vocab", None),
        P(),
        P(),
        P(),
        P(),
        P(),
        P(),
        P(),
        P(),
        P(),
        P(("dp", "vocab"), None, None),
    )
    out_specs = (
        P(("dp", "vocab"), None, None),
        P("vocab", None),
        P("vocab", None),
        P(None, "vocab"),
        P(None, "vocab"),
        P(None, "vocab"),
        P(None, "vocab", None),
        P(None, "vocab", None),
        P(None, "vocab"),
        P(None, "vocab", None),
        P(None, "vocab", None),
    )

    def run(*args):
        return on_device(cube, *args)

    return jax.shard_map(run, mesh=mesh, in_specs=in_specs, out_specs=out_specs, check_vma=False)
```

time: 1300 us -> 710 us (0.55)
  waiting for transfers between devices: 912 us -> 236 us
  starting transfers between devices: 9.33 us -> 103 us
  local copies, waits for them, and re-layouts: 48.4 us -> 78.7 us
  blocking collectives: 19.3 us -> 0 us
  matrix products: 189 us -> 205 us
  between operations: 17.4 us -> 3.88 us
  other arithmetic: 92.1 us -> 79 us
    reduce_scatter x5 -> x0, waiting for transfers between devices: 484 us -> none  [the longest x1 166 us: on_device(): lax.psum_scatter(two_sums.astype(jnp.bfloat16), 'vocab', scatter_dimensio...]
    unnamed x14 -> x0, waiting for transfers between devices: 255 us -> none
    ppermute x0 -> x55, waiting for transfers between devices: none -> 199 us  [permute(): return lax.ppermute(value, AXES, pairs)]
    psum x1 -> x0, waiting for transfers between devices: 94.9 us -> none  [on_device(): lax.psum(table_part.astype(jnp.bfloat16), 'dp').astype(jnp.float32)]
    ppermute x0 -> x55, starting transfers between devices: none -> 86.6 us  [permute(): return lax.ppermute(value, AXES, pairs)]
    all_to_all x2 -> x3, waiting for transfers between devices: 78.8 us -> 36.8 us  [the longest x1 32.8 us: on_device(): lax.all_to_all(found_rows.reshape(owners, slot_count, model_width), 'voca...]
    dynamic_slice x0 -> x12, local copies, waits for them, and re-layouts: none -> 13.8 us  [the longest x8 12.4 us: halves(): keep = lax.dynamic_slice_in_dim(matrix, mine * width, width, 1)]
    all_to_all x1 -> x0, blocking collectives: 13.5 us -> none  [on_device(): lax.all_to_all(requests, 'vocab', split_axis=0, concat_axis=0, tiled=True)]
  transfers between devices with their start and end apart: 12 -> 58, of which waited for: 11 -> 21; matrix products, arithmetic and copies ran while one was open for 7% -> 23% of each run, Pallas kernels for 0% -> 0%
where the time goes in v1:
time: 710 us; the launch traced here: 705 us
  waiting for transfers between devices  236 us (33%)
  matrix products  205 us (29%)
  starting transfers between devices  103 us (15%)
  other arithmetic  79 us (11%)
  local copies, waits for them, and re-layouts  78.7 us (11%)
    ppermute x55, waiting for transfers between devices, permute(): return lax.ppermute(value, AXES, pairs)  199 us
    ppermute x55, starting transfers between devices, permute(): return lax.ppermute(value, AXES, pairs)  86.6 us
    dot_general x9, matrix products, contract_rows(): lax.dot_general(left_op, right_op, (((0,), (0,)), ((), ())), preferred_el...  41.8 us
    dot_general x8, matrix products, contract_cols(): lax.dot_general(left_op, right_op, (((1,), (1,)), ((), ())), preferred_el...  39.5 us
    dot_general x2, matrix products, on_device(): jnp.dot(middle_low, w_ff1[layer_num], preferred_element_type=jnp.float32)  39.2 us
    all_to_all x1, waiting for transfers between devices, on_device(): lax.all_to_all(found_rows.reshape(owners, slot_count, model_width), 'voca...  32.8 us
    dot_general x2, matrix products, attend_back(): jnp.einsum('qhd,khd->hqk', grad_split, split_heads(values), preferred_ele...  22.7 us
    unnamed x271, local copies, waits for them, and re-layouts  22.5 us
  transfers between devices with their start and end apart: 58, of which 21 were waited for; matrix products, arithmetic and copies ran while one was open for 23% of the time, Pallas kernels for 0%

profile of v1, /device:TPU:0, one launch (start us, length us, event | category | flops | bytes accessed | tf_op | source)
XLA Modules:
  0.0 705.1 jit_solution(1444616542219085373)
XLA Ops:
  2.1 7.3 %all-to-all-start = ((s32[8,1,512]{2,1,0:T(1,128)}), s32[8,1,512]{2,1,0:T(1,128)S(1)}, u32[]{:S(2)}, u32[]{:S(2)}) async-start(s32[8,1,512]{2,1,0:T(1,128)} %broadcast_in_dim.138), calls=%async_computation | async-start | bytes 32768 | tf_op jit(solution)/shard_map/all_to_all | solution.py:231
  28.0 32.8 %all-to-all-done.1 = bf16[8,128,768]{2,1,0:T(8,128)(2,1)S(1)} async-done(((bf16[8,128,768]{2,1,0:T(8,128)(2,1)}), bf16[8,128,768]{2,1,0:T(8,128)(2,1)S(1)}, u32[]{:S(2)}, u32[]{:S(2)}) %all-to-all-start.1) | async-done | bytes 1572896 | tf_op jit(solution)/shard_map/all_to_all | solution.py:252
  94.3 20.2 %multiply_convert_fusion.3 = (bf16[512,3072]{1,0:T(8,128)(2,1)}, f32[512,3072]{1,0:T(8,128)}, f32[512,3072]{1,0:T(8,128)}) fusion(f32[3072]{0:T(1024)S(1)} %bitcast.417, bf16[512,768]{1,0:T(8,128)(2,1)} %fusion.155, bf16[2,768,3072]{2,1,0:T(8,128)(2,1)S(1)} %bitcast.429), kind=kOutput, calls=%fused_computation.47 | convolution fusion | flops 2519728128 | bytes 21245952 | tf_op jit(solution)/shard_map/dot_general | solution.py:297
  139.4 8.1 %fusion.152 = bf16[12,64,512]{2,1,0:T(8,128)(2,1)} fusion(bf16[512,12,64]{0,2,1:T(8,128)(2,1)} %bitcast.387, f32[12,512,512]{1,2,0:T(8,128)} %copy-done.3, f32[12,512]{1,0:T(8,128)S(1)} %fusion.1, f32[12,512]{1,0:T(8,128)S(1)} %get-tuple-element.139), kind=kOutput, calls=%fused_computation.249 | convolution fusion | flops 412483584 | bytes 14204928 | tf_op jit(solution)/shard_map/hqk,khd->qhd/dot_general | solution.py:66
  150.7 19.0 %multiply_convert_fusion.2 = (bf16[512,3072]{1,0:T(8,128)(2,1)S(1)}, f32[512,3072]{1,0:T(8,128)}, f32[512,3072]{1,0:T(8,128)}) fusion(f32[3072]{0:T(1024)S(1)} %bitcast.419, bf16[512,768]{1,0:T(8,128)(2,1)S(1)} %fusion.157, bf16[2,768,3072]{2,1,0:T(8,128)(2,1)} %param.25), kind=kOutput, calls=%fused_computation.34 | convolution fusion | flops 2519728128 | bytes 21245952 | tf_op jit(solution)/shard_map/dot_general | solution.py:297
  175.3 8.0 %fusion.229 = (bf16[3072]{0:T(1024)(128)(2,1)S(1)}, bf16[512,3072]{1,0:T(8,128)(2,1)S(1)}) fusion(f32[512,3072]{1,0:T(8,128)} %get-tuple-element.64, bf16[512,768]{1,0:T(8,128)(2,1)S(1)} %convert_element_type.586, bf16[2,3072,768]{2,1,0:T(8,128)(2,1)S(1)} %bitcast.425, f32[512,3072]{1,0:T(8,128)} %get-tuple-element.143, f32[3072]{0:T(1024)S(1)} %bitcast.420), kind=kOutput, calls=%fused_computation.492 | convolution fusion | flops 2441081856 | bytes 21252096 | tf_op jit(solution)/shard_map/dot_general | solution.py:36
  183.3 6.6 multiply_reduce_fusion.2
  196.6 12.3 %multiply_reduce_fusion.1 = (f32[12,512]{1,0:T(8,128)S(1)}, f32[12,512,512]{1,2,0:T(8,128)}) fusion(f32[12,512,512]{1,2,0:T(8,128)} %copy-done.3, f32[12,512]{1,0:T(8,128)S(1)} %log_add_fusion.1, bf16[512,12,64]{0,2,1:T(8,128)(2,1)} %bitcast.372, bf16[512,12,64]{0,2,1:T(8,128)(2,1)} %bitcast.388), kind=kOutput, calls=%fused_computation.4 | convolution fusion | flops 412084224 | bytes 26787840 | tf_op jit(solution)/shard_map/qhd,khd->hqk/dot_general | solution.py:79
  208.9 7.1 %multiply_convert_fusion.1 = bf16[12,512,512]{1,2,0:T(8,128)(2,1)S(1)} fusion(f32[12,512,512]{1,2,0:T(8,128)} %get-tuple-element.151, f32[12,512,512]{1,2,0:T(8,128)S(1)} %bitcast.356, f32[12,512]{1,0:T(8,128)S(1)} %get-tuple-element.150, f32[12,512]{1,0:T(8,128)S(1)} %log_add_fusion.1), kind=kLoop, calls=%fused_computation.3 | loop fusion | flops 12582912 | bytes 31506432 | tf_op jit(solution)/shard_map/convert_element_type | solution.py:89
  232.5 8.7 %fusion.228 = (bf16[3072]{0:T(1024)(128)(2,1)S(1)}, bf16[512,3072]{1,0:T(8,128)(2,1)S(1)}) fusion(f32[512,3072]{1,0:T(8,128)} %get-tuple-element.66, bf16[512,768]{1,0:T(8,128)(2,1)S(1)} %convert_element_type.592, bf16[2,3072,768]{2,1,0:T(8,128)(2,1)S(1)} %bitcast.427, f32[512,3072]{1,0:T(8,128)} %get-tuple-element.136, f32[3072]{0:T(1024)S(1)} %bitcast.418), kind=kOutput, calls=%fused_computation.491 | convolution fusion | flops 2441081856 | bytes 21252096 | tf_op jit(solution)/shard_map/dot_general | solution.py:36
  250.6 10.5 %multiply_reduce_fusion = (f32[12,512]{1,0:T(8,128)S(1)}, f32[12,512,512]{1,2,0:T(8,128)}) fusion(f32[12,512,512]{1,2,0:T(8,128)} %copy-done.2, f32[12,512]{1,0:T(8,128)S(1)} %log_add_fusion, bf16[512,12,64]{0,2,1:T(8,128)(2,1)S(1)} %bitcast.374, bf16[512,12,64]{0,2,1:T(8,128)(2,1)S(1)} %bitcast.386), kind=kOutput, calls=%fused_computation.1 | convolution fusion | flops 412084224 | bytes 26787840 | tf_op jit(solution)/shard_map/qhd,khd->hqk/dot_general | solution.py:79
  263.1 7.1 %multiply_convert_fusion = bf16[12,512,512]{1,2,0:T(8,128)(2,1)S(1)} fusion(f32[12,512,512]{1,2,0:T(8,128)} %get-tuple-element.160, f32[12,512,512]{1,2,0:T(8,128)S(1)} %bitcast.354, f32[12,512]{1,0:T(8,128)S(1)} %get-tuple-element.159, f32[12,512]{1,0:T(8,128)S(1)} %log_add_fusion), kind=kLoop, calls=%fused_computation | loop fusion | flops 12582912 | bytes 31506432 | tf_op jit(solution)/shard_map/convert_element_type | solution.py:89
  391.0 17.2 %collective-permute-done.13 = bf16[2,2,96,1536]{3,2,1,0:T(8,128)(2,1)} collective-permute-done((bf16[2,2,96,1536]{3,2,1,0:T(8,128)(2,1)}, bf16[2,2,96,1536]{3,2,1,0:T(8,128)(2,1)}, u32[]{:S(2)}, u32[]{:S(2)}) %collective-permute-start.13) | collective-permute-done | bytes 1179680 | tf_op jit(solution)/shard_map/ppermute | solution.py:126
  408.2 24.4 %collective-permute-start.29 = (bf16[2,2,96,1536]{3,2,1,0:T(8,128)(2,1)}, bf16[2,2,96,1536]{3,2,1,0:T(8,128)(2,1)}, u32[]{:S(2)}, u32[]{:S(2)}) collective-permute-start(bf16[2,2,96,1536]{3,2,1,0:T(8,128)(2,1)} %dynamic-slice_bitcast_fusion.2), channel_id=1, source_target_pairs={{0,2},{1,3},{2,0},{3,1},{4,6},{5,7},{6,4},{7,5},{8,10},{9,11},{10,... | collective-permute-start | bytes 3538952 | tf_op jit(solution)/shard_map/ppermute | solution.py:126
  444.1 15.3 %collective-permute-done.29 = bf16[2,2,96,1536]{3,2,1,0:T(8,128)(2,1)} collective-permute-done((bf16[2,2,96,1536]{3,2,1,0:T(8,128)(2,1)}, bf16[2,2,96,1536]{3,2,1,0:T(8,128)(2,1)}, u32[]{:S(2)}, u32[]{:S(2)}) %collective-permute-start.29) | collective-permute-done | bytes 1179680 | tf_op jit(solution)/shard_map/ppermute | solution.py:126
  462.5 23.4 %collective-permute-done.35 = bf16[2,2,96,1536]{3,2,1,0:T(8,128)(2,1)} collective-permute-done((bf16[2,2,96,1536]{3,2,1,0:T(8,128)(2,1)}, bf16[2,2,96,1536]{3,2,1,0:T(8,128)(2,1)}, u32[]{:S(2)}, u32[]{:S(2)}) %collective-permute-start.35) | collective-permute-done | bytes 1179680 | tf_op jit(solution)/shard_map/ppermute | solution.py:126
  491.0 10.2 %collective-permute-done.22 = bf16[2,96,1536]{2,1,0:T(8,128)(2,1)S(1)} collective-permute-done((bf16[2,96,1536]{2,1,0:T(8,128)(2,1)S(1)}, bf16[2,96,1536]{2,1,0:T(8,128)(2,1)S(1)}, u32[]{:S(2)}, u32[]{:S(2)}) %collective-permute-start.22) | collective-permute-done | bytes 589856 | tf_op jit(solution)/shard_map/ppermute | solution.py:126
  513.6 23.8 %collective-permute-start.15 = (bf16[96,1536]{1,0:T(8,128)(2,1)}, bf16[96,1536]{1,0:T(8,128)(2,1)S(1)}, u32[]{:S(2)}, u32[]{:S(2)}) collective-permute-start(bf16[96,1536]{1,0:T(8,128)(2,1)} %dynamic-slice_bitcast_fusion.16), channel_id=1, source_target_pairs={{0,2},{1,3},{2,0},{3,1},{4,6},{5,7},{6,4},{7,5},{8,10},{9,11},{10,... | collective-permute-start | bytes 884744 | tf_op jit(solution)/shard_map/ppermute | solution.py:126
  538.0 6.7 fusion.48
  560.8 50.7 %collective-permute-done.16 = bf16[96,1536]{1,0:T(8,128)(2,1)S(1)} collective-permute-done((bf16[96,1536]{1,0:T(8,128)(2,1)S(1)}, bf16[96,1536]{1,0:T(8,128)(2,1)S(1)}, u32[]{:S(2)}, u32[]{:S(2)}) %collective-permute-start.16) | collective-permute-done | bytes 294944 | tf_op jit(solution)/shard_map/ppermute | solution.py:126
  620.7 18.6 %collective-permute-done.32 = bf16[96,1536]{1,0:T(8,128)(2,1)S(1)} collective-permute-done((bf16[96,1536]{1,0:T(8,128)(2,1)S(1)}, bf16[96,1536]{1,0:T(8,128)(2,1)S(1)}, u32[]{:S(2)}, u32[]{:S(2)}) %collective-permute-start.32) | collective-permute-done | bytes 294944 | tf_op jit(solution)/shard_map/ppermute | solution.py:126
  651.5 13.6 %collective-permute-done.43 = bf16[2,2,192,384]{3,2,1,0:T(8,128)(2,1)S(1)} collective-permute-done((bf16[2,2,192,384]{3,2,1,0:T(8,128)(2,1)S(1)}, bf16[2,2,192,384]{3,2,1,0:T(8,128)(2,1)S(1)}, u32[]{:S(2)}, u32[]{:S(2)}) %collective-permute-start.43) | collective-permute-done | bytes 589856 | tf_op jit(solution)/shard_map/ppermute | solution.py:126
  666.1 10.7 %collective-permute-done.50 = bf16[2,2,192,384]{3,2,0,1:T(8,128)(2,1)S(1)} collective-permute-done((bf16[2,2,192,384]{3,2,0,1:T(8,128)(2,1)S(1)}, bf16[2,2,192,384]{3,2,0,1:T(8,128)(2,1)S(1)}, u32[]{:S(2)}, u32[]{:S(2)}) %collective-permute-start.50) | collective-permute-done | bytes 589856 | tf_op jit(solution)/shard_map/ppermute | solution.py:126
  679.6 7.1 %collective-permute-done.51 = bf16[2,192,384]{2,1,0:T(8,128)(2,1)S(1)} collective-permute-done((bf16[2,192,384]{2,1,0:T(8,128)(2,1)S(1)}, bf16[2,192,384]{2,1,0:T(8,128)(2,1)S(1)}, u32[]{:S(2)}, u32[]{:S(2)}) %collective-permute-start.51) | collective-permute-done | bytes 294944 | tf_op jit(solution)/shard_map/ppermute | solution.py:126
  (652 shorter events, 331.9 us)
Async XLA Ops:
  21.0 39.9 %all-to-all-start.1 = ((bf16[8,128,768]{2,1,0:T(8,128)(2,1)}), bf16[8,128,768]{2,1,0:T(8,128)(2,1)S(1)}, u32[]{:S(2)}, u32[]{:S(2)}) async-start(bf16[8,128,768]{2,1,0:T(8,128)(2,1)} %bitcast.406), calls=%async_computation.1 | async-start | bytes 3145728 | tf_op jit(solution)/shard_map/all_to_all | solution.py:252
  246.3 85.0 %collective-permute-start.11 = (bf16[512,768]{0,1:T(8,128)(2,1)}, bf16[512,768]{0,1:T(8,128)(2,1)}, u32[]{:S(2)}, u32[]{:S(2)}) collective-permute-start(bf16[512,768]{0,1:T(8,128)(2,1)} %bitcast.17), channel_id=1, source_target_pairs={{0,8},{1,9},{2,10},{3,11},{4,12},{5,13},{6,14},{7,15},{8,0},{9,1},... | collective-permute-start | bytes 2359304 | tf_op jit(solution)/shard_map/ppermute | solution.py:126
  277.8 59.2 %collective-permute-start.19 = (bf16[512,768]{0,1:T(8,128)(2,1)}, bf16[512,768]{0,1:T(8,128)(2,1)}, u32[]{:S(2)}, u32[]{:S(2)}) collective-permute-start(bf16[512,768]{0,1:T(8,128)(2,1)} %bitcast.27), channel_id=1, source_target_pairs={{0,8},{1,9},{2,10},{3,11},{4,12},{5,13},{6,14},{7,15},{8,0},{9,1},... | collective-permute-start | bytes 2359304 | tf_op jit(solution)/shard_map/ppermute | solution.py:126
  289.2 41.5 %collective-permute-start.12 = (bf16[512,384]{1,0:T(8,128)(2,1)}, bf16[512,384]{1,0:T(8,128)(2,1)}, u32[]{:S(2)}, u32[]{:S(2)}) collective-permute-start(bf16[512,384]{1,0:T(8,128)(2,1)} %get-tuple-element.113), channel_id=1, source_target_pairs={{0,8},{1,9},{2,10},{3,11},{4,12},{5,13},{6,14},{7,15},{8,0},{9,1},... | collective-permute-start | bytes 1179656 | tf_op jit(solution)/shard_map/ppermute | solution.py:126
  304.9 39.0 %collective-permute-start.10 = (bf16[512,1152]{0,1:T(8,128)(2,1)}, bf16[512,1152]{0,1:T(8,128)(2,1)}, u32[]{:S(2)}, u32[]{:S(2)}) collective-permute-start(bf16[512,1152]{0,1:T(8,128)(2,1)} %get-tuple-element.94), channel_id=1, source_target_pairs={{0,8},{1,9},{2,10},{3,11},{4,12},{5,13},{6,14},{7,15},{8,0},{9,1},... | collective-permute-start | bytes 3538952 | tf_op jit(solution)/shard_map/ppermute | solution.py:126
  325.8 113.5 %all-to-all-start.2 = ((bf16[8,128,768]{2,1,0:T(8,128)(2,1)}), bf16[8,128,768]{2,1,0:T(8,128)(2,1)}, u32[]{:S(2)}, u32[]{:S(2)}) async-start(bf16[8,128,768]{2,1,0:T(8,128)(2,1)} %bitcast.48), calls=%async_computation.2 | async-start | bytes 3145728 | tf_op jit(solution)/shard_map/all_to_all | solution.py:402
  340.2 164.5 %collective-permute-start.40 = (bf16[512,3072]{1,0:T(8,128)(2,1)}, bf16[512,3072]{1,0:T(8,128)(2,1)}, u32[]{:S(2)}, u32[]{:S(2)}) collective-permute-start(bf16[512,3072]{1,0:T(8,128)(2,1)} %get-tuple-element.65), channel_id=1, source_target_pairs={{0,8},{1,9},{2,10},{3,11},{4,12},{5,13},{6,14},{7,15},{8,0},{9,1},... | collective-permute-start | bytes 9437192 | tf_op jit(solution)/shard_map/ppermute | solution.py:126
  343.8 193.6 %collective-permute-start.47 = (bf16[512,3072]{1,0:T(8,128)(2,1)}, bf16[512,3072]{1,0:T(8,128)(2,1)}, u32[]{:S(2)}, u32[]{:S(2)}) collective-permute-start(bf16[512,3072]{1,0:T(8,128)(2,1)} %copy-done.108), channel_id=1, source_target_pairs={{0,8},{1,9},{2,10},{3,11},{4,12},{5,13},{6,14},{7,15},{8,0},{9,1},... | collective-permute-start | bytes 9437192 | tf_op jit(solution)/shard_map/ppermute | solution.py:126
  348.6 32.3 %collective-permute-start.34 = (bf16[512,1536]{1,0:T(8,128)(2,1)}, bf16[512,1536]{1,0:T(8,128)(2,1)}, u32[]{:S(2)}, u32[]{:S(2)}) collective-permute-start(bf16[512,1536]{1,0:T(8,128)(2,1)} %get-tuple-element.80), channel_id=1, source_target_pairs={{0,8},{1,9},{2,10},{3,11},{4,12},{5,13},{6,14},{7,15},{8,0},{9,1},... | collective-permute-start | bytes 4718600 | tf_op jit(solution)/shard_map/ppermute | solution.py:126
  367.9 135.1 %collective-permute-start.41 = (bf16[512,384]{1,0:T(8,128)(2,1)}, bf16[512,384]{1,0:T(8,128)(2,1)}, u32[]{:S(2)}, u32[]{:S(2)}) collective-permute-start(bf16[512,384]{1,0:T(8,128)(2,1)} %get-tuple-element.109), channel_id=1, source_target_pairs={{0,8},{1,9},{2,10},{3,11},{4,12},{5,13},{6,14},{7,15},{8,0},{9,1},... | collective-permute-start | bytes 1179656 | tf_op jit(solution)/shard_map/ppermute | solution.py:126
  380.9 53.4 %collective-permute-start.21 = (bf16[2,2,96,1536]{3,2,1,0:T(8,128)(2,1)}, bf16[2,2,96,1536]{3,2,1,0:T(8,128)(2,1)}, u32[]{:S(2)}, u32[]{:S(2)}) collective-permute-start(bf16[2,2,96,1536]{3,2,1,0:T(8,128)(2,1)} %dynamic-slice_bitcast_fusion.3), channel_id=1, source_target_pairs={{0,2},{1,3},{2,0},{3,1},{4,6},{5,7},{6,4},{7,5},{8,10},{9,11},{10,... | collective-permute-start | bytes 3538952 | tf_op jit(solution)/shard_map/ppermute | solution.py:126
  408.2 51.2 %collective-permute-start.29 = (bf16[2,2,96,1536]{3,2,1,0:T(8,128)(2,1)}, bf16[2,2,96,1536]{3,2,1,0:T(8,128)(2,1)}, u32[]{:S(2)}, u32[]{:S(2)}) collective-permute-start(bf16[2,2,96,1536]{3,2,1,0:T(8,128)(2,1)} %dynamic-slice_bitcast_fusion.2), channel_id=1, source_target_pairs={{0,2},{1,3},{2,0},{3,1},{4,6},{5,7},{6,4},{7,5},{8,10},{9,11},{10,... | collective-permute-start | bytes 3538952 | tf_op jit(solution)/shard_map/ppermute | solution.py:126
  434.3 51.5 %collective-permute-start.35 = (bf16[2,2,96,1536]{3,2,1,0:T(8,128)(2,1)}, bf16[2,2,96,1536]{3,2,1,0:T(8,128)(2,1)}, u32[]{:S(2)}, u32[]{:S(2)}) collective-permute-start(bf16[2,2,96,1536]{3,2,1,0:T(8,128)(2,1)} %dynamic-slice_bitcast_fusion.1), channel_id=1, source_target_pairs={{0,6},{1,7},{2,4},{3,5},{4,2},{5,3},{6,0},{7,1},{8,14},{9,15},{10,... | collective-permute-start | bytes 3538952 | tf_op jit(solution)/shard_map/ppermute | solution.py:126
  501.2 56.7 %collective-permute-start = (bf16[960,384]{1,0:T(8,128)(2,1)}, bf16[960,384]{1,0:T(8,128)(2,1)}, u32[]{:S(2)}, u32[]{:S(2)}) collective-permute-start(bf16[960,384]{1,0:T(8,128)(2,1)} %constant_dynamic-slice_fusion.20), channel_id=1, source_target_pairs={{0,8},{1,9},{2,10},{3,11},{4,12},{5,13},{6,14},{7,15},{8,0},{9,1},... | collective-permute-start | bytes 2211848 | tf_op jit(solution)/shard_map/ppermute | solution.py:126
  503.0 50.3 %collective-permute-start.30 = (bf16[2,96,1536]{2,1,0:T(8,128)(2,1)}, bf16[2,96,1536]{2,1,0:T(8,128)(2,1)}, u32[]{:S(2)}, u32[]{:S(2)}) collective-permute-start(bf16[2,96,1536]{2,1,0:T(8,128)(2,1)} %dynamic-slice_bitcast_fusion.8), channel_id=1, source_target_pairs={{0,6},{1,7},{2,4},{3,5},{4,2},{5,3},{6,0},{7,1},{8,14},{9,15},{10,... | collective-permute-start | bytes 1769480 | tf_op jit(solution)/shard_map/ppermute | solution.py:126
  504.7 50.5 %collective-permute-start.36 = (bf16[2,96,1536]{2,1,0:T(8,128)(2,1)}, bf16[2,96,1536]{2,1,0:T(8,128)(2,1)}, u32[]{:S(2)}, u32[]{:S(2)}) collective-permute-start(bf16[2,96,1536]{2,1,0:T(8,128)(2,1)} %dynamic-slice_bitcast_fusion.7), channel_id=1, source_target_pairs={{0,1},{1,0},{2,3},{3,2},{4,5},{5,4},{6,7},{7,6},{8,9},{9,8},{10,11... | collective-permute-start | bytes 1769480 | tf_op jit(solution)/shard_map/ppermute | solution.py:126
  513.6 37.2 %collective-permute-start.15 = (bf16[96,1536]{1,0:T(8,128)(2,1)}, bf16[96,1536]{1,0:T(8,128)(2,1)S(1)}, u32[]{:S(2)}, u32[]{:S(2)}) collective-permute-start(bf16[96,1536]{1,0:T(8,128)(2,1)} %dynamic-slice_bitcast_fusion.16), channel_id=1, source_target_pairs={{0,2},{1,3},{2,0},{3,1},{4,6},{5,7},{6,4},{7,5},{8,10},{9,11},{10,... | collective-permute-start | bytes 884744 | tf_op jit(solution)/shard_map/ppermute | solution.py:126
  550.9 97.6 %collective-permute-start.42 = (bf16[2,2,2,192,384]{4,3,2,1,0:T(8,128)(2,1)S(1)}, bf16[2,2,2,192,384]{4,3,2,1,0:T(8,128)(2,1)S(1)}, u32[]{:S(2)}, u32[]{:S(2)}) collective-permute-start(bf16[2,2,2,192,384]{4,3,2,1,0:T(8,128)(2,1)S(1)} %dynamic-slice_bitcast_fusion), channel_id=1, source_target_pairs={{0,16},{1,17},{2,18},{3,19},{4,20},{5,21},{6,22},{7,23},{8,24},{9,... | collective-permute-start | bytes 3538952 | tf_op jit(solution)/shard_map/ppermute | solution.py:126
  551.7 98.7 %collective-permute-start.49 = (bf16[2,2,2,192,384]{4,3,0,1,2:T(8,128)(2,1)S(1)}, bf16[2,2,2,192,384]{4,3,0,1,2:T(8,128)(2,1)S(1)}, u32[]{:S(2)}, u32[]{:S(2)}) collective-permute-start(bf16[2,2,2,192,384]{4,3,0,1,2:T(8,128)(2,1)S(1)} %bitcast.407), channel_id=1, source_target_pairs={{0,16},{1,17},{2,18},{3,19},{4,20},{5,21},{6,22},{7,23},{8,24},{9,... | collective-permute-start | bytes 3538952 | tf_op jit(solution)/shard_map/ppermute | solution.py:126
  553.2 58.2 %collective-permute-start.16 = (bf16[96,1536]{1,0:T(8,128)(2,1)S(1)}, bf16[96,1536]{1,0:T(8,128)(2,1)S(1)}, u32[]{:S(2)}, u32[]{:S(2)}) collective-permute-start(bf16[96,1536]{1,0:T(8,128)(2,1)S(1)} %fusion.200), channel_id=1, source_target_pairs={{0,16},{1,17},{2,18},{3,19},{4,20},{5,21},{6,22},{7,23},{8,24},{9,... | collective-permute-start | bytes 884744 | tf_op jit(solution)/shard_map/ppermute | solution.py:126
  555.2 60.9 %collective-permute-start.24 = (bf16[96,1536]{1,0:T(8,128)(2,1)S(1)}, bf16[96,1536]{1,0:T(8,128)(2,1)S(1)}, u32[]{:S(2)}, u32[]{:S(2)}) collective-permute-start(bf16[96,1536]{1,0:T(8,128)(2,1)S(1)} %fusion.199), channel_id=1, source_target_pairs={{0,16},{1,17},{2,18},{3,19},{4,20},{5,21},{6,22},{7,23},{8,24},{9,... | collective-permute-start | bytes 884744 | tf_op jit(solution)/shard_map/ppermute | solution.py:126
  557.9 59.1 %collective-permute-start.31 = (bf16[96,1536]{1,0:T(8,128)(2,1)S(1)}, bf16[96,1536]{1,0:T(8,128)(2,1)S(1)}, u32[]{:S(2)}, u32[]{:S(2)}) collective-permute-start(bf16[96,1536]{1,0:T(8,128)(2,1)S(1)} %dynamic-slice_bitcast_fusion.14), channel_id=1, source_target_pairs={{0,1},{1,0},{2,3},{3,2},{4,5},{5,4},{6,7},{7,6},{8,9},{9,8},{10,11... | collective-permute-start | bytes 884744 | tf_op jit(solution)/shard_map/ppermute | solution.py:126
  616.1 31.6 %collective-permute-start.1 = (bf16[960,384]{1,0:T(8,128)(2,1)S(1)}, bf16[960,384]{1,0:T(8,128)(2,1)S(1)}, u32[]{:S(2)}, u32[]{:S(2)}) collective-permute-start(bf16[960,384]{1,0:T(8,128)(2,1)S(1)} %add_convert_fusion.2), channel_id=1, source_target_pairs={{0,16},{1,17},{2,18},{3,19},{4,20},{5,21},{6,22},{7,23},{8,24},{9,... | collective-permute-start | bytes 2211848 | tf_op jit(solution)/shard_map/ppermute | solution.py:126
  647.9 53.3 %collective-permute-start.2 = (bf16[960,384]{1,0:T(8,128)(2,1)S(1)}, bf16[960,384]{1,0:T(8,128)(2,1)S(1)}, u32[]{:S(2)}, u32[]{:S(2)}) collective-permute-start(bf16[960,384]{1,0:T(8,128)(2,1)S(1)} %add_convert_fusion.1), channel_id=1, source_target_pairs={{0,8},{1,9},{2,10},{3,11},{4,12},{5,13},{6,14},{7,15},{8,0},{9,1},... | collective-permute-start | bytes 2211848 | tf_op jit(solution)/shard_map/ppermute | solution.py:126
  (169 other events, 1837.7 us)

commit v2 on v0

v2 whole, which is shorter than its diff:
```python
import functools
import jax
import jax.numpy as jnp
from jax import lax
from jax.experimental import pallas as pl
from jax.experimental.pallas import tpu as pltpu
from jax.sharding import PartitionSpec as P

HEADS = 12
HEAD_DIM = 64
NL = 2
norm_eps = 1e-12
SCALE = HEAD_DIM ** (-0.5)
ANY = pl.BlockSpec(memory_space=pl.ANY)
VM = pl.BlockSpec(memory_space=pltpu.VMEM)
SM = pl.BlockSpec(memory_space=pltpu.SMEM)
F32, LOW = jnp.float32, jnp.bfloat16


def run(kernel, after, out_shape, in_specs, operands, **options):
    count = len(operands)

    def body(*refs):
        kernel(*refs[:count], *refs[count + len(after) :])

    return pl.pallas_call(
        body,
        out_shape=out_shape,
        in_specs=list(in_specs) + [ANY] * len(after),
        compiler_params=PARAMS,
        **options,
    )(*operands, *after)


PARAMS = pltpu.CompilerParams(vmem_limit_bytes=60 * 1024 * 1024)


def normalize(inputs):
    centered = inputs - jnp.mean(inputs, axis=-1, keepdims=True)
    spread = lax.rsqrt(jnp.mean(centered * centered, axis=-1, keepdims=True) + norm_eps)
    return (centered * spread, spread)


def norm_back(grad_out, normed, spread, gain_row):
    scaled = grad_out * gain_row
    return spread * (
        scaled
        - jnp.mean(scaled, axis=-1, keepdims=True)
        - normed * jnp.mean(scaled * normed, axis=-1, keepdims=True)
    )


def dot(left_op, right_op, dims=((1,), (0,))):
    return lax.dot_general(left_op, right_op, (dims, ((), ())), preferred_element_type=F32)


ROWS = ((0,), (0,))
COLS = ((1,), (1,))


def gelu_pair(inputs):
    size = jnp.abs(inputs)
    bell = jnp.exp2(inputs * inputs * (-0.5 * 1.4426950408889634))
    t = 1.0 / (1.0 + size * (0.3275911 * 0.7071067811865476))
    tail = t * (
        0.5 * 0.254829592
        + t * (0.5 * -0.284496736 + t * (0.5 * 1.421413741 + t * (0.5 * -1.453152027 + t * (0.5 * 1.061405429))))
    )
    tail = tail * bell
    phi = jnp.where(inputs >= 0.0, 1.0 - tail, tail)
    return inputs * phi, phi + inputs * bell * 0.3989422804014327


def forward_kernel(
    layer,
    length_ref, x_ref, rows_ref, qkv_bias_ref, ffn_bias_ref, wqkv_hbm, wout_hbm, w1_hbm, w2_hbm,
    xlow_ref, mixed_ref, lse_ref, ctxt_ref, n1_ref, s1_ref, mlow_ref, gp_ref, act_ref, n2_ref, s2_ref, next_ref,
    wqkv, wout, w1, w2, sems,
    xlow, mixed, ctxt, mlow, gp, act, n1, n2, nxt, middle, acc, osems,
):
    loads = [
        pltpu.make_async_copy(src.at[layer], dst, sems.at[i])
        for i, (src, dst) in enumerate([(wqkv_hbm, wqkv), (wout_hbm, wout), (w1_hbm, w1), (w2_hbm, w2)])
    ]
    for load in loads:
        load.start()
    stores = []

    def emit(src, dst):
        copy = pltpu.make_async_copy(src, dst, osems.at[len(stores)])
        copy.start()
        stores.append(copy)

    tokens, width = x_ref.shape
    xlow[...] = x_ref[...].astype(LOW)
    emit(xlow, xlow_ref)
    loads[0].wait()

    def qkv_step(i, carry):
        cols = pl.ds(pl.multiple_of(i * 256, 256), 256)
        mixed[:, cols] = (dot(xlow[...], wqkv[:, cols]) + qkv_bias_ref[:, cols]).astype(LOW)
        return carry

    lax.fori_loop(0, 3 * width // 256, qkv_step, 0)
    emit(mixed, mixed_ref)

    key_slot = lax.broadcasted_iota(jnp.int32, (tokens, 128), 0)
    visible = jnp.where(key_slot < length_ref[0], 0.0, -1e30)[:, :1]
    lane = lax.broadcasted_iota(jnp.int32, (tokens, 128), 1)

    def pair_step(j, carry):
        at = pl.multiple_of(j * 128, 128)
        q = mixed[:, pl.ds(at, 128)] * jnp.asarray(SCALE, LOW)
        k = mixed[:, pl.ds(pl.multiple_of(width + at, 128), 128)]
        v = mixed[:, pl.ds(pl.multiple_of(2 * width + at, 128), 128)]
        vt = v.T
        for h in range(2):
            kh = jnp.where((lane < 64) == (h == 0), k, jnp.zeros_like(k))
            scores = dot(kh, q, COLS) + visible
            top = jnp.max(scores, axis=0, keepdims=True)
            weights = jnp.exp(scores - top)
            total = jnp.sum(weights, axis=0, keepdims=True)
            out = dot(vt[h * 64 : (h + 1) * 64], weights.astype(LOW)) * (1.0 / total)
            ctxt[pl.ds(pl.multiple_of(at + h * 64, 64), 64), :] = out.astype(LOW)
            lse_ref[pl.ds(2 * j + h, 1), :] = top + jnp.log(total)
        return carry

    lax.fori_loop(0, HEADS // 2, pair_step, 0)
    emit(ctxt, ctxt_ref)
    loads[1].wait()
    attended = dot(ctxt[...], wout[...], ROWS) + rows_ref[0:1]
    normed, spread = normalize(x_ref[...] + attended)
    n1[...] = normed
    emit(n1, n1_ref)
    s1_ref[...] = jnp.broadcast_to(spread, s1_ref.shape)
    middle[...] = normed * rows_ref[1:2] + rows_ref[2:3]
    mlow[...] = middle[...].astype(LOW)
    emit(mlow, mlow_ref)
    loads[2].wait()
    loads[3].wait()
    acc[...] = middle[...] + rows_ref[3:4]
    chunk = 512

    def ffn_step(i, carry):
        cols = pl.ds(pl.multiple_of(i * chunk, chunk), chunk)
        pre = dot(mlow[...], w1[:, cols]) + ffn_bias_ref[:, cols]
        active, slope = gelu_pair(pre)
        gp[:, cols] = slope.astype(LOW)
        active = active.astype(LOW)
        act[:, cols] = active
        acc[...] += dot(active, w2[cols, :])
        return carry

    lax.fori_loop(0, w1.shape[1] // chunk, ffn_step, 0)
    emit(gp, gp_ref)
    emit(act, act_ref)
    normed, spread = normalize(acc[...])
    n2[...] = normed
    emit(n2, n2_ref)
    s2_ref[...] = jnp.broadcast_to(spread, s2_ref.shape)
    nxt[...] = normed * rows_ref[4:5] + rows_ref[5:6]
    emit(nxt, next_ref)
    for store in stores:
        store.wait()


def forward_layer(layer, length, states, rows, qkv_bias, ffn_bias, w_qkv, w_out, w_ff1, w_ff2, after=()):
    tokens, width = states.shape
    ff = w_ff1.shape[2]
    s = jax.ShapeDtypeStruct
    outs = (
        s((tokens, width), LOW), s((tokens, 3 * width), LOW), s((HEADS, tokens), F32), s((width, tokens), LOW),
        s((tokens, width), F32), s((tokens, 128), F32), s((tokens, width), LOW), s((tokens, ff), LOW), s((tokens, ff), LOW),
        s((tokens, width), F32), s((tokens, 128), F32), s((tokens, width), F32),
    )
    ospec = (ANY, ANY, VM, ANY, ANY, VM, ANY, ANY, ANY, ANY, VM, ANY)
    v = pltpu.VMEM
    scratch = [
        v((width, 3 * width), LOW), v((width, width), LOW), v((width, ff), LOW), v((ff, width), LOW), pltpu.SemaphoreType.DMA((4,)),
        v((tokens, width), LOW), v((tokens, 3 * width), LOW), v((width, tokens), LOW), v((tokens, width), LOW),
        v((tokens, ff), LOW), v((tokens, ff), LOW), v((tokens, width), F32), v((tokens, width), F32), v((tokens, width), F32),
        v((tokens, width), F32), v((tokens, width), F32), pltpu.SemaphoreType.DMA((9,)),
    ]
    flops = 2 * tokens * width * (4 * width + 2 * ff) + 8 * tokens * tokens * width
    return run(
        functools.partial(forward_kernel, layer),
        after,
        out_shape=outs,
        in_specs=[SM, VM, VM, VM, VM, ANY, ANY, ANY, ANY],
        operands=(length, states, rows, qkv_bias, ffn_bias, w_qkv, w_out, w_ff1, w_ff2),
        out_specs=ospec,
        scratch_shapes=scratch,
        cost_estimate=pl.CostEstimate(flops=flops, bytes_accessed=30 << 20, transcendentals=0),
        name="forward_layer",
    )


def feed_back_kernel(
    layer,
    core_ref, grad_ref, n2_ref, s2_ref, n1_ref, s1_ref, rows_ref, gp_hbm, wout_hbm, w1_hbm, w2_hbm,
    pre_keep_ref, pre_send_ref, sec_keep_ref, sec_send_ref, first_ref, fst_keep_ref, fst_send_ref, gctx_ref, sums_ref, bias_ref,
    wout, w1, w2, gp, sems, second, grad_mid, keep, send,
):
    loads = [
        pltpu.make_async_copy(src, dst, sems.at[i])
        for i, (src, dst) in enumerate([(w2_hbm.at[layer], w2), (gp_hbm, gp), (w1_hbm.at[layer], w1), (wout_hbm.at[layer], wout)])
    ]
    for load in loads:
        load.start()
    mine = core_ref[0]
    width = second.shape[1]
    half = width // 2
    grad = grad_ref[...].astype(F32)
    n2 = n2_ref[...]
    sums_ref[0:1] = jnp.sum(grad * n2, axis=0, keepdims=True)
    sums_ref[1:2] = jnp.sum(grad, axis=0, keepdims=True)
    e = norm_back(grad, n2, s2_ref[:, :1], rows_ref[4:5])
    sums_ref[2:3] = jnp.sum(e, axis=0, keepdims=True)
    grad_mid[...] = e
    second[...] = e.astype(LOW)

    def part(source, keep_to, send_to):
        @pl.when(mine == 0)
        def _():
            keep_to[...] = source[:, :half]
            send_to[...] = source[:, half:]

        @pl.when(mine == 1)
        def _():
            keep_to[...] = source[:, half:]
            send_to[...] = source[:, :half]

    part(second, sec_keep_ref, sec_send_ref)
    loads[0].wait()
    loads[1].wait()
    loads[2].wait()
    chunk = 512
    steps = w1.shape[1] // chunk

    def step(i, carry):
        cols = pl.ds(pl.multiple_of(i * chunk, chunk), chunk)
        grad_pre = dot(second[...], w2[cols, :], COLS) * gp[:, cols].astype(F32)
        bias_ref[:, cols] = jnp.sum(grad_pre, axis=0, keepdims=True)
        low = grad_pre.astype(LOW)
        there = pl.ds(pl.multiple_of(lax.rem(i, steps // 2) * chunk, chunk), chunk)
        side = (i >= steps // 2).astype(jnp.int32)

        @pl.when(side == mine)
        def _():
            keep[:, there] = low

        @pl.when(side != mine)
        def _():
            send[:, there] = low

        grad_mid[...] += dot(low, w1[:, cols], COLS)
        return carry

    lax.fori_loop(0, steps, step, 0)
    stores = [
        pltpu.make_async_copy(send, pre_send_ref, sems.at[4]),
        pltpu.make_async_copy(keep, pre_keep_ref, sems.at[5]),
    ]
    for store in stores:
        store.start()
    grad = grad_mid[...]
    n1 = n1_ref[...]
    sums_ref[3:4] = jnp.sum(grad * n1, axis=0, keepdims=True)
    sums_ref[4:5] = jnp.sum(grad, axis=0, keepdims=True)
    c = norm_back(grad, n1, s1_ref[:, :1], rows_ref[1:2])
    sums_ref[5:6] = jnp.sum(c, axis=0, keepdims=True)
    first_ref[...] = c
    second[...] = c.astype(LOW)
    part(second, fst_keep_ref, fst_send_ref)
    loads[3].wait()
    gctx_ref[...] = dot(second[...], wout[...], COLS).astype(LOW)
    for store in stores:
        store.wait()


def feed_back(layer, core, grad, n2, s2, n1, s1, rows, gp, w_out, w_ff1, w_ff2, after=()):
    tokens, width = n2.shape
    ff = gp.shape[1]
    s = jax.ShapeDtypeStruct
    v = pltpu.VMEM
    halfs = s((tokens, width // 2), LOW)
    return run(
        functools.partial(feed_back_kernel, layer),
        after,
        out_shape=(
            s((tokens, ff // 2), LOW), s((tokens, ff // 2), LOW), halfs, halfs, s((tokens, width), F32), halfs, halfs,
            s((tokens, width), LOW), s((6, width), F32), s((1, ff), F32),
        ),
        in_specs=[SM, VM, VM, VM, VM, VM, VM, ANY, ANY, ANY, ANY],
        operands=(core, grad, n2, s2, n1, s1, rows, gp, w_out, w_ff1, w_ff2),
        out_specs=(ANY, ANY) + (VM,) * 8,
        scratch_shapes=[
            v((width, width), LOW), v((width, ff), LOW), v((ff, width), LOW), v((tokens, ff), LOW), pltpu.SemaphoreType.DMA((6,)),
            v((tokens, width), LOW), v((tokens, width), F32), v((tokens, ff // 2), LOW), v((tokens, ff // 2), LOW),
        ],
        cost_estimate=pl.CostEstimate(flops=2 * tokens * width * (width + 2 * ff), bytes_accessed=20 << 20, transcendentals=0),
        name="feed_back",
    )


def attend_back_kernel(
    layer,
    core_ref, length_ref, mixed_ref, lse_ref, gctx_ref, first_ref, wqkv_hbm,
    keep_ref, send_ref, next_ref, sums_ref,
    wqkv, dmix, sems,
):
    load = pltpu.make_async_copy(wqkv_hbm.at[layer], wqkv, sems.at[0])
    load.start()
    tokens, width = first_ref.shape
    key_slot = lax.broadcasted_iota(jnp.int32, (tokens, 128), 0)
    visible = jnp.where(key_slot < length_ref[0], 0.0, -1e30)[:, :1]
    lane = lax.broadcasted_iota(jnp.int32, (tokens, 128), 1)

    def pair_step(j, carry):
        at = pl.multiple_of(j * 128, 128)
        qcols = pl.ds(at, 128)
        kcols = pl.ds(pl.multiple_of(width + at, 128), 128)
        vcols = pl.ds(pl.multiple_of(2 * width + at, 128), 128)
        q = mixed_ref[:, qcols] * jnp.asarray(SCALE, LOW)
        k = mixed_ref[:, kcols]
        v = mixed_ref[:, vcols]
        g = gctx_ref[:, qcols]
        kt = k.T
        grad_v, grad_k, grad_qt = [], [], []
        for h in range(2):
            mask = (lane < 64) == (h == 0)
            kh = jnp.where(mask, k, jnp.zeros_like(k))
            vh = jnp.where(mask, v, jnp.zeros_like(v))
            probs = jnp.exp(dot(kh, q, COLS) + visible - lse_ref[pl.ds(2 * j + h, 1), :])
            grad_probs = dot(vh, g, COLS)
            weighted = jnp.sum(probs * grad_probs, axis=0, keepdims=True)
            grad_scores = (probs * (grad_probs - weighted)).astype(LOW)
            grad_v.append(dot(probs.astype(LOW), g))
            grad_k.append(dot(grad_scores, q))
            grad_qt.append(dot(kt[h * 64 : (h + 1) * 64], grad_scores))
        grad_q = jnp.concatenate(grad_qt, axis=0).T * SCALE
        grad_v = jnp.where(lane < 64, grad_v[0], grad_v[1])
        grad_k = jnp.where(lane < 64, grad_k[0], grad_k[1])
        sums_ref[0:1, qcols] = jnp.sum(grad_q, axis=0, keepdims=True)
        sums_ref[1:2, qcols] = jnp.sum(grad_v, axis=0, keepdims=True)
        dmix[:, qcols] = grad_q.astype(LOW)
        dmix[:, kcols] = grad_k.astype(LOW)
        dmix[:, vcols] = grad_v.astype(LOW)
        return carry

    lax.fori_loop(0, HEADS // 2, pair_step, 0)
    half = 3 * width // 2
    mine = core_ref[0]

    @pl.when(mine == 0)
    def _():
        keep_ref[...] = dmix[:, :half]
        send_ref[...] = dmix[:, half:]

    @pl.when(mine == 1)
    def _():
        keep_ref[...] = dmix[:, half:]
        send_ref[...] = dmix[:, :half]

    load.wait()
    next_ref[...] = first_ref[...] + dot(dmix[...], wqkv[...], COLS)


def attend_back(layer, core, length, mixed, lse, gctx, first, w_qkv, after=()):
    tokens, width = first.shape
    s = jax.ShapeDtypeStruct
    v = pltpu.VMEM
    halfs = s((tokens, 3 * width // 2), LOW)
    return run(
        functools.partial(attend_back_kernel, layer),
        after,
        out_shape=(halfs, halfs, s((tokens, width), F32), s((2, width), F32)),
        in_specs=[SM, SM, VM, VM, VM, VM, ANY],
        operands=(core, length, mixed, lse, gctx, first, w_qkv),
        out_specs=(VM,) * 4,
        scratch_shapes=[v((width, 3 * width), LOW), v((tokens, 3 * width), LOW), pltpu.SemaphoreType.DMA((1,))],
        cost_estimate=pl.CostEstimate(
            flops=6 * tokens * width * width + 24 * tokens * tokens * width, bytes_accessed=12 << 20, transcendentals=0
        ),
        name="attend_back",
    )


COORDS = ("core", "x", "a", "b", "y")


def place(coords_ref, dims, result, keep_ref, send_ref):
    count = keep_ref.shape[0]
    for i in range(2 * count):
        block = i
        if dims is not None:
            bit = {}
            for n, dim in enumerate(dims):
                relative = (i >> (len(dims) - 1 - n)) & 1
                whole = dim == "y" and n == len(dims) - 1
                bit[dim] = relative if whole else coords_ref[COORDS.index(dim)] ^ relative
            block = 8 * bit["b"] + 4 * (bit["a"] ^ bit["b"]) + 2 * bit["x"] + bit["y"]
        if i < count:
            keep_ref[i] = result[block]
        else:
            send_ref[i - count] = result[block]


def feed_weights_kernel(
    blocks, dims_one, dims_two, coords_ref, mid_own, mid_oth, pre_own, pre_oth, sec_own, sec_oth, act_own, act_oth,
    one_keep_ref, one_send_ref, two_keep_ref, two_send_ref,
    mid, pre, sec, act, midt, sect, one, two, sems,
):
    tokens = mid_own.shape[0]
    loads = []
    for own, oth, dst in ((mid_own, mid_oth, mid), (pre_own, pre_oth, pre), (sec_own, sec_oth, sec), (act_own, act_oth, act)):
        for n, src in enumerate((own, oth)):
            load = pltpu.make_async_copy(src, dst.at[pl.ds(n * tokens, tokens)], sems.at[len(loads)])
            load.start()
            loads.append(load)
    width = mid.shape[1]
    for load in loads[:4]:
        load.wait()
    midt[...] = mid[...].T
    chunk = 512

    def step_one(i, carry):
        cols = pl.ds(pl.multiple_of(i * chunk, chunk), chunk)
        one[:, :, cols] = dot(midt[...], pre[:, cols]).astype(LOW).reshape(one.shape[:2] + (chunk,))
        return carry

    lax.fori_loop(0, pre.shape[1] // chunk, step_one, 0)
    place(coords_ref, dims_one, one, one_keep_ref, one_send_ref)
    for load in loads[4:]:
        load.wait()
    sect[...] = sec[...].T
    per = one.shape[0] // blocks
    part = act.shape[1] // blocks

    def step_two(i, carry):
        cols = pl.ds(pl.multiple_of(i * part, part), part)
        got = dot(sect[...], act[:, cols]).astype(LOW)
        for n in range(per):
            two[i * per + n] = got[n * two.shape[1] : (n + 1) * two.shape[1]]
        return carry

    lax.fori_loop(0, blocks, step_two, 0)
    place(coords_ref, dims_two, two, two_keep_ref, two_send_ref)


def feed_weights(blocks, dims_one, dims_two, coords, mid, pre, sec, act, after=()):
    tokens, width = mid[0].shape
    s = jax.ShapeDtypeStruct
    v = pltpu.VMEM
    count = 2 * blocks
    one = (count, width // count, pre[0].shape[1])
    two = (count, sec[0].shape[1] * blocks // count, act[0].shape[1] // blocks)
    half = lambda t: s((t[0] // 2,) + t[1:], LOW)
    return run(
        functools.partial(feed_weights_kernel, blocks, dims_one, dims_two),
        after,
        out_shape=(half(one), half(one), half(two), half(two)),
        in_specs=[SM] + [ANY] * 8,
        operands=(coords, *mid, *pre, *sec, *act),
        out_specs=(VM,) * 4,
        scratch_shapes=[
            v((2 * tokens, width), LOW), v((2 * tokens, pre[0].shape[1]), LOW), v((2 * tokens, sec[0].shape[1]), LOW),
            v((2 * tokens, act[0].shape[1]), LOW), v((width, 2 * tokens), LOW), v((sec[0].shape[1], 2 * tokens), LOW),
            v(one, LOW), v(two, LOW), pltpu.SemaphoreType.DMA((8,)),
        ],
        cost_estimate=pl.CostEstimate(
            flops=4 * tokens * (width * pre[0].shape[1] + sec[0].shape[1] * act[0].shape[1]), bytes_accessed=16 << 20, transcendentals=0
        ),
        name="feed_weights",
    )


def attend_weights_kernel(
    dims,
    coords_ref, x_own, x_oth, mix_own, mix_oth, ctx_own, ctx_oth, fst_own, fst_oth,
    keep_ref, send_ref,
    x, mix, ctxt, fst, xt, res, sems,
):
    tokens = x_own.shape[0]
    loads = []
    for own, oth, dst in ((x_own, x_oth, x), (mix_own, mix_oth, mix), (fst_own, fst_oth, fst)):
        for n, src in enumerate((own, oth)):
            loads.append(pltpu.make_async_copy(src, dst.at[pl.ds(n * tokens, tokens)], sems.at[len(loads)]))
    for n, src in enumerate((ctx_own, ctx_oth)):
        loads.append(pltpu.make_async_copy(src, ctxt.at[:, pl.ds(n * tokens, tokens)], sems.at[len(loads)]))
    for load in loads:
        load.start()
    loads[0].wait()
    loads[1].wait()
    xt[...] = x[...].T
    for load in loads[2:]:
        load.wait()
    chunk = fst.shape[1]
    steps = mix.shape[1] // chunk
    shape = res.shape[:2] + (chunk,)
    for i in range(steps):
        res[:, :, i * chunk : (i + 1) * chunk] = dot(xt[...], mix[:, i * chunk : (i + 1) * chunk]).astype(LOW).reshape(shape)
    res[:, :, steps * chunk :] = dot(ctxt[...], fst[...]).astype(LOW).reshape(shape)
    place(coords_ref, dims, res, keep_ref, send_ref)


def attend_weights(blocks, dims, coords, x, mix, ctx, fst, after=()):
    tokens, width = x[0].shape
    s = jax.ShapeDtypeStruct
    v = pltpu.VMEM
    count = 2 * blocks
    cols = mix[0].shape[1] + fst[0].shape[1]
    res = (count, width // count, cols)
    half = s((count // 2,) + res[1:], LOW)
    return run(
        functools.partial(attend_weights_kernel, dims),
        after,
        out_shape=(half, half),
        in_specs=[SM] + [ANY] * 8,
        operands=(coords, *x, *mix, *ctx, *fst),
        out_specs=(VM, VM),
        scratch_shapes=[
            v((2 * tokens, width), LOW), v((2 * tokens, mix[0].shape[1]), LOW), v((width, 2 * tokens), LOW),
            v((2 * tokens, fst[0].shape[1]), LOW), v((width, 2 * tokens), LOW), v(res, LOW), pltpu.SemaphoreType.DMA((8,)),
        ],
        cost_estimate=pl.CostEstimate(flops=4 * tokens * width * cols, bytes_accessed=10 << 20, transcendentals=0),
        name="attend_weights",
    )


AXES = ("dp", "vocab")
VOCAB_MASK = {"x": 1, "a": 2, "b": 6}


def add(left_op, right_op):
    return (left_op.astype(F32) + right_op.astype(F32)).astype(LOW)


class Cube:
    def __init__(self, dp_size, vocab_size):
        self.dp_size = dp_size
        self.vocab_size = vocab_size
        self.dp_bits = dp_size.bit_length() - 1
        self.vocab_bits = vocab_size.bit_length() - 1
        assert 1 << self.dp_bits == dp_size and 1 << self.vocab_bits == vocab_size
        self.small = self.dp_bits == 2 and self.vocab_bits == 3

    def permute(self, value, dp_mask, vocab_mask):
        count = self.vocab_size
        pairs = [
            (d * count + v, (d ^ dp_mask) * count + (v ^ vocab_mask))
            for d in range(self.dp_size)
            for v in range(count)
        ]
        return lax.ppermute(value, AXES, pairs)

    def core(self, value):
        return self.permute(value, 1, 0)

    def along(self, value, dim):
        return self.permute(value, 2, 0) if dim == "y" else self.permute(value, 0, VOCAB_MASK[dim])

    def core_is_first(self):
        return (lax.axis_index("dp") & 1) == 0

    def coords(self):
        dp, vocab = lax.axis_index("dp"), lax.axis_index("vocab")
        b = (vocab >> 2) & 1
        return jnp.stack([dp & 1, vocab & 1, ((vocab >> 1) & 1) ^ b, b, (dp >> 1) & 1])

    def halves(self, matrix):
        mine = lax.axis_index("dp") & 1
        width = matrix.shape[1] // 2
        keep = lax.dynamic_slice_in_dim(matrix, mine * width, width, 1)
        send = lax.dynamic_slice_in_dim(matrix, (1 - mine) * width, width, 1)
        return keep, send

    def ordered(self, first, mine, other, axis):
        return jnp.concatenate(
            [jnp.where(first, mine, other), jnp.where(first, other, mine)], axis=axis
        )

    def join_core(self, share, axis):
        return self.ordered(self.core_is_first(), share, self.core(share), axis).astype(F32)

    def reduce(self, matrix):
        for bit in reversed(range(self.vocab_bits)):
            mine = (lax.axis_index("vocab") >> bit) & 1
            rows = matrix.shape[0] // 2
            keep = lax.dynamic_slice_in_dim(matrix, mine * rows, rows, 0)
            send = lax.dynamic_slice_in_dim(matrix, (1 - mine) * rows, rows, 0)
            matrix = add(keep, self.permute(send, 0, 1 << bit))
        for bit in range(1, self.dp_bits):
            matrix = add(matrix, self.permute(matrix, 1 << bit, 0))
        return matrix


class Chain:
    def __init__(self, cube, dims, keep, send):
        self.cube, self.dims, self.keep, self.send = cube, dims, keep, send
        self.got = []
        for n, dim in enumerate(dims):
            if dim == "y" and n == len(dims) - 1:
                got = cube.along(self.keep, "y")
                self.got.append(got)
                self.keep = add(self.keep, got)
                break
            got = cube.along(self.send, dim)
            self.got.append(got)
            half = self.keep.shape[0] // 2
            last = n == len(dims) - 1 or (n == len(dims) - 2 and dims[-1] == "y")
            if last:
                self.keep = add(self.keep, got)
            else:
                self.keep, self.send = (
                    add(self.keep[:half], got[:half]),
                    add(self.keep[half:], got[half:]),
                )
        if dims[-1] != "y":
            other = cube.along(self.keep, "y")
            first = ((lax.axis_index("dp") >> 1) & 1) == 0
            self.share = cube.ordered(first, self.keep, other, 0)
        else:
            self.share = self.keep
        self.share = self.share.reshape(-1, self.share.shape[-1])


def on_device(
    cube,
    token_ids,
    lengths,
    type_ids,
    word_table,
    pos_table,
    type_table,
    gains,
    shifts,
    w_qkv,
    w_out,
    b_ff1,
    w_ff1,
    w_ff2,
    cotangent,
):
    owners = cube.vocab_size
    local_rows, width = word_table.shape
    assert token_ids.shape[0] == 1
    tokens = token_ids.shape[1]
    slot_count = 2 * tokens // owners
    slots = owners * slot_count
    gain_vals = gains.astype(F32)
    shift_vals = shifts.astype(F32)
    flat_ids = token_ids.reshape(tokens)
    me = lax.axis_index("vocab")
    coords = cube.coords()

    all_ids = lax.all_to_all(
        jnp.broadcast_to(flat_ids[None, :], (owners, tokens)), "vocab", split_axis=0, concat_axis=0, tiled=True
    )
    local = all_ids - me * local_rows
    here = (local >= 0) & (local < local_rows)
    rank = jnp.cumsum(here.astype(jnp.int32), axis=1) - 1
    slot_hit = (
        jnp.where(here, rank, -1)[:, None, :] == jnp.arange(slot_count, dtype=jnp.int32)[None, :, None]
    )
    asked = jnp.sum(jnp.where(slot_hit, local[:, None, :] + 1, 0), axis=2).reshape(slots) - 1
    row_hit = (asked[:, None] == jnp.arange(local_rows, dtype=jnp.int32)[None, :]).astype(LOW)
    found_rows = dot(row_hit, word_table).astype(LOW)
    replies = lax.all_to_all(
        found_rows.reshape(owners, slot_count, width), "vocab", split_axis=0, concat_axis=0, tiled=True
    ).reshape(slots, width)
    owner_of = flat_ids // local_rows
    chosen = (owner_of[:, None] == jnp.arange(owners, dtype=jnp.int32)[None, :]).astype(jnp.int32)
    before = jnp.cumsum(chosen, axis=0) - chosen
    slot_of = owner_of * slot_count + jnp.sum(before * chosen, axis=1)
    dispatch = (slot_of[:, None] == jnp.arange(slots, dtype=jnp.int32)[None, :]).astype(LOW)
    word_rows = dot(dispatch, replies)
    type_flat = type_ids.reshape(tokens)
    type_rows = jnp.where(type_flat[:, None] == 1, type_table[1].astype(F32)[None, :], type_table[0].astype(F32)[None, :])
    embedded = word_rows + pos_table.astype(F32) + type_rows
    normed_emb, spread_emb = normalize(embedded)
    states = normed_emb * gain_vals[0] + shift_vals[0]

    saved, layer_rows = [], []
    for layer in range(NL):
        base = 1 + 6 * layer
        rows = jnp.stack(
            [
                shift_vals[base + 2],
                gain_vals[1 + 2 * layer],
                shift_vals[base + 3],
                shift_vals[base + 4],
                gain_vals[2 + 2 * layer],
                shift_vals[base + 5],
            ]
        )
        qkv_bias = jnp.concatenate([shift_vals[base], jnp.zeros((width,), F32), shift_vals[base + 1]])[None, :]
        ffn_bias = b_ff1[layer].astype(F32)[None, :]
        out = forward_layer(layer, lengths, states, rows, qkv_bias, ffn_bias, w_qkv, w_out, w_ff1, w_ff2)
        xlow, mixed, lse, ctxt, n1, s1, mlow, gp, act, n2, s2, states = out
        saved.append((mixed, lse, n1, s1, gp, n2, s2) + tuple((own, cube.core(own)) for own in (xlow, ctxt, mlow, act)))
        layer_rows.append(rows)
    hidden_out = states.astype(LOW).reshape(1, tokens, width)

    small = cube.small
    blocks = 8
    plans = {1: (("x", "a", "b", "y"), ("a", "b", "x", "y"), ("b", "x", "a", "y")),
             0: (("y", "x", "a", "b"), ("x", "a", "b", "y"), ("a", "b", "x", "y"))}
    gain_grads = [None] * (2 * NL + 1)
    shift_grads = [None] * (6 * NL + 1)
    bias_grads = [None] * NL
    shares = [None] * NL
    grad = cotangent.reshape(tokens, width)
    core = coords[:1]
    for layer in reversed(range(NL)):
        base = 1 + 6 * layer
        mixed, lse, n1, s1, gp, n2, s2, x2, ctx2, mid2, act2 = saved[layer]
        plan = plans[layer] if small else (None, None, None)
        pre_keep, pre_send, sec_keep, sec_send, first, fst_keep, fst_send, gctx, sums, bias = feed_back(
            layer, core, grad, n2, s2, n1, s1, layer_rows[layer], gp, w_out, w_ff1, w_ff2
        )
        gain_grads[2 + 2 * layer] = sums[0]
        shift_grads[base + 5] = sums[1]
        shift_grads[base + 4] = sums[2]
        gain_grads[1 + 2 * layer] = sums[3]
        shift_grads[base + 3] = sums[4]
        shift_grads[base + 2] = sums[5]
        bias_grads[layer] = bias[0]
        pre2 = (pre_keep, cube.core(pre_send))
        sec2 = (sec_keep, cube.core(sec_send))
        fst2 = (fst_keep, cube.core(fst_send))
        mix_keep, mix_send, grad, att_sums = attend_back(layer, core, lengths, mixed, lse, gctx, first, w_qkv)
        shift_grads[base] = att_sums[0]
        shift_grads[base + 1] = att_sums[1]
        mix2 = (mix_keep, cube.core(mix_send))
        one = feed_weights(blocks, plan[0], plan[1], coords, mid2, pre2, sec2, act2, after=())
        mix = attend_weights(blocks, plan[2], coords, x2, mix2, ctx2, fst2, after=one[:1])
        if small:
            chains = [
                Chain(cube, plan[0], one[0], one[1]),
                Chain(cube, plan[1], one[2], one[3]),
                Chain(cube, plan[2], mix[0], mix[1]),
            ]
            share_one, share_two, share_mix = [chain.share for chain in chains]
            if layer == 1:
                grad = lax.optimization_barrier((grad, mix[0]))[0]
        else:
            whole = lambda keep, send: jnp.concatenate([keep, send], axis=0)
            share_one = cube.reduce(whole(one[0], one[1]).reshape(width, -1))
            two = whole(one[2], one[3])
            two = two.reshape(blocks, width // 2, -1).transpose(0, 2, 1).reshape(-1, width // 2)
            share_two = cube.reduce(two).T
            share_mix = cube.reduce(whole(mix[0], mix[1]).reshape(width, -1))
        shares[layer] = (share_one, share_two, share_mix)

    gain_grads[0] = jnp.sum(grad * normed_emb, axis=0)
    shift_grads[0] = jnp.sum(grad, axis=0)
    grad_embedded = norm_back(grad, normed_emb, spread_emb, gain_vals[0])
    emb_low = grad_embedded.astype(LOW)
    outgoing = dot(dispatch, emb_low, ROWS).astype(LOW)
    incoming = lax.all_to_all(
        outgoing.reshape(owners, slot_count, width), "vocab", split_axis=0, concat_axis=0, tiled=True
    ).reshape(slots, width)
    table_part = dot(row_hit, incoming, ROWS).astype(LOW)
    keep, send = cube.halves(table_part)
    table_part = add(keep, cube.core(send))
    for bit in range(1, cube.dp_bits):
        table_part = add(table_part, cube.permute(table_part, 1 << bit, 0))
    table_out = cube.join_core(table_part, -1)

    type_zero = jnp.sum(jnp.where(type_flat[:, None] == 0, grad_embedded, 0.0), axis=0)
    type_one = jnp.sum(jnp.where(type_flat[:, None] == 1, grad_embedded, 0.0), axis=0)
    share_width = width // owners
    small_sums = jnp.concatenate(
        [
            jnp.stack([type_zero, type_one] + gain_grads + shift_grads).reshape(-1, owners, share_width),
            jnp.stack(bias_grads).reshape(NL, owners, -1, share_width).transpose(0, 2, 1, 3).reshape(-1, owners, share_width),
        ],
        axis=0,
    )
    small_rows = small_sums.shape[0]
    small_sums = small_sums.transpose(1, 0, 2).reshape(owners, -1)
    packed_rows = -(-small_sums.shape[1] // width)
    small_sums = jnp.pad(small_sums, ((0, 0), (0, packed_rows * width - small_sums.shape[1])))
    pos_rows = tokens // owners
    packed = jnp.concatenate(
        [grad_embedded.reshape(owners, pos_rows, width), small_sums.reshape(owners, packed_rows, width)], axis=1
    ).astype(LOW)
    keep, send = cube.halves(packed.reshape(-1, width))
    share_pack = cube.reduce(add(keep, cube.core(send)))

    wide = 3 * width // 2
    one_out = cube.join_core(jnp.stack([share[0] for share in shares]), 2)
    two_out = cube.join_core(jnp.stack([share[1] for share in shares]), 1).transpose(0, 2, 1)
    mix = jnp.stack([share[2] for share in shares])
    mix_other = cube.core(mix)
    first = cube.core_is_first()
    qkv_out = cube.ordered(first, mix[..., :wide], mix_other[..., :wide], 2).astype(F32)
    wout_out = cube.ordered(first, mix[..., wide:], mix_other[..., wide:], 2).astype(F32)
    pack_out = cube.join_core(share_pack, 1)
    pos_out = pack_out[:pos_rows]
    small_out = pack_out[pos_rows:].reshape(-1)[: small_rows * share_width].reshape(small_rows, share_width)
    at_gain, at_shift, at_bias = 2, 2 + 2 * NL + 1, 2 + 2 * NL + 1 + 6 * NL + 1
    return (
        hidden_out,
        table_out,
        pos_out,
        small_out[:at_gain],
        small_out[at_gain:at_shift],
        small_out[at_shift:at_bias],
        qkv_out,
        wout_out,
        small_out[at_bias:].reshape(NL, -1),
        one_out,
        two_out,
    )


def solution(mesh):
    cube = Cube(mesh.shape["dp"], mesh.shape["vocab"])
    both = ("dp", "vocab")
    in_specs = (
        P(both, None),
        P(both),
        P(both, None),
        P("vocab", None),
        P(),
        P(),
        P(),
        P(),
        P(),
        P(),
        P(),
        P(),
        P(),
        P(both, None, None),
    )
    out_specs = (
        P(both, None, None),
        P("vocab", None),
        P("vocab", None),
        P(None, "vocab"),
        P(None, "vocab"),
        P(None, "vocab"),
        P(None, "vocab", None),
        P(None, "vocab", None),
        P(None, "vocab"),
        P(None, "vocab", None),
        P(None, "vocab", None),
    )
    return jax.shard_map(
        functools.partial(on_device, cube), mesh=mesh, in_specs=in_specs, out_specs=out_specs, check_vma=False
    )
```

time: 1300 us -> 512 us (0.39)
  waiting for transfers between devices: 912 us -> 176 us
  Pallas kernels: 0 us -> 180 us
  matrix products: 189 us -> 10.5 us
  starting transfers between devices: 9.33 us -> 78.2 us
  other arithmetic: 92.1 us -> 44.4 us
  local copies, waits for them, and re-layouts: 48.4 us -> 14.2 us
  blocking collectives: 19.3 us -> 0 us
  between operations: 17.4 us -> 2.58 us
    reduce_scatter x5 -> x0, waiting for transfers between devices: 484 us -> none  [the longest x1 166 us: on_device(): lax.psum_scatter(two_sums.astype(jnp.bfloat16), 'vocab', scatter_dimensio...]
    unnamed x14 -> x0, waiting for transfers between devices: 255 us -> none
    pallas_call x0 -> x10, Pallas kernels: none -> 180 us  [run(): pl.pallas_call(body, out_shape=out_shape, in_specs=list(in_specs) + [ANY]...]
    dot_general x36 -> x4, matrix products: 189 us -> 10.5 us  [dot(): lax.dot_general(left_op, right_op, (dims, ((), ())), preferred_element_ty...]
    ppermute x0 -> x53, waiting for transfers between devices: none -> 140 us  [permute(): return lax.ppermute(value, AXES, pairs)]
    psum x1 -> x0, waiting for transfers between devices: 94.9 us -> none  [on_device(): lax.psum(table_part.astype(jnp.bfloat16), 'dp').astype(jnp.float32)]
    ppermute x0 -> x53, starting transfers between devices: none -> 61.9 us  [permute(): return lax.ppermute(value, AXES, pairs)]
    all_to_all x2 -> x3, waiting for transfers between devices: 78.8 us -> 35.6 us  [the longest x1 31.1 us: on_device(): lax.all_to_all(found_rows.reshape(owners, slot_count, width), 'vocab', sp...]
  transfers between devices with their start and end apart: 12 -> 56, of which waited for: 11 -> 24; matrix products, arithmetic and copies ran while one was open for 7% -> 9% of each run, Pallas kernels for 0% -> 15%
where the time goes in v2:
time: 512 us; the launch traced here: 506 us
  Pallas kernels  180 us (35%)
  waiting for transfers between devices  176 us (34%)
  starting transfers between devices  78.2 us (15%)
  other arithmetic  44.4 us (9%)
  local copies, waits for them, and re-layouts  14.2 us (3%)
  matrix products  10.5 us (2%)
    pallas_call x10, Pallas kernels, run(): pl.pallas_call(body, out_shape=out_shape, in_specs=list(in_specs) + [ANY]...  180 us
    ppermute x53, waiting for transfers between devices, permute(): return lax.ppermute(value, AXES, pairs)  140 us
    ppermute x53, starting transfers between devices, permute(): return lax.ppermute(value, AXES, pairs)  61.9 us
    all_to_all x1, waiting for transfers between devices, on_device(): lax.all_to_all(found_rows.reshape(owners, slot_count, width), 'vocab', sp...  31.1 us
    convert_element_type x31, other arithmetic, add(): return (left_op.astype(F32) + right_op.astype(F32)).astype(LOW)  20.4 us
    dot_general x4, matrix products, dot(): lax.dot_general(left_op, right_op, (dims, ((), ())), preferred_element_ty...  10.5 us
  transfers between devices with their start and end apart: 56, of which 24 were waited for; matrix products, arithmetic and copies ran while one was open for 9% of the time, Pallas kernels for 15%

profile of v2, /device:TPU:0, one launch (start us, length us, event | category | flops | bytes accessed | tf_op | source)
XLA Modules:
  0.0 505.8 jit_solution(13340202181677028830)
XLA Ops:
  2.1 7.3 %all-to-all-start = ((s32[8,1,512]{2,1,0:T(1,128)}), s32[8,1,512]{2,1,0:T(1,128)S(1)}, u32[]{:S(2)}, u32[]{:S(2)}) async-start(s32[8,1,512]{2,1,0:T(1,128)} %broadcast_in_dim.94), calls=%async_computation | async-start | bytes 32768 | tf_op jit(solution)/shard_map/all_to_all | solution.py:657
  30.5 31.1 %all-to-all-done.1 = bf16[8,128,768]{2,1,0:T(8,128)(2,1)} async-done(((bf16[8,128,768]{2,1,0:T(8,128)(2,1)}), bf16[8,128,768]{2,1,0:T(8,128)(2,1)}, u32[]{:S(2)}, u32[]{:S(2)}) %all-to-all-start.1) | async-done | bytes 1572896 | tf_op jit(solution)/shard_map/all_to_all | solution.py:669
  66.2 30.3 %forward_layer.2 = (bf16[512,768]{1,0:T(8,128)(2,1)}, bf16[512,2304]{1,0:T(8,128)(2,1)}, f32[12,512]{1,0:T(8,128)}, bf16[768,512]{1,0:T(8,128)(2,1)}, f32[512,76...) custom-call(s32[1]{0:T(128)S(6)} %copy.82.refs_0_.refs_1_, ...), custom_call_target="tpu_custom_call" | custom-call | flops 8858370048 | bytes 31457280 | tf_op jit(solution)/shard_map/forward_layer/pallas_call | solution.py:26
  96.5 30.2 %forward_layer.3 = (bf16[512,768]{1,0:T(8,128)(2,1)}, bf16[512,2304]{1,0:T(8,128)(2,1)}, f32[12,512]{1,0:T(8,128)}, bf16[768,512]{1,0:T(8,128)(2,1)}, f32[512,76...) custom-call(s32[1]{0:T(128)S(6)} %copy.82.refs_0_.refs_1_, ...), custom_call_target="tpu_custom_call" | custom-call | flops 8858370048 | bytes 31457280 | tf_op jit(solution)/shard_map/forward_layer/pallas_call | solution.py:26
  126.9 19.9 %feed_back.2 = (bf16[512,1536]{1,0:T(8,128)(2,1)}, bf16[512,1536]{1,0:T(8,128)(2,1)}, bf16[512,384]{1,0:T(8,128)(2,1)}, bf16[512,384]{1,0:T(8,128)(2,1)}, f32[51...) custom-call(s32[1]{0:T(128)} %bitcast.12.refs_0_, ...), custom_call_target="tpu_custom_call" | custom-call | flops 5435817984 | bytes 20971520 | tf_op jit(solution)/shard_map/feed_back/pallas_call | solution.py:26
  147.8 17.2 %attend_back.2 = (bf16[512,1152]{1,0:T(8,128)(2,1)}, bf16[512,1152]{1,0:T(8,128)(2,1)}, f32[512,768]{1,0:T(8,128)}, f32[2,768]{1,0:T(2,128)}) custom-call(s32[1]{0:T(128)} %bitcast.12.refs_0_, s32[1]{0:T(128)S(6)} %copy.82.refs_0_.refs_1_, bf16[512,2304]{1,0:T(8,128)(2,1)} %get-tuple-element.80.refs_2_, f32[12,512]{1,0:T(8,128)} %get-tuple-element.81.refs_3_, ...), custom_call_target="tpu_custom_call" | custom-call | flops 6643777536 | bytes 12582912 | tf_op jit(solution)/shard_map/attend_back/pallas_call | solution.py:26
  168.6 14.1 %feed_weights.2 = (bf16[8,48,1536]{2,1,0:T(8,128)(2,1)}, bf16[8,48,1536]{2,1,0:T(8,128)(2,1)}, bf16[8,192,384]{2,1,0:T(8,128)(2,1)}, bf16[8,192,384]{2,1,0:T(8,128)(2,1)}) custom-call(s32[5]{0:T(128)} %stack.86.refs_0_, bf16[512,768]{1,0:T(8,128)(2,1)} %get-tuple-element.96.refs_1_, bf16[512,768]{1,0:T(8,128)(2,1)} %collective-permute-done.4.refs_2_, ...), custom_call_target="tpu_custom_call" | custom-call | flops 4831838208 | bytes 16777216 | tf_op jit(solution)/shard_map/feed_weights/pallas_call | solution.py:26
  183.5 8.4 %attend_weights.2 = (bf16[8,48,1536]{2,1,0:T(8,128)(2,1)}, bf16[8,48,1536]{2,1,0:T(8,128)(2,1)}) custom-call(s32[5]{0:T(128)} %stack.86.refs_0_, bf16[512,768]{1,0:T(8,128)(2,1)} %get-tuple-element.90.refs_1_, bf16[512,768]{1,0:T(8,128)(2,1)} %collective-permute-done.refs_2_, bf16[512,1152]{1,0:T(8,128)(2,1)} %get-tuple-element.91.refs_3_, ...), custom_call_target="tpu_custom_call" | custom-call | flops 2415919104 | bytes 10485760 | tf_op jit(solution)/shard_map/attend_weights/pallas_call | solution.py:26
  191.9 20.1 %feed_back.3 = (bf16[512,1536]{1,0:T(8,128)(2,1)}, bf16[512,1536]{1,0:T(8,128)(2,1)}, bf16[512,384]{1,0:T(8,128)(2,1)}, bf16[512,384]{1,0:T(8,128)(2,1)}, f32[51...) custom-call(s32[1]{0:T(128)} %bitcast.12.refs_0_, ...), custom_call_target="tpu_custom_call" | custom-call | flops 5435817984 | bytes 20971520 | tf_op jit(solution)/shard_map/feed_back/pallas_call | solution.py:26
  212.0 17.2 %attend_back.3 = (bf16[512,1152]{1,0:T(8,128)(2,1)}, bf16[512,1152]{1,0:T(8,128)(2,1)}, f32[512,768]{1,0:T(8,128)}, f32[2,768]{1,0:T(2,128)}) custom-call(s32[1]{0:T(128)} %bitcast.12.refs_0_, s32[1]{0:T(128)S(6)} %copy.82.refs_0_.refs_1_, bf16[512,2304]{1,0:T(8,128)(2,1)} %get-tuple-element.78.refs_2_, f32[12,512]{1,0:T(8,128)} %get-tuple-element.79.refs_3_, ...), custom_call_target="tpu_custom_call" | custom-call | flops 6643777536 | bytes 12582912 | tf_op jit(solution)/shard_map/attend_back/pallas_call | solution.py:26
  236.6 11.2 %collective-permute-done.12 = bf16[272,384]{1,0:T(8,128)(2,1)S(1)} collective-permute-done((bf16[272,384]{1,0:T(8,128)(2,1)S(1)}, bf16[272,384]{1,0:T(8,128)(2,1)S(1)}, u32[]{:S(2)}, u32[]{:S(2)}) %collective-permute-start.12) | collective-permute-done | bytes 208928 | tf_op jit(solution)/shard_map/ppermute | solution.py:555
  270.0 9.8 %collective-permute-done.29 = bf16[8,48,1536]{2,1,0:T(8,128)(2,1)} collective-permute-done((bf16[8,48,1536]{2,1,0:T(8,128)(2,1)}, bf16[8,48,1536]{2,1,0:T(8,128)(2,1)}, u32[]{:S(2)}, u32[]{:S(2)}) %collective-permute-start.29) | collective-permute-done | bytes 1179680 | tf_op jit(solution)/shard_map/ppermute | solution.py:555
  289.6 14.8 %collective-permute-done.48 = bf16[8,192,384]{2,1,0:T(8,128)(2,1)} collective-permute-done((bf16[8,192,384]{2,1,0:T(8,128)(2,1)}, bf16[8,192,384]{2,1,0:T(8,128)(2,1)}, u32[]{:S(2)}, u32[]{:S(2)}) %collective-permute-start.48) | collective-permute-done | bytes 1179680 | tf_op jit(solution)/shard_map/ppermute | solution.py:555
  313.8 14.3 %feed_weights.3 = (bf16[8,48,1536]{2,1,0:T(8,128)(2,1)}, bf16[8,48,1536]{2,1,0:T(8,128)(2,1)}, bf16[8,192,384]{2,1,0:T(8,128)(2,1)}, bf16[8,192,384]{2,1,0:T(8,128)(2,1)}) custom-call(s32[5]{0:T(128)} %stack.86.refs_0_, bf16[512,768]{1,0:T(8,128)(2,1)} %get-tuple-element.125.refs_1_, bf16[512,768]{1,0:T(8,128)(2,1)} %collective-permute-done.21.refs_2_, ...), custom_call_target="tpu_custom_call" | custom-call | flops 4831838208 | bytes 16777216 | tf_op jit(solution)/shard_map/feed_weights/pallas_call | solution.py:26
  328.1 5.5 %collective-permute-start.40 = (bf16[4,48,1536]{2,1,0:T(8,128)(2,1)}, bf16[4,48,1536]{2,1,0:T(8,128)(2,1)}, u32[]{:S(2)}, u32[]{:S(2)}) collective-permute-start(bf16[4,48,1536]{2,1,0:T(8,128)(2,1)} %get-tuple-element.178), channel_id=1, source_target_pairs={{0,2},{1,3},{2,0},{3,1},{4,6},{5,7},{6,4},{7,5},{8,10},{9,11},{10,... | collective-permute-start | bytes 1769480 | tf_op jit(solution)/shard_map/ppermute | solution.py:555
  337.2 8.4 %attend_weights.3 = (bf16[8,48,1536]{2,1,0:T(8,128)(2,1)}, bf16[8,48,1536]{2,1,0:T(8,128)(2,1)}) custom-call(s32[5]{0:T(128)} %stack.86.refs_0_, bf16[512,768]{1,0:T(8,128)(2,1)} %get-tuple-element.119.refs_1_, bf16[512,768]{1,0:T(8,128)(2,1)} %collective-permute-done.17.refs_2_, bf16[512,1152]{1,0:T(8,128)(2,1)} %get-tuple-element.120.refs_3_, ...), custom_call_target="tpu_custom_call" | custom-call | flops 2415919104 | bytes 10485760 | tf_op jit(solution)/shard_map/attend_weights/pallas_call | solution.py:26
  353.4 10.9 %collective-permute-done.49 = bf16[4,192,384]{2,1,0:T(8,128)(2,1)} collective-permute-done((bf16[4,192,384]{2,1,0:T(8,128)(2,1)}, bf16[4,192,384]{2,1,0:T(8,128)(2,1)}, u32[]{:S(2)}, u32[]{:S(2)}) %collective-permute-start.49) | collective-permute-done | bytes 589856 | tf_op jit(solution)/shard_map/ppermute | solution.py:555
  366.2 27.0 %collective-permute-done.31 = bf16[2,48,1536]{2,1,0:T(8,128)(2,1)S(1)} collective-permute-done((bf16[2,48,1536]{2,1,0:T(8,128)(2,1)S(1)}, bf16[2,48,1536]{2,1,0:T(8,128)(2,1)S(1)}, u32[]{:S(2)}, u32[]{:S(2)}) %collective-permute-start.31) | collective-permute-done | bytes 294944 | tf_op jit(solution)/shard_map/ppermute | solution.py:555
  395.9 5.4 %collective-permute-done.41 = bf16[2,48,1536]{2,1,0:T(8,128)(2,1)S(1)} collective-permute-done((bf16[2,48,1536]{2,1,0:T(8,128)(2,1)S(1)}, bf16[2,48,1536]{2,1,0:T(8,128)(2,1)S(1)}, u32[]{:S(2)}, u32[]{:S(2)}) %collective-permute-start.41) | collective-permute-done | bytes 294944 | tf_op jit(solution)/shard_map/ppermute | solution.py:555
  405.5 5.7 %collective-permute-done.32 = bf16[2,48,1536]{2,1,0:T(8,128)(2,1)S(1)} collective-permute-done((bf16[2,48,1536]{2,1,0:T(8,128)(2,1)S(1)}, bf16[2,48,1536]{2,1,0:T(8,128)(2,1)S(1)}, u32[]{:S(2)}, u32[]{:S(2)}) %collective-permute-start.32) | collective-permute-done | bytes 294944 | tf_op jit(solution)/shard_map/ppermute | solution.py:555
  435.1 10.7 %collective-permute-done.26 = bf16[4,48,1536]{2,1,0:T(8,128)(2,1)S(1)} collective-permute-done((bf16[4,48,1536]{2,1,0:T(8,128)(2,1)S(1)}, bf16[4,48,1536]{2,1,0:T(8,128)(2,1)S(1)}, u32[]{:S(2)}, u32[]{:S(2)}) %collective-permute-start.26) | collective-permute-done | bytes 589856 | tf_op jit(solution)/shard_map/ppermute | solution.py:555
  449.1 7.2 %collective-permute-start.36 = (bf16[2,48,1536]{2,1,0:T(8,128)(2,1)S(1)}, bf16[2,48,1536]{2,1,0:T(8,128)(2,1)S(1)}, u32[]{:S(2)}, u32[]{:S(2)}) collective-permute-start(bf16[2,48,1536]{2,1,0:T(8,128)(2,1)S(1)} %get-tuple-element.190), channel_id=1, source_target_pairs={{0,2},{1,3},{2,0},{3,1},{4,6},{5,7},{6,4},{7,5},{8,10},{9,11},{10,... | collective-permute-start | bytes 884744 | tf_op jit(solution)/shard_map/ppermute | solution.py:555
  475.3 11.4 %collective-permute-done.28 = bf16[2,48,1536]{2,1,0:T(8,128)(2,1)S(1)} collective-permute-done((bf16[2,48,1536]{2,1,0:T(8,128)(2,1)S(1)}, bf16[2,48,1536]{2,1,0:T(8,128)(2,1)S(1)}, u32[]{:S(2)}, u32[]{:S(2)}) %collective-permute-start.28) | collective-permute-done | bytes 294944 | tf_op jit(solution)/shard_map/ppermute | solution.py:555
  487.7 5.4 %collective-permute-done.47 = bf16[2,192,384]{2,1,0:T(8,128)(2,1)S(1)} collective-permute-done((bf16[2,192,384]{2,1,0:T(8,128)(2,1)S(1)}, bf16[2,192,384]{2,1,0:T(8,128)(2,1)S(1)}, u32[]{:S(2)}, u32[]{:S(2)}) %collective-permute-start.47) | collective-permute-done | bytes 294944 | tf_op jit(solution)/shard_map/ppermute | solution.py:555
  (314 shorter events, 159.9 us)
Async XLA Ops:
  20.9 40.7 %all-to-all-start.1 = ((bf16[8,128,768]{2,1,0:T(8,128)(2,1)}), bf16[8,128,768]{2,1,0:T(8,128)(2,1)}, u32[]{:S(2)}, u32[]{:S(2)}) async-start(bf16[8,128,768]{2,1,0:T(8,128)(2,1)} %bitcast.9), calls=%async_computation.1 | async-start | bytes 3145728 | tf_op jit(solution)/shard_map/all_to_all | solution.py:669
  126.8 41.8 %collective-permute-start.7 = (bf16[512,3072]{1,0:T(8,128)(2,1)}, bf16[512,3072]{1,0:T(8,128)(2,1)}, u32[]{:S(2)}, u32[]{:S(2)}) collective-permute-start(bf16[512,3072]{1,0:T(8,128)(2,1)} %get-tuple-element.101.refs_7_), channel_id=1, source_target_pairs={{0,8},{1,9},{2,10},{3,11},{4,12},{5,13},{6,14},{7,15},{8,0},{9,1},... | collective-permute-start | bytes 9437192 | tf_op jit(solution)/shard_map/ppermute | solution.py:555
  235.0 51.4 %collective-permute-start.24 = (bf16[512,3072]{1,0:T(8,128)(2,1)}, bf16[512,3072]{1,0:T(8,128)(2,1)}, u32[]{:S(2)}, u32[]{:S(2)}) collective-permute-start(bf16[512,3072]{1,0:T(8,128)(2,1)} %get-tuple-element.130.refs_7_), channel_id=1, source_target_pairs={{0,8},{1,9},{2,10},{3,11},{4,12},{5,13},{6,14},{7,15},{8,0},{9,1},... | collective-permute-start | bytes 9437192 | tf_op jit(solution)/shard_map/ppermute | solution.py:555
  248.0 31.9 %collective-permute-start.29 = (bf16[8,48,1536]{2,1,0:T(8,128)(2,1)}, bf16[8,48,1536]{2,1,0:T(8,128)(2,1)}, u32[]{:S(2)}, u32[]{:S(2)}) collective-permute-start(bf16[8,48,1536]{2,1,0:T(8,128)(2,1)} %get-tuple-element.134), channel_id=1, source_target_pairs={{0,6},{1,7},{2,4},{3,5},{4,2},{5,3},{6,0},{7,1},{8,14},{9,15},{10,... | collective-permute-start | bytes 3538952 | tf_op jit(solution)/shard_map/ppermute | solution.py:555
  261.2 28.4 %collective-permute-start.39 = (bf16[8,48,1536]{2,1,0:T(8,128)(2,1)}, bf16[8,48,1536]{2,1,0:T(8,128)(2,1)}, u32[]{:S(2)}, u32[]{:S(2)}) collective-permute-start(bf16[8,48,1536]{2,1,0:T(8,128)(2,1)} %get-tuple-element.136), channel_id=1, source_target_pairs={{0,1},{1,0},{2,3},{3,2},{4,5},{5,4},{6,7},{7,6},{8,9},{9,8},{10,11... | collective-permute-start | bytes 3538952 | tf_op jit(solution)/shard_map/ppermute | solution.py:555
  262.8 41.6 %collective-permute-start.48 = (bf16[8,192,384]{2,1,0:T(8,128)(2,1)}, bf16[8,192,384]{2,1,0:T(8,128)(2,1)}, u32[]{:S(2)}, u32[]{:S(2)}) collective-permute-start(bf16[8,192,384]{2,1,0:T(8,128)(2,1)} %get-tuple-element.140), channel_id=1, source_target_pairs={{0,2},{1,3},{2,0},{3,1},{4,6},{5,7},{6,4},{7,5},{8,10},{9,11},{10,... | collective-permute-start | bytes 3538952 | tf_op jit(solution)/shard_map/ppermute | solution.py:555
  265.4 157.0 %all-to-all-start.2 = ((bf16[8,128,768]{2,1,0:T(8,128)(2,1)}), bf16[8,128,768]{2,1,0:T(8,128)(2,1)S(1)}, u32[]{:S(2)}, u32[]{:S(2)}) async-start(bf16[8,128,768]{2,1,0:T(8,128)(2,1)} %bitcast.66), calls=%async_computation.2 | async-start | bytes 3145728 | tf_op jit(solution)/shard_map/all_to_all | solution.py:761
  279.8 30.6 %collective-permute-start.22 = (bf16[512,1536]{1,0:T(8,128)(2,1)}, bf16[512,1536]{1,0:T(8,128)(2,1)}, u32[]{:S(2)}, u32[]{:S(2)}) collective-permute-start(bf16[512,1536]{1,0:T(8,128)(2,1)} %get-tuple-element.127), channel_id=1, source_target_pairs={{0,8},{1,9},{2,10},{3,11},{4,12},{5,13},{6,14},{7,15},{8,0},{9,1},... | collective-permute-start | bytes 4718600 | tf_op jit(solution)/shard_map/ppermute | solution.py:555
  285.8 42.2 %collective-permute-start.17 = (bf16[512,768]{1,0:T(8,128)(2,1)}, bf16[512,768]{1,0:T(8,128)(2,1)}, u32[]{:S(2)}, u32[]{:S(2)}) collective-permute-start(bf16[512,768]{1,0:T(8,128)(2,1)} %get-tuple-element.119.refs_1_), channel_id=1, source_target_pairs={{0,8},{1,9},{2,10},{3,11},{4,12},{5,13},{6,14},{7,15},{8,0},{9,1},... | collective-permute-start | bytes 2359304 | tf_op jit(solution)/shard_map/ppermute | solution.py:555
  286.4 47.2 %collective-permute-start.19 = (bf16[768,512]{1,0:T(8,128)(2,1)}, bf16[768,512]{1,0:T(8,128)(2,1)}, u32[]{:S(2)}, u32[]{:S(2)}) collective-permute-start(bf16[768,512]{1,0:T(8,128)(2,1)} %get-tuple-element.122.refs_5_), channel_id=1, source_target_pairs={{0,8},{1,9},{2,10},{3,11},{4,12},{5,13},{6,14},{7,15},{8,0},{9,1},... | collective-permute-start | bytes 2359304 | tf_op jit(solution)/shard_map/ppermute | solution.py:555
  289.6 47.6 %collective-permute-start.18 = (bf16[512,1152]{1,0:T(8,128)(2,1)}, bf16[512,1152]{1,0:T(8,128)(2,1)}, u32[]{:S(2)}, u32[]{:S(2)}) collective-permute-start(bf16[512,1152]{1,0:T(8,128)(2,1)} %get-tuple-element.121), channel_id=1, source_target_pairs={{0,8},{1,9},{2,10},{3,11},{4,12},{5,13},{6,14},{7,15},{8,0},{9,1},... | collective-permute-start | bytes 3538952 | tf_op jit(solution)/shard_map/ppermute | solution.py:555
  310.0 27.2 %collective-permute-start.20 = (bf16[512,384]{1,0:T(8,128)(2,1)}, bf16[512,384]{1,0:T(8,128)(2,1)}, u32[]{:S(2)}, u32[]{:S(2)}) collective-permute-start(bf16[512,384]{1,0:T(8,128)(2,1)} %get-tuple-element.124), channel_id=1, source_target_pairs={{0,8},{1,9},{2,10},{3,11},{4,12},{5,13},{6,14},{7,15},{8,0},{9,1},... | collective-permute-start | bytes 1179656 | tf_op jit(solution)/shard_map/ppermute | solution.py:555
  310.4 36.8 %collective-permute-start.30 = (bf16[4,48,1536]{2,1,0:T(8,128)(2,1)}, bf16[4,48,1536]{2,1,0:T(8,128)(2,1)}, u32[]{:S(2)}, u32[]{:S(2)}) collective-permute-start(bf16[4,48,1536]{2,1,0:T(8,128)(2,1)} %get-tuple-element.182), channel_id=1, source_target_pairs={{0,1},{1,0},{2,3},{3,2},{4,5},{5,4},{6,7},{7,6},{8,9},{9,8},{10,11... | collective-permute-start | bytes 1769480 | tf_op jit(solution)/shard_map/ppermute | solution.py:555
  328.1 22.3 %collective-permute-start.40 = (bf16[4,48,1536]{2,1,0:T(8,128)(2,1)}, bf16[4,48,1536]{2,1,0:T(8,128)(2,1)}, u32[]{:S(2)}, u32[]{:S(2)}) collective-permute-start(bf16[4,48,1536]{2,1,0:T(8,128)(2,1)} %get-tuple-element.178), channel_id=1, source_target_pairs={{0,2},{1,3},{2,0},{3,1},{4,6},{5,7},{6,4},{7,5},{8,10},{9,11},{10,... | collective-permute-start | bytes 1769480 | tf_op jit(solution)/shard_map/ppermute | solution.py:555
  333.5 30.7 %collective-permute-start.49 = (bf16[4,192,384]{2,1,0:T(8,128)(2,1)}, bf16[4,192,384]{2,1,0:T(8,128)(2,1)}, u32[]{:S(2)}, u32[]{:S(2)}) collective-permute-start(bf16[4,192,384]{2,1,0:T(8,128)(2,1)} %get-tuple-element.174), channel_id=1, source_target_pairs={{0,6},{1,7},{2,4},{3,5},{4,2},{5,3},{6,0},{7,1},{8,14},{9,15},{10,... | collective-permute-start | bytes 1769480 | tf_op jit(solution)/shard_map/ppermute | solution.py:555
  345.6 79.3 %collective-permute-start.25 = (bf16[8,48,1536]{2,1,0:T(8,128)(2,1)}, bf16[8,48,1536]{2,1,0:T(8,128)(2,1)}, u32[]{:S(2)}, u32[]{:S(2)}) collective-permute-start(bf16[8,48,1536]{2,1,0:T(8,128)(2,1)} %get-tuple-element.133), channel_id=1, source_target_pairs={{0,2},{1,3},{2,0},{3,1},{4,6},{5,7},{6,4},{7,5},{8,10},{9,11},{10,... | collective-permute-start | bytes 3538952 | tf_op jit(solution)/shard_map/ppermute | solution.py:555
  345.7 85.6 %collective-permute-start.34 = (bf16[8,48,1536]{2,1,0:T(8,128)(2,1)}, bf16[8,48,1536]{2,1,0:T(8,128)(2,1)}, u32[]{:S(2)}, u32[]{:S(2)}) collective-permute-start(bf16[8,48,1536]{2,1,0:T(8,128)(2,1)} %get-tuple-element.135), channel_id=1, source_target_pairs={{0,16},{1,17},{2,18},{3,19},{4,20},{5,21},{6,22},{7,23},{8,24},{9,... | collective-permute-start | bytes 3538952 | tf_op jit(solution)/shard_map/ppermute | solution.py:555
  347.3 86.2 %collective-permute-start.44 = (bf16[8,192,384]{2,1,0:T(8,128)(2,1)}, bf16[8,192,384]{2,1,0:T(8,128)(2,1)}, u32[]{:S(2)}, u32[]{:S(2)}) collective-permute-start(bf16[8,192,384]{2,1,0:T(8,128)(2,1)} %get-tuple-element.138), channel_id=1, source_target_pairs={{0,1},{1,0},{2,3},{3,2},{4,5},{5,4},{6,7},{7,6},{8,9},{9,8},{10,11... | collective-permute-start | bytes 3538952 | tf_op jit(solution)/shard_map/ppermute | solution.py:555
  350.3 42.8 %collective-permute-start.31 = (bf16[2,48,1536]{2,1,0:T(8,128)(2,1)S(1)}, bf16[2,48,1536]{2,1,0:T(8,128)(2,1)S(1)}, u32[]{:S(2)}, u32[]{:S(2)}) collective-permute-start(bf16[2,48,1536]{2,1,0:T(8,128)(2,1)S(1)} %add_convert_fusion.31), channel_id=1, source_target_pairs={{0,2},{1,3},{2,0},{3,1},{4,6},{5,7},{6,4},{7,5},{8,10},{9,11},{10,... | collective-permute-start | bytes 884744 | tf_op jit(solution)/shard_map/ppermute | solution.py:555
  364.3 37.0 %collective-permute-start.41 = (bf16[2,48,1536]{2,1,0:T(8,128)(2,1)S(1)}, bf16[2,48,1536]{2,1,0:T(8,128)(2,1)S(1)}, u32[]{:S(2)}, u32[]{:S(2)}) collective-permute-start(bf16[2,48,1536]{2,1,0:T(8,128)(2,1)S(1)} %add_convert_fusion.25), channel_id=1, source_target_pairs={{0,6},{1,7},{2,4},{3,5},{4,2},{5,3},{6,0},{7,1},{8,14},{9,15},{10,... | collective-permute-start | bytes 884744 | tf_op jit(solution)/shard_map/ppermute | solution.py:555
  424.8 35.9 %collective-permute-start.8 = (bf16[960,384]{1,0:T(8,128)(2,1)S(1)}, bf16[960,384]{1,0:T(8,128)(2,1)S(1)}, u32[]{:S(2)}, u32[]{:S(2)}) collective-permute-start(bf16[960,384]{1,0:T(8,128)(2,1)S(1)} %constant_dynamic-slice_fusion.4), channel_id=1, source_target_pairs={{0,8},{1,9},{2,10},{3,11},{4,12},{5,13},{6,14},{7,15},{8,0},{9,1},... | collective-permute-start | bytes 2211848 | tf_op jit(solution)/shard_map/ppermute | solution.py:555
  435.0 22.3 %collective-permute-start.45 = (bf16[4,192,384]{2,1,0:T(8,128)(2,1)S(1)}, bf16[4,192,384]{2,1,0:T(8,128)(2,1)S(1)}, u32[]{:S(2)}, u32[]{:S(2)}) collective-permute-start(bf16[4,192,384]{2,1,0:T(8,128)(2,1)S(1)} %get-tuple-element.172), channel_id=1, source_target_pairs={{0,2},{1,3},{2,0},{3,1},{4,6},{5,7},{6,4},{7,5},{8,10},{9,11},{10,... | collective-permute-start | bytes 1769480 | tf_op jit(solution)/shard_map/ppermute | solution.py:555
  460.9 34.1 %collective-permute-start.9 = (bf16[960,384]{1,0:T(8,128)(2,1)S(1)}, bf16[960,384]{1,0:T(8,128)(2,1)S(1)}, u32[]{:S(2)}, u32[]{:S(2)}) collective-permute-start(bf16[960,384]{1,0:T(8,128)(2,1)S(1)} %add_convert_fusion.1), channel_id=1, source_target_pairs={{0,16},{1,17},{2,18},{3,19},{4,20},{5,21},{6,22},{7,23},{8,24},{9,... | collective-permute-start | bytes 2211848 | tf_op jit(solution)/shard_map/ppermute | solution.py:555
  462.6 24.1 %collective-permute-start.28 = (bf16[2,48,1536]{2,1,0:T(8,128)(2,1)S(1)}, bf16[2,48,1536]{2,1,0:T(8,128)(2,1)S(1)}, u32[]{:S(2)}, u32[]{:S(2)}) collective-permute-start(bf16[2,48,1536]{2,1,0:T(8,128)(2,1)S(1)} %add_convert_fusion.34), channel_id=1, source_target_pairs={{0,16},{1,17},{2,18},{3,19},{4,20},{5,21},{6,22},{7,23},{8,24},{9,... | collective-permute-start | bytes 884744 | tf_op jit(solution)/shard_map/ppermute | solution.py:555
  (57 other events, 612.3 us)

commit v3 on v2

v3 whole, which is shorter than its diff:
```python
import functools
import jax
import jax.numpy as jnp
from jax import lax
from jax.experimental import pallas as pl
from jax.experimental.pallas import tpu as pltpu
from jax.sharding import PartitionSpec as P

HEADS = 12
HEAD_DIM = 64
NL = 2
norm_eps = 1e-12
SCALE = HEAD_DIM ** (-0.5)
ANY = pl.BlockSpec(memory_space=pl.ANY)
HBM = pl.BlockSpec(memory_space=pltpu.HBM)
VM = pl.BlockSpec(memory_space=pltpu.VMEM)
SM = pl.BlockSpec(memory_space=pltpu.SMEM)
F32, LOW = jnp.float32, jnp.bfloat16

CHEAP = pl.CostEstimate(flops=1, bytes_accessed=1, transcendentals=0)
DEAR = pl.CostEstimate(flops=10**10, bytes_accessed=1, transcendentals=0)
LONG = pl.CostEstimate(flops=10**11, bytes_accessed=1, transcendentals=0)


def run(kernel, after, out_shape, in_specs, operands, vmem, **options):
    count = len(operands)

    def body(*refs):
        kernel(*refs[:count], *refs[count + len(after) :])

    return pl.pallas_call(
        body,
        out_shape=out_shape,
        in_specs=list(in_specs) + [ANY] * len(after),
        compiler_params=pltpu.CompilerParams(vmem_limit_bytes=vmem * 1024 * 1024),
        **options,
    )(*operands, *after)


def normalize(inputs):
    centered = inputs - jnp.mean(inputs, axis=-1, keepdims=True)
    spread = lax.rsqrt(jnp.mean(centered * centered, axis=-1, keepdims=True) + norm_eps)
    return (centered * spread, spread)


def norm_back(grad_out, normed, spread, gain_row):
    scaled = grad_out * gain_row
    return spread * (
        scaled
        - jnp.mean(scaled, axis=-1, keepdims=True)
        - normed * jnp.mean(scaled * normed, axis=-1, keepdims=True)
    )


def dot(left_op, right_op, dims=((1,), (0,))):
    return lax.dot_general(left_op, right_op, (dims, ((), ())), preferred_element_type=F32)


ROWS = ((0,), (0,))
COLS = ((1,), (1,))


def gelu_pair(inputs):
    size = jnp.abs(inputs)
    bell = jnp.exp2(inputs * inputs * (-0.5 * 1.4426950408889634))
    t = 1.0 / (1.0 + size * (0.3275911 * 0.7071067811865476))
    tail = t * (
        0.5 * 0.254829592
        + t * (0.5 * -0.284496736 + t * (0.5 * 1.421413741 + t * (0.5 * -1.453152027 + t * (0.5 * 1.061405429))))
    )
    tail = tail * bell
    phi = jnp.where(inputs >= 0.0, 1.0 - tail, tail)
    return inputs * phi, phi + inputs * bell * 0.3989422804014327


def forward_kernel(
    coords_ref, length_ref, replies_ref, slot_ref, kind_ref, pos_ref, type_ref, gains_ref, shifts_ref, ffn_bias_ref,
    grad_ref, wqkv_hbm, wout_hbm, w1_hbm, w2_hbm,
    *refs,
):
    n0_ref, s0_ref, hidden_ref = refs[:3]
    top = refs[3:8]
    outs = [refs[8 + 11 * layer : 19 + 11 * layer] for layer in range(NL)]
    wqkv, wout, w1, w2, sems, xlow, mixed, ctxt, mlow, gp, act, n0, n1, n2, x, osems = refs[6 + 11 * NL :]
    tokens, width = x.shape
    ff = w1.shape[2]
    loads = []
    for layer in range(NL):
        for i, (src, dst) in enumerate([(wqkv_hbm, wqkv), (wout_hbm, wout), (w1_hbm, w1), (w2_hbm, w2)]):
            loads.append(pltpu.make_async_copy(src.at[layer], dst.at[layer], sems.at[4 * layer + i]))
    for load in loads:
        load.start()
    pending, used = {}, [0]

    def emit(name, src, dst, at=None):
        if at is not None:
            src, dst = src.at[:, at], dst.at[:, at]
        copy = pltpu.make_async_copy(src, dst, osems.at[used[0]])
        used[0] += 1
        copy.start()
        pending.setdefault(name, []).append(copy)

    def reuse(name):
        for copy in pending.pop(name, ()):
            copy.wait()

    gains = gains_ref[...].astype(F32)
    shifts = shifts_ref[...].astype(F32)
    number = lax.broadcasted_iota(jnp.int32, (tokens, replies_ref.shape[0]), 1)
    hit = jnp.where(number == slot_ref[:, :1], 1.0, 0.0).astype(LOW)
    types = type_ref[...].astype(F32)
    embedded = dot(hit, replies_ref[...]) + pos_ref[...].astype(F32)
    embedded = embedded + jnp.where(kind_ref[:, :1] > 0.5, types[1:2], types[0:1])
    normed, spread = normalize(embedded)
    n0[...] = normed
    emit("n0", n0, n0_ref)
    s0_ref[...] = jnp.broadcast_to(spread, s0_ref.shape)
    x[...] = normed * gains[0:1] + shifts[0:1]

    key_slot = lax.broadcasted_iota(jnp.int32, (tokens, 128), 0)
    visible = jnp.where(key_slot < length_ref[0], 0.0, -1e30)[:, :1]
    lane = lax.broadcasted_iota(jnp.int32, (tokens, 128), 1)
    chunk = 512

    for layer in range(NL):
        base = 1 + 6 * layer
        xlow_ref, mixed_ref, lse_ref, ctxt_ref, n1_ref, s1_ref, mlow_ref, gp_ref, act_ref = outs[layer][:9]

        reuse("xlow")
        xlow[...] = x[...].astype(LOW)
        emit("xlow", xlow, xlow_ref)
        loads[4 * layer].wait()
        reuse("mixed")
        for i in range(3):
            cols = slice(i * width, (i + 1) * width)
            got = dot(xlow[...], wqkv[layer, :, cols])
            if i != 1:
                row = base + (0 if i == 0 else 1)
                got = got + shifts[row : row + 1]
            mixed[:, cols] = got.astype(LOW)
        emit("mixed", mixed, mixed_ref)
        reuse("ctxt")

        def pair_step(j, carry):
            at = pl.multiple_of(j * 128, 128)
            q = mixed[:, pl.ds(at, 128)] * jnp.asarray(SCALE, LOW)
            k = mixed[:, pl.ds(pl.multiple_of(width + at, 128), 128)]
            v = mixed[:, pl.ds(pl.multiple_of(2 * width + at, 128), 128)]
            vt = v.T
            for h in range(2):
                kh = jnp.where((lane < 64) == (h == 0), k, jnp.zeros_like(k))
                scores = dot(kh, q, COLS) + visible
                top = jnp.max(scores, axis=0, keepdims=True)
                weights = jnp.exp(scores - top)
                total = jnp.sum(weights, axis=0, keepdims=True)
                out = dot(vt[h * 64 : (h + 1) * 64], weights.astype(LOW)) * (1.0 / total)
                ctxt[pl.ds(pl.multiple_of(at + h * 64, 64), 64), :] = out.astype(LOW)
                lse_ref[pl.ds(2 * j + h, 1), :] = top + jnp.log(total)
            return carry

        lax.fori_loop(0, HEADS // 2, pair_step, 0)
        emit("ctxt", ctxt, ctxt_ref)
        loads[4 * layer + 1].wait()
        attended = dot(ctxt[...], wout[layer], ROWS) + shifts[base + 2 : base + 3]
        normed, spread = normalize(x[...] + attended)
        reuse("n1")
        n1[...] = normed
        emit("n1", n1, n1_ref)
        s1_ref[...] = jnp.broadcast_to(spread, s1_ref.shape)
        x[...] = normed * gains[1 + 2 * layer : 2 + 2 * layer] + shifts[base + 3 : base + 4]
        reuse("mlow")
        mlow[...] = x[...].astype(LOW)
        emit("mlow", mlow, mlow_ref)
        loads[4 * layer + 2].wait()
        reuse("gp")
        reuse("act")
        for i in range(ff // chunk):
            cols = slice(i * chunk, (i + 1) * chunk)
            pre = dot(mlow[...], w1[layer, :, cols]) + ffn_bias_ref[layer : layer + 1, cols]
            active, slope = gelu_pair(pre)
            gp[:, cols] = slope.astype(LOW)
            act[:, cols] = active.astype(LOW)
            emit("gp", gp, gp_ref, pl.ds(i * chunk, chunk))
            emit("act", act, act_ref, pl.ds(i * chunk, chunk))
        loads[4 * layer + 3].wait()
        normed, spread = normalize(x[...] + shifts[base + 4 : base + 5] + dot(act[...], w2[layer]))
        if layer < NL - 1:
            n2_ref, s2_ref = outs[layer][9:11]
            n2[...] = normed
            emit("n2", n2, n2_ref)
            s2_ref[...] = jnp.broadcast_to(spread, s2_ref.shape)
        else:
            gain = gains[2 * NL : 2 * NL + 1]
            norm_end(coords_ref[0], grad_ref[...].astype(F32), normed, spread, gain, *top)
        x[...] = normed * gains[2 + 2 * layer : 3 + 2 * layer] + shifts[base + 5 : base + 6]
    hidden_ref[...] = x[...].astype(LOW)
    for name in list(pending):
        reuse(name)


def forward(
    coords, length, replies, slot_col, kind_col, pos, types, gains, shifts, ffn_bias, cotangent, w_qkv, w_out, w_ff1, w_ff2
):
    tokens, width = pos.shape
    ff = w_ff1.shape[2]
    s = jax.ShapeDtypeStruct
    v = pltpu.VMEM
    spread = s((tokens, 128), F32)
    wide = s((tokens, width), F32)
    low = s((tokens, width), LOW)
    layer_out = (
        low, s((tokens, 3 * width), LOW), s((HEADS, tokens), F32), s((width, tokens), LOW),
        wide, spread, low, s((tokens, ff), LOW), s((tokens, ff), LOW), wide, spread,
    )
    layer_spec = (ANY, ANY, VM, ANY, ANY, VM, ANY, ANY, ANY, ANY, VM)
    chunks = ff // 512
    end = norm_end_shapes(tokens, width)
    outs = run(
        forward_kernel,
        (),
        out_shape=(wide, spread, low) + end + layer_out * (NL - 1) + layer_out[:9],
        in_specs=[SM, SM] + [VM] * 9 + [HBM] * 4,
        operands=(
            coords, length, replies, slot_col, kind_col, pos, types, gains, shifts, ffn_bias, cotangent, w_qkv, w_out, w_ff1, w_ff2
        ),
        out_specs=(ANY, VM, VM) + (VM,) * 5 + layer_spec * (NL - 1) + layer_spec[:9],
        scratch_shapes=[
            v((NL, width, 3 * width), LOW), v((NL, width, width), LOW), v((NL, width, ff), LOW), v((NL, ff, width), LOW),
            pltpu.SemaphoreType.DMA((4 * NL,)),
            v((tokens, width), LOW), v((tokens, 3 * width), LOW), v((width, tokens), LOW), v((tokens, width), LOW),
            v((tokens, ff), LOW), v((tokens, ff), LOW), v((tokens, width), F32), v((tokens, width), F32),
            v((tokens, width), F32), v((tokens, width), F32), pltpu.SemaphoreType.DMA((1 + NL * (6 + 2 * chunks),)),
        ],
        cost_estimate=CHEAP,
        vmem=60,
        name="forward",
    )
    return outs[:3], outs[3:8], [outs[8 + 11 * layer : 19 + 11 * layer] for layer in range(NL)]


def part(mine, source, keep_to, send_to):
    half = source.shape[1] // 2

    @pl.when(mine == 0)
    def _():
        keep_to[...] = source[:, :half]
        send_to[...] = source[:, half:]

    @pl.when(mine == 1)
    def _():
        keep_to[...] = source[:, half:]
        send_to[...] = source[:, :half]


def norm_end(mine, grad, n, s, gain, back_ref, low_ref, keep_ref, send_ref, sums_ref):
    sums_ref[0:1] = jnp.sum(grad * n, axis=0, keepdims=True)
    sums_ref[1:2] = jnp.sum(grad, axis=0, keepdims=True)
    back = norm_back(grad, n, s, gain)
    sums_ref[2:3] = jnp.sum(back, axis=0, keepdims=True)
    back_ref[...] = back
    low_ref[...] = back.astype(LOW)
    if keep_ref is not None:
        part(mine, low_ref, keep_ref, send_ref)


def norm_end_shapes(tokens, width):
    s = jax.ShapeDtypeStruct
    half = s((tokens, width // 2), LOW)
    return (s((tokens, width), F32), s((tokens, width), LOW), half, half, s((3, width), F32))


def feed_back_body(mine, second, gp, w2, ready, bias_ref, keep, send):
    chunk = 512
    steps = gp.shape[1] // chunk
    for i in range(steps):
        ready(i)
        cols = slice(i * chunk, (i + 1) * chunk)
        grad_pre = dot(second[...], w2[cols, :], COLS) * gp[:, cols].astype(F32)
        bias_ref[:, cols] = jnp.sum(grad_pre, axis=0, keepdims=True)
        side, at = divmod(i, steps // 2)
        there = slice(at * chunk, (at + 1) * chunk)
        low = grad_pre.astype(LOW)

        @pl.when(mine == side)
        def _():
            keep[:, there] = low

        @pl.when(mine != side)
        def _():
            send[:, there] = low


def both_halves(mine, keep, send, weight):
    half = keep.shape[1]
    first = jnp.where(mine == 0, keep[...], send[...])
    second = jnp.where(mine == 0, send[...], keep[...])
    return dot(first, weight[:, :half], COLS) + dot(second, weight[:, half:], COLS)


def attend_back_body(length_ref, mixed_ref, lse_ref, gctx_ref, att_ref, dmix):
    tokens, width = gctx_ref.shape
    key_slot = lax.broadcasted_iota(jnp.int32, (tokens, 128), 0)
    visible = jnp.where(key_slot < length_ref[0], 0.0, -1e30)[:, :1]
    lane = lax.broadcasted_iota(jnp.int32, (tokens, 128), 1)

    def pair_step(j, carry):
        at = pl.multiple_of(j * 128, 128)
        qcols = pl.ds(at, 128)
        kcols = pl.ds(pl.multiple_of(width + at, 128), 128)
        vcols = pl.ds(pl.multiple_of(2 * width + at, 128), 128)
        q = mixed_ref[:, qcols] * jnp.asarray(SCALE, LOW)
        k = mixed_ref[:, kcols]
        v = mixed_ref[:, vcols]
        g = gctx_ref[:, qcols]
        kt = k.T
        grad_v, grad_k, grad_qt = [], [], []
        for h in range(2):
            mask = (lane < 64) == (h == 0)
            kh = jnp.where(mask, k, jnp.zeros_like(k))
            vh = jnp.where(mask, v, jnp.zeros_like(v))
            probs = jnp.exp(dot(kh, q, COLS) + visible - lse_ref[pl.ds(2 * j + h, 1), :])
            grad_probs = dot(vh, g, COLS)
            weighted = jnp.sum(probs * grad_probs, axis=0, keepdims=True)
            grad_scores = (probs * (grad_probs - weighted)).astype(LOW)
            grad_v.append(dot(probs.astype(LOW), g))
            grad_k.append(dot(grad_scores, q))
            grad_qt.append(dot(kt[h * 64 : (h + 1) * 64], grad_scores))
        grad_q = jnp.concatenate(grad_qt, axis=0).T * SCALE
        grad_v = jnp.where(lane < 64, grad_v[0], grad_v[1])
        grad_k = jnp.where(lane < 64, grad_k[0], grad_k[1])
        att_ref[0:1, qcols] = jnp.sum(grad_q, axis=0, keepdims=True)
        att_ref[1:2, qcols] = jnp.sum(grad_v, axis=0, keepdims=True)
        dmix[:, qcols] = grad_q.astype(LOW)
        dmix[:, kcols] = grad_k.astype(LOW)
        dmix[:, vcols] = grad_v.astype(LOW)
        return carry

    lax.fori_loop(0, HEADS // 2, pair_step, 0)


def chunk_loads(sems, at, pairs, chunk=512):
    loads = []
    (w2_src, w2), (gp_src, gp) = pairs
    for i in range(gp.shape[1] // chunk):
        there = pl.ds(i * chunk, chunk)
        loads.append(
            (
                pltpu.make_async_copy(w2_src.at[there], w2.at[there], sems.at[at + 2 * i]),
                pltpu.make_async_copy(gp_src.at[:, there], gp.at[:, there], sems.at[at + 2 * i + 1]),
            )
        )
    return loads


def feed_kernel(
    layer, coords_ref, e_ref, second, n1_ref, s1_ref, gains_ref, gp_hbm, wout_hbm, w1_hbm, w2_hbm,
    keep_ref, send_ref, bias_ref, first_ref, low_ref, fst_keep_ref, fst_send_ref, gctx_ref, sums_ref,
    gp, wout, w1, w2, keep, send, sems,
):
    mine = coords_ref[0]
    loads = chunk_loads(sems, 4, ((w2_hbm.at[layer], w2), (gp_hbm, gp)))
    for pair in loads:
        for load in pair:
            load.start()
    late = [
        pltpu.make_async_copy(w1_hbm.at[layer], w1, sems.at[0]),
        pltpu.make_async_copy(wout_hbm.at[layer], wout, sems.at[1]),
    ]
    for load in late:
        load.start()

    def ready(i):
        for load in loads[i]:
            load.wait()

    feed_back_body(mine, second, gp, w2, ready, bias_ref, keep, send)
    stores = [
        pltpu.make_async_copy(send, send_ref, sems.at[2]),
        pltpu.make_async_copy(keep, keep_ref, sems.at[3]),
    ]
    for store in stores:
        store.start()
    late[0].wait()
    grad = e_ref[...] + both_halves(mine, keep, send, w1)
    gain = gains_ref[...].astype(F32)[1 + 2 * layer : 2 + 2 * layer]
    norm_end(mine, grad, n1_ref[...], s1_ref[:, :1], gain, first_ref, low_ref, fst_keep_ref, fst_send_ref, sums_ref)
    late[1].wait()
    gctx_ref[...] = dot(low_ref[...], wout[...], COLS).astype(LOW)
    for store in stores:
        store.wait()


def feed(layer, coords, e, second, n1, s1, gains, gp, w_out, w_ff1, w_ff2, after=()):
    tokens, width = n1.shape
    ff = gp.shape[1]
    s = jax.ShapeDtypeStruct
    v = pltpu.VMEM
    half = s((tokens, ff // 2), LOW)
    end = norm_end_shapes(tokens, width)
    return run(
        functools.partial(feed_kernel, layer),
        after,
        out_shape=(half, half, s((1, ff), F32)) + end[:4] + (s((tokens, width), LOW), end[4]),
        in_specs=[SM] + [VM] * 5 + [HBM] * 4,
        operands=(coords, e, second, n1, s1, gains, gp, w_out, w_ff1, w_ff2),
        out_specs=(ANY, ANY) + (VM,) * 7,
        scratch_shapes=[
            v((tokens, ff), LOW), v((width, width), LOW), v((width, ff), LOW), v((ff, width), LOW),
            v((tokens, ff // 2), LOW), v((tokens, ff // 2), LOW), pltpu.SemaphoreType.DMA((4 + 2 * (ff // 512),)),
        ],
        cost_estimate=CHEAP,
        vmem=52,
        name="feed",
    )


def between_kernel(
    layer, coords_ref, length_ref, mixed_ref, lse_ref, gctx_in, first_in, n2_ref, s2_ref, n1_ref, s1_ref, gains_ref,
    gp_hbm, wqkv_hbm, wout_hbm, w1_hbm, w2_hbm,
    mix_keep_ref, mix_send_ref, pre_keep_ref, pre_send_ref,
    att_ref, sec_keep_ref, sec_send_ref, top_ref, bias_ref, first_ref, low_ref, gctx_ref, sums_ref,
    gp, wqkv, wout, w1, w2, dmix, mix_keep, mix_send, keep, send, e, second, sems,
):
    mine = coords_ref[0]
    below = layer - 1
    early = pltpu.make_async_copy(wqkv_hbm.at[layer], wqkv, sems.at[0])
    early.start()
    loads = chunk_loads(sems, 7, ((w2_hbm.at[below], w2), (gp_hbm, gp)))
    for pair in loads:
        for load in pair:
            load.start()
    late = [
        pltpu.make_async_copy(w1_hbm.at[below], w1, sems.at[1]),
        pltpu.make_async_copy(wout_hbm.at[below], wout, sems.at[2]),
    ]
    for load in late:
        load.start()
    stores = []

    def emit(src, dst):
        stores.append(pltpu.make_async_copy(src, dst, sems.at[3 + len(stores)]))
        stores[-1].start()

    attend_back_body(length_ref, mixed_ref, lse_ref, gctx_in, att_ref, dmix)
    part(mine, dmix, mix_keep, mix_send)
    emit(mix_send, mix_send_ref)
    emit(mix_keep, mix_keep_ref)
    early.wait()
    grad = first_in[...] + dot(dmix[...], wqkv[...], COLS)
    gains = gains_ref[...].astype(F32)
    norm_end(
        mine, grad, n2_ref[...], s2_ref[:, :1], gains[2 * layer : 2 * layer + 1], e, second, sec_keep_ref, sec_send_ref, top_ref
    )

    def ready(i):
        for load in loads[i]:
            load.wait()

    feed_back_body(mine, second, gp, w2, ready, bias_ref, keep, send)
    emit(send, pre_send_ref)
    emit(keep, pre_keep_ref)
    late[0].wait()
    grad = e[...] + both_halves(mine, keep, send, w1)
    norm_end(
        mine, grad, n1_ref[...], s1_ref[:, :1], gains[1 + 2 * below : 2 + 2 * below], first_ref, low_ref, None, None, sums_ref
    )
    late[1].wait()
    gctx_ref[...] = dot(low_ref[...], wout[...], COLS).astype(LOW)
    for store in stores:
        store.wait()


def between(layer, coords, length, mixed, lse, gctx, first, n2, s2, n1, s1, gains, gp, w_qkv, w_out, w_ff1, w_ff2, after=()):
    tokens, width = first.shape
    ff = gp.shape[1]
    s = jax.ShapeDtypeStruct
    v = pltpu.VMEM
    mix = s((tokens, 3 * width // 2), LOW)
    pre = s((tokens, ff // 2), LOW)
    sec = s((tokens, width // 2), LOW)
    low = s((tokens, width), LOW)
    three = s((3, width), F32)
    return run(
        functools.partial(between_kernel, layer),
        after,
        out_shape=(
            mix, mix, pre, pre, s((2, width), F32), sec, sec, three, s((1, ff), F32), s((tokens, width), F32), low, low, three,
        ),
        in_specs=[SM, SM] + [VM] * 9 + [HBM] * 5,
        operands=(coords, length, mixed, lse, gctx, first, n2, s2, n1, s1, gains, gp, w_qkv, w_out, w_ff1, w_ff2),
        out_specs=(ANY,) * 4 + (VM,) * 9,
        scratch_shapes=[
            v((tokens, ff), LOW), v((width, 3 * width), LOW), v((width, width), LOW), v((width, ff), LOW), v((ff, width), LOW),
            v((tokens, 3 * width), LOW), v(mix.shape, LOW), v(mix.shape, LOW), v(pre.shape, LOW), v(pre.shape, LOW),
            v((tokens, width), F32), v((tokens, width), LOW), pltpu.SemaphoreType.DMA((7 + 2 * (ff // 512),)),
        ],
        cost_estimate=CHEAP,
        vmem=58,
        name="between",
    )


COORDS = ("core", "x", "a", "b", "y")


def place(coords_ref, plan, result, *outs):
    count = result.shape[0]
    size = count // len(outs)
    dims = [] if plan is None else [dim for turn in plan for dim in turn]
    for i in range(count):
        block = i
        if plan is not None:
            bit = {}
            for n, dim in enumerate(dims):
                relative = (i >> (len(dims) - 1 - n)) & 1
                whole = plan[-1] == ("y",) and n == len(dims) - 1
                bit[dim] = relative if whole else coords_ref[COORDS.index(dim)] ^ relative
            block = 16 * bit.get("core", 0) + 8 * bit["b"] + 4 * bit["a"] + 2 * bit["x"] + bit["y"]
        out = outs[i // size]
        out[i % size] = result[block].astype(out.dtype)


def parts_of(plan):
    return 2 if plan is None else 2 ** len(plan[0])


def load_both(pairs, sems):
    loads = []
    for own, oth, dst in pairs:
        for n, src in enumerate((own, oth)):
            size = own.shape[0]
            load = pltpu.make_async_copy(src, dst.at[pl.ds(n * size, size)], sems.at[len(loads)])
            load.start()
            loads.append(load)
    return loads


def weights_kernel(plans, blocks, coords_ref, *refs):
    count = 8 if len(plans) == 2 else 16
    sources, refs = refs[:count], refs[count:]
    outs = []
    for plan in plans:
        outs.append(refs[: parts_of(plan)])
        refs = refs[parts_of(plan) :]
    sec, act, mid, pre, sect, midt, two, one = refs[:8]
    rest, sems = refs[8:-1], refs[-1]
    tokens = sources[0].shape[0]
    loads = []
    targets = [sec, act, mid, pre]
    if rest:
        x, mix, ctxt, fst, xt, mixed = rest
        targets += [x, mix, ctxt, fst]
    for n, target in enumerate(targets):
        for side in range(2):
            there = pl.ds(side * tokens, tokens)
            view = target.at[:, there] if rest and n == 6 else target.at[there]
            loads.append(pltpu.make_async_copy(sources[2 * n + side], view, sems.at[2 * n + side]))
            loads[-1].start()

    def ready(n):
        loads[2 * n].wait()
        loads[2 * n + 1].wait()

    ready(0)
    sect[...] = sec[...].T
    ready(1)
    rows = two.shape[1]
    cols = act.shape[1] // blocks

    def step_two(i, carry):
        got = dot(sect[...], act[:, pl.ds(pl.multiple_of(i * cols, cols), cols)]).astype(LOW)
        for y in range(2):
            for n in range(4):
                at = (4 * y + n) * rows
                two[2 * i + y, :, n * cols : (n + 1) * cols] = got[at : at + rows]
        return carry

    lax.fori_loop(0, blocks, step_two, 0)
    place(coords_ref, plans[0], two, *outs[0])
    ready(2)
    midt[...] = mid[...].T
    ready(3)
    chunk = 512

    def step_one(i, carry):
        there = pl.ds(pl.multiple_of(i * chunk, chunk), chunk)
        one[:, :, there] = dot(midt[...], pre[:, there]).astype(LOW).reshape(one.shape[:2] + (chunk,))
        return carry

    lax.fori_loop(0, pre.shape[1] // chunk, step_one, 0)
    place(coords_ref, plans[1], one, *outs[1])
    if rest:
        ready(4)
        xt[...] = x[...].T
        ready(5)
        width = fst.shape[1]
        shape = mixed.shape[:2] + (width,)
        for i in range(mix.shape[1] // width):
            there = slice(i * width, (i + 1) * width)
            mixed[:, :, there] = dot(xt[...], mix[:, there]).astype(LOW).reshape(shape)
        ready(6)
        ready(7)
        mixed[:, :, mix.shape[1] :] = dot(ctxt[...], fst[...]).astype(LOW).reshape(shape)
        place(coords_ref, plans[2], mixed, *outs[2])


def weights(blocks, plans, coords, sec, act, mid, pre, attention=(), after=()):
    tokens, width = mid[0].shape
    s = jax.ShapeDtypeStruct
    v = pltpu.VMEM
    count = 2 * blocks
    block = (count, width // count, 2 * width)
    outs = sum(((s((count // parts_of(plan),) + block[1:], LOW),) * parts_of(plan) for plan in plans), ())
    pairs = (sec, act, mid, pre) + tuple(attention)
    both = lambda pair: v((2 * tokens, pair[0].shape[1]), LOW)
    scratch = [both(pair) for pair in (sec, act, mid, pre)]
    scratch += [v((sec[0].shape[1], 2 * tokens), LOW), v((width, 2 * tokens), LOW), v(block, LOW), v(block, LOW)]
    if attention:
        x, mix, ctx, fst = attention
        scratch += [both(x), both(mix), v((width, 2 * tokens), LOW), both(fst), v((width, 2 * tokens), LOW), v(block, LOW)]
    got = run(
        functools.partial(weights_kernel, plans, blocks),
        after,
        out_shape=outs,
        in_specs=[SM] + [ANY] * (2 * len(pairs)),
        operands=(coords,) + tuple(array for pair in pairs for array in pair),
        out_specs=(VM,) * len(outs),
        scratch_shapes=scratch + [pltpu.SemaphoreType.DMA((2 * len(pairs),))],
        cost_estimate=CHEAP,
        vmem=52 if attention else 34,
        name="weights",
    )
    parts = []
    for plan in plans:
        parts.append(got[: parts_of(plan)])
        got = got[parts_of(plan) :]
    return parts


def combine_kernel(forms, *refs):
    count = sum(sum(form[0]) for form in forms)
    ins, outs = refs[:count], refs[count:]
    for terms_of, parts, axis in forms:
        results, outs = outs[:parts], outs[parts:]
        at = 0
        for terms in terms_of:
            mine, ins = ins[:terms], ins[terms:]
            size = mine[0].shape[0] // parts
            rows = mine[0].shape[1]
            for part in range(parts):
                for i in range(size):
                    total = mine[0][part * size + i].astype(F32)
                    for term in mine[1:]:
                        total = total + term[part * size + i].astype(F32)
                    if axis == 0:
                        results[part][at + i] = total.astype(LOW)
                    else:
                        results[part][i, at : at + rows] = total.astype(LOW)
            at += size if axis == 0 else rows


def combine(items, after=(), cost=CHEAP):
    forms = tuple((tuple(len(terms) for terms in sums), parts, axis) for sums, parts, axis in items)
    shapes = []
    for sums, parts, axis in items:
        shape = list(sums[0][0].shape)
        shape[axis] = sum(terms[0].shape[axis] for terms in sums)
        shape[0] //= parts
        shapes += [jax.ShapeDtypeStruct(tuple(shape), LOW)] * parts
    operands = tuple(array for sums, _, _ in items for terms in sums for array in terms)
    size = sum(array.size for array in operands)
    outs = run(
        functools.partial(combine_kernel, forms),
        after,
        out_shape=tuple(shapes),
        in_specs=[VM] * len(operands),
        operands=operands,
        out_specs=(VM,) * len(shapes),
        cost_estimate=cost,
        vmem=6 + 4 * size // (1 << 20),
        name="combine",
    )
    got = []
    for _, parts, _ in forms:
        got.append(outs[:parts])
        outs = outs[parts:]
    return got


def last_kernel(
    plan, coords_ref, length_ref, mixed_ref, lse_ref, gctx_ref, first_ref, n_ref, s_ref, gains_ref, x_ref, ctxt_ref, low_ref,
    slot_ref, type_ref, top0, top1, low0, low1, att1, bias0, bias1, wqkv_hbm,
    out_ref, keep_ref, send_ref,
    wqkv, dmix, xt, res, back_ref, back_low, att0, emb, small, sems,
):
    tokens, width = back_ref.shape
    load = pltpu.make_async_copy(wqkv_hbm.at[0], wqkv, sems.at[0])
    load.start()
    attend_back_body(length_ref, mixed_ref, lse_ref, gctx_ref, att0, dmix)
    load.wait()
    grad = first_ref[...] + dot(dmix[...], wqkv[...], COLS)
    gain = gains_ref[...].astype(F32)[0:1]
    norm_end(coords_ref[0], grad, n_ref[...], s_ref[:, :1], gain, back_ref, back_low, None, None, emb)
    slots = out_ref.shape[0]
    chunk = 256

    def step(i, carry):
        there = pl.ds(pl.multiple_of(i * chunk, chunk), chunk)
        number = lax.broadcasted_iota(jnp.int32, (chunk, tokens), 0) + i * chunk
        hit = jnp.where(number == slot_ref[...], 1.0, 0.0).astype(LOW)
        out_ref[there, :] = dot(hit, back_low[...]).astype(LOW)
        return carry

    lax.fori_loop(0, slots // chunk, step, 0)
    xt[...] = x_ref[...].T
    blocks = res.shape[0] // 2
    piece = width // blocks
    half = width // 2
    wide = 3 * half
    for core in range(2):
        there = slice(core * blocks, (core + 1) * blocks)
        for i in range(3):
            cols = slice(core * wide + i * half, core * wide + (i + 1) * half)
            got = dot(xt[...], dmix[:, cols]).astype(LOW)
            res[there, :piece, i * half : (i + 1) * half] = got.reshape(blocks, piece, half)
        got = dot(ctxt_ref[...], low_ref[:, core * half : (core + 1) * half]).astype(LOW)
        res[there, :piece, wide:] = got.reshape(blocks, piece, half)
    back = back_ref[...]
    kind = type_ref[:, :1]
    small[0:1] = jnp.sum(back * (1.0 - kind), axis=0, keepdims=True)
    small[1:2] = jnp.sum(back * kind, axis=0, keepdims=True)
    sources = [(emb, 0)]
    for top, low in ((top0, low0), (top1, low1)):
        sources += [(low, 0), (top, 0)]
    sources += [(emb, 1)]
    for top, low, att in ((top0, low0, att0), (top1, low1, att1)):
        sources += [(att, 0), (att, 1), (low, 2), (low, 1), (top, 2), (top, 1)]
    at = 2
    for ref, row in sources:
        small[at : at + 1] = ref[row : row + 1]
        at += 1
    for bias in (bias0, bias1):
        for i in range(bias.shape[1] // width):
            small[at : at + 1] = bias[:, i * width : (i + 1) * width]
            at += 1
    quarter = at // 4
    group = tokens // blocks // 4
    fill = res.shape[1] - piece
    parts = back.reshape(blocks, 4, group, width)
    for core in range(2):
        pos = jnp.concatenate([parts[:, i, :, core * half : (core + 1) * half] for i in range(4)], axis=2)
        for y in range(2):
            mine = small[(2 * core + y) * quarter : (2 * core + y + 1) * quarter]
            mine = jnp.concatenate([mine, jnp.zeros((fill - group - quarter, width), F32)], axis=0)
            mine = jnp.concatenate([mine, jnp.zeros_like(mine)], axis=1)
            for v in range(blocks // 2):
                block = 2 * v + y
                res[core * blocks + block, piece:, :] = jnp.concatenate([pos[block], mine], axis=0).astype(LOW)
    place(coords_ref, plan, res, keep_ref, send_ref)


def last(plan, coords, length, mixed, lse, gctx, first, n, sp, gains, x, ctxt, low, slot_of, types, sums, w_qkv, slots, blocks, after=()):
    tokens, width = first.shape
    s = jax.ShapeDtypeStruct
    v = pltpu.VMEM
    block = (blocks, width // blocks + 16, 2 * width)
    operands = (coords, length, mixed, lse, gctx, first, n, sp, gains, x, ctxt, low, slot_of, types, *sums, w_qkv)
    return run(
        functools.partial(last_kernel, plan),
        after,
        out_shape=(s((slots, width), LOW), s(block, LOW), s(block, LOW)),
        in_specs=[SM, SM] + [VM] * (len(operands) - 3) + [HBM],
        operands=operands,
        out_specs=(VM,) * 3,
        scratch_shapes=[
            v((width, 3 * width), LOW), v((tokens, 3 * width), LOW), v((width, tokens), LOW),
            v((2 * blocks,) + block[1:], LOW), v((tokens, width), F32), v((tokens, width), LOW),
            v((2, width), F32), v((3, width), F32), v((28, width), F32), pltpu.SemaphoreType.DMA((1,)),
        ],
        cost_estimate=CHEAP,
        vmem=52,
        name="last",
    )


def table_back_kernel(coords_ref, asked_ref, rows_ref, keep_ref, send_ref, total):
    count = total.shape[0]
    chunk = count // 5 if count % 5 == 0 else count

    def step(i, carry):
        at = pl.multiple_of(i * chunk, 8)
        number = lax.broadcasted_iota(jnp.int32, (chunk, rows_ref.shape[0]), 0) + at
        hit = jnp.where(number == asked_ref[...], 1.0, 0.0).astype(LOW)
        total[pl.ds(at, chunk), :] = dot(hit, rows_ref[...])
        return carry

    lax.fori_loop(0, count // chunk, step, 0)
    mine = coords_ref[0]
    half = total.shape[1] // 2

    @pl.when(mine == 0)
    def _():
        keep_ref[...] = total[:, :half].astype(LOW)
        send_ref[...] = total[:, half:].astype(LOW)

    @pl.when(mine == 1)
    def _():
        keep_ref[...] = total[:, half:].astype(LOW)
        send_ref[...] = total[:, :half].astype(LOW)


def table_back(coords, asked, rows, local_rows, after=()):
    width = rows.shape[1]
    half = jax.ShapeDtypeStruct((local_rows, width // 2), LOW)
    return run(
        table_back_kernel,
        after,
        out_shape=(half, half),
        in_specs=[SM, VM, VM],
        operands=(coords, asked, rows),
        out_specs=(VM, VM),
        scratch_shapes=[pltpu.VMEM((local_rows, width), F32)],
        cost_estimate=CHEAP,
        vmem=16,
        name="table_back",
    )


def finish_kernel(coords_ref, *refs):
    five, one = refs[:4], refs[4:8]
    qkv_ref, wout_ref, one_ref, two_ref, pos_ref, small_ref = refs[8:]
    mine_core, mine_y = coords_ref[0] == 0, coords_ref[4] == 0
    half = wout_ref.shape[2] // 2
    wide = 3 * half
    part = wout_ref.shape[1] // 2

    def piece(four, n, core, y):
        own, over_y, over_core, over_both = (ref[n] for ref in four)
        same_y = mine_y if y == 0 else jnp.logical_not(mine_y)
        same_core = mine_core if core == 0 else jnp.logical_not(mine_core)
        here = jnp.where(same_y, own, over_y)
        there = jnp.where(same_y, over_core, over_both)
        return jnp.where(same_core, here, there).astype(F32)

    for layer in range(NL):
        for core in range(2):
            columns = []
            for y in range(2):
                rows = slice(y * part, (y + 1) * part)
                mix = piece(one, 0, core, y) if layer == 0 else piece(five, MIX1, core, y)
                qkv_ref[layer, rows, core * wide : (core + 1) * wide] = mix[:part, :wide]
                wout_ref[layer, rows, core * half : (core + 1) * half] = mix[:part, wide:]
                if layer == 0:
                    for i in range(4):
                        at = (4 * y + i) * 8
                        pos_ref[at : at + 8, core * half : (core + 1) * half] = mix[part : part + 8, i * half : (i + 1) * half]
                    at = (2 * core + y) * 7
                    small_ref[at : at + 7] = mix[part + 8 : part + 15, : 2 * half]
                first = piece(five, ONE0 if layer == 0 else ONE1, core, y)
                one_ref[layer, rows, core * 4 * half : (core + 1) * 4 * half] = first
                second = piece(five, TWO0 if layer == 0 else TWO1, core, y)
                columns += [second[:, i * half : (i + 1) * half] for i in range(4)]
            two_ref[layer, :, core * half : (core + 1) * half] = jnp.concatenate(columns, axis=0).T


MIX1, TWO0, ONE0, TWO1, ONE1 = range(5)


def finish(coords, five, one, width, ff, owners):
    s = jax.ShapeDtypeStruct
    rows = width // owners
    return run(
        finish_kernel,
        (),
        out_shape=(
            s((NL, rows, 3 * width), F32), s((NL, rows, width), F32), s((NL, rows, ff), F32), s((NL, ff // owners, width), F32),
            s((64, width), F32), s((28, width), F32),
        ),
        in_specs=[SM] + [VM] * 8,
        operands=(coords, *five, *one),
        out_specs=(VM,) * 6,
        cost_estimate=CHEAP,
        vmem=24,
        name="finish",
    )


AXES = ("dp", "vocab")
VOCAB_MASK = {"x": 1, "a": 2, "b": 4}


def add(left_op, right_op):
    return (left_op.astype(F32) + right_op.astype(F32)).astype(LOW)


class Cube:
    def __init__(self, dp_size, vocab_size):
        self.dp_size = dp_size
        self.vocab_size = vocab_size
        self.dp_bits = dp_size.bit_length() - 1
        self.vocab_bits = vocab_size.bit_length() - 1
        assert 1 << self.dp_bits == dp_size and 1 << self.vocab_bits == vocab_size
        self.small = self.dp_bits == 2 and self.vocab_bits == 3

    def permute(self, value, dp_mask, vocab_mask):
        count = self.vocab_size
        pairs = [
            (d * count + v, (d ^ dp_mask) * count + (v ^ vocab_mask))
            for d in range(self.dp_size)
            for v in range(count)
        ]
        return lax.ppermute(value, AXES, pairs)

    def core(self, value):
        return self.permute(value, 1, 0)

    def along(self, value, dims):
        return self.permute(
            value, 2 * ("y" in dims) + ("core" in dims), sum(VOCAB_MASK[dim] for dim in dims if dim in VOCAB_MASK)
        )

    def core_is_first(self):
        return (lax.axis_index("dp") & 1) == 0

    def coords(self):
        dp, vocab = lax.axis_index("dp"), lax.axis_index("vocab")
        return jnp.stack([dp & 1, vocab & 1, (vocab >> 1) & 1, (vocab >> 2) & 1, (dp >> 1) & 1])

    def halves(self, matrix):
        mine = lax.axis_index("dp") & 1
        width = matrix.shape[1] // 2
        keep = lax.dynamic_slice_in_dim(matrix, mine * width, width, 1)
        send = lax.dynamic_slice_in_dim(matrix, (1 - mine) * width, width, 1)
        return keep, send

    def ordered(self, first, mine, other, axis):
        return jnp.concatenate(
            [jnp.where(first, mine, other), jnp.where(first, other, mine)], axis=axis
        )

    def join_core(self, share, axis):
        return self.ordered(self.core_is_first(), share, self.core(share), axis).astype(F32)

    def reduce(self, matrix):
        for bit in reversed(range(self.vocab_bits)):
            mine = (lax.axis_index("vocab") >> bit) & 1
            rows = matrix.shape[0] // 2
            keep = lax.dynamic_slice_in_dim(matrix, mine * rows, rows, 0)
            send = lax.dynamic_slice_in_dim(matrix, (1 - mine) * rows, rows, 0)
            matrix = add(keep, self.permute(send, 0, 1 << bit))
        for bit in range(1, self.dp_bits):
            matrix = add(matrix, self.permute(matrix, 1 << bit, 0))
        return matrix


def on_device(
    cube,
    token_ids,
    lengths,
    type_ids,
    word_table,
    pos_table,
    type_table,
    gains,
    shifts,
    w_qkv,
    w_out,
    b_ff1,
    w_ff1,
    w_ff2,
    cotangent,
):
    owners = cube.vocab_size
    local_rows, width = word_table.shape
    assert token_ids.shape[0] == 1
    tokens = token_ids.shape[1]
    slot_count = 2 * tokens // owners
    slots = owners * slot_count
    flat_ids = token_ids.reshape(tokens)
    me = lax.axis_index("vocab")
    coords = cube.coords()

    all_ids = lax.all_to_all(
        jnp.broadcast_to(flat_ids[None, :], (owners, tokens)), "vocab", split_axis=0, concat_axis=0, tiled=True
    )
    local = all_ids - me * local_rows
    here = (local >= 0) & (local < local_rows)
    rank = jnp.cumsum(here.astype(jnp.int32), axis=1) - 1
    slot_hit = (
        jnp.where(here, rank, -1)[:, None, :] == jnp.arange(slot_count, dtype=jnp.int32)[None, :, None]
    )
    asked = jnp.sum(jnp.where(slot_hit, local[:, None, :] + 1, 0), axis=2).reshape(slots) - 1
    row_hit = (asked[:, None] == jnp.arange(local_rows, dtype=jnp.int32)[None, :]).astype(LOW)
    found_rows = dot(row_hit, word_table).astype(LOW)
    replies = lax.all_to_all(
        found_rows.reshape(owners, slot_count, width), "vocab", split_axis=0, concat_axis=0, tiled=True
    ).reshape(slots, width)
    owner_of = flat_ids // local_rows
    chosen = (owner_of[:, None] == jnp.arange(owners, dtype=jnp.int32)[None, :]).astype(jnp.int32)
    before = jnp.cumsum(chosen, axis=0) - chosen
    slot_of = owner_of * slot_count + jnp.sum(before * chosen, axis=1)
    kind = type_ids.reshape(tokens).astype(F32)
    column = lambda row: jnp.broadcast_to(row[:, None], (tokens, 128))
    (n0, s0, hidden), top, layers = forward(
        coords, lengths, replies, column(slot_of), column(kind), pos_table, type_table, gains, shifts, b_ff1.astype(F32),
        cotangent.reshape(tokens, width), w_qkv, w_out, w_ff1, w_ff2,
    )
    norms, saved = [(n0, s0)], []
    for xlow, mixed, lse, ctxt, n1, s1, mlow, gp, act, *end in layers:
        saved.append((mixed, lse, n1, s1, gp) + tuple((own, cube.core(own)) for own in (xlow, ctxt, mlow, act)))
        norms.append(tuple(end))
    hidden_out = hidden.reshape(1, tokens, width)

    gradients = gradients_small if cube.small else gradients_any
    outs = gradients(
        cube, coords, lengths, top, saved, gains, w_qkv, w_out, w_ff1, w_ff2,
        norms, (kind, row_hit, slot_of, asked),
    )
    return (hidden_out,) + outs


def exchange_rows(outgoing, owners):
    shape = outgoing.shape
    return lax.all_to_all(
        outgoing.reshape(owners, -1, shape[1]), "vocab", split_axis=0, concat_axis=0, tiled=True
    ).reshape(shape)


def unpack(pack):
    cores, blocks, _, cols = pack.shape
    pos = pack[:, :, :8].reshape(cores, blocks, 8, 4, cols // 4).transpose(1, 3, 2, 0, 4)
    return pos.reshape(blocks * 32, cols // 2), pack[:, :2, 8:15, : cols // 2].reshape(28, cols // 2)


def small_outs(cube, rows):
    place_of = lax.axis_index("vocab")

    def mine(array):
        size = array.shape[1] // cube.vocab_size
        return lax.dynamic_slice_in_dim(array, place_of * size, size, 1)

    few = mine(rows[:20])
    return few[:2], few[2 : 2 + 2 * NL + 1], few[2 + 2 * NL + 1 :], mine(rows[20:].reshape(NL, -1))


def gradients_any(cube, coords, lengths, top, saved, gains, w_qkv, w_out, w_ff1, w_ff2, norms, embed):
    owners = cube.vocab_size
    width = w_out.shape[1]
    tokens = top[0].shape[0]
    blocks = 8
    half = width // 2
    kind, row_hit, slot_of, asked = embed
    mixed1, lse1, n1_1, s1_1, gp1, x1, ctx1, mid1, act1 = saved[1]
    mixed0, lse0, n1_0, s1_0, gp0, x0, ctx0, mid0, act0 = saved[0]
    e, low, sec_keep, sec_send, top1 = top
    pre_keep, pre_send, bias1, first, _, fst_keep, fst_send, gctx, sums1 = feed(
        1, coords, e, low, n1_1, s1_1, gains, gp1, w_out, w_ff1, w_ff2
    )
    pair = lambda keep, send: (keep, cube.core(send))
    two1, one1 = weights(blocks, (None, None), coords, pair(sec_keep, sec_send), act1, mid1, pair(pre_keep, pre_send))
    fst1 = pair(fst_keep, fst_send)
    (
        mix_keep, mix_send, pre_keep, pre_send, att1, sec_keep, sec_send, top0, bias0, first, low, gctx, sums0
    ) = between(
        1, coords, lengths, mixed1, lse1, gctx, first, *norms[1], n1_0, s1_0, gains, gp0, w_qkv, w_out, w_ff1, w_ff2
    )
    two0, one0, mix1 = weights(
        blocks, (None, None, None), coords, pair(sec_keep, sec_send), act0, mid0, pair(pre_keep, pre_send),
        (x1, pair(mix_keep, mix_send), ctx1, fst1),
    )
    column = jnp.broadcast_to(kind[:, None], (tokens, 128))
    outgoing, first_core, second_core = last(
        None, coords, lengths, mixed0, lse0, gctx, first, *norms[0], gains, x0[0], ctx0[0], low, slot_of[None, :], column,
        (top0, top1, sums0, sums1, att1, bias0, bias1), w_qkv, row_hit.shape[0], 2 * blocks,
    )
    mine = cube.core_is_first()

    def over_cores(first, second):
        return add(jnp.where(mine, first, second), cube.core(jnp.where(mine, second, first)))

    table_part = dot(row_hit, exchange_rows(outgoing, owners), ROWS).astype(LOW)
    table_part = over_cores(table_part[:, :half], table_part[:, half:])
    for bit in range(1, cube.dp_bits):
        table_part = add(table_part, cube.permute(table_part, 1 << bit, 0))
    part = width // blocks // 2
    packs = over_cores(first_core[:, part:], second_core[:, part:])
    other = cube.core(packs)
    pos, small = unpack(jnp.stack([jnp.where(mine, packs, other), jnp.where(mine, other, packs)]))
    pos_out = cube.reduce(pos).astype(F32)
    for bit in range(cube.vocab_bits):
        small = add(small, cube.permute(small, 0, 1 << bit))
    for bit in range(1, cube.dp_bits):
        small = add(small, cube.permute(small, 1 << bit, 0))
    types, gains_out, shifts_out, biases = small_outs(cube, small.astype(F32))
    whole = lambda parts: jnp.concatenate(parts, axis=0)
    one = lambda parts: cube.reduce(whole(parts).reshape(width, -1))
    two = lambda parts: cube.reduce(
        whole(parts).reshape(blocks, 2, width // 16, 4, -1).transpose(0, 4, 1, 3, 2).reshape(-1, half)
    )
    mix0 = over_cores(first_core[:, :part], second_core[:, :part]).reshape(width, -1)
    mixes = jnp.stack([cube.reduce(mix0), one(mix1)])
    wide = 3 * half
    return (
        cube.join_core(table_part, -1), pos_out, types, gains_out, shifts_out,
        cube.join_core(mixes[..., :wide], 2), cube.join_core(mixes[..., wide:], 2), biases,
        cube.join_core(jnp.stack([one(one0), one(one1)]), 2), cube.join_core(jnp.stack([two(two0), two(two1)]), 2),
    )


class Bucket:
    def __init__(self, cube, plan, parts):
        self.cube, self.plan, self.parts = cube, tuple(plan), tuple(parts)

    def start(self):
        turn = self.plan[0]
        if self.plan == (("y",),):
            self.got = (self.parts[0], self.cube.along(self.parts[0], turn))
            return
        self.got = self.parts[:1]
        for n in range(1, len(self.parts)):
            there = [dim for i, dim in enumerate(turn) if (n >> (len(turn) - 1 - i)) & 1]
            self.got += (self.cube.along(self.parts[n], there),)


    def keep(self):
        self.got, self.plan = self.parts, (None,)


def joined(buckets, parts_axis):
    return (tuple(buckets), parts_axis)


def step(groups, after=(), cost=CHEAP):
    groups = [group if isinstance(group, tuple) else ((group,), 0) for group in groups]
    items = []
    for buckets, axis in groups:
        rest = buckets[0].plan[1:]
        assert all(bucket.plan[1:] == rest for bucket in buckets)
        parts = 1 if rest in ((), (("y",),)) else 2 ** len(rest[0])
        items.append((tuple(bucket.got for bucket in buckets), parts, axis))
    for (buckets, _), parts in zip(groups, combine(items, after, cost)):
        buckets[0].plan, buckets[0].parts = buckets[0].plan[1:], tuple(parts)
    return groups[0][0][0].parts[0]


def gradients_small(cube, coords, lengths, top, saved, gains, w_qkv, w_out, w_ff1, w_ff2, norms, embed):
    owners = cube.vocab_size
    width = w_out.shape[1]
    tokens = top[0].shape[0]
    blocks = owners
    half = width // 2
    single = lambda dims: tuple((dim,) for dim in dims)
    plan_two1, plan_one1, plan_mix1 = (("x", "y"), ("a",), ("b",)), single("abxy"), single("ayxb")
    plan_two0, plan_one0, plan_mix0 = single("xayb"), single("yxab"), (("core",), ("y",), ("x", "a"), ("b",))
    kind, row_hit, slot_of, asked = embed
    local_rows = row_hit.shape[1]
    mixed1, lse1, n1_1, s1_1, gp1, x1, ctx1, mid1, act1 = saved[1]
    mixed0, lse0, n1_0, s1_0, gp0, x0, ctx0, mid0, act0 = saved[0]
    pair = lambda keep, send: (keep, cube.core(send))
    e, low, sec_keep, sec_send, top1 = top
    pre_keep, pre_send, bias1, first, _, fst_keep, fst_send, gctx, sums1 = feed(
        1, coords, e, low, n1_1, s1_1, gains, gp1, w_out, w_ff1, w_ff2
    )
    fst1 = pair(fst_keep, fst_send)
    got = weights(
        blocks, (plan_two1, plan_one1), coords, pair(sec_keep, sec_send), act1, mid1, pair(pre_keep, pre_send)
    )
    two1, one1 = Bucket(cube, plan_two1, got[0]), Bucket(cube, plan_one1, got[1])
    two1.start()
    one1.start()
    (
        mix_keep, mix_send, pre_keep, pre_send, att1, sec_keep, sec_send, top0, bias0, first, low, gctx, sums0
    ) = between(
        1, coords, lengths, mixed1, lse1, gctx, first, *norms[1], n1_0, s1_0, gains, gp0, w_qkv, w_out, w_ff1, w_ff2,
        after=got[0][:1],
    )
    mark = step([two1, one1], after=(gctx,), cost=LONG)
    two1.start()
    one1.start()
    got = weights(
        blocks, (plan_two0, plan_one0, plan_mix1), coords, pair(sec_keep, sec_send), act0, mid0, pair(pre_keep, pre_send),
        (x1, pair(mix_keep, mix_send), ctx1, fst1), after=(mark,),
    )
    two0, one0, mix1 = [Bucket(cube, plan, parts) for plan, parts in zip((plan_two0, plan_one0, plan_mix1), got)]
    for bucket in (mix1, two0, one0):
        bucket.start()
    mark = step([two1, one1], after=got[0][:1], cost=LONG)
    two1.start()
    one1.start()
    types = jnp.broadcast_to(kind[:, None], (tokens, 128))
    outgoing, *got = last(
        plan_mix0, coords, lengths, mixed0, lse0, gctx, first, *norms[0], gains, x0[0], ctx0[0], low, slot_of[None, :], types,
        (top0, top1, sums0, sums1, att1, bias0, bias1), w_qkv, row_hit.shape[0], 2 * owners, after=(mark,),
    )
    incoming = exchange_rows(outgoing, owners)
    mix0 = Bucket(cube, plan_mix0, got)
    mix0.start()
    mark = step([two1, one1, mix1, two0, one0], after=got[:1], cost=LONG)
    for bucket in (one1, mix1, two0, one0):
        bucket.start()
    mark = step([mix0], after=(mark,))
    mix0.start()
    mark = step([mix1, two0, one0, one1], after=(mark,), cost=LONG)
    for bucket in (mix1, two0, one0):
        bucket.start()
    folded = (local_rows // 48, 48, half)
    got = table_back(coords, asked[None, :], incoming, local_rows, after=(mark,))
    table = Bucket(cube, single(("core", "y")), [part.reshape(folded) for part in got])
    table.start()
    mark = step([mix0, joined((mix1, two0, one0), 0), table], after=got[:1], cost=LONG)
    mix0.start()
    mix1.start()
    table.start()
    mark = step([mix0], after=(mark,), cost=LONG)
    mix0.start()
    two1.keep()
    mark = step([joined((mix1, two1), 0), table], after=(mark,))
    step([mix0], after=(mark,))
    half_of = lambda n: one1.parts[0][n : n + 1]
    mine_y = (lax.axis_index("dp") >> 1) & 1 == 0
    one1_own = jnp.where(mine_y, half_of(0), half_of(1))
    one1_other = jnp.where(mine_y, half_of(1), half_of(0))
    four = mix1.parts[0]
    own = jnp.concatenate([four, one1_own], axis=0)
    over_y = jnp.concatenate([cube.along(four, ("y",)), one1_other], axis=0)
    last_y = cube.along(mix0.parts[0], ("y",))
    qkv_out, wout_out, one_out, two_out, pos_out, small = finish(
        coords,
        (own, over_y, cube.core(own), cube.core(over_y)),
        (mix0.parts[0], last_y, cube.core(mix0.parts[0]), cube.core(last_y)),
        width, w_ff1.shape[2], owners,
    )
    types, gains, shifts, biases = small_outs(cube, small)
    return (
        cube.join_core(table.parts[0].reshape(local_rows, half), -1), pos_out, types, gains, shifts, qkv_out, wout_out,
        biases, one_out, two_out,
    )


def solution(mesh):
    cube = Cube(mesh.shape["dp"], mesh.shape["vocab"])
    both = ("dp", "vocab")
    in_specs = (
        P(both, None),
        P(both),
        P(both, None),
        P("vocab", None),
        P(),
        P(),
        P(),
        P(),
        P(),
        P(),
        P(),
        P(),
        P(),
        P(both, None, None),
    )
    out_specs = (
        P(both, None, None),
        P("vocab", None),
        P("vocab", None),
        P(None, "vocab"),
        P(None, "vocab"),
        P(None, "vocab"),
        P(None, "vocab", None),
        P(None, "vocab", None),
        P(None, "vocab"),
        P(None, "vocab", None),
        P(None, "vocab", None),
    )
    return jax.shard_map(
        functools.partial(on_device, cube), mesh=mesh, in_specs=in_specs, out_specs=out_specs, check_vma=False
    )
```

time: 512 us -> 395 us (0.77)
  waiting for transfers between devices: 176 us -> 122 us
  other arithmetic: 44.4 us -> 5.72 us
  starting transfers between devices: 78.2 us -> 51.8 us
  local copies, waits for them, and re-layouts: 14.2 us -> 27.8 us
  matrix products: 10.5 us -> 3.13 us
    ppermute x53 -> x46, waiting for transfers between devices: 140 us -> 71.7 us  [permute(): return lax.ppermute(value, AXES, pairs)]
    ppermute x53 -> x46, starting transfers between devices: 61.9 us -> 36.8 us  [permute(): return lax.ppermute(value, AXES, pairs)]
    convert_element_type x36 -> x2, other arithmetic: 23.2 us -> 0.62 us  [the longest x1 0.62 us: on_device(): b_ff1.astype(F32)]
    unnamed x68 -> x124, local copies, waits for them, and re-layouts: 3.21 us -> 21 us
    all_to_all x1, waiting for transfers between devices: 0.01 us -> 10.8 us  [exchange_rows(): lax.all_to_all(outgoing.reshape(owners, -1, shape[1]), 'vocab', split_axi...]
    dot_general x4 -> x1, matrix products: 10.5 us -> 3.13 us  [dot(): lax.dot_general(left_op, right_op, (dims, ((), ())), preferred_element_ty...]
    pallas_call x10 -> x17, Pallas kernels: 180 us -> 175 us  [run(): pl.pallas_call(body, out_shape=out_shape, in_specs=list(in_specs) + [ANY]...]
  transfers between devices with their start and end apart: 56 -> 49, of which waited for: 24 -> 16; matrix products, arithmetic and copies ran while one was open for 9% -> 1% of each run, Pallas kernels for 15% -> 27%
where the time goes in v3:
time: 395 us; the launch traced here: 388 us
  Pallas kernels  175 us (44%)
  waiting for transfers between devices  122 us (31%)
  starting transfers between devices  51.8 us (13%)
  local copies, waits for them, and re-layouts  27.8 us (7%)
  other arithmetic  5.72 us (1%)
    pallas_call x17, Pallas kernels, run(): pl.pallas_call(body, out_shape=out_shape, in_specs=list(in_specs) + [ANY]...  175 us
    ppermute x46, waiting for transfers between devices, permute(): return lax.ppermute(value, AXES, pairs)  71.7 us
    ppermute x46, starting transfers between devices, permute(): return lax.ppermute(value, AXES, pairs)  36.8 us
    all_to_all x1, waiting for transfers between devices, on_device(): lax.all_to_all(found_rows.reshape(owners, slot_count, width), 'vocab', sp...  32.5 us
    unnamed x124, local copies, waits for them, and re-layouts  21 us
    all_to_all x1, waiting for transfers between devices, exchange_rows(): lax.all_to_all(outgoing.reshape(owners, -1, shape[1]), 'vocab', split_axi...  10.8 us
  transfers between devices with their start and end apart: 49, of which 16 were waited for; matrix products, arithmetic and copies ran while one was open for 1% of the time, Pallas kernels for 27%

profile of v3, /device:TPU:0, one launch (start us, length us, event | category | flops | bytes accessed | tf_op | source)
XLA Modules:
  0.0 387.7 jit_solution(3113953674193440781)
XLA Ops:
  2.1 7.3 %all-to-all-start = ((s32[8,1,512]{2,1,0:T(1,128)}), s32[8,1,512]{2,1,0:T(1,128)S(1)}, u32[]{:S(2)}, u32[]{:S(2)}) async-start(s32[8,1,512]{2,1,0:T(1,128)} %broadcast_in_dim.22), calls=%async_computation | async-start | bytes 32768 | tf_op jit(solution)/shard_map/all_to_all | solution.py:983
  9.3 6.6 %all-to-all-done = s32[8,1,512]{2,1,0:T(1,128)S(1)} async-done(((s32[8,1,512]{2,1,0:T(1,128)}), s32[8,1,512]{2,1,0:T(1,128)S(1)}, u32[]{:S(2)}, u32[]{:S(2)}) %all-to-all-start) | async-done | bytes 16416 | tf_op jit(solution)/shard_map/all_to_all | solution.py:983
  17.7 3.1 fusion.2
  20.8 3.7 all-to-all-start.1
  28.1 32.5 %all-to-all-done.1 = bf16[8,128,768]{2,1,0:T(8,128)(2,1)S(1)} async-done(((bf16[8,128,768]{2,1,0:T(8,128)(2,1)}), bf16[8,128,768]{2,1,0:T(8,128)(2,1)S(1)}, u32[]{:S(2)}, u32[]{:S(2)}) %all-to-all-start.1) | async-done | bytes 1572896 | tf_op jit(solution)/shard_map/all_to_all | solution.py:995
  62.3 52.6 %forward.1 = (f32[512,768]{1,0:T(8,128)}, f32[512,128]{1,0:T(8,128)}, bf16[512,768]{1,0:T(8,128)(2,1)}, f32[512,768]{1,0:T(8,128)}, bf16[512,768]{1,0:T(8,128)(2...) custom-call(s32[5]{0:T(128)} %stack.23.refs_0_, ...), custom_call_target="tpu_custom_call" | custom-call | flops 1 | bytes 1 | tf_op jit(solution)/shard_map/forward/pallas_call | solution.py:31
  116.0 15.2 %feed.1 = (bf16[512,1536]{1,0:T(8,128)(2,1)}, bf16[512,1536]{1,0:T(8,128)(2,1)}, f32[1,3072]{1,0:T(1,128)S(1)}, f32[512,768]{1,0:T(8,128)}, bf16[512,768]{1,0:T(...) custom-call(s32[5]{0:T(128)S(1)} %copy-done.18, ...), custom_call_target="tpu_custom_call" | custom-call | flops 1 | bytes 1 | tf_op jit(solution)/shard_map/feed/pallas_call | solution.py:31
  132.3 4.2 %collective-permute-done.refs_2_ = bf16[512,384]{1,0:T(8,128)(2,1)S(1)} collective-permute-done((bf16[512,384]{1,0:T(8,128)(2,1)S(1)}, bf16[512,384]{1,0:T(8,128)(2,1)S(1)}, u32[]{:S(2)}, u32[]{:S(2)}) %collective-permute-start) | collective-permute-done | bytes 393248 | tf_op jit(solution)/shard_map/ppermute | solution.py:912
  138.0 11.6 %weights.2 = (bf16[4,48,1536]{2,1,0:T(8,128)(2,1)S(1)}, bf16[4,48,1536]{2,1,0:T(8,128)(2,1)}, bf16[4,48,1536]{2,1,0:T(8,128)(2,1)}, bf16[4,48,1536]{2,1,0:T(8,12...) custom-call(s32[5]{0:T(128)S(1)} %copy-done.18, bf16[512,384]{1,0:T(8,128)(2,1)S(1)} %copy-done.12, ...), custom_call_target="tpu_custom_call" | custom-call | flops 1 | bytes 1 | tf_op jit(solution)/shard_map/weights/pallas_call | solution.py:31
  154.4 30.2 %between.1 = (bf16[512,1152]{1,0:T(8,128)(2,1)}, bf16[512,1152]{1,0:T(8,128)(2,1)}, bf16[512,1536]{1,0:T(8,128)(2,1)}, bf16[512,1536]{1,0:T(8,128)(2,1)}, f32[2,...) custom-call(s32[5]{0:T(128)} %stack.23.refs_0_, ...), custom_call_target="tpu_custom_call" | custom-call | flops 1 | bytes 1 | tf_op jit(solution)/shard_map/between/pallas_call | solution.py:31
  188.6 4.2 %collective-permute-done.14.refs_10_ = bf16[512,768]{1,0:T(8,128)(2,1)S(1)} collective-permute-done((bf16[512,768]{1,0:T(8,128)(2,1)}, bf16[512,768]{1,0:T(8,128)(2,1)S(1)}, u32[]{:S(2)}, u32[]{:S(2)}) %collective-permute-start.14) | collective-permute-done | bytes 786464 | tf_op jit(solution)/shard_map/ppermute | solution.py:912
  197.3 18.8 %weights.3 = (bf16[8,48,1536]{2,1,0:T(8,128)(2,1)}, bf16[8,48,1536]{2,1,0:T(8,128)(2,1)}, bf16[8,48,1536]{2,1,0:T(8,128)(2,1)}, bf16[8,48,1536]{2,1,0:T(8,128)(2...) custom-call(s32[5]{0:T(128)S(1)} %copy-done.19, bf16[512,384]{1,0:T(8,128)(2,1)S(1)} %copy-done.13, ...), custom_call_target="tpu_custom_call" | custom-call | flops 1 | bytes 1 | tf_op jit(solution)/shard_map/weights/pallas_call | solution.py:31
  224.9 25.9 %last.1 = (bf16[1024,768]{1,0:T(8,128)(2,1)}, bf16[16,64,1536]{2,1,0:T(8,128)(2,1)}, bf16[16,64,1536]{2,1,0:T(8,128)(2,1)}) custom-call(s32[5]{0:T(128)S(1)} %copy-done.19, s32[1]{0:T(128)S(6)} %copy.33.refs_1_, bf16[512,2304]{1,0:T(8,128)(2,1)} %get-tuple-element.120.refs_2_, f32[12,512]{1,0:T(8,128)S(1)} %copy-done.22, bf16[512,768]{1,0:T(8,128)(2,1)S(1)} %copy-done.8, ...), custom_call_target="tpu_custom_call" | custom-call | flops 1 | bytes 1 | tf_op jit(solution)/shard_map/last/pallas_call | solution.py:31
  262.1 4.0 %all-to-all-start.2 = ((bf16[8,128,768]{2,1,0:T(8,128)(2,1)}), bf16[8,128,768]{2,1,0:T(8,128)(2,1)S(1)}, u32[]{:S(2)}, u32[]{:S(2)}) async-start(bf16[8,128,768]{2,1,0:T(8,128)(2,1)} %bitcast.50), calls=%async_computation.2 | async-start | bytes 3145728 | tf_op jit(solution)/shard_map/all_to_all | solution.py:1024
  268.0 3.5 combine.12
  273.1 8.2 %collective-permute-done.28.refs_7_ = bf16[2,48,1536]{2,1,0:T(8,128)(2,1)} collective-permute-done((bf16[2,48,1536]{2,1,0:T(8,128)(2,1)}, bf16[2,48,1536]{2,1,0:T(8,128)(2,1)}, u32[]{:S(2)}, u32[]{:S(2)}) %collective-permute-start.28) | collective-permute-done | bytes 294944 | tf_op jit(solution)/shard_map/ppermute | solution.py:912
  291.9 10.8 %all-to-all-done.2 = bf16[8,128,768]{2,1,0:T(8,128)(2,1)S(1)} async-done(((bf16[8,128,768]{2,1,0:T(8,128)(2,1)}), bf16[8,128,768]{2,1,0:T(8,128)(2,1)S(1)}, u32[]{:S(2)}, u32[]{:S(2)}) %all-to-all-start.2) | async-done | bytes 1572896 | tf_op jit(solution)/shard_map/all_to_all | solution.py:1024
  308.9 6.4 %collective-permute-done.29.refs_3_ = bf16[2,48,1536]{2,1,0:T(8,128)(2,1)S(1)} collective-permute-done((bf16[2,48,1536]{2,1,0:T(8,128)(2,1)S(1)}, bf16[2,48,1536]{2,1,0:T(8,128)(2,1)S(1)}, u32[]{:S(2)}, u32[]{:S(2)}) %collective-permute-start.29) | collective-permute-done | bytes 294944 | tf_op jit(solution)/shard_map/ppermute | solution.py:912
  315.3 3.9 %collective-permute-done.30.refs_5_ = bf16[2,48,1536]{2,1,0:T(8,128)(2,1)S(1)} collective-permute-done((bf16[2,48,1536]{2,1,0:T(8,128)(2,1)S(1)}, bf16[2,48,1536]{2,1,0:T(8,128)(2,1)S(1)}, u32[]{:S(2)}, u32[]{:S(2)}) %collective-permute-start.30) | collective-permute-done | bytes 294944 | tf_op jit(solution)/shard_map/ppermute | solution.py:912
  331.6 14.1 %collective-permute-done.35.refs_1_ = bf16[2,64,1536]{2,1,0:T(8,128)(2,1)} collective-permute-done((bf16[2,64,1536]{2,1,0:T(8,128)(2,1)}, bf16[2,64,1536]{2,1,0:T(8,128)(2,1)}, u32[]{:S(2)}, u32[]{:S(2)}) %collective-permute-start.35) | collective-permute-done | bytes 393248 | tf_op jit(solution)/shard_map/ppermute | solution.py:912
  345.8 7.7 %collective-permute-done.37.refs_3_ = bf16[2,64,1536]{2,1,0:T(8,128)(2,1)} collective-permute-done((bf16[2,64,1536]{2,1,0:T(8,128)(2,1)S(1)}, bf16[2,64,1536]{2,1,0:T(8,128)(2,1)}, u32[]{:S(2)}, u32[]{:S(2)}) %collective-permute-start.37) | collective-permute-done | bytes 393248 | tf_op jit(solution)/shard_map/ppermute | solution.py:912
  358.6 11.9 %collective-permute-done.39 = bf16[4,48,1536]{2,1,0:T(8,128)(2,1)S(1)} collective-permute-done((bf16[4,48,1536]{2,1,0:T(8,128)(2,1)S(1)}, bf16[4,48,1536]{2,1,0:T(8,128)(2,1)S(1)}, u32[]{:S(2)}, u32[]{:S(2)}) %collective-permute-start.39) | collective-permute-done | bytes 589856 | tf_op jit(solution)/shard_map/ppermute | solution.py:912
  372.5 5.6 %collective-permute-done.43.refs_6_ = bf16[1,64,1536]{2,1,0:T(8,128)(2,1)S(1)} collective-permute-done((bf16[1,64,1536]{2,1,0:T(8,128)(2,1)S(1)}, bf16[1,64,1536]{2,1,0:T(8,128)(2,1)S(1)}, u32[]{:S(2)}, u32[]{:S(2)}) %collective-permute-start.43) | collective-permute-done | bytes 196640 | tf_op jit(solution)/shard_map/ppermute | solution.py:912
  380.2 4.7 %finish.1 = (f32[2,96,2304]{2,1,0:T(8,128)}, f32[2,96,768]{2,1,0:T(8,128)}, f32[2,96,3072]{2,1,0:T(8,128)}, f32[2,384,768]{2,1,0:T(8,128)}, f32[64,768]{1,0:T(8,128)}, /*index=5*/f32[28,768]{1,0:T(8,128)S(1)}) custom-call(s32[5]{0:T(128)S(1)} %copy-done.21, bf16[5,48,1536]{2,1,0:T(8,128)(2,1)S(1)} %pad_maximum_fusion.refs_1_, ...), custom_call_target="tpu_custom_call" | custom-call | flops 1 | bytes 1 | tf_op jit(solution)/shard_map/finish/pallas_call | solution.py:31
  (254 shorter events, 88.7 us)
Async XLA Ops:
  20.8 39.7 %all-to-all-start.1 = ((bf16[8,128,768]{2,1,0:T(8,128)(2,1)}), bf16[8,128,768]{2,1,0:T(8,128)(2,1)S(1)}, u32[]{:S(2)}, u32[]{:S(2)}) async-start(bf16[8,128,768]{2,1,0:T(8,128)(2,1)} %bitcast.51), calls=%async_computation.1 | async-start | bytes 3145728 | tf_op jit(solution)/shard_map/all_to_all | solution.py:995
  115.0 21.5 %collective-permute-start.1 = (bf16[512,3072]{1,0:T(8,128)(2,1)}, bf16[512,3072]{1,0:T(8,128)(2,1)S(1)}, u32[]{:S(2)}, u32[]{:S(2)}) collective-permute-start(bf16[512,3072]{1,0:T(8,128)(2,1)} %get-tuple-element.138.refs_3_), channel_id=1, source_target_pairs={{0,8},{1,9},{2,10},{3,11},{4,12},{5,13},{6,14},{7,15},{8,0},{9,1},... | collective-permute-start | bytes 9437192 | tf_op jit(solution)/shard_map/ppermute | solution.py:912
  150.4 35.3 %collective-permute-start.7 = (bf16[8,48,1536]{2,1,0:T(8,128)(2,1)}, bf16[8,48,1536]{2,1,0:T(8,128)(2,1)S(1)}, u32[]{:S(2)}, u32[]{:S(2)}) collective-permute-start(bf16[8,48,1536]{2,1,0:T(8,128)(2,1)} %get-tuple-element.161), channel_id=1, source_target_pairs={{0,2},{1,3},{2,0},{3,1},{4,6},{5,7},{6,4},{7,5},{8,10},{9,11},{10,... | collective-permute-start | bytes 3538952 | tf_op jit(solution)/shard_map/ppermute | solution.py:912
  150.8 33.8 %collective-permute-start.12 = (bf16[512,768]{1,0:T(8,128)(2,1)}, bf16[512,768]{1,0:T(8,128)(2,1)}, u32[]{:S(2)}, u32[]{:S(2)}) collective-permute-start(bf16[512,768]{1,0:T(8,128)(2,1)} %get-tuple-element.169.refs_5_), channel_id=1, source_target_pairs={{0,8},{1,9},{2,10},{3,11},{4,12},{5,13},{6,14},{7,15},{8,0},{9,1},... | collective-permute-start | bytes 2359304 | tf_op jit(solution)/shard_map/ppermute | solution.py:912
  150.9 33.8 %collective-permute-start.4 = (bf16[4,48,1536]{2,1,0:T(8,128)(2,1)}, bf16[4,48,1536]{2,1,0:T(8,128)(2,1)S(1)}, u32[]{:S(2)}, u32[]{:S(2)}) collective-permute-start(bf16[4,48,1536]{2,1,0:T(8,128)(2,1)} %get-tuple-element.157), channel_id=1, source_target_pairs={{0,16},{1,17},{2,18},{3,19},{4,20},{5,21},{6,22},{7,23},{8,24},{9,... | collective-permute-start | bytes 1769480 | tf_op jit(solution)/shard_map/ppermute | solution.py:912
  152.4 32.7 %collective-permute-start.5 = (bf16[4,48,1536]{2,1,0:T(8,128)(2,1)}, bf16[4,48,1536]{2,1,0:T(8,128)(2,1)S(1)}, u32[]{:S(2)}, u32[]{:S(2)}) collective-permute-start(bf16[4,48,1536]{2,1,0:T(8,128)(2,1)} %get-tuple-element.158), channel_id=1, source_target_pairs={{0,1},{1,0},{2,3},{3,2},{4,5},{5,4},{6,7},{7,6},{8,9},{9,8},{10,11... | collective-permute-start | bytes 1769480 | tf_op jit(solution)/shard_map/ppermute | solution.py:912
  153.7 31.6 %collective-permute-start.6 = (bf16[4,48,1536]{2,1,0:T(8,128)(2,1)S(1)}, bf16[4,48,1536]{2,1,0:T(8,128)(2,1)}, u32[]{:S(2)}, u32[]{:S(2)}) collective-permute-start(bf16[4,48,1536]{2,1,0:T(8,128)(2,1)S(1)} %get-tuple-element.159), channel_id=1, source_target_pairs={{0,17},{1,16},{2,19},{3,18},{4,21},{5,20},{6,23},{7,22},{8,25},{9,... | collective-permute-start | bytes 1769480 | tf_op jit(solution)/shard_map/ppermute | solution.py:912
  192.8 29.0 %collective-permute-start.9 = (bf16[4,48,1536]{2,1,0:T(8,128)(2,1)S(1)}, bf16[4,48,1536]{2,1,0:T(8,128)(2,1)S(1)}, u32[]{:S(2)}, u32[]{:S(2)}) collective-permute-start(bf16[4,48,1536]{2,1,0:T(8,128)(2,1)S(1)} %get-tuple-element.165), channel_id=1, source_target_pairs={{0,4},{1,5},{2,6},{3,7},{4,0},{5,1},{6,2},{7,3},{8,12},{9,13},{10,... | collective-permute-start | bytes 1769480 | tf_op jit(solution)/shard_map/ppermute | solution.py:912
  195.2 25.6 %collective-permute-start.8 = (bf16[2,48,1536]{2,1,0:T(8,128)(2,1)S(1)}, bf16[2,48,1536]{2,1,0:T(8,128)(2,1)S(1)}, u32[]{:S(2)}, u32[]{:S(2)}) collective-permute-start(bf16[2,48,1536]{2,1,0:T(8,128)(2,1)S(1)} %get-tuple-element.163), channel_id=1, source_target_pairs={{0,2},{1,3},{2,0},{3,1},{4,6},{5,7},{6,4},{7,5},{8,10},{9,11},{10,... | collective-permute-start | bytes 884744 | tf_op jit(solution)/shard_map/ppermute | solution.py:912
  216.1 36.2 %collective-permute-start.21 = (bf16[8,48,1536]{2,1,0:T(8,128)(2,1)}, bf16[8,48,1536]{2,1,0:T(8,128)(2,1)S(1)}, u32[]{:S(2)}, u32[]{:S(2)}) collective-permute-start(bf16[8,48,1536]{2,1,0:T(8,128)(2,1)} %get-tuple-element.186), channel_id=1, source_target_pairs={{0,2},{1,3},{2,0},{3,1},{4,6},{5,7},{6,4},{7,5},{8,10},{9,11},{10,... | collective-permute-start | bytes 3538952 | tf_op jit(solution)/shard_map/ppermute | solution.py:912
  218.0 34.3 %collective-permute-start.22 = (bf16[8,48,1536]{2,1,0:T(8,128)(2,1)}, bf16[8,48,1536]{2,1,0:T(8,128)(2,1)S(1)}, u32[]{:S(2)}, u32[]{:S(2)}) collective-permute-start(bf16[8,48,1536]{2,1,0:T(8,128)(2,1)} %get-tuple-element.187), channel_id=1, source_target_pairs={{0,1},{1,0},{2,3},{3,2},{4,5},{5,4},{6,7},{7,6},{8,9},{9,8},{10,11... | collective-permute-start | bytes 3538952 | tf_op jit(solution)/shard_map/ppermute | solution.py:912
  219.2 33.0 %collective-permute-start.23 = (bf16[8,48,1536]{2,1,0:T(8,128)(2,1)}, bf16[8,48,1536]{2,1,0:T(8,128)(2,1)S(1)}, u32[]{:S(2)}, u32[]{:S(2)}) collective-permute-start(bf16[8,48,1536]{2,1,0:T(8,128)(2,1)} %get-tuple-element.189), channel_id=1, source_target_pairs={{0,16},{1,17},{2,18},{3,19},{4,20},{5,21},{6,22},{7,23},{8,24},{9,... | collective-permute-start | bytes 3538952 | tf_op jit(solution)/shard_map/ppermute | solution.py:912
  223.4 28.9 %collective-permute-start.20 = (bf16[2,48,1536]{2,1,0:T(8,128)(2,1)S(1)}, bf16[2,48,1536]{2,1,0:T(8,128)(2,1)S(1)}, u32[]{:S(2)}, u32[]{:S(2)}) collective-permute-start(bf16[2,48,1536]{2,1,0:T(8,128)(2,1)S(1)} %get-tuple-element.184), channel_id=1, source_target_pairs={{0,1},{1,0},{2,3},{3,2},{4,5},{5,4},{6,7},{7,6},{8,9},{9,8},{10,11... | collective-permute-start | bytes 884744 | tf_op jit(solution)/shard_map/ppermute | solution.py:912
  224.7 26.1 %collective-permute-start.19 = (bf16[1,48,1536]{2,1,0:T(8,128)(2,1)S(1)}, bf16[1,48,1536]{2,1,0:T(8,128)(2,1)S(1)}, u32[]{:S(2)}, u32[]{:S(2)}) collective-permute-start(bf16[1,48,1536]{2,1,0:T(8,128)(2,1)S(1)} %get-tuple-element.182), channel_id=1, source_target_pairs={{0,4},{1,5},{2,6},{3,7},{4,0},{5,1},{6,2},{7,3},{8,12},{9,13},{10,... | collective-permute-start | bytes 442376 | tf_op jit(solution)/shard_map/ppermute | solution.py:912
  258.4 22.9 %collective-permute-start.25 = (bf16[4,48,1536]{2,1,0:T(8,128)(2,1)}, bf16[4,48,1536]{2,1,0:T(8,128)(2,1)S(1)}, u32[]{:S(2)}, u32[]{:S(2)}) collective-permute-start(bf16[4,48,1536]{2,1,0:T(8,128)(2,1)} %get-tuple-element.194), channel_id=1, source_target_pairs={{0,16},{1,17},{2,18},{3,19},{4,20},{5,21},{6,22},{7,23},{8,24},{9,... | collective-permute-start | bytes 1769480 | tf_op jit(solution)/shard_map/ppermute | solution.py:912
  259.9 22.2 %collective-permute-start.26 = (bf16[4,48,1536]{2,1,0:T(8,128)(2,1)}, bf16[4,48,1536]{2,1,0:T(8,128)(2,1)S(1)}, u32[]{:S(2)}, u32[]{:S(2)}) collective-permute-start(bf16[4,48,1536]{2,1,0:T(8,128)(2,1)} %get-tuple-element.196), channel_id=1, source_target_pairs={{0,2},{1,3},{2,0},{3,1},{4,6},{5,7},{6,4},{7,5},{8,10},{9,11},{10,... | collective-permute-start | bytes 1769480 | tf_op jit(solution)/shard_map/ppermute | solution.py:912
  260.8 24.7 %collective-permute-start.27 = (bf16[4,48,1536]{2,1,0:T(8,128)(2,1)S(1)}, bf16[4,48,1536]{2,1,0:T(8,128)(2,1)}, u32[]{:S(2)}, u32[]{:S(2)}) collective-permute-start(bf16[4,48,1536]{2,1,0:T(8,128)(2,1)S(1)} %get-tuple-element.198), channel_id=1, source_target_pairs={{0,1},{1,0},{2,3},{3,2},{4,5},{5,4},{6,7},{7,6},{8,9},{9,8},{10,11... | collective-permute-start | bytes 1769480 | tf_op jit(solution)/shard_map/ppermute | solution.py:912
  262.1 40.6 %all-to-all-start.2 = ((bf16[8,128,768]{2,1,0:T(8,128)(2,1)}), bf16[8,128,768]{2,1,0:T(8,128)(2,1)S(1)}, u32[]{:S(2)}, u32[]{:S(2)}) async-start(bf16[8,128,768]{2,1,0:T(8,128)(2,1)} %bitcast.50), calls=%async_computation.2 | async-start | bytes 3145728 | tf_op jit(solution)/shard_map/all_to_all | solution.py:1024
  271.6 47.7 %collective-permute-start.24 = (bf16[8,64,1536]{2,1,0:T(8,128)(2,1)}, bf16[8,64,1536]{2,1,0:T(8,128)(2,1)}, u32[]{:S(2)}, u32[]{:S(2)}) collective-permute-start(bf16[8,64,1536]{2,1,0:T(8,128)(2,1)} %get-tuple-element.192), channel_id=1, source_target_pairs={{0,16},{1,17},{2,18},{3,19},{4,20},{5,21},{6,22},{7,23},{8,24},{9,... | collective-permute-start | bytes 4718600 | tf_op jit(solution)/shard_map/ppermute | solution.py:912
  323.7 22.1 %collective-permute-start.35 = (bf16[2,64,1536]{2,1,0:T(8,128)(2,1)}, bf16[2,64,1536]{2,1,0:T(8,128)(2,1)}, u32[]{:S(2)}, u32[]{:S(2)}) collective-permute-start(bf16[2,64,1536]{2,1,0:T(8,128)(2,1)} %get-tuple-element.213), channel_id=1, source_target_pairs={{0,2},{1,3},{2,0},{3,1},{4,6},{5,7},{6,4},{7,5},{8,10},{9,11},{10,... | collective-permute-start | bytes 1179656 | tf_op jit(solution)/shard_map/ppermute | solution.py:912
  326.8 26.6 %collective-permute-start.37 = (bf16[2,64,1536]{2,1,0:T(8,128)(2,1)S(1)}, bf16[2,64,1536]{2,1,0:T(8,128)(2,1)}, u32[]{:S(2)}, u32[]{:S(2)}) collective-permute-start(bf16[2,64,1536]{2,1,0:T(8,128)(2,1)S(1)} %get-tuple-element.215), channel_id=1, source_target_pairs={{0,3},{1,2},{2,1},{3,0},{4,7},{5,6},{6,5},{7,4},{8,11},{9,10},{10,... | collective-permute-start | bytes 1179656 | tf_op jit(solution)/shard_map/ppermute | solution.py:912
  327.5 28.4 %collective-permute-start.34 = (bf16[20,48,384]{2,1,0:T(8,128)(2,1)S(1)}, bf16[20,48,384]{2,1,0:T(8,128)(2,1)S(1)}, u32[]{:S(2)}, u32[]{:S(2)}) collective-permute-start(bf16[20,48,384]{2,1,0:T(8,128)(2,1)S(1)} %get-tuple-element.211.refs_3_), channel_id=1, source_target_pairs={{0,16},{1,17},{2,18},{3,19},{4,20},{5,21},{6,22},{7,23},{8,24},{9,... | collective-permute-start | bytes 2211848 | tf_op jit(solution)/shard_map/ppermute | solution.py:912
  329.0 26.9 %collective-permute-start.33 = (bf16[3,48,1536]{2,1,0:T(8,128)(2,1)S(1)}, bf16[3,48,1536]{2,1,0:T(8,128)(2,1)S(1)}, u32[]{:S(2)}, u32[]{:S(2)}) collective-permute-start(bf16[3,48,1536]{2,1,0:T(8,128)(2,1)S(1)} %get-tuple-element.210), channel_id=1, source_target_pairs={{0,4},{1,5},{2,6},{3,7},{4,0},{5,1},{6,2},{7,3},{8,12},{9,13},{10,... | collective-permute-start | bytes 1327112 | tf_op jit(solution)/shard_map/ppermute | solution.py:912
  358.0 22.1 %collective-permute-start.40 = (bf16[5,48,1536]{2,1,0:T(8,128)(2,1)S(1)}, bf16[5,48,1536]{2,1,0:T(8,128)(2,1)}, u32[]{:S(2)}, u32[]{:S(2)}) collective-permute-start(bf16[5,48,1536]{2,1,0:T(8,128)(2,1)S(1)} %pad_maximum_fusion.refs_1_), channel_id=1, source_target_pairs={{0,8},{1,9},{2,10},{3,11},{4,12},{5,13},{6,14},{7,15},{8,0},{9,1},... | collective-permute-start | bytes 2211848 | tf_op jit(solution)/shard_map/ppermute | solution.py:912
  (87 other events, 863.3 us)

commit v4 on v3

--- a/solution.py
+++ b/solution.py
@@ -147,11 +147,13 @@
             k = mixed[:, pl.ds(pl.multiple_of(width + at, 128), 128)]
             v = mixed[:, pl.ds(pl.multiple_of(2 * width + at, 128), 128)]
             vt = v.T
+            scores = []
             for h in range(2):
                 kh = jnp.where((lane < 64) == (h == 0), k, jnp.zeros_like(k))
-                scores = dot(kh, q, COLS) + visible
-                top = jnp.max(scores, axis=0, keepdims=True)
-                weights = jnp.exp(scores - top)
+                scores.append(dot(kh, q, COLS) + visible)
+            for h in range(2):
+                top = jnp.max(scores[h], axis=0, keepdims=True)
+                weights = jnp.exp(scores[h] - top)
                 total = jnp.sum(weights, axis=0, keepdims=True)
                 out = dot(vt[h * 64 : (h + 1) * 64], weights.astype(LOW)) * (1.0 / total)
                 ctxt[pl.ds(pl.multiple_of(at + h * 64, 64), 64), :] = out.astype(LOW)
@@ -314,14 +316,17 @@
         g = gctx_ref[:, qcols]
         kt = k.T
         grad_v, grad_k, grad_qt = [], [], []
+        scores, grad_probs = [], []
         for h in range(2):
             mask = (lane < 64) == (h == 0)
             kh = jnp.where(mask, k, jnp.zeros_like(k))
             vh = jnp.where(mask, v, jnp.zeros_like(v))
-            probs = jnp.exp(dot(kh, q, COLS) + visible - lse_ref[pl.ds(2 * j + h, 1), :])
-            grad_probs = dot(vh, g, COLS)
-            weighted = jnp.sum(probs * grad_probs, axis=0, keepdims=True)
-            grad_scores = (probs * (grad_probs - weighted)).astype(LOW)
+            scores.append(dot(kh, q, COLS))
+            grad_probs.append(dot(vh, g, COLS))
+        for h in range(2):
+            probs = jnp.exp(scores[h] + visible - lse_ref[pl.ds(2 * j + h, 1), :])
+            weighted = jnp.sum(probs * grad_probs[h], axis=0, keepdims=True)
+            grad_scores = (probs * (grad_probs[h] - weighted)).astype(LOW)
             grad_v.append(dot(probs.astype(LOW), g))
             grad_k.append(dot(grad_scores, q))
             grad_qt.append(dot(kt[h * 64 : (h + 1) * 64], grad_scores))
@@ -690,9 +695,9 @@
 def last_kernel(
     plan, coords_ref, length_ref, mixed_ref, lse_ref, gctx_ref, first_ref, n_ref, s_ref, gains_ref, x_ref, ctxt_ref, low_ref,
     slot_ref, type_ref, top0, top1, low0, low1, att1, bias0, bias1, wqkv_hbm,
-    out_ref, keep_ref, send_ref,
-    wqkv, dmix, xt, res, back_ref, back_low, att0, emb, small, sems,
+    out_ref, *parts_and_scratch
 ):
+    outs, (wqkv, dmix, xt, res, back_ref, back_low, att0, emb, small, sems) = parts_and_scratch[:-10], parts_and_scratch[-10:]
     tokens, width = back_ref.shape
     load = pltpu.make_async_copy(wqkv_hbm.at[0], wqkv, sems.at[0])
     load.start()
@@ -756,10 +761,10 @@
             for v in range(blocks // 2):
                 block = 2 * v + y
                 res[core * blocks + block, piece:, :] = jnp.concatenate([pos[block], mine], axis=0).astype(LOW)
-    place(coords_ref, plan, res, keep_ref, send_ref)
-
-
-def last(plan, coords, length, mixed, lse, gctx, first, n, sp, gains, x, ctxt, low, slot_of, types, sums, w_qkv, slots, blocks, after=()):
+    place(coords_ref, plan, res, *outs)
+
+
+def last(plan, coords, length, mixed, lse, gctx, first, n, sp, gains, x, ctxt, low, slot_of, types, sums, w_qkv, slots, blocks, parts=2, after=()):
     tokens, width = first.shape
     s = jax.ShapeDtypeStruct
     v = pltpu.VMEM
@@ -768,10 +773,10 @@
     return run(
         functools.partial(last_kernel, plan),
         after,
-        out_shape=(s((slots, width), LOW), s(block, LOW), s(block, LOW)),
+        out_shape=(s((slots, width), LOW),) + (s((2 * blocks // parts,) + block[1:], LOW),) * parts,
         in_specs=[SM, SM] + [VM] * (len(operands) - 3) + [HBM],
         operands=operands,
-        out_specs=(VM,) * 3,
+        out_specs=(VM,) * (1 + parts),
         scratch_shapes=[
             v((width, 3 * width), LOW), v((tokens, 3 * width), LOW), v((width, tokens), LOW),
             v((2 * blocks,) + block[1:], LOW), v((tokens, width), F32), v((tokens, width), LOW),
@@ -1150,7 +1155,8 @@
     blocks = owners
     half = width // 2
     single = lambda dims: tuple((dim,) for dim in dims)
-    plan_two1, plan_one1, plan_mix1 = (("x", "y"), ("a",), ("b",)), single("abxy"), single("ayxb")
+    plan_two1, plan_one1 = (("x", "y"), ("a",), ("b",)), (("a",), ("x", "y"), ("b",))
+    plan_mix1 = single("ayxb")
     plan_two0, plan_one0, plan_mix0 = single("xayb"), single("yxab"), (("core",), ("y",), ("x", "a"), ("b",))
     kind, row_hit, slot_of, asked = embed
     local_rows = row_hit.shape[1]
@@ -1184,9 +1190,8 @@
     two0, one0, mix1 = [Bucket(cube, plan, parts) for plan, parts in zip((plan_two0, plan_one0, plan_mix1), got)]
     for bucket in (mix1, two0, one0):
         bucket.start()
-    mark = step([two1, one1], after=got[0][:1], cost=LONG)
+    mark = step([joined((two1, one1), 0)], after=got[0][:1], cost=LONG)
     two1.start()
-    one1.start()
     types = jnp.broadcast_to(kind[:, None], (tokens, 128))
     outgoing, *got = last(
         plan_mix0, coords, lengths, mixed0, lse0, gctx, first, *norms[0], gains, x0[0], ctx0[0], low, slot_of[None, :], types,
@@ -1195,35 +1200,36 @@
     incoming = exchange_rows(outgoing, owners)
     mix0 = Bucket(cube, plan_mix0, got)
     mix0.start()
-    mark = step([two1, one1, mix1, two0, one0], after=got[:1], cost=LONG)
-    for bucket in (one1, mix1, two0, one0):
+    mark = step([two1, mix1, two0, one0], after=got[:1], cost=LONG)
+    for bucket in (mix1, two0, one0):
         bucket.start()
     mark = step([mix0], after=(mark,))
     mix0.start()
-    mark = step([mix1, two0, one0, one1], after=(mark,), cost=LONG)
+    mark = step([mix1, two0, one0], after=(mark,), cost=LONG)
     for bucket in (mix1, two0, one0):
         bucket.start()
     folded = (local_rows // 48, 48, half)
     got = table_back(coords, asked[None, :], incoming, local_rows, after=(mark,))
     table = Bucket(cube, single(("core", "y")), [part.reshape(folded) for part in got])
     table.start()
-    mark = step([mix0, joined((mix1, two0, one0), 0), table], after=got[:1], cost=LONG)
+    mark = step([mix0, joined((mix1, two0, one0), 0)], after=got[:1], cost=LONG)
     mix0.start()
     mix1.start()
+    mark = step([table], after=(mark,))
     table.start()
     mark = step([mix0], after=(mark,), cost=LONG)
     mix0.start()
     two1.keep()
     mark = step([joined((mix1, two1), 0), table], after=(mark,))
-    step([mix0], after=(mark,))
-    half_of = lambda n: one1.parts[0][n : n + 1]
-    mine_y = (lax.axis_index("dp") >> 1) & 1 == 0
-    one1_own = jnp.where(mine_y, half_of(0), half_of(1))
-    one1_other = jnp.where(mine_y, half_of(1), half_of(0))
-    four = mix1.parts[0]
-    own = jnp.concatenate([four, one1_own], axis=0)
-    over_y = jnp.concatenate([cube.along(four, ("y",)), one1_other], axis=0)
-    last_y = cube.along(mix0.parts[0], ("y",))
+    later = Bucket(cube, (), (cube.along(mix1.parts[0], ("y",)),))
+    later.keep()
+    mark = step([mix0], after=(mark,))
+    last_y = Bucket(cube, (), (cube.along(mix0.parts[0], ("y",)),))
+    last_y.keep()
+    step([last_y], after=(mark,))
+    step([later], after=(last_y.parts[0],))
+    own = mix1.parts[0]
+    over_y, last_y = later.parts[0], last_y.parts[0]
     qkv_out, wout_out, one_out, two_out, pos_out, small = finish(
         coords,
         (own, over_y, cube.core(own), cube.core(over_y)),

time: 395 us -> 380 us (0.962)
  local copies, waits for them, and re-layouts: 27.8 us -> 20.4 us
  starting transfers between devices: 51.8 us -> 45.8 us
    unnamed x124 -> x114, local copies, waits for them, and re-layouts: 21 us -> 13.6 us
    ppermute x46, waiting for transfers between devices: 71.7 us -> 78.2 us  [permute(): return lax.ppermute(value, AXES, pairs)]
    ppermute x46, starting transfers between devices: 36.8 us -> 31 us  [permute(): return lax.ppermute(value, AXES, pairs)]
    all_to_all x1, waiting for transfers between devices: 10.8 us -> 5.78 us  [exchange_rows(): lax.all_to_all(outgoing.reshape(owners, -1, shape[1]), 'vocab', split_axi...]
    pallas_call x17 -> x20, Pallas kernels: 175 us -> 172 us  [run(): pl.pallas_call(body, out_shape=out_shape, in_specs=list(in_specs) + [ANY]...]
  transfers between devices with their start and end apart: 49 -> 49, of which waited for: 16 -> 15; matrix products, arithmetic and copies ran while one was open for 1% -> 2% of each run, Pallas kernels for 27% -> 31%
where the time goes in v4:
time: 380 us; the launch traced here: 373 us
  Pallas kernels  172 us (45%)
  waiting for transfers between devices  123 us (32%)
  starting transfers between devices  45.8 us (12%)
  local copies, waits for them, and re-layouts  20.4 us (5%)
  other arithmetic  6.6 us (2%)
    pallas_call x20, Pallas kernels, run(): pl.pallas_call(body, out_shape=out_shape, in_specs=list(in_specs) + [ANY]...  172 us
    ppermute x46, waiting for transfers between devices, permute(): return lax.ppermute(value, AXES, pairs)  78.2 us
    all_to_all x1, waiting for transfers between devices, on_device(): lax.all_to_all(found_rows.reshape(owners, slot_count, width), 'vocab', sp...  32.4 us
    ppermute x46, starting transfers between devices, permute(): return lax.ppermute(value, AXES, pairs)  31 us
    unnamed x114, local copies, waits for them, and re-layouts  13.6 us
  transfers between devices with their start and end apart: 49, of which 15 were waited for; matrix products, arithmetic and copies ran while one was open for 2% of the time, Pallas kernels for 31%

profile of v4, /device:TPU:0, one launch (start us, length us, event | category | flops | bytes accessed | tf_op | source)
XLA Modules:
  0.0 373.5 jit_solution(16431465891887121601)
XLA Ops:
  2.1 7.3 %all-to-all-start = ((s32[8,1,512]{2,1,0:T(1,128)}), s32[8,1,512]{2,1,0:T(1,128)S(1)}, u32[]{:S(2)}, u32[]{:S(2)}) async-start(s32[8,1,512]{2,1,0:T(1,128)} %broadcast_in_dim.22), calls=%async_computation | async-start | bytes 32768 | tf_op jit(solution)/shard_map/all_to_all | solution.py:988
  9.3 6.6 %all-to-all-done = s32[8,1,512]{2,1,0:T(1,128)S(1)} async-done(((s32[8,1,512]{2,1,0:T(1,128)}), s32[8,1,512]{2,1,0:T(1,128)S(1)}, u32[]{:S(2)}, u32[]{:S(2)}) %all-to-all-start) | async-done | bytes 16416 | tf_op jit(solution)/shard_map/all_to_all | solution.py:988
  17.7 3.1 fusion.2
  20.8 3.7 all-to-all-start.1
  28.1 32.4 %all-to-all-done.1 = bf16[8,128,768]{2,1,0:T(8,128)(2,1)S(1)} async-done(((bf16[8,128,768]{2,1,0:T(8,128)(2,1)}), bf16[8,128,768]{2,1,0:T(8,128)(2,1)S(1)}, u32[]{:S(2)}, u32[]{:S(2)}) %all-to-all-start.1) | async-done | bytes 1572896 | tf_op jit(solution)/shard_map/all_to_all | solution.py:1000
  62.3 50.2 %forward.1 = (f32[512,768]{1,0:T(8,128)}, f32[512,128]{1,0:T(8,128)}, bf16[512,768]{1,0:T(8,128)(2,1)}, f32[512,768]{1,0:T(8,128)}, bf16[512,768]{1,0:T(8,128)(2...) custom-call(s32[5]{0:T(128)} %stack.23.refs_0_, ...), custom_call_target="tpu_custom_call" | custom-call | flops 1 | bytes 1 | tf_op jit(solution)/shard_map/forward/pallas_call | solution.py:31
  113.6 15.5 %feed.1 = (bf16[512,1536]{1,0:T(8,128)(2,1)}, bf16[512,1536]{1,0:T(8,128)(2,1)}, f32[1,3072]{1,0:T(1,128)S(1)}, f32[512,768]{1,0:T(8,128)}, bf16[512,768]{1,0:T(...) custom-call(s32[5]{0:T(128)S(1)} %copy-done.20, ...), custom_call_target="tpu_custom_call" | custom-call | flops 1 | bytes 1 | tf_op jit(solution)/shard_map/feed/pallas_call | solution.py:31
  130.2 4.1 %collective-permute-done.refs_2_ = bf16[512,384]{1,0:T(8,128)(2,1)S(1)} collective-permute-done((bf16[512,384]{1,0:T(8,128)(2,1)S(1)}, bf16[512,384]{1,0:T(8,128)(2,1)S(1)}, u32[]{:S(2)}, u32[]{:S(2)}) %collective-permute-start) | collective-permute-done | bytes 393248 | tf_op jit(solution)/shard_map/ppermute | solution.py:917
  135.8 11.7 %weights.2 = (bf16[4,48,1536]{2,1,0:T(8,128)(2,1)S(1)}, bf16[4,48,1536]{2,1,0:T(8,128)(2,1)}, bf16[4,48,1536]{2,1,0:T(8,128)(2,1)}, bf16[4,48,1536]{2,1,0:T(8,12...) custom-call(s32[5]{0:T(128)S(1)} %copy-done.20, bf16[512,384]{1,0:T(8,128)(2,1)S(1)} %copy-done.14, ...), custom_call_target="tpu_custom_call" | custom-call | flops 1 | bytes 1 | tf_op jit(solution)/shard_map/weights/pallas_call | solution.py:31
  153.1 29.9 %between.1 = (bf16[512,1152]{1,0:T(8,128)(2,1)}, bf16[512,1152]{1,0:T(8,128)(2,1)}, bf16[512,1536]{1,0:T(8,128)(2,1)}, bf16[512,1536]{1,0:T(8,128)(2,1)}, f32[2,...) custom-call(s32[5]{0:T(128)} %stack.23.refs_0_, ...), custom_call_target="tpu_custom_call" | custom-call | flops 1 | bytes 1 | tf_op jit(solution)/shard_map/between/pallas_call | solution.py:31
  187.1 4.0 %collective-permute-done.18.refs_14_ = bf16[768,512]{1,0:T(8,128)(2,1)S(1)} collective-permute-done((bf16[768,512]{1,0:T(8,128)(2,1)}, bf16[768,512]{1,0:T(8,128)(2,1)S(1)}, u32[]{:S(2)}, u32[]{:S(2)}) %collective-permute-start.18) | collective-permute-done | bytes 786464 | tf_op jit(solution)/shard_map/ppermute | solution.py:917
  197.6 18.7 %weights.3 = (bf16[8,48,1536]{2,1,0:T(8,128)(2,1)}, bf16[8,48,1536]{2,1,0:T(8,128)(2,1)}, bf16[8,48,1536]{2,1,0:T(8,128)(2,1)}, bf16[8,48,1536]{2,1,0:T(8,128)(2...) custom-call(s32[5]{0:T(128)S(1)} %copy-done.21, bf16[512,384]{1,0:T(8,128)(2,1)S(1)} %copy-done.15, ...), custom_call_target="tpu_custom_call" | custom-call | flops 1 | bytes 1 | tf_op jit(solution)/shard_map/weights/pallas_call | solution.py:31
  222.5 25.6 %last.1 = (bf16[1024,768]{1,0:T(8,128)(2,1)}, bf16[16,64,1536]{2,1,0:T(8,128)(2,1)}, bf16[16,64,1536]{2,1,0:T(8,128)(2,1)}) custom-call(s32[5]{0:T(128)S(1)} %copy-done.21, s32[1]{0:T(128)S(6)} %copy.33.refs_1_, bf16[512,2304]{1,0:T(8,128)(2,1)} %get-tuple-element.117.refs_2_, f32[12,512]{1,0:T(8,128)S(1)} %copy-done.24, bf16[512,768]{1,0:T(8,128)(2,1)S(1)} %copy-done.10, ...), custom_call_target="tpu_custom_call" | custom-call | flops 1 | bytes 1 | tf_op jit(solution)/shard_map/last/pallas_call | solution.py:31
  259.2 3.9 %all-to-all-start.2 = ((bf16[8,128,768]{2,1,0:T(8,128)(2,1)}), bf16[8,128,768]{2,1,0:T(8,128)(2,1)S(1)}, u32[]{:S(2)}, u32[]{:S(2)}) async-start(bf16[8,128,768]{2,1,0:T(8,128)(2,1)} %bitcast.50), calls=%async_computation.2 | async-start | bytes 3145728 | tf_op jit(solution)/shard_map/all_to_all | solution.py:1029
  265.0 3.5 combine.15
  269.7 3.7 collective-permute-done.26.refs_1_
  273.4 15.7 %collective-permute-done.27.refs_3_ = bf16[4,48,1536]{2,1,0:T(8,128)(2,1)} collective-permute-done((bf16[4,48,1536]{2,1,0:T(8,128)(2,1)}, bf16[4,48,1536]{2,1,0:T(8,128)(2,1)}, u32[]{:S(2)}, u32[]{:S(2)}) %collective-permute-start.27) | collective-permute-done | bytes 589856 | tf_op jit(solution)/shard_map/ppermute | solution.py:917
  294.3 5.8 %all-to-all-done.2 = bf16[8,128,768]{2,1,0:T(8,128)(2,1)S(1)} async-done(((bf16[8,128,768]{2,1,0:T(8,128)(2,1)}), bf16[8,128,768]{2,1,0:T(8,128)(2,1)S(1)}, u32[]{:S(2)}, u32[]{:S(2)}) %all-to-all-start.2) | async-done | bytes 1572896 | tf_op jit(solution)/shard_map/all_to_all | solution.py:1029
  303.3 8.1 %collective-permute-done.30.refs_5_ = bf16[2,48,1536]{2,1,0:T(8,128)(2,1)} collective-permute-done((bf16[2,48,1536]{2,1,0:T(8,128)(2,1)}, bf16[2,48,1536]{2,1,0:T(8,128)(2,1)}, u32[]{:S(2)}, u32[]{:S(2)}) %collective-permute-start.30) | collective-permute-done | bytes 294944 | tf_op jit(solution)/shard_map/ppermute | solution.py:917
  319.4 15.7 %collective-permute-done.35.refs_1_ = bf16[2,64,1536]{2,1,0:T(8,128)(2,1)S(1)} collective-permute-done((bf16[2,64,1536]{2,1,0:T(8,128)(2,1)S(1)}, bf16[2,64,1536]{2,1,0:T(8,128)(2,1)S(1)}, u32[]{:S(2)}, u32[]{:S(2)}) %collective-permute-start.35) | collective-permute-done | bytes 393248 | tf_op jit(solution)/shard_map/ppermute | solution.py:917
  335.2 6.3 %collective-permute-done.37.refs_3_ = bf16[2,64,1536]{2,1,0:T(8,128)(2,1)S(1)} collective-permute-done((bf16[2,64,1536]{2,1,0:T(8,128)(2,1)S(1)}, bf16[2,64,1536]{2,1,0:T(8,128)(2,1)S(1)}, u32[]{:S(2)}, u32[]{:S(2)}) %collective-permute-start.37) | collective-permute-done | bytes 393248 | tf_op jit(solution)/shard_map/ppermute | solution.py:917
  343.2 10.8 %collective-permute-done.40.refs_1_ = bf16[1,64,1536]{2,1,0:T(8,128)(2,1)S(1)} collective-permute-done((bf16[1,64,1536]{2,1,0:T(8,128)(2,1)S(1)}, bf16[1,64,1536]{2,1,0:T(8,128)(2,1)S(1)}, u32[]{:S(2)}, u32[]{:S(2)}) %collective-permute-start.40) | collective-permute-done | bytes 196640 | tf_op jit(solution)/shard_map/ppermute | solution.py:917
  356.1 6.0 %collective-permute-done.41.refs_0_ = bf16[1,64,1536]{2,1,0:T(8,128)(2,1)S(1)} collective-permute-done((bf16[1,64,1536]{2,1,0:T(8,128)(2,1)S(1)}, bf16[1,64,1536]{2,1,0:T(8,128)(2,1)S(1)}, u32[]{:S(2)}, u32[]{:S(2)}) %collective-permute-start.41) | collective-permute-done | bytes 196640 | tf_op jit(solution)/shard_map/ppermute | solution.py:917
  366.0 4.7 %finish.1 = (f32[2,96,2304]{2,1,0:T(8,128)}, f32[2,96,768]{2,1,0:T(8,128)}, f32[2,96,3072]{2,1,0:T(8,128)}, f32[2,384,768]{2,1,0:T(8,128)}, f32[64,768]{1,0:T(8,128)}, /*index=5*/f32[28,768]{1,0:T(8,128)S(1)}) custom-call(s32[5]{0:T(128)S(1)} %copy-done.23, bf16[5,48,1536]{2,1,0:T(8,128)(2,1)S(1)} %get-tuple-element.213.refs_2_.refs_1_, ...), custom_call_target="tpu_custom_call" | custom-call | flops 1 | bytes 1 | tf_op jit(solution)/shard_map/finish/pallas_call | solution.py:31
  (244 shorter events, 74.1 us)
Async XLA Ops:
  20.8 39.7 %all-to-all-start.1 = ((bf16[8,128,768]{2,1,0:T(8,128)(2,1)}), bf16[8,128,768]{2,1,0:T(8,128)(2,1)S(1)}, u32[]{:S(2)}, u32[]{:S(2)}) async-start(bf16[8,128,768]{2,1,0:T(8,128)(2,1)} %bitcast.51), calls=%async_computation.1 | async-start | bytes 3145728 | tf_op jit(solution)/shard_map/all_to_all | solution.py:1000
  112.5 21.9 %collective-permute-start.1 = (bf16[512,3072]{1,0:T(8,128)(2,1)}, bf16[512,3072]{1,0:T(8,128)(2,1)S(1)}, u32[]{:S(2)}, u32[]{:S(2)}) collective-permute-start(bf16[512,3072]{1,0:T(8,128)(2,1)} %get-tuple-element.135.refs_3_), channel_id=1, source_target_pairs={{0,8},{1,9},{2,10},{3,11},{4,12},{5,13},{6,14},{7,15},{8,0},{9,1},... | collective-permute-start | bytes 9437192 | tf_op jit(solution)/shard_map/ppermute | solution.py:917
  148.3 35.7 %collective-permute-start.7 = (bf16[8,48,1536]{2,1,0:T(8,128)(2,1)}, bf16[8,48,1536]{2,1,0:T(8,128)(2,1)S(1)}, u32[]{:S(2)}, u32[]{:S(2)}) collective-permute-start(bf16[8,48,1536]{2,1,0:T(8,128)(2,1)} %get-tuple-element.158), channel_id=1, source_target_pairs={{0,2},{1,3},{2,0},{3,1},{4,6},{5,7},{6,4},{7,5},{8,10},{9,11},{10,... | collective-permute-start | bytes 3538952 | tf_op jit(solution)/shard_map/ppermute | solution.py:917
  148.7 34.2 %collective-permute-start.16 = (bf16[512,768]{1,0:T(8,128)(2,1)}, bf16[512,768]{1,0:T(8,128)(2,1)}, u32[]{:S(2)}, u32[]{:S(2)}) collective-permute-start(bf16[512,768]{1,0:T(8,128)(2,1)} %get-tuple-element.171.refs_9_), channel_id=1, source_target_pairs={{0,8},{1,9},{2,10},{3,11},{4,12},{5,13},{6,14},{7,15},{8,0},{9,1},... | collective-permute-start | bytes 2359304 | tf_op jit(solution)/shard_map/ppermute | solution.py:917
  148.9 34.2 %collective-permute-start.4 = (bf16[4,48,1536]{2,1,0:T(8,128)(2,1)}, bf16[4,48,1536]{2,1,0:T(8,128)(2,1)S(1)}, u32[]{:S(2)}, u32[]{:S(2)}) collective-permute-start(bf16[4,48,1536]{2,1,0:T(8,128)(2,1)} %get-tuple-element.154), channel_id=1, source_target_pairs={{0,16},{1,17},{2,18},{3,19},{4,20},{5,21},{6,22},{7,23},{8,24},{9,... | collective-permute-start | bytes 1769480 | tf_op jit(solution)/shard_map/ppermute | solution.py:917
  150.4 33.2 %collective-permute-start.5 = (bf16[4,48,1536]{2,1,0:T(8,128)(2,1)}, bf16[4,48,1536]{2,1,0:T(8,128)(2,1)}, u32[]{:S(2)}, u32[]{:S(2)}) collective-permute-start(bf16[4,48,1536]{2,1,0:T(8,128)(2,1)} %get-tuple-element.155), channel_id=1, source_target_pairs={{0,1},{1,0},{2,3},{3,2},{4,5},{5,4},{6,7},{7,6},{8,9},{9,8},{10,11... | collective-permute-start | bytes 1769480 | tf_op jit(solution)/shard_map/ppermute | solution.py:917
  151.6 32.0 %collective-permute-start.6 = (bf16[4,48,1536]{2,1,0:T(8,128)(2,1)S(1)}, bf16[4,48,1536]{2,1,0:T(8,128)(2,1)}, u32[]{:S(2)}, u32[]{:S(2)}) collective-permute-start(bf16[4,48,1536]{2,1,0:T(8,128)(2,1)S(1)} %get-tuple-element.156), channel_id=1, source_target_pairs={{0,17},{1,16},{2,19},{3,18},{4,21},{5,20},{6,23},{7,22},{8,25},{9,... | collective-permute-start | bytes 1769480 | tf_op jit(solution)/shard_map/ppermute | solution.py:917
  191.1 25.3 %collective-permute-start.10 = (bf16[2,48,1536]{2,1,0:T(8,128)(2,1)S(1)}, bf16[2,48,1536]{2,1,0:T(8,128)(2,1)S(1)}, u32[]{:S(2)}, u32[]{:S(2)}) collective-permute-start(bf16[2,48,1536]{2,1,0:T(8,128)(2,1)S(1)} %get-tuple-element.163), channel_id=1, source_target_pairs={{0,1},{1,0},{2,3},{3,2},{4,5},{5,4},{6,7},{7,6},{8,9},{9,8},{10,11... | collective-permute-start | bytes 884744 | tf_op jit(solution)/shard_map/ppermute | solution.py:917
  192.4 25.3 %collective-permute-start.11 = (bf16[2,48,1536]{2,1,0:T(8,128)(2,1)S(1)}, bf16[2,48,1536]{2,1,0:T(8,128)(2,1)S(1)}, u32[]{:S(2)}, u32[]{:S(2)}) collective-permute-start(bf16[2,48,1536]{2,1,0:T(8,128)(2,1)S(1)} %get-tuple-element.164), channel_id=1, source_target_pairs={{0,17},{1,16},{2,19},{3,18},{4,21},{5,20},{6,23},{7,22},{8,25},{9,... | collective-permute-start | bytes 884744 | tf_op jit(solution)/shard_map/ppermute | solution.py:917
  194.5 24.2 %collective-permute-start.8 = (bf16[2,48,1536]{2,1,0:T(8,128)(2,1)S(1)}, bf16[2,48,1536]{2,1,0:T(8,128)(2,1)S(1)}, u32[]{:S(2)}, u32[]{:S(2)}) collective-permute-start(bf16[2,48,1536]{2,1,0:T(8,128)(2,1)S(1)} %get-tuple-element.160), channel_id=1, source_target_pairs={{0,2},{1,3},{2,0},{3,1},{4,6},{5,7},{6,4},{7,5},{8,10},{9,11},{10,... | collective-permute-start | bytes 884744 | tf_op jit(solution)/shard_map/ppermute | solution.py:917
  196.5 22.2 %collective-permute-start.9 = (bf16[2,48,1536]{2,1,0:T(8,128)(2,1)S(1)}, bf16[2,48,1536]{2,1,0:T(8,128)(2,1)S(1)}, u32[]{:S(2)}, u32[]{:S(2)}) collective-permute-start(bf16[2,48,1536]{2,1,0:T(8,128)(2,1)S(1)} %get-tuple-element.162), channel_id=1, source_target_pairs={{0,16},{1,17},{2,18},{3,19},{4,20},{5,21},{6,22},{7,23},{8,24},{9,... | collective-permute-start | bytes 884744 | tf_op jit(solution)/shard_map/ppermute | solution.py:917
  216.3 34.3 %collective-permute-start.22 = (bf16[8,48,1536]{2,1,0:T(8,128)(2,1)}, bf16[8,48,1536]{2,1,0:T(8,128)(2,1)S(1)}, u32[]{:S(2)}, u32[]{:S(2)}) collective-permute-start(bf16[8,48,1536]{2,1,0:T(8,128)(2,1)} %get-tuple-element.183), channel_id=1, source_target_pairs={{0,2},{1,3},{2,0},{3,1},{4,6},{5,7},{6,4},{7,5},{8,10},{9,11},{10,... | collective-permute-start | bytes 3538952 | tf_op jit(solution)/shard_map/ppermute | solution.py:917
  216.4 34.2 %collective-permute-start.23 = (bf16[8,48,1536]{2,1,0:T(8,128)(2,1)}, bf16[8,48,1536]{2,1,0:T(8,128)(2,1)S(1)}, u32[]{:S(2)}, u32[]{:S(2)}) collective-permute-start(bf16[8,48,1536]{2,1,0:T(8,128)(2,1)} %get-tuple-element.184), channel_id=1, source_target_pairs={{0,1},{1,0},{2,3},{3,2},{4,5},{5,4},{6,7},{7,6},{8,9},{9,8},{10,11... | collective-permute-start | bytes 3538952 | tf_op jit(solution)/shard_map/ppermute | solution.py:917
  217.7 32.9 %collective-permute-start.24 = (bf16[8,48,1536]{2,1,0:T(8,128)(2,1)}, bf16[8,48,1536]{2,1,0:T(8,128)(2,1)S(1)}, u32[]{:S(2)}, u32[]{:S(2)}) collective-permute-start(bf16[8,48,1536]{2,1,0:T(8,128)(2,1)} %get-tuple-element.186), channel_id=1, source_target_pairs={{0,16},{1,17},{2,18},{3,19},{4,20},{5,21},{6,22},{7,23},{8,24},{9,... | collective-permute-start | bytes 3538952 | tf_op jit(solution)/shard_map/ppermute | solution.py:917
  220.3 28.1 %collective-permute-start.21 = (bf16[2,48,1536]{2,1,0:T(8,128)(2,1)S(1)}, bf16[2,48,1536]{2,1,0:T(8,128)(2,1)S(1)}, u32[]{:S(2)}, u32[]{:S(2)}) collective-permute-start(bf16[2,48,1536]{2,1,0:T(8,128)(2,1)S(1)} %get-tuple-element.181), channel_id=1, source_target_pairs={{0,4},{1,5},{2,6},{3,7},{4,0},{5,1},{6,2},{7,3},{8,12},{9,13},{10,... | collective-permute-start | bytes 884744 | tf_op jit(solution)/shard_map/ppermute | solution.py:917
  257.7 31.5 %collective-permute-start.27 = (bf16[4,48,1536]{2,1,0:T(8,128)(2,1)}, bf16[4,48,1536]{2,1,0:T(8,128)(2,1)}, u32[]{:S(2)}, u32[]{:S(2)}) collective-permute-start(bf16[4,48,1536]{2,1,0:T(8,128)(2,1)} %get-tuple-element.193), channel_id=1, source_target_pairs={{0,2},{1,3},{2,0},{3,1},{4,6},{5,7},{6,4},{7,5},{8,10},{9,11},{10,... | collective-permute-start | bytes 1769480 | tf_op jit(solution)/shard_map/ppermute | solution.py:917
  257.8 31.4 %collective-permute-start.28 = (bf16[4,48,1536]{2,1,0:T(8,128)(2,1)}, bf16[4,48,1536]{2,1,0:T(8,128)(2,1)}, u32[]{:S(2)}, u32[]{:S(2)}) collective-permute-start(bf16[4,48,1536]{2,1,0:T(8,128)(2,1)} %get-tuple-element.195), channel_id=1, source_target_pairs={{0,1},{1,0},{2,3},{3,2},{4,5},{5,4},{6,7},{7,6},{8,9},{9,8},{10,11... | collective-permute-start | bytes 1769480 | tf_op jit(solution)/shard_map/ppermute | solution.py:917
  259.2 40.9 %all-to-all-start.2 = ((bf16[8,128,768]{2,1,0:T(8,128)(2,1)}), bf16[8,128,768]{2,1,0:T(8,128)(2,1)S(1)}, u32[]{:S(2)}, u32[]{:S(2)}) async-start(bf16[8,128,768]{2,1,0:T(8,128)(2,1)} %bitcast.50), calls=%async_computation.2 | async-start | bytes 3145728 | tf_op jit(solution)/shard_map/all_to_all | solution.py:1029
  268.5 42.9 %collective-permute-start.25 = (bf16[8,64,1536]{2,1,0:T(8,128)(2,1)}, bf16[8,64,1536]{2,1,0:T(8,128)(2,1)}, u32[]{:S(2)}, u32[]{:S(2)}) collective-permute-start(bf16[8,64,1536]{2,1,0:T(8,128)(2,1)} %get-tuple-element.189), channel_id=1, source_target_pairs={{0,16},{1,17},{2,18},{3,19},{4,20},{5,21},{6,22},{7,23},{8,24},{9,... | collective-permute-start | bytes 4718600 | tf_op jit(solution)/shard_map/ppermute | solution.py:917
  313.6 21.6 %collective-permute-start.35 = (bf16[2,64,1536]{2,1,0:T(8,128)(2,1)S(1)}, bf16[2,64,1536]{2,1,0:T(8,128)(2,1)S(1)}, u32[]{:S(2)}, u32[]{:S(2)}) collective-permute-start(bf16[2,64,1536]{2,1,0:T(8,128)(2,1)S(1)} %get-tuple-element.208), channel_id=1, source_target_pairs={{0,2},{1,3},{2,0},{3,1},{4,6},{5,7},{6,4},{7,5},{8,10},{9,11},{10,... | collective-permute-start | bytes 1179656 | tf_op jit(solution)/shard_map/ppermute | solution.py:917
  313.7 21.5 %collective-permute-start.36 = (bf16[2,64,1536]{2,1,0:T(8,128)(2,1)S(1)}, bf16[2,64,1536]{2,1,0:T(8,128)(2,1)S(1)}, u32[]{:S(2)}, u32[]{:S(2)}) collective-permute-start(bf16[2,64,1536]{2,1,0:T(8,128)(2,1)S(1)} %get-tuple-element.209), channel_id=1, source_target_pairs={{0,1},{1,0},{2,3},{3,2},{4,5},{5,4},{6,7},{7,6},{8,9},{9,8},{10,11... | collective-permute-start | bytes 1179656 | tf_op jit(solution)/shard_map/ppermute | solution.py:917
  315.5 26.0 %collective-permute-start.37 = (bf16[2,64,1536]{2,1,0:T(8,128)(2,1)S(1)}, bf16[2,64,1536]{2,1,0:T(8,128)(2,1)S(1)}, u32[]{:S(2)}, u32[]{:S(2)}) collective-permute-start(bf16[2,64,1536]{2,1,0:T(8,128)(2,1)S(1)} %get-tuple-element.210), channel_id=1, source_target_pairs={{0,3},{1,2},{2,1},{3,0},{4,7},{5,6},{6,5},{7,4},{8,11},{9,10},{10,... | collective-permute-start | bytes 1179656 | tf_op jit(solution)/shard_map/ppermute | solution.py:917
  317.3 24.4 %collective-permute-start.34 = (bf16[20,48,384]{2,1,0:T(8,128)(2,1)S(1)}, bf16[20,48,384]{2,1,0:T(8,128)(2,1)S(1)}, u32[]{:S(2)}, u32[]{:S(2)}) collective-permute-start(bf16[20,48,384]{2,1,0:T(8,128)(2,1)S(1)} %combine.18.refs_4_.refs_3_), channel_id=1, source_target_pairs={{0,16},{1,17},{2,18},{3,19},{4,20},{5,21},{6,22},{7,23},{8,24},{9,... | collective-permute-start | bytes 2211848 | tf_op jit(solution)/shard_map/ppermute | solution.py:917
  318.0 23.7 %collective-permute-start.32 = (bf16[3,48,1536]{2,1,0:T(8,128)(2,1)S(1)}, bf16[3,48,1536]{2,1,0:T(8,128)(2,1)S(1)}, u32[]{:S(2)}, u32[]{:S(2)}) collective-permute-start(bf16[3,48,1536]{2,1,0:T(8,128)(2,1)S(1)} %get-tuple-element.205), channel_id=1, source_target_pairs={{0,4},{1,5},{2,6},{3,7},{4,0},{5,1},{6,2},{7,3},{8,12},{9,13},{10,... | collective-permute-start | bytes 1327112 | tf_op jit(solution)/shard_map/ppermute | solution.py:917
  (82 other events, 931.5 us)

commit v5 on v4

--- a/solution.py
+++ b/solution.py
@@ -71,6 +71,10 @@
     tail = tail * bell
     phi = jnp.where(inputs >= 0.0, 1.0 - tail, tail)
     return inputs * phi, phi + inputs * bell * 0.3989422804014327
+
+
+def as_column(row):
+    return jnp.broadcast_to(row, (128, row.shape[1])).T[:, :1]
 
 
 def forward_kernel(
@@ -107,10 +111,10 @@
     gains = gains_ref[...].astype(F32)
     shifts = shifts_ref[...].astype(F32)
     number = lax.broadcasted_iota(jnp.int32, (tokens, replies_ref.shape[0]), 1)
-    hit = jnp.where(number == slot_ref[:, :1], 1.0, 0.0).astype(LOW)
+    hit = jnp.where(number == as_column(slot_ref[...].astype(F32)).astype(jnp.int32), 1.0, 0.0).astype(LOW)
     types = type_ref[...].astype(F32)
     embedded = dot(hit, replies_ref[...]) + pos_ref[...].astype(F32)
-    embedded = embedded + jnp.where(kind_ref[:, :1] > 0.5, types[1:2], types[0:1])
+    embedded = embedded + jnp.where(as_column(kind_ref[...].astype(F32)) > 0.5, types[1:2], types[0:1])
     normed, spread = normalize(embedded)
     n0[...] = normed
     emit("n0", n0, n0_ref)
@@ -201,7 +205,7 @@
 
 
 def forward(
-    coords, length, replies, slot_col, kind_col, pos, types, gains, shifts, ffn_bias, cotangent, w_qkv, w_out, w_ff1, w_ff2
+    coords, length, replies, slot_of, kinds, pos, types, gains, shifts, ffn_bias, cotangent, w_qkv, w_out, w_ff1, w_ff2
 ):
     tokens, width = pos.shape
     ff = w_ff1.shape[2]
@@ -223,7 +227,7 @@
         out_shape=(wide, spread, low) + end + layer_out * (NL - 1) + layer_out[:9],
         in_specs=[SM, SM] + [VM] * 9 + [HBM] * 4,
         operands=(
-            coords, length, replies, slot_col, kind_col, pos, types, gains, shifts, ffn_bias, cotangent, w_qkv, w_out, w_ff1, w_ff2
+            coords, length, replies, slot_of, kinds, pos, types, gains, shifts, ffn_bias, cotangent, w_qkv, w_out, w_ff1, w_ff2
         ),
         out_specs=(ANY, VM, VM) + (VM,) * 5 + layer_spec * (NL - 1) + layer_spec[:9],
         scratch_shapes=[
@@ -423,8 +427,8 @@
     layer, coords_ref, length_ref, mixed_ref, lse_ref, gctx_in, first_in, n2_ref, s2_ref, n1_ref, s1_ref, gains_ref,
     gp_hbm, wqkv_hbm, wout_hbm, w1_hbm, w2_hbm,
     mix_keep_ref, mix_send_ref, pre_keep_ref, pre_send_ref,
-    att_ref, sec_keep_ref, sec_send_ref, top_ref, bias_ref, first_ref, low_ref, gctx_ref, sums_ref,
-    gp, wqkv, wout, w1, w2, dmix, mix_keep, mix_send, keep, send, e, second, sems,
+    att_ref, sec_keep_ref, sec_send_ref, top_ref, bias_ref, first_ref, fst_keep_ref, fst_send_ref, gctx_ref, sums_ref,
+    gp, wqkv, wout, w1, w2, dmix, mix_keep, mix_send, keep, send, e, second, low_ref, sems,
 ):
     mine = coords_ref[0]
     below = layer - 1
@@ -467,7 +471,8 @@
     late[0].wait()
     grad = e[...] + both_halves(mine, keep, send, w1)
     norm_end(
-        mine, grad, n1_ref[...], s1_ref[:, :1], gains[1 + 2 * below : 2 + 2 * below], first_ref, low_ref, None, None, sums_ref
+        mine, grad, n1_ref[...], s1_ref[:, :1], gains[1 + 2 * below : 2 + 2 * below], first_ref, low_ref, fst_keep_ref,
+        fst_send_ref, sums_ref,
     )
     late[1].wait()
     gctx_ref[...] = dot(low_ref[...], wout[...], COLS).astype(LOW)
@@ -489,15 +494,16 @@
         functools.partial(between_kernel, layer),
         after,
         out_shape=(
-            mix, mix, pre, pre, s((2, width), F32), sec, sec, three, s((1, ff), F32), s((tokens, width), F32), low, low, three,
+            mix, mix, pre, pre, s((2, width), F32), sec, sec, three, s((1, ff), F32), s((tokens, width), F32), sec, sec, low, three,
         ),
         in_specs=[SM, SM] + [VM] * 9 + [HBM] * 5,
         operands=(coords, length, mixed, lse, gctx, first, n2, s2, n1, s1, gains, gp, w_qkv, w_out, w_ff1, w_ff2),
-        out_specs=(ANY,) * 4 + (VM,) * 9,
+        out_specs=(ANY,) * 4 + (VM,) * 10,
         scratch_shapes=[
             v((tokens, ff), LOW), v((width, 3 * width), LOW), v((width, width), LOW), v((width, ff), LOW), v((ff, width), LOW),
             v((tokens, 3 * width), LOW), v(mix.shape, LOW), v(mix.shape, LOW), v(pre.shape, LOW), v(pre.shape, LOW),
-            v((tokens, width), F32), v((tokens, width), LOW), pltpu.SemaphoreType.DMA((7 + 2 * (ff // 512),)),
+            v((tokens, width), F32), v((tokens, width), LOW), v((tokens, width), LOW),
+            pltpu.SemaphoreType.DMA((7 + 2 * (ff // 512),)),
         ],
         cost_estimate=CHEAP,
         vmem=58,
@@ -541,7 +547,7 @@
 
 
 def weights_kernel(plans, blocks, coords_ref, *refs):
-    count = 8 if len(plans) == 2 else 16
+    count = 8 if len(plans) == 2 else 20
     sources, refs = refs[:count], refs[count:]
     outs = []
     for plan in plans:
@@ -553,12 +559,12 @@
     loads = []
     targets = [sec, act, mid, pre]
     if rest:
-        x, mix, ctxt, fst, xt, mixed = rest
-        targets += [x, mix, ctxt, fst]
+        x, mix, ctxt, fst, below_ctxt, below_fst, xt, mixed = rest
+        targets += [x, mix, ctxt, fst, below_ctxt, below_fst]
     for n, target in enumerate(targets):
         for side in range(2):
             there = pl.ds(side * tokens, tokens)
-            view = target.at[:, there] if rest and n == 6 else target.at[there]
+            view = target.at[:, there] if n in (6, 8) else target.at[there]
             loads.append(pltpu.make_async_copy(sources[2 * n + side], view, sems.at[2 * n + side]))
             loads[-1].start()
 
@@ -572,40 +578,54 @@
     rows = two.shape[1]
     cols = act.shape[1] // blocks
 
+    group = 4 if blocks % 4 == 0 else 1
+
     def step_two(i, carry):
-        got = dot(sect[...], act[:, pl.ds(pl.multiple_of(i * cols, cols), cols)]).astype(LOW)
-        for y in range(2):
-            for n in range(4):
-                at = (4 * y + n) * rows
-                two[2 * i + y, :, n * cols : (n + 1) * cols] = got[at : at + rows]
+        there = pl.ds(pl.multiple_of(i * group * cols, cols), group * cols)
+        got = dot(sect[...], act[:, there]).astype(LOW)
+        for v in range(group):
+            for y in range(2):
+                for n in range(4):
+                    at = (4 * y + n) * rows
+                    piece = got[at : at + rows, v * cols : (v + 1) * cols]
+                    two[2 * (i * group + v) + y, :, n * cols : (n + 1) * cols] = piece
         return carry
 
-    lax.fori_loop(0, blocks, step_two, 0)
+    lax.fori_loop(0, blocks // group, step_two, 0)
     place(coords_ref, plans[0], two, *outs[0])
     ready(2)
     midt[...] = mid[...].T
     ready(3)
     chunk = 512
+    high = midt.shape[0] // one.shape[0]
 
     def step_one(i, carry):
         there = pl.ds(pl.multiple_of(i * chunk, chunk), chunk)
-        one[:, :, there] = dot(midt[...], pre[:, there]).astype(LOW).reshape(one.shape[:2] + (chunk,))
+        one[:, :high, there] = dot(midt[...], pre[:, there]).astype(LOW).reshape(one.shape[0], high, chunk)
         return carry
 
-    lax.fori_loop(0, pre.shape[1] // chunk, step_one, 0)
+    if rest:
+        lax.fori_loop(0, pre.shape[1] // chunk, step_one, 0)
+        ready(8)
+        ready(9)
+        part_cols, group_rows = below_fst.shape[1], one.shape[1] - high
+        got = dot(below_ctxt[...], below_fst[...]).astype(LOW).reshape(one.shape[0], high, part_cols)
+        for n in range(high // group_rows):
+            there = slice(n * part_cols, (n + 1) * part_cols)
+            one[:, high:, there] = got[:, n * group_rows : (n + 1) * group_rows]
+        one[:, high:, high // group_rows * part_cols :] = jnp.zeros((one.shape[0], group_rows, part_cols), LOW)
+    else:
+        one[...] = dot(midt[...], pre[...]).astype(LOW).reshape(one.shape)
     place(coords_ref, plans[1], one, *outs[1])
     if rest:
         ready(4)
         xt[...] = x[...].T
         ready(5)
-        width = fst.shape[1]
-        shape = mixed.shape[:2] + (width,)
-        for i in range(mix.shape[1] // width):
-            there = slice(i * width, (i + 1) * width)
-            mixed[:, :, there] = dot(xt[...], mix[:, there]).astype(LOW).reshape(shape)
+        wide = mix.shape[1]
+        mixed[:, :, :wide] = dot(xt[...], mix[...]).astype(LOW).reshape(mixed.shape[:2] + (wide,))
         ready(6)
         ready(7)
-        mixed[:, :, mix.shape[1] :] = dot(ctxt[...], fst[...]).astype(LOW).reshape(shape)
+        mixed[:, :, wide:] = dot(ctxt[...], fst[...]).astype(LOW).reshape(mixed.shape[:2] + (fst.shape[1],))
         place(coords_ref, plans[2], mixed, *outs[2])
 
 
@@ -615,14 +635,19 @@
     v = pltpu.VMEM
     count = 2 * blocks
     block = (count, width // count, 2 * width)
-    outs = sum(((s((count // parts_of(plan),) + block[1:], LOW),) * parts_of(plan) for plan in plans), ())
+    high = (count, width // count + 16, 2 * width) if attention else block
+    sizes = (block, high, block)
+    outs = sum(
+        ((s((count // parts_of(plan),) + size[1:], LOW),) * parts_of(plan) for plan, size in zip(plans, sizes)), ()
+    )
     pairs = (sec, act, mid, pre) + tuple(attention)
     both = lambda pair: v((2 * tokens, pair[0].shape[1]), LOW)
     scratch = [both(pair) for pair in (sec, act, mid, pre)]
-    scratch += [v((sec[0].shape[1], 2 * tokens), LOW), v((width, 2 * tokens), LOW), v(block, LOW), v(block, LOW)]
+    scratch += [v((sec[0].shape[1], 2 * tokens), LOW), v((width, 2 * tokens), LOW), v(block, LOW), v(high, LOW)]
     if attention:
-        x, mix, ctx, fst = attention
-        scratch += [both(x), both(mix), v((width, 2 * tokens), LOW), both(fst), v((width, 2 * tokens), LOW), v(block, LOW)]
+        x, mix, _, fst, _, below_fst = attention
+        across = v((width, 2 * tokens), LOW)
+        scratch += [both(x), both(mix), across, both(fst), across, both(below_fst), across, v(block, LOW)]
     got = run(
         functools.partial(weights_kernel, plans, blocks),
         after,
@@ -632,7 +657,7 @@
         out_specs=(VM,) * len(outs),
         scratch_shapes=scratch + [pltpu.SemaphoreType.DMA((2 * len(pairs),))],
         cost_estimate=CHEAP,
-        vmem=52 if attention else 34,
+        vmem=56 if attention else 34,
         name="weights",
     )
     parts = []
@@ -693,7 +718,7 @@
 
 
 def last_kernel(
-    plan, coords_ref, length_ref, mixed_ref, lse_ref, gctx_ref, first_ref, n_ref, s_ref, gains_ref, x_ref, ctxt_ref, low_ref,
+    plan, coords_ref, length_ref, mixed_ref, lse_ref, gctx_ref, first_ref, n_ref, s_ref, gains_ref, x_ref,
     slot_ref, type_ref, top0, top1, low0, low1, att1, bias0, bias1, wqkv_hbm,
     out_ref, *parts_and_scratch
 ):
@@ -718,20 +743,16 @@
 
     lax.fori_loop(0, slots // chunk, step, 0)
     xt[...] = x_ref[...].T
-    blocks = res.shape[0] // 2
-    piece = width // blocks
+    blocks, piece, _ = res.shape
+    blocks //= 2
     half = width // 2
     wide = 3 * half
     for core in range(2):
         there = slice(core * blocks, (core + 1) * blocks)
-        for i in range(3):
-            cols = slice(core * wide + i * half, core * wide + (i + 1) * half)
-            got = dot(xt[...], dmix[:, cols]).astype(LOW)
-            res[there, :piece, i * half : (i + 1) * half] = got.reshape(blocks, piece, half)
-        got = dot(ctxt_ref[...], low_ref[:, core * half : (core + 1) * half]).astype(LOW)
-        res[there, :piece, wide:] = got.reshape(blocks, piece, half)
+        got = dot(xt[...], dmix[:, core * wide : (core + 1) * wide]).astype(LOW)
+        res[there, :, :wide] = got.reshape(blocks, piece, wide)
     back = back_ref[...]
-    kind = type_ref[:, :1]
+    kind = as_column(type_ref[...].astype(F32))
     small[0:1] = jnp.sum(back * (1.0 - kind), axis=0, keepdims=True)
     small[1:2] = jnp.sum(back * kind, axis=0, keepdims=True)
     sources = [(emb, 0)]
@@ -749,27 +770,26 @@
             small[at : at + 1] = bias[:, i * width : (i + 1) * width]
             at += 1
     quarter = at // 4
-    group = tokens // blocks // 4
-    fill = res.shape[1] - piece
-    parts = back.reshape(blocks, 4, group, width)
+    group = tokens // blocks
+    positions = back.reshape(blocks, group, width).astype(LOW)
     for core in range(2):
-        pos = jnp.concatenate([parts[:, i, :, core * half : (core + 1) * half] for i in range(4)], axis=2)
+        there = slice(core * blocks, (core + 1) * blocks)
+        res[there, :group, wide:] = positions[:, :, core * half : (core + 1) * half]
         for y in range(2):
             mine = small[(2 * core + y) * quarter : (2 * core + y + 1) * quarter]
-            mine = jnp.concatenate([mine, jnp.zeros((fill - group - quarter, width), F32)], axis=0)
-            mine = jnp.concatenate([mine, jnp.zeros_like(mine)], axis=1)
+            rest = jnp.zeros((piece - group - 2 * quarter, half), F32)
+            mine = jnp.concatenate([mine[:, :half], mine[:, half:], rest], axis=0).astype(LOW)
             for v in range(blocks // 2):
-                block = 2 * v + y
-                res[core * blocks + block, piece:, :] = jnp.concatenate([pos[block], mine], axis=0).astype(LOW)
+                res[core * blocks + 2 * v + y, group:, wide:] = mine
     place(coords_ref, plan, res, *outs)
 
 
-def last(plan, coords, length, mixed, lse, gctx, first, n, sp, gains, x, ctxt, low, slot_of, types, sums, w_qkv, slots, blocks, parts=2, after=()):
+def last(plan, coords, length, mixed, lse, gctx, first, n, sp, gains, x, slot_of, types, sums, w_qkv, slots, blocks, parts=2, after=()):
     tokens, width = first.shape
     s = jax.ShapeDtypeStruct
     v = pltpu.VMEM
-    block = (blocks, width // blocks + 16, 2 * width)
-    operands = (coords, length, mixed, lse, gctx, first, n, sp, gains, x, ctxt, low, slot_of, types, *sums, w_qkv)
+    block = (blocks, width // blocks, 2 * width)
+    operands = (coords, length, mixed, lse, gctx, first, n, sp, gains, x, slot_of, types, *sums, w_qkv)
     return run(
         functools.partial(last_kernel, plan),
         after,
@@ -832,46 +852,50 @@
 
 
 def finish_kernel(coords_ref, *refs):
-    five, one = refs[:4], refs[4:8]
+    many, few = refs[:4], refs[4:8]
     qkv_ref, wout_ref, one_ref, two_ref, pos_ref, small_ref = refs[8:]
     mine_core, mine_y = coords_ref[0] == 0, coords_ref[4] == 0
     half = wout_ref.shape[2] // 2
     wide = 3 * half
     part = wout_ref.shape[1] // 2
 
-    def piece(four, n, core, y):
-        own, over_y, over_core, over_both = (ref[n] for ref in four)
+    def piece(four, rows, core, y):
+        own, over_y, over_core, over_both = (ref[0, rows] for ref in four)
         same_y = mine_y if y == 0 else jnp.logical_not(mine_y)
         same_core = mine_core if core == 0 else jnp.logical_not(mine_core)
         here = jnp.where(same_y, own, over_y)
         there = jnp.where(same_y, over_core, over_both)
         return jnp.where(same_core, here, there).astype(F32)
 
+    at = lambda n: slice(n * part, (n + 1) * part)
+    mix1, two0, one0, two1, one1 = at(0), at(1), at(2), slice(3 * part + 16, 4 * part + 16), slice(4 * part + 16, 5 * part + 16)
     for layer in range(NL):
         for core in range(2):
             columns = []
+            mine = slice(core * half, (core + 1) * half)
             for y in range(2):
                 rows = slice(y * part, (y + 1) * part)
-                mix = piece(one, 0, core, y) if layer == 0 else piece(five, MIX1, core, y)
-                qkv_ref[layer, rows, core * wide : (core + 1) * wide] = mix[:part, :wide]
-                wout_ref[layer, rows, core * half : (core + 1) * half] = mix[:part, wide:]
+                mix = piece(few, slice(0, part), core, y) if layer == 0 else piece(many, mix1, core, y)
+                qkv_ref[layer, rows, core * wide : (core + 1) * wide] = mix[:, :wide]
                 if layer == 0:
-                    for i in range(4):
-                        at = (4 * y + i) * 8
-                        pos_ref[at : at + 8, core * half : (core + 1) * half] = mix[part : part + 8, i * half : (i + 1) * half]
-                    at = (2 * core + y) * 7
-                    small_ref[at : at + 7] = mix[part + 8 : part + 15, : 2 * half]
-                first = piece(five, ONE0 if layer == 0 else ONE1, core, y)
-                one_ref[layer, rows, core * 4 * half : (core + 1) * 4 * half] = first
-                second = piece(five, TWO0 if layer == 0 else TWO1, core, y)
+                    group = pos_ref.shape[0] // 2
+                    pos_ref[y * group : (y + 1) * group, mine] = mix[:group, wide:]
+                    first = (2 * core + y) * 7
+                    small_ref[first : first + 7, :half] = mix[group : group + 7, wide:]
+                    small_ref[first : first + 7, half:] = mix[group + 7 : group + 14, wide:]
+                    out = piece(many, slice(3 * part, 3 * part + 16), core, y)
+                    for n in range(part // 16):
+                        there = slice(y * part + 16 * n, y * part + 16 * (n + 1))
+                        wout_ref[layer, there, mine] = out[:, n * half : (n + 1) * half]
+                else:
+                    wout_ref[layer, rows, mine] = mix[:, wide:]
+                one_ref[layer, rows, core * 4 * half : (core + 1) * 4 * half] = piece(many, one0 if layer == 0 else one1, core, y)
+                second = piece(many, two0 if layer == 0 else two1, core, y)
                 columns += [second[:, i * half : (i + 1) * half] for i in range(4)]
-            two_ref[layer, :, core * half : (core + 1) * half] = jnp.concatenate(columns, axis=0).T
-
-
-MIX1, TWO0, ONE0, TWO1, ONE1 = range(5)
-
-
-def finish(coords, five, one, width, ff, owners):
+            two_ref[layer, :, mine] = jnp.concatenate(columns, axis=0).T
+
+
+def finish(coords, many, few, width, ff, owners):
     s = jax.ShapeDtypeStruct
     rows = width // owners
     return run(
@@ -882,7 +906,7 @@
             s((64, width), F32), s((28, width), F32),
         ),
         in_specs=[SM] + [VM] * 8,
-        operands=(coords, *five, *one),
+        operands=(coords, *many, *few),
         out_specs=(VM,) * 6,
         cost_estimate=CHEAP,
         vmem=24,
@@ -929,7 +953,7 @@
 
     def coords(self):
         dp, vocab = lax.axis_index("dp"), lax.axis_index("vocab")
-        return jnp.stack([dp & 1, vocab & 1, (vocab >> 1) & 1, (vocab >> 2) & 1, (dp >> 1) & 1])
+        return jnp.stack([dp & 1, vocab & 1, (vocab >> 1) & 1, (vocab >> 2) & 1, (dp >> 1) & 1, vocab])
 
     def halves(self, matrix):
         mine = lax.axis_index("dp") & 1
@@ -981,14 +1005,12 @@
     tokens = token_ids.shape[1]
     slot_count = 2 * tokens // owners
     slots = owners * slot_count
-    flat_ids = token_ids.reshape(tokens)
-    me = lax.axis_index("vocab")
     coords = cube.coords()
 
     all_ids = lax.all_to_all(
-        jnp.broadcast_to(flat_ids[None, :], (owners, tokens)), "vocab", split_axis=0, concat_axis=0, tiled=True
-    )
-    local = all_ids - me * local_rows
+        jnp.broadcast_to(token_ids, (owners, tokens)), "vocab", split_axis=0, concat_axis=0, tiled=True
+    )
+    local = all_ids - lax.axis_index("vocab") * local_rows
     here = (local >= 0) & (local < local_rows)
     rank = jnp.cumsum(here.astype(jnp.int32), axis=1) - 1
     slot_hit = (
@@ -996,18 +1018,14 @@
     )
     asked = jnp.sum(jnp.where(slot_hit, local[:, None, :] + 1, 0), axis=2).reshape(slots) - 1
     row_hit = (asked[:, None] == jnp.arange(local_rows, dtype=jnp.int32)[None, :]).astype(LOW)
-    found_rows = dot(row_hit, word_table).astype(LOW)
-    replies = lax.all_to_all(
-        found_rows.reshape(owners, slot_count, width), "vocab", split_axis=0, concat_axis=0, tiled=True
-    ).reshape(slots, width)
-    owner_of = flat_ids // local_rows
-    chosen = (owner_of[:, None] == jnp.arange(owners, dtype=jnp.int32)[None, :]).astype(jnp.int32)
-    before = jnp.cumsum(chosen, axis=0) - chosen
-    slot_of = owner_of * slot_count + jnp.sum(before * chosen, axis=1)
-    kind = type_ids.reshape(tokens).astype(F32)
-    column = lambda row: jnp.broadcast_to(row[:, None], (tokens, 128))
+    replies = exchange_rows(dot(row_hit, word_table).astype(LOW), owners)
+    number = jnp.arange(owners, dtype=jnp.int32)[:, None]
+    chosen = (token_ids >= number * local_rows) & (token_ids < (number + 1) * local_rows)
+    own_rank = jnp.cumsum(chosen.astype(jnp.int32), axis=1) - 1
+    slot_row = jnp.sum(jnp.where(chosen, number * slot_count + own_rank, 0), axis=0, keepdims=True)
+    asked = asked[None, :]
     (n0, s0, hidden), top, layers = forward(
-        coords, lengths, replies, column(slot_of), column(kind), pos_table, type_table, gains, shifts, b_ff1.astype(F32),
+        coords, lengths, replies, slot_row, type_ids, pos_table, type_table, gains, shifts, b_ff1.astype(F32),
         cotangent.reshape(tokens, width), w_qkv, w_out, w_ff1, w_ff2,
     )
     norms, saved = [(n0, s0)], []
@@ -1019,7 +1037,7 @@
     gradients = gradients_small if cube.small else gradients_any
     outs = gradients(
         cube, coords, lengths, top, saved, gains, w_qkv, w_out, w_ff1, w_ff2,
-        norms, (kind, row_hit, slot_of, asked),
+        norms, (type_ids, slot_row, asked, local_rows),
     )
     return (hidden_out,) + outs
 
@@ -1032,9 +1050,10 @@
 
 
 def unpack(pack):
-    cores, blocks, _, cols = pack.shape
-    pos = pack[:, :, :8].reshape(cores, blocks, 8, 4, cols // 4).transpose(1, 3, 2, 0, 4)
-    return pos.reshape(blocks * 32, cols // 2), pack[:, :2, 8:15, : cols // 2].reshape(28, cols // 2)
+    cores, blocks, _, half = pack.shape
+    pos = pack[:, :, :32].transpose(1, 2, 0, 3).reshape(blocks * 32, 2 * half)
+    small = pack[:, :2, 32:46].reshape(cores, 2, 2, 7, half).transpose(0, 1, 3, 2, 4)
+    return pos, small.reshape(28, 2 * half)
 
 
 def small_outs(cube, rows):
@@ -1054,7 +1073,7 @@
     tokens = top[0].shape[0]
     blocks = 8
     half = width // 2
-    kind, row_hit, slot_of, asked = embed
+    kinds, slot_row, asked, local_rows = embed
     mixed1, lse1, n1_1, s1_1, gp1, x1, ctx1, mid1, act1 = saved[1]
     mixed0, lse0, n1_0, s1_0, gp0, x0, ctx0, mid0, act0 = saved[0]
     e, low, sec_keep, sec_send, top1 = top
@@ -1065,30 +1084,30 @@
     two1, one1 = weights(blocks, (None, None), coords, pair(sec_keep, sec_send), act1, mid1, pair(pre_keep, pre_send))
     fst1 = pair(fst_keep, fst_send)
     (
-        mix_keep, mix_send, pre_keep, pre_send, att1, sec_keep, sec_send, top0, bias0, first, low, gctx, sums0
+        mix_keep, mix_send, pre_keep, pre_send, att1, sec_keep, sec_send, top0, bias0, first, fst_keep, fst_send, gctx, sums0
     ) = between(
         1, coords, lengths, mixed1, lse1, gctx, first, *norms[1], n1_0, s1_0, gains, gp0, w_qkv, w_out, w_ff1, w_ff2
     )
     two0, one0, mix1 = weights(
         blocks, (None, None, None), coords, pair(sec_keep, sec_send), act0, mid0, pair(pre_keep, pre_send),
-        (x1, pair(mix_keep, mix_send), ctx1, fst1),
-    )
-    column = jnp.broadcast_to(kind[:, None], (tokens, 128))
+        (x1, pair(mix_keep, mix_send), ctx1, fst1, ctx0, pair(fst_keep, fst_send)),
+    )
     outgoing, first_core, second_core = last(
-        None, coords, lengths, mixed0, lse0, gctx, first, *norms[0], gains, x0[0], ctx0[0], low, slot_of[None, :], column,
-        (top0, top1, sums0, sums1, att1, bias0, bias1), w_qkv, row_hit.shape[0], 2 * blocks,
+        None, coords, lengths, mixed0, lse0, gctx, first, *norms[0], gains, x0[0], slot_row, kinds,
+        (top0, top1, sums0, sums1, att1, bias0, bias1), w_qkv, asked.shape[1], 2 * blocks,
     )
     mine = cube.core_is_first()
 
     def over_cores(first, second):
         return add(jnp.where(mine, first, second), cube.core(jnp.where(mine, second, first)))
 
-    table_part = dot(row_hit, exchange_rows(outgoing, owners), ROWS).astype(LOW)
-    table_part = over_cores(table_part[:, :half], table_part[:, half:])
+    table_keep, table_send = table_back(coords, asked, exchange_rows(outgoing, owners), local_rows)
+    table_part = add(table_keep, cube.core(table_send))
     for bit in range(1, cube.dp_bits):
         table_part = add(table_part, cube.permute(table_part, 1 << bit, 0))
-    part = width // blocks // 2
-    packs = over_cores(first_core[:, part:], second_core[:, part:])
+    wide = 3 * half
+    sums_last = over_cores(first_core, second_core)
+    packs = sums_last[..., wide:]
     other = cube.core(packs)
     pos, small = unpack(jnp.stack([jnp.where(mine, packs, other), jnp.where(mine, other, packs)]))
     pos_out = cube.reduce(pos).astype(F32)
@@ -1098,13 +1117,18 @@
         small = add(small, cube.permute(small, 1 << bit, 0))
     types, gains_out, shifts_out, biases = small_outs(cube, small.astype(F32))
     whole = lambda parts: jnp.concatenate(parts, axis=0)
-    one = lambda parts: cube.reduce(whole(parts).reshape(width, -1))
+    part = width // blocks // 2
+    one = lambda parts: cube.reduce(whole(parts)[:, :part].reshape(width, -1))
     two = lambda parts: cube.reduce(
         whole(parts).reshape(blocks, 2, width // 16, 4, -1).transpose(0, 4, 1, 3, 2).reshape(-1, half)
     )
-    mix0 = over_cores(first_core[:, :part], second_core[:, :part]).reshape(width, -1)
-    mixes = jnp.stack([cube.reduce(mix0), one(mix1)])
-    wide = 3 * half
+    out0 = whole(one0)[:, part:].reshape(2 * blocks, 16, 4, half)[:, :, : part // 16].transpose(0, 2, 1, 3)
+    mixes = jnp.stack(
+        [
+            cube.reduce(jnp.concatenate([sums_last[..., :wide].reshape(width, -1), out0.reshape(width, -1)], axis=1)),
+            one(mix1),
+        ]
+    )
     return (
         cube.join_core(table_part, -1), pos_out, types, gains_out, shifts_out,
         cube.join_core(mixes[..., :wide], 2), cube.join_core(mixes[..., wide:], 2), biases,
@@ -1158,8 +1182,7 @@
     plan_two1, plan_one1 = (("x", "y"), ("a",), ("b",)), (("a",), ("x", "y"), ("b",))
     plan_mix1 = single("ayxb")
     plan_two0, plan_one0, plan_mix0 = single("xayb"), single("yxab"), (("core",), ("y",), ("x", "a"), ("b",))
-    kind, row_hit, slot_of, asked = embed
-    local_rows = row_hit.shape[1]
+    kinds, slot_row, asked, local_rows = embed
     mixed1, lse1, n1_1, s1_1, gp1, x1, ctx1, mid1, act1 = saved[1]
     mixed0, lse0, n1_0, s1_0, gp0, x0, ctx0, mid0, act0 = saved[0]
     pair = lambda keep, send: (keep, cube.core(send))
@@ -1175,7 +1198,7 @@
     two1.start()
     one1.start()
     (
-        mix_keep, mix_send, pre_keep, pre_send, att1, sec_keep, sec_send, top0, bias0, first, low, gctx, sums0
+        mix_keep, mix_send, pre_keep, pre_send, att1, sec_keep, sec_send, top0, bias0, first, fst_keep, fst_send, gctx, sums0
     ) = between(
         1, coords, lengths, mixed1, lse1, gctx, first, *norms[1], n1_0, s1_0, gains, gp0, w_qkv, w_out, w_ff1, w_ff2,
         after=got[0][:1],
@@ -1185,17 +1208,16 @@
     one1.start()
     got = weights(
         blocks, (plan_two0, plan_one0, plan_mix1), coords, pair(sec_keep, sec_send), act0, mid0, pair(pre_keep, pre_send),
-        (x1, pair(mix_keep, mix_send), ctx1, fst1), after=(mark,),
+        (x1, pair(mix_keep, mix_send), ctx1, fst1, ctx0, pair(fst_keep, fst_send)), after=(mark,),
     )
     two0, one0, mix1 = [Bucket(cube, plan, parts) for plan, parts in zip((plan_two0, plan_one0, plan_mix1), got)]
     for bucket in (mix1, two0, one0):
         bucket.start()
-    mark = step([joined((two1, one1), 0)], after=got[0][:1], cost=LONG)
+    mark = step([joined((two1, one1), 1)], after=got[0][:1], cost=LONG)
     two1.start()
-    types = jnp.broadcast_to(kind[:, None], (tokens, 128))
     outgoing, *got = last(
-        plan_mix0, coords, lengths, mixed0, lse0, gctx, first, *norms[0], gains, x0[0], ctx0[0], low, slot_of[None, :], types,
-        (top0, top1, sums0, sums1, att1, bias0, bias1), w_qkv, row_hit.shape[0], 2 * owners, after=(mark,),
+        plan_mix0, coords, lengths, mixed0, lse0, gctx, first, *norms[0], gains, x0[0], slot_row, kinds,
+        (top0, top1, sums0, sums1, att1, bias0, bias1), w_qkv, asked.shape[1], 2 * owners, after=(mark,),
     )
     incoming = exchange_rows(outgoing, owners)
     mix0 = Bucket(cube, plan_mix0, got)
@@ -1209,10 +1231,10 @@
     for bucket in (mix1, two0, one0):
         bucket.start()
     folded = (local_rows // 48, 48, half)
-    got = table_back(coords, asked[None, :], incoming, local_rows, after=(mark,))
+    got = table_back(coords, asked, incoming, local_rows, after=(mark,))
     table = Bucket(cube, single(("core", "y")), [part.reshape(folded) for part in got])
     table.start()
-    mark = step([mix0, joined((mix1, two0, one0), 0)], after=got[:1], cost=LONG)
+    mark = step([mix0, joined((mix1, two0, one0), 1)], after=got[:1], cost=LONG)
     mix0.start()
     mix1.start()
     mark = step([table], after=(mark,))
@@ -1220,7 +1242,7 @@
     mark = step([mix0], after=(mark,), cost=LONG)
     mix0.start()
     two1.keep()
-    mark = step([joined((mix1, two1), 0), table], after=(mark,))
+    mark = step([joined((mix1, two1), 1), table], after=(mark,))
     later = Bucket(cube, (), (cube.along(mix1.parts[0], ("y",)),))
     later.keep()
     mark = step([mix0], after=(mark,))

time: 380 us -> 372 us (0.979)
  the two profiles are of different devices: /device:TPU:0 before, /device:TPU:9 now
where the time goes in v5:
time: 372 us; the launch traced here: 366 us
  Pallas kernels  168 us (45%)
  waiting for transfers between devices  97.3 us (26%)
  starting transfers between devices  63.8 us (17%)
  local copies, waits for them, and re-layouts  24.5 us (7%)
  other arithmetic  7.14 us (2%)
    pallas_call x20, Pallas kernels, run(): pl.pallas_call(body, out_shape=out_shape, in_specs=list(in_specs) + [ANY]...  168 us
    ppermute x48, waiting for transfers between devices, permute(): return lax.ppermute(value, AXES, pairs)  54.8 us
    ppermute x48, starting transfers between devices, permute(): return lax.ppermute(value, AXES, pairs)  49.3 us
    all_to_all x2, waiting for transfers between devices, exchange_rows(): lax.all_to_all(outgoing.reshape(owners, -1, shape[1]), 'vocab', split_axi...  38.4 us
    unnamed x128, local copies, waits for them, and re-layouts  19.5 us
    all_to_all x2, starting transfers between devices, exchange_rows(): lax.all_to_all(outgoing.reshape(owners, -1, shape[1]), 'vocab', split_axi...  8.76 us
  transfers between devices with their start and end apart: 51, of which 16 were waited for; matrix products, arithmetic and copies ran while one was open for 2% of the time, Pallas kernels for 31%

profile of v5, /device:TPU:9, one launch (start us, length us, event | category | flops | bytes accessed | tf_op | source)
XLA Modules:
  0.0 365.9 jit_solution(17465744432572848726)
XLA Ops:
  2.1 5.7 %all-to-all-start = ((s32[8,1,512]{2,1,0:T(1,128)}), s32[8,1,512]{2,1,0:T(1,128)S(1)}, u32[]{:S(2)}, u32[]{:S(2)}) async-start(s32[8,1,512]{2,1,0:T(1,128)} %broadcast_in_dim.36), calls=%async_computation | async-start | bytes 32768 | tf_op jit(solution)/shard_map/all_to_all | solution.py:1010
  7.8 4.2 %all-to-all-done = s32[8,1,512]{2,1,0:T(1,128)S(1)} async-done(((s32[8,1,512]{2,1,0:T(1,128)}), s32[8,1,512]{2,1,0:T(1,128)S(1)}, u32[]{:S(2)}, u32[]{:S(2)}) %all-to-all-start) | async-done | bytes 16416 | tf_op jit(solution)/shard_map/all_to_all | solution.py:1010
  16.9 4.9 %all-to-all-start.1 = ((bf16[8,128,768]{2,1,0:T(8,128)(2,1)}), bf16[8,128,768]{2,1,0:T(8,128)(2,1)S(1)}, u32[]{:S(2)}, u32[]{:S(2)}) async-start(bf16[8,128,768]{2,1,0:T(8,128)(2,1)} %bitcast.43), calls=%async_computation.1 | async-start | bytes 3145728 | tf_op jit(solution)/shard_map/all_to_all | solution.py:1047
  25.7 29.8 %all-to-all-done.1 = bf16[8,128,768]{2,1,0:T(8,128)(2,1)S(1)} async-done(((bf16[8,128,768]{2,1,0:T(8,128)(2,1)}), bf16[8,128,768]{2,1,0:T(8,128)(2,1)S(1)}, u32[]{:S(2)}, u32[]{:S(2)}) %all-to-all-start.1) | async-done | bytes 1572896 | tf_op jit(solution)/shard_map/all_to_all | solution.py:1047
  56.7 50.1 %forward.1 = (f32[512,768]{1,0:T(8,128)}, f32[512,128]{1,0:T(8,128)}, bf16[512,768]{1,0:T(8,128)(2,1)}, f32[512,768]{1,0:T(8,128)}, bf16[512,768]{1,0:T(8,128)(2...) custom-call(s32[6]{0:T(128)} %stack.27.refs_0_, ...), custom_call_target="tpu_custom_call" | custom-call | flops 1 | bytes 1 | tf_op jit(solution)/shard_map/forward/pallas_call | solution.py:31
  108.8 15.7 %feed.1 = (bf16[512,1536]{1,0:T(8,128)(2,1)}, bf16[512,1536]{1,0:T(8,128)(2,1)}, f32[1,3072]{1,0:T(1,128)S(1)}, f32[512,768]{1,0:T(8,128)}, bf16[512,768]{1,0:T(...) custom-call(s32[6]{0:T(128)S(1)} %copy-done.21, ...), custom_call_target="tpu_custom_call" | custom-call | flops 1 | bytes 1 | tf_op jit(solution)/shard_map/feed/pallas_call | solution.py:31
  125.6 4.1 %collective-permute-done.refs_2_ = bf16[512,384]{1,0:T(8,128)(2,1)S(1)} collective-permute-done((bf16[512,384]{1,0:T(8,128)(2,1)S(1)}, bf16[512,384]{1,0:T(8,128)(2,1)S(1)}, u32[]{:S(2)}, u32[]{:S(2)}) %collective-permute-start) | collective-permute-done | bytes 393248 | tf_op jit(solution)/shard_map/ppermute | solution.py:941
  131.8 9.4 %weights.2 = (bf16[4,48,1536]{2,1,0:T(8,128)(2,1)S(1)}, bf16[4,48,1536]{2,1,0:T(8,128)(2,1)}, bf16[4,48,1536]{2,1,0:T(8,128)(2,1)}, bf16[4,48,1536]{2,1,0:T(8,12...) custom-call(s32[6]{0:T(128)S(1)} %copy-done.21, bf16[512,384]{1,0:T(8,128)(2,1)S(1)} %copy-done.13, ...), custom_call_target="tpu_custom_call" | custom-call | flops 1 | bytes 1 | tf_op jit(solution)/shard_map/weights/pallas_call | solution.py:31
  142.0 3.5 collective-permute-start.7
  149.3 30.2 %between.1 = (bf16[512,1152]{1,0:T(8,128)(2,1)}, bf16[512,1152]{1,0:T(8,128)(2,1)}, bf16[512,1536]{1,0:T(8,128)(2,1)}, bf16[512,1536]{1,0:T(8,128)(2,1)}, f32[2,...) custom-call(s32[6]{0:T(128)} %stack.27.refs_0_, ...), custom_call_target="tpu_custom_call" | custom-call | flops 1 | bytes 1 | tf_op jit(solution)/shard_map/between/pallas_call | solution.py:31
  186.5 3.6 collective-permute-done.12.refs_2_
  194.5 18.2 %weights.3 = (bf16[8,48,1536]{2,1,0:T(8,128)(2,1)}, bf16[8,48,1536]{2,1,0:T(8,128)(2,1)}, bf16[8,64,1536]{2,1,0:T(8,128)(2,1)}, bf16[8,64,1536]{2,1,0:T(8,128)(2...) custom-call(s32[6]{0:T(128)} %stack.27.refs_0_, bf16[512,384]{1,0:T(8,128)(2,1)} %get-tuple-element.164.refs_1_, ...), custom_call_target="tpu_custom_call" | custom-call | flops 1 | bytes 1 | tf_op jit(solution)/shard_map/weights/pallas_call | solution.py:31
  219.5 23.5 %last.1 = (bf16[1024,768]{1,0:T(8,128)(2,1)}, bf16[16,48,1536]{2,1,0:T(8,128)(2,1)}, bf16[16,48,1536]{2,1,0:T(8,128)(2,1)}) custom-call(s32[6]{0:T(128)S(1)} %copy-done.22, s32[1]{0:T(128)S(6)} %copy.33.refs_1_, bf16[512,2304]{1,0:T(8,128)(2,1)} %get-tuple-element.118.refs_2_, f32[12,512]{1,0:T(8,128)S(1)} %copy-done.25, bf16[512,768]{1,0:T(8,128)(2,1)S(1)} %copy-done.9, ...), custom_call_target="tpu_custom_call" | custom-call | flops 1 | bytes 1 | tf_op jit(solution)/shard_map/last/pallas_call | solution.py:31
  257.1 3.9 %all-to-all-start.2 = ((bf16[8,128,768]{2,1,0:T(8,128)(2,1)}), bf16[8,128,768]{2,1,0:T(8,128)(2,1)S(1)}, u32[]{:S(2)}, u32[]{:S(2)}) async-start(bf16[8,128,768]{2,1,0:T(8,128)(2,1)} %bitcast.42), calls=%async_computation.2 | async-start | bytes 3145728 | tf_op jit(solution)/shard_map/all_to_all | solution.py:1047
  262.6 3.2 combine.15
  268.7 7.6 %collective-permute-done.30.refs_5_ = bf16[4,64,1536]{2,1,0:T(8,128)(2,1)} collective-permute-done((bf16[4,64,1536]{2,1,0:T(8,128)(2,1)}, bf16[4,64,1536]{2,1,0:T(8,128)(2,1)}, u32[]{:S(2)}, u32[]{:S(2)}) %collective-permute-start.30) | collective-permute-done | bytes 786464 | tf_op jit(solution)/shard_map/ppermute | solution.py:941
  284.8 8.6 %all-to-all-done.2 = bf16[8,128,768]{2,1,0:T(8,128)(2,1)S(1)} async-done(((bf16[8,128,768]{2,1,0:T(8,128)(2,1)}), bf16[8,128,768]{2,1,0:T(8,128)(2,1)S(1)}, u32[]{:S(2)}, u32[]{:S(2)}) %all-to-all-start.2) | async-done | bytes 1572896 | tf_op jit(solution)/shard_map/all_to_all | solution.py:1047
  296.5 6.4 %collective-permute-start.35 = (bf16[20,48,384]{2,1,0:T(8,128)(2,1)S(1)}, bf16[20,48,384]{2,1,0:T(8,128)(2,1)S(1)}, u32[]{:S(2)}, u32[]{:S(2)}) collective-permute-start(bf16[20,48,384]{2,1,0:T(8,128)(2,1)S(1)} %bitcast.40), channel_id=1, source_target_pairs={{0,8},{1,9},{2,10},{3,11},{4,12},{5,13},{6,14},{7,15},{8,0},{9,1},... | collective-permute-start | bytes 2211848 | tf_op jit(solution)/shard_map/ppermute | solution.py:941
  310.5 9.3 %collective-permute-done.37.refs_1_ = bf16[2,48,1536]{2,1,0:T(8,128)(2,1)S(1)} collective-permute-done((bf16[2,48,1536]{2,1,0:T(8,128)(2,1)S(1)}, bf16[2,48,1536]{2,1,0:T(8,128)(2,1)S(1)}, u32[]{:S(2)}, u32[]{:S(2)}) %collective-permute-start.37) | collective-permute-done | bytes 294944 | tf_op jit(solution)/shard_map/ppermute | solution.py:941
  319.8 7.8 %collective-permute-done.39.refs_3_ = bf16[2,48,1536]{2,1,0:T(8,128)(2,1)S(1)} collective-permute-done((bf16[2,48,1536]{2,1,0:T(8,128)(2,1)S(1)}, bf16[2,48,1536]{2,1,0:T(8,128)(2,1)S(1)}, u32[]{:S(2)}, u32[]{:S(2)}) %collective-permute-start.39) | collective-permute-done | bytes 294944 | tf_op jit(solution)/shard_map/ppermute | solution.py:941
  327.7 3.3 collective-permute-done.34.refs_1_
  337.5 6.5 %collective-permute-done.42.refs_1_ = bf16[1,48,1536]{2,1,0:T(8,128)(2,1)S(1)} collective-permute-done((bf16[1,48,1536]{2,1,0:T(8,128)(2,1)S(1)}, bf16[1,48,1536]{2,1,0:T(8,128)(2,1)S(1)}, u32[]{:S(2)}, u32[]{:S(2)}) %collective-permute-start.42) | collective-permute-done | bytes 147488 | tf_op jit(solution)/shard_map/ppermute | solution.py:941
  345.1 6.7 %collective-permute-done.43.refs_0_ = bf16[1,48,1536]{2,1,0:T(8,128)(2,1)S(1)} collective-permute-done((bf16[1,48,1536]{2,1,0:T(8,128)(2,1)S(1)}, bf16[1,48,1536]{2,1,0:T(8,128)(2,1)S(1)}, u32[]{:S(2)}, u32[]{:S(2)}) %collective-permute-start.43) | collective-permute-done | bytes 147488 | tf_op jit(solution)/shard_map/ppermute | solution.py:941
  358.3 4.8 %finish.1 = (f32[2,96,2304]{2,1,0:T(8,128)}, f32[2,96,768]{2,1,0:T(8,128)}, f32[2,96,3072]{2,1,0:T(8,128)}, f32[2,384,768]{2,1,0:T(8,128)}, f32[64,768]{1,0:T(8,128)}, /*index=5*/f32[28,768]{1,0:T(8,128)S(1)}) custom-call(s32[6]{0:T(128)S(1)} %copy-done.24, bf16[1,256,1536]{2,1,0:T(8,128)(2,1)S(1)} %get-tuple-element.215.refs_2_.refs_1_, ...), custom_call_target="tpu_custom_call" | custom-call | flops 1 | bytes 1 | tf_op jit(solution)/shard_map/finish/pallas_call | solution.py:31
  (255 shorter events, 92.9 us)
Async XLA Ops:
  16.9 38.6 %all-to-all-start.1 = ((bf16[8,128,768]{2,1,0:T(8,128)(2,1)}), bf16[8,128,768]{2,1,0:T(8,128)(2,1)S(1)}, u32[]{:S(2)}, u32[]{:S(2)}) async-start(bf16[8,128,768]{2,1,0:T(8,128)(2,1)} %bitcast.43), calls=%async_computation.1 | async-start | bytes 3145728 | tf_op jit(solution)/shard_map/all_to_all | solution.py:1047
  106.8 23.6 %collective-permute-start.1 = (bf16[512,3072]{1,0:T(8,128)(2,1)}, bf16[512,3072]{1,0:T(8,128)(2,1)S(1)}, u32[]{:S(2)}, u32[]{:S(2)}) collective-permute-start(bf16[512,3072]{1,0:T(8,128)(2,1)} %get-tuple-element.136.refs_3_), channel_id=1, source_target_pairs={{0,8},{1,9},{2,10},{3,11},{4,12},{5,13},{6,14},{7,15},{8,0},{9,1},... | collective-permute-start | bytes 9437192 | tf_op jit(solution)/shard_map/ppermute | solution.py:941
  125.2 20.9 %collective-permute-start.14 = (bf16[512,768]{1,0:T(8,128)(2,1)S(1)}, bf16[512,768]{1,0:T(8,128)(2,1)S(1)}, u32[]{:S(2)}, u32[]{:S(2)}) collective-permute-start(bf16[512,768]{1,0:T(8,128)(2,1)S(1)} %copy-done.53), channel_id=1, source_target_pairs={{0,8},{1,9},{2,10},{3,11},{4,12},{5,13},{6,14},{7,15},{8,0},{9,1},... | collective-permute-start | bytes 2359304 | tf_op jit(solution)/shard_map/ppermute | solution.py:941
  142.0 38.8 %collective-permute-start.7 = (bf16[8,48,1536]{2,1,0:T(8,128)(2,1)S(1)}, bf16[8,48,1536]{2,1,0:T(8,128)(2,1)S(1)}, u32[]{:S(2)}, u32[]{:S(2)}) collective-permute-start(bf16[8,48,1536]{2,1,0:T(8,128)(2,1)S(1)} %get-tuple-element.157), channel_id=1, source_target_pairs={{0,2},{1,3},{2,0},{3,1},{4,6},{5,7},{6,4},{7,5},{8,10},{9,11},{10,... | collective-permute-start | bytes 3538952 | tf_op jit(solution)/shard_map/ppermute | solution.py:941
  145.5 34.0 %collective-permute-start.20 = (bf16[768,512]{1,0:T(8,128)(2,1)}, bf16[768,512]{1,0:T(8,128)(2,1)}, u32[]{:S(2)}, u32[]{:S(2)}) collective-permute-start(bf16[768,512]{1,0:T(8,128)(2,1)} %get-tuple-element.176.refs_17_), channel_id=1, source_target_pairs={{0,8},{1,9},{2,10},{3,11},{4,12},{5,13},{6,14},{7,15},{8,0},{9,1},... | collective-permute-start | bytes 2359304 | tf_op jit(solution)/shard_map/ppermute | solution.py:941
  146.1 34.0 %collective-permute-start.4 = (bf16[4,48,1536]{2,1,0:T(8,128)(2,1)}, bf16[4,48,1536]{2,1,0:T(8,128)(2,1)S(1)}, u32[]{:S(2)}, u32[]{:S(2)}) collective-permute-start(bf16[4,48,1536]{2,1,0:T(8,128)(2,1)} %get-tuple-element.153), channel_id=1, source_target_pairs={{0,16},{1,17},{2,18},{3,19},{4,20},{5,21},{6,22},{7,23},{8,24},{9,... | collective-permute-start | bytes 1769480 | tf_op jit(solution)/shard_map/ppermute | solution.py:941
  147.4 32.9 %collective-permute-start.5 = (bf16[4,48,1536]{2,1,0:T(8,128)(2,1)}, bf16[4,48,1536]{2,1,0:T(8,128)(2,1)S(1)}, u32[]{:S(2)}, u32[]{:S(2)}) collective-permute-start(bf16[4,48,1536]{2,1,0:T(8,128)(2,1)} %get-tuple-element.154), channel_id=1, source_target_pairs={{0,1},{1,0},{2,3},{3,2},{4,5},{5,4},{6,7},{7,6},{8,9},{9,8},{10,11... | collective-permute-start | bytes 1769480 | tf_op jit(solution)/shard_map/ppermute | solution.py:941
  148.4 32.3 %collective-permute-start.6 = (bf16[4,48,1536]{2,1,0:T(8,128)(2,1)}, bf16[4,48,1536]{2,1,0:T(8,128)(2,1)}, u32[]{:S(2)}, u32[]{:S(2)}) collective-permute-start(bf16[4,48,1536]{2,1,0:T(8,128)(2,1)} %get-tuple-element.155), channel_id=1, source_target_pairs={{0,17},{1,16},{2,19},{3,18},{4,21},{5,20},{6,23},{7,22},{8,25},{9,... | collective-permute-start | bytes 1769480 | tf_op jit(solution)/shard_map/ppermute | solution.py:941
  185.7 28.4 %collective-permute-start.10 = (bf16[2,48,1536]{2,1,0:T(8,128)(2,1)S(1)}, bf16[2,48,1536]{2,1,0:T(8,128)(2,1)S(1)}, u32[]{:S(2)}, u32[]{:S(2)}) collective-permute-start(bf16[2,48,1536]{2,1,0:T(8,128)(2,1)S(1)} %get-tuple-element.162), channel_id=1, source_target_pairs={{0,1},{1,0},{2,3},{3,2},{4,5},{5,4},{6,7},{7,6},{8,9},{9,8},{10,11... | collective-permute-start | bytes 884744 | tf_op jit(solution)/shard_map/ppermute | solution.py:941
  190.2 25.3 %collective-permute-start.11 = (bf16[2,48,1536]{2,1,0:T(8,128)(2,1)S(1)}, bf16[2,48,1536]{2,1,0:T(8,128)(2,1)S(1)}, u32[]{:S(2)}, u32[]{:S(2)}) collective-permute-start(bf16[2,48,1536]{2,1,0:T(8,128)(2,1)S(1)} %get-tuple-element.163), channel_id=1, source_target_pairs={{0,17},{1,16},{2,19},{3,18},{4,21},{5,20},{6,23},{7,22},{8,25},{9,... | collective-permute-start | bytes 884744 | tf_op jit(solution)/shard_map/ppermute | solution.py:941
  192.0 24.0 %collective-permute-start.8 = (bf16[2,48,1536]{2,1,0:T(8,128)(2,1)}, bf16[2,48,1536]{2,1,0:T(8,128)(2,1)S(1)}, u32[]{:S(2)}, u32[]{:S(2)}) collective-permute-start(bf16[2,48,1536]{2,1,0:T(8,128)(2,1)} %get-tuple-element.159), channel_id=1, source_target_pairs={{0,2},{1,3},{2,0},{3,1},{4,6},{5,7},{6,4},{7,5},{8,10},{9,11},{10,... | collective-permute-start | bytes 884744 | tf_op jit(solution)/shard_map/ppermute | solution.py:941
  193.1 22.8 %collective-permute-start.9 = (bf16[2,48,1536]{2,1,0:T(8,128)(2,1)S(1)}, bf16[2,48,1536]{2,1,0:T(8,128)(2,1)S(1)}, u32[]{:S(2)}, u32[]{:S(2)}) collective-permute-start(bf16[2,48,1536]{2,1,0:T(8,128)(2,1)S(1)} %get-tuple-element.161), channel_id=1, source_target_pairs={{0,16},{1,17},{2,18},{3,19},{4,20},{5,21},{6,22},{7,23},{8,24},{9,... | collective-permute-start | bytes 884744 | tf_op jit(solution)/shard_map/ppermute | solution.py:941
  212.7 35.2 %collective-permute-start.26 = (bf16[8,64,1536]{2,1,0:T(8,128)(2,1)}, bf16[8,64,1536]{2,1,0:T(8,128)(2,1)S(1)}, u32[]{:S(2)}, u32[]{:S(2)}) collective-permute-start(bf16[8,64,1536]{2,1,0:T(8,128)(2,1)} %get-tuple-element.188), channel_id=1, source_target_pairs={{0,16},{1,17},{2,18},{3,19},{4,20},{5,21},{6,22},{7,23},{8,24},{9,... | collective-permute-start | bytes 4718600 | tf_op jit(solution)/shard_map/ppermute | solution.py:941
  214.1 32.7 %collective-permute-start.24 = (bf16[8,48,1536]{2,1,0:T(8,128)(2,1)}, bf16[8,48,1536]{2,1,0:T(8,128)(2,1)S(1)}, u32[]{:S(2)}, u32[]{:S(2)}) collective-permute-start(bf16[8,48,1536]{2,1,0:T(8,128)(2,1)} %get-tuple-element.185), channel_id=1, source_target_pairs={{0,2},{1,3},{2,0},{3,1},{4,6},{5,7},{6,4},{7,5},{8,10},{9,11},{10,... | collective-permute-start | bytes 3538952 | tf_op jit(solution)/shard_map/ppermute | solution.py:941
  215.4 31.4 %collective-permute-start.25 = (bf16[8,48,1536]{2,1,0:T(8,128)(2,1)}, bf16[8,48,1536]{2,1,0:T(8,128)(2,1)S(1)}, u32[]{:S(2)}, u32[]{:S(2)}) collective-permute-start(bf16[8,48,1536]{2,1,0:T(8,128)(2,1)} %get-tuple-element.186), channel_id=1, source_target_pairs={{0,1},{1,0},{2,3},{3,2},{4,5},{5,4},{6,7},{7,6},{8,9},{9,8},{10,11... | collective-permute-start | bytes 3538952 | tf_op jit(solution)/shard_map/ppermute | solution.py:941
  218.5 28.3 %collective-permute-start.23 = (bf16[1,96,1536]{2,1,0:T(8,128)(2,1)S(1)}, bf16[1,96,1536]{2,1,0:T(8,128)(2,1)S(1)}, u32[]{:S(2)}, u32[]{:S(2)}) collective-permute-start(bf16[1,96,1536]{2,1,0:T(8,128)(2,1)S(1)} %get-tuple-element.183), channel_id=1, source_target_pairs={{0,4},{1,5},{2,6},{3,7},{4,0},{5,1},{6,2},{7,3},{8,12},{9,13},{10,... | collective-permute-start | bytes 884744 | tf_op jit(solution)/shard_map/ppermute | solution.py:941
  254.2 22.1 %collective-permute-start.30 = (bf16[4,64,1536]{2,1,0:T(8,128)(2,1)}, bf16[4,64,1536]{2,1,0:T(8,128)(2,1)}, u32[]{:S(2)}, u32[]{:S(2)}) collective-permute-start(bf16[4,64,1536]{2,1,0:T(8,128)(2,1)} %get-tuple-element.197), channel_id=1, source_target_pairs={{0,1},{1,0},{2,3},{3,2},{4,5},{5,4},{6,7},{7,6},{8,9},{9,8},{10,11... | collective-permute-start | bytes 2359304 | tf_op jit(solution)/shard_map/ppermute | solution.py:941
  257.1 36.3 %all-to-all-start.2 = ((bf16[8,128,768]{2,1,0:T(8,128)(2,1)}), bf16[8,128,768]{2,1,0:T(8,128)(2,1)S(1)}, u32[]{:S(2)}, u32[]{:S(2)}) async-start(bf16[8,128,768]{2,1,0:T(8,128)(2,1)} %bitcast.42), calls=%async_computation.2 | async-start | bytes 3145728 | tf_op jit(solution)/shard_map/all_to_all | solution.py:1047
  265.8 37.1 %collective-permute-start.27 = (bf16[8,48,1536]{2,1,0:T(8,128)(2,1)}, bf16[8,48,1536]{2,1,0:T(8,128)(2,1)}, u32[]{:S(2)}, u32[]{:S(2)}) collective-permute-start(bf16[8,48,1536]{2,1,0:T(8,128)(2,1)} %get-tuple-element.191), channel_id=1, source_target_pairs={{0,16},{1,17},{2,18},{3,19},{4,20},{5,21},{6,22},{7,23},{8,24},{9,... | collective-permute-start | bytes 3538952 | tf_op jit(solution)/shard_map/ppermute | solution.py:941
  280.4 22.5 %collective-permute-start.33 = (bf16[2,64,1536]{2,1,0:T(8,128)(2,1)}, bf16[2,64,1536]{2,1,0:T(8,128)(2,1)S(1)}, u32[]{:S(2)}, u32[]{:S(2)}) collective-permute-start(bf16[2,64,1536]{2,1,0:T(8,128)(2,1)} %get-tuple-element.203), channel_id=1, source_target_pairs={{0,2},{1,3},{2,0},{3,1},{4,6},{5,7},{6,4},{7,5},{8,10},{9,11},{10,... | collective-permute-start | bytes 1179656 | tf_op jit(solution)/shard_map/ppermute | solution.py:941
  280.8 22.1 %collective-permute-start.31 = (bf16[2,48,1536]{2,1,0:T(8,128)(2,1)}, bf16[2,48,1536]{2,1,0:T(8,128)(2,1)}, u32[]{:S(2)}, u32[]{:S(2)}) collective-permute-start(bf16[2,48,1536]{2,1,0:T(8,128)(2,1)} %get-tuple-element.199), channel_id=1, source_target_pairs={{0,1},{1,0},{2,3},{3,2},{4,5},{5,4},{6,7},{7,6},{8,9},{9,8},{10,11... | collective-permute-start | bytes 884744 | tf_op jit(solution)/shard_map/ppermute | solution.py:941
  308.9 22.1 %collective-permute-start.36 = (bf16[20,48,384]{2,1,0:T(8,128)(2,1)S(1)}, bf16[20,48,384]{2,1,0:T(8,128)(2,1)S(1)}, u32[]{:S(2)}, u32[]{:S(2)}) collective-permute-start(bf16[20,48,384]{2,1,0:T(8,128)(2,1)S(1)} %combine.18.refs_4_.refs_3_), channel_id=1, source_target_pairs={{0,16},{1,17},{2,18},{3,19},{4,20},{5,21},{6,22},{7,23},{8,24},{9,... | collective-permute-start | bytes 2211848 | tf_op jit(solution)/shard_map/ppermute | solution.py:941
  309.1 21.8 %collective-permute-start.34 = (bf16[1,160,1536]{2,1,0:T(8,128)(2,1)S(1)}, bf16[1,160,1536]{2,1,0:T(8,128)(2,1)S(1)}, u32[]{:S(2)}, u32[]{:S(2)}) collective-permute-start(bf16[1,160,1536]{2,1,0:T(8,128)(2,1)S(1)} %get-tuple-element.207), channel_id=1, source_target_pairs={{0,4},{1,5},{2,6},{3,7},{4,0},{5,1},{6,2},{7,3},{8,12},{9,13},{10,... | collective-permute-start | bytes 1474568 | tf_op jit(solution)/shard_map/ppermute | solution.py:941
  331.4 23.8 %collective-permute-start.40 = (bf16[960,384]{1,0:T(8,128)(2,1)S(1)}, bf16[960,384]{1,0:T(8,128)(2,1)}, u32[]{:S(2)}, u32[]{:S(2)}) collective-permute-start(bf16[960,384]{1,0:T(8,128)(2,1)S(1)} %bitcast.35), channel_id=1, source_target_pairs={{0,8},{1,9},{2,10},{3,11},{4,12},{5,13},{6,14},{7,15},{8,0},{9,1},... | collective-permute-start | bytes 2211848 | tf_op jit(solution)/shard_map/ppermute | solution.py:941
  (91 other events, 910.9 us)

commit v6 on v5

--- a/solution.py
+++ b/solution.py
@@ -657,7 +657,7 @@
         out_specs=(VM,) * len(outs),
         scratch_shapes=scratch + [pltpu.SemaphoreType.DMA((2 * len(pairs),))],
         cost_estimate=CHEAP,
-        vmem=56 if attention else 34,
+        vmem=50 if attention else 34,
         name="weights",
     )
     parts = []
@@ -720,7 +720,7 @@
 def last_kernel(
     plan, coords_ref, length_ref, mixed_ref, lse_ref, gctx_ref, first_ref, n_ref, s_ref, gains_ref, x_ref,
     slot_ref, type_ref, top0, top1, low0, low1, att1, bias0, bias1, wqkv_hbm,
-    out_ref, *parts_and_scratch
+    out_keep_ref, out_send_ref, *parts_and_scratch
 ):
     outs, (wqkv, dmix, xt, res, back_ref, back_low, att0, emb, small, sems) = parts_and_scratch[:-10], parts_and_scratch[-10:]
     tokens, width = back_ref.shape
@@ -731,21 +731,32 @@
     grad = first_ref[...] + dot(dmix[...], wqkv[...], COLS)
     gain = gains_ref[...].astype(F32)[0:1]
     norm_end(coords_ref[0], grad, n_ref[...], s_ref[:, :1], gain, back_ref, back_low, None, None, emb)
-    slots = out_ref.shape[0]
+    mine = coords_ref[0]
+    slots, half = out_keep_ref.shape
     chunk = 256
 
     def step(i, carry):
         there = pl.ds(pl.multiple_of(i * chunk, chunk), chunk)
         number = lax.broadcasted_iota(jnp.int32, (chunk, tokens), 0) + i * chunk
         hit = jnp.where(number == slot_ref[...], 1.0, 0.0).astype(LOW)
-        out_ref[there, :] = dot(hit, back_low[...]).astype(LOW)
+        got = dot(hit, back_low[...]).astype(LOW)
+
+        @pl.when(mine == 0)
+        def _():
+            out_keep_ref[there, :] = got[:, :half]
+            out_send_ref[there, :] = got[:, half:]
+
+        @pl.when(mine == 1)
+        def _():
+            out_keep_ref[there, :] = got[:, half:]
+            out_send_ref[there, :] = got[:, :half]
+
         return carry
 
     lax.fori_loop(0, slots // chunk, step, 0)
     xt[...] = x_ref[...].T
     blocks, piece, _ = res.shape
     blocks //= 2
-    half = width // 2
     wide = 3 * half
     for core in range(2):
         there = slice(core * blocks, (core + 1) * blocks)
@@ -793,10 +804,10 @@
     return run(
         functools.partial(last_kernel, plan),
         after,
-        out_shape=(s((slots, width), LOW),) + (s((2 * blocks // parts,) + block[1:], LOW),) * parts,
+        out_shape=(s((slots, width // 2), LOW),) * 2 + (s((2 * blocks // parts,) + block[1:], LOW),) * parts,
         in_specs=[SM, SM] + [VM] * (len(operands) - 3) + [HBM],
         operands=operands,
-        out_specs=(VM,) * (1 + parts),
+        out_specs=(VM,) * (2 + parts),
         scratch_shapes=[
             v((width, 3 * width), LOW), v((tokens, 3 * width), LOW), v((width, tokens), LOW),
             v((2 * blocks,) + block[1:], LOW), v((tokens, width), F32), v((tokens, width), LOW),
@@ -808,52 +819,37 @@
     )
 
 
-def table_back_kernel(coords_ref, asked_ref, rows_ref, keep_ref, send_ref, total):
-    count = total.shape[0]
-    chunk = count // 5 if count % 5 == 0 else count
+def table_back_kernel(asked_ref, rows_ref, out_ref):
+    count = out_ref.shape[0]
+    chunk = count // 5 if count % 80 == 0 else count
 
     def step(i, carry):
-        at = pl.multiple_of(i * chunk, 8)
+        at = pl.multiple_of(i * chunk, 16)
         number = lax.broadcasted_iota(jnp.int32, (chunk, rows_ref.shape[0]), 0) + at
         hit = jnp.where(number == asked_ref[...], 1.0, 0.0).astype(LOW)
-        total[pl.ds(at, chunk), :] = dot(hit, rows_ref[...])
+        out_ref[pl.ds(at, chunk), :] = dot(hit, rows_ref[...]).astype(LOW)
         return carry
 
     lax.fori_loop(0, count // chunk, step, 0)
-    mine = coords_ref[0]
-    half = total.shape[1] // 2
-
-    @pl.when(mine == 0)
-    def _():
-        keep_ref[...] = total[:, :half].astype(LOW)
-        send_ref[...] = total[:, half:].astype(LOW)
-
-    @pl.when(mine == 1)
-    def _():
-        keep_ref[...] = total[:, half:].astype(LOW)
-        send_ref[...] = total[:, :half].astype(LOW)
-
-
-def table_back(coords, asked, rows, local_rows, after=()):
-    width = rows.shape[1]
-    half = jax.ShapeDtypeStruct((local_rows, width // 2), LOW)
+
+
+def table_back(asked, rows, local_rows, after=()):
     return run(
         table_back_kernel,
         after,
-        out_shape=(half, half),
-        in_specs=[SM, VM, VM],
-        operands=(coords, asked, rows),
-        out_specs=(VM, VM),
-        scratch_shapes=[pltpu.VMEM((local_rows, width), F32)],
+        out_shape=jax.ShapeDtypeStruct((local_rows, rows.shape[1]), LOW),
+        in_specs=[VM, VM],
+        operands=(asked, rows),
+        out_specs=VM,
         cost_estimate=CHEAP,
-        vmem=16,
+        vmem=20,
         name="table_back",
     )
 
 
 def finish_kernel(coords_ref, *refs):
-    many, few = refs[:4], refs[4:8]
-    qkv_ref, wout_ref, one_ref, two_ref, pos_ref, small_ref = refs[8:]
+    many, early, few = refs[:4], refs[4:8], refs[8:12]
+    qkv_ref, wout_ref, one_ref, two_ref, pos_ref, type_ref, gain_ref, shift_ref, bias_ref, small_ref = refs[12:]
     mine_core, mine_y = coords_ref[0] == 0, coords_ref[4] == 0
     half = wout_ref.shape[2] // 2
     wide = 3 * half
@@ -868,14 +864,13 @@
         return jnp.where(same_core, here, there).astype(F32)
 
     at = lambda n: slice(n * part, (n + 1) * part)
-    mix1, two0, one0, two1, one1 = at(0), at(1), at(2), slice(3 * part + 16, 4 * part + 16), slice(4 * part + 16, 5 * part + 16)
     for layer in range(NL):
         for core in range(2):
             columns = []
             mine = slice(core * half, (core + 1) * half)
             for y in range(2):
                 rows = slice(y * part, (y + 1) * part)
-                mix = piece(few, slice(0, part), core, y) if layer == 0 else piece(many, mix1, core, y)
+                mix = piece(few, slice(0, part), core, y) if layer == 0 else piece(many, at(0), core, y)
                 qkv_ref[layer, rows, core * wide : (core + 1) * wide] = mix[:, :wide]
                 if layer == 0:
                     group = pos_ref.shape[0] // 2
@@ -889,13 +884,31 @@
                         wout_ref[layer, there, mine] = out[:, n * half : (n + 1) * half]
                 else:
                     wout_ref[layer, rows, mine] = mix[:, wide:]
-                one_ref[layer, rows, core * 4 * half : (core + 1) * 4 * half] = piece(many, one0 if layer == 0 else one1, core, y)
-                second = piece(many, two0 if layer == 0 else two1, core, y)
+                first = piece(many, at(2), core, y) if layer == 0 else piece(early, at(1), core, y)
+                one_ref[layer, rows, core * 4 * half : (core + 1) * 4 * half] = first
+                second = piece(many, at(1), core, y) if layer == 0 else piece(early, at(0), core, y)
                 columns += [second[:, i * half : (i + 1) * half] for i in range(4)]
             two_ref[layer, :, mine] = jnp.concatenate(columns, axis=0).T
-
-
-def finish(coords, many, few, width, ff, owners):
+    owners = small_ref.shape[1] // type_ref.shape[1]
+    size, long = type_ref.shape[1], bias_ref.shape[1]
+    per = long * owners // small_ref.shape[1]
+    few_rows = small_ref[:20]
+    mine, bias = few_rows[:, :size], [small_ref[20 + n * per : 21 + n * per, :long] for n in range(NL)]
+    for owner in range(1, owners):
+        chosen = coords_ref[5] == owner
+        mine = jnp.where(chosen, few_rows[:, owner * size : (owner + 1) * size], mine)
+        row, at_lane = divmod(owner * long, small_ref.shape[1])
+        for n in range(NL):
+            there = small_ref[20 + n * per + row : 21 + n * per + row, at_lane : at_lane + long]
+            bias[n] = jnp.where(chosen, there, bias[n])
+    type_ref[...] = mine[:2]
+    gain_ref[...] = mine[2 : 2 + 2 * NL + 1]
+    shift_ref[...] = mine[2 + 2 * NL + 1 :]
+    for n in range(NL):
+        bias_ref[n : n + 1] = bias[n]
+
+
+def finish(coords, many, early, few, width, ff, owners):
     s = jax.ShapeDtypeStruct
     rows = width // owners
     return run(
@@ -903,14 +916,37 @@
         (),
         out_shape=(
             s((NL, rows, 3 * width), F32), s((NL, rows, width), F32), s((NL, rows, ff), F32), s((NL, ff // owners, width), F32),
-            s((64, width), F32), s((28, width), F32),
+            s((64, width), F32), s((2, rows), F32), s((2 * NL + 1, rows), F32), s((6 * NL + 1, rows), F32), s((NL, ff // owners), F32),
         ),
-        in_specs=[SM] + [VM] * 8,
-        operands=(coords, *many, *few),
-        out_specs=(VM,) * 6,
+        in_specs=[SM] + [VM] * 12,
+        operands=(coords, *many, *early, *few),
+        out_specs=(VM,) * 9,
+        scratch_shapes=[pltpu.VMEM((28, width), F32)],
         cost_estimate=CHEAP,
         vmem=24,
         name="finish",
+    )
+
+
+def table_finish_kernel(coords_ref, own_ref, other_ref, out_ref, mark_ref):
+    mark_ref[...] = jnp.zeros_like(mark_ref)
+    half = own_ref.shape[1]
+    first = coords_ref[0] == 0
+    out_ref[:, :half] = jnp.where(first, own_ref[...], other_ref[...]).astype(F32)
+    out_ref[:, half:] = jnp.where(first, other_ref[...], own_ref[...]).astype(F32)
+
+
+def table_finish(coords, own, other, after=()):
+    return run(
+        table_finish_kernel,
+        after,
+        out_shape=(jax.ShapeDtypeStruct((own.shape[0], 2 * own.shape[1]), F32), jax.ShapeDtypeStruct((8, 128), F32)),
+        in_specs=[SM, VM, VM],
+        operands=(coords, own, other),
+        out_specs=(VM, VM),
+        cost_estimate=CHEAP,
+        vmem=16,
+        name="table_finish",
     )
 
 
@@ -1023,7 +1059,7 @@
     chosen = (token_ids >= number * local_rows) & (token_ids < (number + 1) * local_rows)
     own_rank = jnp.cumsum(chosen.astype(jnp.int32), axis=1) - 1
     slot_row = jnp.sum(jnp.where(chosen, number * slot_count + own_rank, 0), axis=0, keepdims=True)
-    asked = asked[None, :]
+    asked = both_cores(asked[:, None], cube.core(asked[:, None]), owners).reshape(1, -1)
     (n0, s0, hidden), top, layers = forward(
         coords, lengths, replies, slot_row, type_ids, pos_table, type_table, gains, shifts, b_ff1.astype(F32),
         cotangent.reshape(tokens, width), w_qkv, w_out, w_ff1, w_ff2,
@@ -1047,6 +1083,11 @@
     return lax.all_to_all(
         outgoing.reshape(owners, -1, shape[1]), "vocab", split_axis=0, concat_axis=0, tiled=True
     ).reshape(shape)
+
+
+def both_cores(own, other, owners):
+    fold = lambda array: array.reshape(owners, 1, -1, array.shape[1])
+    return jnp.concatenate([fold(own), fold(other)], axis=1).reshape(-1, own.shape[1])
 
 
 def unpack(pack):
@@ -1092,17 +1133,17 @@
         blocks, (None, None, None), coords, pair(sec_keep, sec_send), act0, mid0, pair(pre_keep, pre_send),
         (x1, pair(mix_keep, mix_send), ctx1, fst1, ctx0, pair(fst_keep, fst_send)),
     )
-    outgoing, first_core, second_core = last(
+    out_keep, out_send, first_core, second_core = last(
         None, coords, lengths, mixed0, lse0, gctx, first, *norms[0], gains, x0[0], slot_row, kinds,
-        (top0, top1, sums0, sums1, att1, bias0, bias1), w_qkv, asked.shape[1], 2 * blocks,
+        (top0, top1, sums0, sums1, att1, bias0, bias1), w_qkv, asked.shape[1] // 2, 2 * blocks,
     )
     mine = cube.core_is_first()
 
     def over_cores(first, second):
         return add(jnp.where(mine, first, second), cube.core(jnp.where(mine, second, first)))
 
-    table_keep, table_send = table_back(coords, asked, exchange_rows(outgoing, owners), local_rows)
-    table_part = add(table_keep, cube.core(table_send))
+    outgoing = both_cores(out_keep, cube.core(out_send), owners)
+    table_part = table_back(asked, exchange_rows(outgoing, owners), local_rows)
     for bit in range(1, cube.dp_bits):
         table_part = add(table_part, cube.permute(table_part, 1 << bit, 0))
     wide = 3 * half
@@ -1201,7 +1242,7 @@
         mix_keep, mix_send, pre_keep, pre_send, att1, sec_keep, sec_send, top0, bias0, first, fst_keep, fst_send, gctx, sums0
     ) = between(
         1, coords, lengths, mixed1, lse1, gctx, first, *norms[1], n1_0, s1_0, gains, gp0, w_qkv, w_out, w_ff1, w_ff2,
-        after=got[0][:1],
+        after=got[0][:1] + (act0[1], mid0[1], ctx0[1], x1[1], ctx1[1]),
     )
     mark = step([two1, one1], after=(gctx,), cost=LONG)
     two1.start()
@@ -1215,11 +1256,11 @@
         bucket.start()
     mark = step([joined((two1, one1), 1)], after=got[0][:1], cost=LONG)
     two1.start()
-    outgoing, *got = last(
+    out_keep, out_send, *got = last(
         plan_mix0, coords, lengths, mixed0, lse0, gctx, first, *norms[0], gains, x0[0], slot_row, kinds,
-        (top0, top1, sums0, sums1, att1, bias0, bias1), w_qkv, asked.shape[1], 2 * owners, after=(mark,),
-    )
-    incoming = exchange_rows(outgoing, owners)
+        (top0, top1, sums0, sums1, att1, bias0, bias1), w_qkv, asked.shape[1] // 2, 2 * owners, after=(mark,),
+    )
+    incoming = exchange_rows(both_cores(out_keep, cube.core(out_send), owners), owners)
     mix0 = Bucket(cube, plan_mix0, got)
     mix0.start()
     mark = step([two1, mix1, two0, one0], after=got[:1], cost=LONG)
@@ -1231,36 +1272,39 @@
     for bucket in (mix1, two0, one0):
         bucket.start()
     folded = (local_rows // 48, 48, half)
-    got = table_back(coords, asked, incoming, local_rows, after=(mark,))
-    table = Bucket(cube, single(("core", "y")), [part.reshape(folded) for part in got])
+    got = table_back(asked, incoming, local_rows, after=(mark,))
+    table = Bucket(cube, single("y"), (got.reshape(folded),))
     table.start()
-    mark = step([mix0, joined((mix1, two0, one0), 1)], after=got[:1], cost=LONG)
+    mark = step([mix0, joined((mix1, two0, one0), 1)], after=(got,), cost=LONG)
     mix0.start()
     mix1.start()
-    mark = step([table], after=(mark,))
-    table.start()
+    two1.keep()
+    mark = step([table, two1], after=(mark,))
+    early = Bucket(cube, (), (cube.along(two1.parts[0], ("y",)),))
+    early.keep()
     mark = step([mix0], after=(mark,), cost=LONG)
     mix0.start()
-    two1.keep()
-    mark = step([joined((mix1, two1), 1), table], after=(mark,))
+    mark = step([mix1, early], after=(mark,))
     later = Bucket(cube, (), (cube.along(mix1.parts[0], ("y",)),))
     later.keep()
-    mark = step([mix0], after=(mark,))
+    table_own = table.parts[0].reshape(local_rows, half)
+    table_out, mark = table_finish(coords, table_own, cube.core(table_own), after=(mark,))
+    others = [Bucket(cube, (), (cube.core(bucket.parts[0]),)) for bucket in (two1, early)]
+    for other in others:
+        other.keep()
+    mark = step([mix0] + others, after=(mark,))
     last_y = Bucket(cube, (), (cube.along(mix0.parts[0], ("y",)),))
     last_y.keep()
     step([last_y], after=(mark,))
     step([later], after=(last_y.parts[0],))
-    own = mix1.parts[0]
-    over_y, last_y = later.parts[0], last_y.parts[0]
-    qkv_out, wout_out, one_out, two_out, pos_out, small = finish(
-        coords,
-        (own, over_y, cube.core(own), cube.core(over_y)),
-        (mix0.parts[0], last_y, cube.core(mix0.parts[0]), cube.core(last_y)),
-        width, w_ff1.shape[2], owners,
-    )
-    types, gains, shifts, biases = small_outs(cube, small)
+    four = lambda own, over_y: (own, over_y, cube.core(own), cube.core(over_y))
+    qkv_out, wout_out, one_out, two_out, pos_out, types, gains, shifts, biases = finish(
+        coords, four(mix1.parts[0], later.parts[0]),
+        (two1.parts[0], early.parts[0], others[0].parts[0], others[1].parts[0]),
+        four(mix0.parts[0], last_y.parts[0]), width, w_ff1.shape[2], owners,
+    )
     return (
-        cube.join_core(table.parts[0].reshape(local_rows, half), -1), pos_out, types, gains, shifts, qkv_out, wout_out,
+        table_out, pos_out, types, gains, shifts, qkv_out, wout_out,
         biases, one_out, two_out,
     )
 

time: 372 us -> 363 us (0.976)
  the two profiles are of different devices: /device:TPU:9 before, /device:TPU:0 now
where the time goes in v6:
time: 363 us; the launch traced here: 356 us
  Pallas kernels  169 us (47%)
  waiting for transfers between devices  107 us (29%)
  starting transfers between devices  50.7 us (14%)
  local copies, waits for them, and re-layouts  19.4 us (5%)
  other arithmetic  4.87 us (1%)
    pallas_call x21, Pallas kernels, run(): pl.pallas_call(body, out_shape=out_shape, in_specs=list(in_specs) + [ANY]...  169 us
    ppermute x52, waiting for transfers between devices, permute(): return lax.ppermute(value, AXES, pairs)  62.5 us
    all_to_all x2, waiting for transfers between devices, exchange_rows(): lax.all_to_all(outgoing.reshape(owners, -1, shape[1]), 'vocab', split_axi...  38.3 us
    ppermute x52, starting transfers between devices, permute(): return lax.ppermute(value, AXES, pairs)  36.2 us
    unnamed x114, local copies, waits for them, and re-layouts  15.5 us
    all_to_all x2, starting transfers between devices, exchange_rows(): lax.all_to_all(outgoing.reshape(owners, -1, shape[1]), 'vocab', split_axi...  7.29 us
  transfers between devices with their start and end apart: 55, of which 21 were waited for; matrix products, arithmetic and copies ran while one was open for 1% of the time, Pallas kernels for 32%

profile of v6, /device:TPU:0, one launch (start us, length us, event | category | flops | bytes accessed | tf_op | source)
XLA Modules:
  0.0 356.4 jit_solution(12656077420225589769)
XLA Ops:
  2.1 7.3 %all-to-all-start = ((s32[8,1,512]{2,1,0:T(1,128)}), s32[8,1,512]{2,1,0:T(1,128)S(1)}, u32[]{:S(2)}, u32[]{:S(2)}) async-start(s32[8,1,512]{2,1,0:T(1,128)} %broadcast_in_dim.36), calls=%async_computation | async-start | bytes 32768 | tf_op jit(solution)/shard_map/all_to_all | solution.py:1046
  9.3 6.6 %all-to-all-done = s32[8,1,512]{2,1,0:T(1,128)S(1)} async-done(((s32[8,1,512]{2,1,0:T(1,128)}), s32[8,1,512]{2,1,0:T(1,128)S(1)}, u32[]{:S(2)}, u32[]{:S(2)}) %all-to-all-start) | async-done | bytes 16416 | tf_op jit(solution)/shard_map/all_to_all | solution.py:1046
  18.3 3.1 fusion.2
  21.4 3.7 %all-to-all-start.1 = ((bf16[8,128,768]{2,1,0:T(8,128)(2,1)}), bf16[8,128,768]{2,1,0:T(8,128)(2,1)S(1)}, u32[]{:S(2)}, u32[]{:S(2)}) async-start(bf16[8,128,768]{2,1,0:T(8,128)(2,1)} %bitcast.47), calls=%async_computation.1 | async-start | bytes 3145728 | tf_op jit(solution)/shard_map/all_to_all | solution.py:1083
  29.3 31.8 %all-to-all-done.1 = bf16[8,128,768]{2,1,0:T(8,128)(2,1)S(1)} async-done(((bf16[8,128,768]{2,1,0:T(8,128)(2,1)}), bf16[8,128,768]{2,1,0:T(8,128)(2,1)S(1)}, u32[]{:S(2)}, u32[]{:S(2)}) %all-to-all-start.1) | async-done | bytes 1572896 | tf_op jit(solution)/shard_map/all_to_all | solution.py:1083
  62.2 50.1 %forward.1 = (f32[512,768]{1,0:T(8,128)}, f32[512,128]{1,0:T(8,128)}, bf16[512,768]{1,0:T(8,128)(2,1)}, f32[512,768]{1,0:T(8,128)}, bf16[512,768]{1,0:T(8,128)(2...) custom-call(s32[6]{0:T(128)} %stack.27.refs_0_, ...), custom_call_target="tpu_custom_call" | custom-call | flops 1 | bytes 1 | tf_op jit(solution)/shard_map/forward/pallas_call | solution.py:31
  113.9 15.6 %feed.1 = (bf16[512,1536]{1,0:T(8,128)(2,1)}, bf16[512,1536]{1,0:T(8,128)(2,1)}, f32[1,3072]{1,0:T(1,128)S(1)}, f32[512,768]{1,0:T(8,128)}, bf16[512,768]{1,0:T(...) custom-call(s32[6]{0:T(128)S(1)} %copy-done.18, ...), custom_call_target="tpu_custom_call" | custom-call | flops 1 | bytes 1 | tf_op jit(solution)/shard_map/feed/pallas_call | solution.py:31
  130.2 3.1 collective-permute-done.1.refs_2_
  136.8 9.2 %weights.2 = (bf16[4,48,1536]{2,1,0:T(8,128)(2,1)S(1)}, bf16[4,48,1536]{2,1,0:T(8,128)(2,1)}, bf16[4,48,1536]{2,1,0:T(8,128)(2,1)}, bf16[4,48,1536]{2,1,0:T(8,12...) custom-call(s32[6]{0:T(128)S(1)} %copy-done.18, bf16[512,384]{1,0:T(8,128)(2,1)S(1)} %copy-done.11, ...), custom_call_target="tpu_custom_call" | custom-call | flops 1 | bytes 1 | tf_op jit(solution)/shard_map/weights/pallas_call | solution.py:31
  150.6 30.2 %between.1 = (bf16[512,1152]{1,0:T(8,128)(2,1)}, bf16[512,1152]{1,0:T(8,128)(2,1)}, bf16[512,1536]{1,0:T(8,128)(2,1)}, bf16[512,1536]{1,0:T(8,128)(2,1)}, f32[2,...) custom-call(s32[6]{0:T(128)} %stack.27.refs_0_, ...), custom_call_target="tpu_custom_call" | custom-call | flops 1 | bytes 1 | tf_op jit(solution)/shard_map/between/pallas_call | solution.py:31
  194.2 18.1 %weights.3 = (bf16[8,48,1536]{2,1,0:T(8,128)(2,1)}, bf16[8,48,1536]{2,1,0:T(8,128)(2,1)}, bf16[8,64,1536]{2,1,0:T(8,128)(2,1)}, bf16[8,64,1536]{2,1,0:T(8,128)(2...) custom-call(s32[6]{0:T(128)S(1)} %copy-done.19, bf16[512,384]{1,0:T(8,128)(2,1)S(1)} %copy-done.12, ...), custom_call_target="tpu_custom_call" | custom-call | flops 1 | bytes 1 | tf_op jit(solution)/shard_map/weights/pallas_call | solution.py:31
  218.7 23.6 %last.1 = (bf16[1024,384]{1,0:T(8,128)(2,1)S(1)}, bf16[1024,384]{1,0:T(8,128)(2,1)}, bf16[16,48,1536]{2,1,0:T(8,128)(2,1)}, bf16[16,48,1536]{2,1,0:T(8,128)(2,1)}) custom-call(s32[6]{0:T(128)S(1)} %copy-done.19, s32[1]{0:T(128)S(6)} %copy.38.refs_1_, bf16[512,2304]{1,0:T(8,128)(2,1)} %get-tuple-element.127.refs_2_, f32[12,512]{1,0:T(8,128)S(1)} %copy-done.21, ...), custom_call_target="tpu_custom_call" | custom-call | flops 1 | bytes 1 | tf_op jit(solution)/shard_map/last/pallas_call | solution.py:31
  246.5 2.7 collective-permute-done.27.refs_7_
  258.2 3.6 %all-to-all-start.2 = ((bf16[8,256,384]{2,1,0:T(8,128)(2,1)}), bf16[8,256,384]{2,1,0:T(8,128)(2,1)S(1)}, u32[]{:S(2)}, u32[]{:S(2)}) async-start(bf16[8,256,384]{2,1,0:T(8,128)(2,1)} %bitcast.24), calls=%async_computation.2 | async-start | bytes 3145728 | tf_op jit(solution)/shard_map/all_to_all | solution.py:1083
  263.5 3.1 combine.15
  269.0 14.0 %collective-permute-done.29.refs_3_ = bf16[4,48,1536]{2,1,0:T(8,128)(2,1)} collective-permute-done((bf16[4,48,1536]{2,1,0:T(8,128)(2,1)}, bf16[4,48,1536]{2,1,0:T(8,128)(2,1)}, u32[]{:S(2)}, u32[]{:S(2)}) %collective-permute-start.29) | collective-permute-done | bytes 589856 | tf_op jit(solution)/shard_map/ppermute | solution.py:977
  290.3 6.5 %all-to-all-done.2 = bf16[8,256,384]{2,1,0:T(8,128)(2,1)S(1)} async-done(((bf16[8,256,384]{2,1,0:T(8,128)(2,1)}), bf16[8,256,384]{2,1,0:T(8,128)(2,1)S(1)}, u32[]{:S(2)}, u32[]{:S(2)}) %all-to-all-start.2) | async-done | bytes 1572896 | tf_op jit(solution)/shard_map/all_to_all | solution.py:1083
  296.8 2.9 table_back.1.refs_8_
  309.3 5.7 %collective-permute-done.32.refs_1_ = bf16[20,48,384]{2,1,0:T(8,128)(2,1)S(1)} collective-permute-done((bf16[20,48,384]{2,1,0:T(8,128)(2,1)S(1)}, bf16[20,48,384]{2,1,0:T(8,128)(2,1)S(1)}, u32[]{:S(2)}, u32[]{:S(2)}) %collective-permute-start.32) | collective-permute-done | bytes 737312 | tf_op jit(solution)/shard_map/ppermute | solution.py:977
  315.3 6.6 %collective-permute-done.40.refs_1_ = bf16[2,48,1536]{2,1,0:T(8,128)(2,1)S(1)} collective-permute-done((bf16[2,48,1536]{2,1,0:T(8,128)(2,1)S(1)}, bf16[2,48,1536]{2,1,0:T(8,128)(2,1)S(1)}, u32[]{:S(2)}, u32[]{:S(2)}) %collective-permute-start.40) | collective-permute-done | bytes 294944 | tf_op jit(solution)/shard_map/ppermute | solution.py:977
  328.0 3.9 %collective-permute-done.39.refs_2_ = bf16[1,96,1536]{2,1,0:T(8,128)(2,1)S(1)} collective-permute-done((bf16[1,96,1536]{2,1,0:T(8,128)(2,1)S(1)}, bf16[1,96,1536]{2,1,0:T(8,128)(2,1)S(1)}, u32[]{:S(2)}, u32[]{:S(2)}) %collective-permute-start.39) | collective-permute-done | bytes 294944 | tf_op jit(solution)/shard_map/ppermute | solution.py:977
  337.0 6.4 %collective-permute-done.44.refs_1_ = bf16[1,48,1536]{2,1,0:T(8,128)(2,1)S(1)} collective-permute-done((bf16[1,48,1536]{2,1,0:T(8,128)(2,1)S(1)}, bf16[1,48,1536]{2,1,0:T(8,128)(2,1)S(1)}, u32[]{:S(2)}, u32[]{:S(2)}) %collective-permute-start.44) | collective-permute-done | bytes 147488 | tf_op jit(solution)/shard_map/ppermute | solution.py:977
  343.7 5.6 %collective-permute-done.47.refs_0_ = bf16[1,48,1536]{2,1,0:T(8,128)(2,1)S(1)} collective-permute-done((bf16[1,48,1536]{2,1,0:T(8,128)(2,1)S(1)}, bf16[1,48,1536]{2,1,0:T(8,128)(2,1)S(1)}, u32[]{:S(2)}, u32[]{:S(2)}) %collective-permute-start.47) | collective-permute-done | bytes 147488 | tf_op jit(solution)/shard_map/ppermute | solution.py:977
  351.7 4.5 %finish.1 = (f32[2,96,2304]{2,1,0:T(8,128)}, f32[2,96,768]{2,1,0:T(8,128)}, f32[2,96,3072]{2,1,0:T(8,128)}, f32[2,384,768]{2,1,0:T(8,128)}, f32[64,768]{1,0:T(8,...) custom-call(s32[6]{0:T(128)S(1)} %copy-done.20, ...), custom_call_target="tpu_custom_call" | custom-call | flops 1 | bytes 1 | tf_op jit(solution)/shard_map/finish/pallas_call | solution.py:31
  (245 shorter events, 86.4 us)
Async XLA Ops:
  21.4 39.7 %all-to-all-start.1 = ((bf16[8,128,768]{2,1,0:T(8,128)(2,1)}), bf16[8,128,768]{2,1,0:T(8,128)(2,1)S(1)}, u32[]{:S(2)}, u32[]{:S(2)}) async-start(bf16[8,128,768]{2,1,0:T(8,128)(2,1)} %bitcast.47), calls=%async_computation.1 | async-start | bytes 3145728 | tf_op jit(solution)/shard_map/all_to_all | solution.py:1083
  112.4 22.9 %collective-permute-start.2 = (bf16[512,3072]{1,0:T(8,128)(2,1)}, bf16[512,3072]{1,0:T(8,128)(2,1)S(1)}, u32[]{:S(2)}, u32[]{:S(2)}) collective-permute-start(bf16[512,3072]{1,0:T(8,128)(2,1)} %get-tuple-element.145.refs_3_), channel_id=1, source_target_pairs={{0,8},{1,9},{2,10},{3,11},{4,12},{5,13},{6,14},{7,15},{8,0},{9,1},... | collective-permute-start | bytes 9437192 | tf_op jit(solution)/shard_map/ppermute | solution.py:977
  112.4 38.0 %collective-permute-start.5 = (bf16[512,3072]{1,0:T(8,128)(2,1)}, bf16[512,3072]{1,0:T(8,128)(2,1)}, u32[]{:S(2)}, u32[]{:S(2)}) collective-permute-start(bf16[512,3072]{1,0:T(8,128)(2,1)} %get-tuple-element.150.refs_3_), channel_id=1, source_target_pairs={{0,8},{1,9},{2,10},{3,11},{4,12},{5,13},{6,14},{7,15},{8,0},{9,1},... | collective-permute-start | bytes 9437192 | tf_op jit(solution)/shard_map/ppermute | solution.py:977
  146.9 35.0 %collective-permute-start.13 = (bf16[8,48,1536]{2,1,0:T(8,128)(2,1)}, bf16[8,48,1536]{2,1,0:T(8,128)(2,1)S(1)}, u32[]{:S(2)}, u32[]{:S(2)}) collective-permute-start(bf16[8,48,1536]{2,1,0:T(8,128)(2,1)} %get-tuple-element.171), channel_id=1, source_target_pairs={{0,2},{1,3},{2,0},{3,1},{4,6},{5,7},{6,4},{7,5},{8,10},{9,11},{10,... | collective-permute-start | bytes 3538952 | tf_op jit(solution)/shard_map/ppermute | solution.py:977
  146.9 34.0 %collective-permute-start.10 = (bf16[4,48,1536]{2,1,0:T(8,128)(2,1)}, bf16[4,48,1536]{2,1,0:T(8,128)(2,1)S(1)}, u32[]{:S(2)}, u32[]{:S(2)}) collective-permute-start(bf16[4,48,1536]{2,1,0:T(8,128)(2,1)} %get-tuple-element.167), channel_id=1, source_target_pairs={{0,16},{1,17},{2,18},{3,19},{4,20},{5,21},{6,22},{7,23},{8,24},{9,... | collective-permute-start | bytes 1769480 | tf_op jit(solution)/shard_map/ppermute | solution.py:977
  148.5 32.9 %collective-permute-start.11 = (bf16[4,48,1536]{2,1,0:T(8,128)(2,1)}, bf16[4,48,1536]{2,1,0:T(8,128)(2,1)}, u32[]{:S(2)}, u32[]{:S(2)}) collective-permute-start(bf16[4,48,1536]{2,1,0:T(8,128)(2,1)} %get-tuple-element.168), channel_id=1, source_target_pairs={{0,1},{1,0},{2,3},{3,2},{4,5},{5,4},{6,7},{7,6},{8,9},{9,8},{10,11... | collective-permute-start | bytes 1769480 | tf_op jit(solution)/shard_map/ppermute | solution.py:977
  149.7 31.7 %collective-permute-start.12 = (bf16[4,48,1536]{2,1,0:T(8,128)(2,1)}, bf16[4,48,1536]{2,1,0:T(8,128)(2,1)}, u32[]{:S(2)}, u32[]{:S(2)}) collective-permute-start(bf16[4,48,1536]{2,1,0:T(8,128)(2,1)} %get-tuple-element.169), channel_id=1, source_target_pairs={{0,17},{1,16},{2,19},{3,18},{4,21},{5,20},{6,23},{7,22},{8,25},{9,... | collective-permute-start | bytes 1769480 | tf_op jit(solution)/shard_map/ppermute | solution.py:977
  150.5 36.8 %collective-permute-start.21 = (bf16[512,384]{1,0:T(8,128)(2,1)}, bf16[512,384]{1,0:T(8,128)(2,1)S(1)}, u32[]{:S(2)}, u32[]{:S(2)}) collective-permute-start(bf16[512,384]{1,0:T(8,128)(2,1)} %get-tuple-element.185), channel_id=1, source_target_pairs={{0,8},{1,9},{2,10},{3,11},{4,12},{5,13},{6,14},{7,15},{8,0},{9,1},... | collective-permute-start | bytes 1179656 | tf_op jit(solution)/shard_map/ppermute | solution.py:977
  187.3 25.3 %collective-permute-start.14 = (bf16[2,48,1536]{2,1,0:T(8,128)(2,1)S(1)}, bf16[2,48,1536]{2,1,0:T(8,128)(2,1)S(1)}, u32[]{:S(2)}, u32[]{:S(2)}) collective-permute-start(bf16[2,48,1536]{2,1,0:T(8,128)(2,1)S(1)} %get-tuple-element.173), channel_id=1, source_target_pairs={{0,2},{1,3},{2,0},{3,1},{4,6},{5,7},{6,4},{7,5},{8,10},{9,11},{10,... | collective-permute-start | bytes 884744 | tf_op jit(solution)/shard_map/ppermute | solution.py:977
  189.3 24.2 %collective-permute-start.15 = (bf16[2,48,1536]{2,1,0:T(8,128)(2,1)S(1)}, bf16[2,48,1536]{2,1,0:T(8,128)(2,1)S(1)}, u32[]{:S(2)}, u32[]{:S(2)}) collective-permute-start(bf16[2,48,1536]{2,1,0:T(8,128)(2,1)S(1)} %get-tuple-element.175), channel_id=1, source_target_pairs={{0,16},{1,17},{2,18},{3,19},{4,20},{5,21},{6,22},{7,23},{8,24},{9,... | collective-permute-start | bytes 884744 | tf_op jit(solution)/shard_map/ppermute | solution.py:977
  190.8 24.2 %collective-permute-start.16 = (bf16[2,48,1536]{2,1,0:T(8,128)(2,1)S(1)}, bf16[2,48,1536]{2,1,0:T(8,128)(2,1)S(1)}, u32[]{:S(2)}, u32[]{:S(2)}) collective-permute-start(bf16[2,48,1536]{2,1,0:T(8,128)(2,1)S(1)} %get-tuple-element.176), channel_id=1, source_target_pairs={{0,1},{1,0},{2,3},{3,2},{4,5},{5,4},{6,7},{7,6},{8,9},{9,8},{10,11... | collective-permute-start | bytes 884744 | tf_op jit(solution)/shard_map/ppermute | solution.py:977
  192.1 23.0 %collective-permute-start.17 = (bf16[2,48,1536]{2,1,0:T(8,128)(2,1)S(1)}, bf16[2,48,1536]{2,1,0:T(8,128)(2,1)S(1)}, u32[]{:S(2)}, u32[]{:S(2)}) collective-permute-start(bf16[2,48,1536]{2,1,0:T(8,128)(2,1)S(1)} %get-tuple-element.177), channel_id=1, source_target_pairs={{0,17},{1,16},{2,19},{3,18},{4,21},{5,20},{6,23},{7,22},{8,25},{9,... | collective-permute-start | bytes 884744 | tf_op jit(solution)/shard_map/ppermute | solution.py:977
  212.4 34.1 %collective-permute-start.25 = (bf16[8,48,1536]{2,1,0:T(8,128)(2,1)}, bf16[8,48,1536]{2,1,0:T(8,128)(2,1)S(1)}, u32[]{:S(2)}, u32[]{:S(2)}) collective-permute-start(bf16[8,48,1536]{2,1,0:T(8,128)(2,1)} %get-tuple-element.194), channel_id=1, source_target_pairs={{0,2},{1,3},{2,0},{3,1},{4,6},{5,7},{6,4},{7,5},{8,10},{9,11},{10,... | collective-permute-start | bytes 3538952 | tf_op jit(solution)/shard_map/ppermute | solution.py:977
  212.6 33.9 %collective-permute-start.26 = (bf16[8,48,1536]{2,1,0:T(8,128)(2,1)}, bf16[8,48,1536]{2,1,0:T(8,128)(2,1)S(1)}, u32[]{:S(2)}, u32[]{:S(2)}) collective-permute-start(bf16[8,48,1536]{2,1,0:T(8,128)(2,1)} %get-tuple-element.195), channel_id=1, source_target_pairs={{0,1},{1,0},{2,3},{3,2},{4,5},{5,4},{6,7},{7,6},{8,9},{9,8},{10,11... | collective-permute-start | bytes 3538952 | tf_op jit(solution)/shard_map/ppermute | solution.py:977
  213.5 35.7 %collective-permute-start.27 = (bf16[8,64,1536]{2,1,0:T(8,128)(2,1)}, bf16[8,64,1536]{2,1,0:T(8,128)(2,1)S(1)}, u32[]{:S(2)}, u32[]{:S(2)}) collective-permute-start(bf16[8,64,1536]{2,1,0:T(8,128)(2,1)} %get-tuple-element.197), channel_id=1, source_target_pairs={{0,16},{1,17},{2,18},{3,19},{4,20},{5,21},{6,22},{7,23},{8,24},{9,... | collective-permute-start | bytes 4718600 | tf_op jit(solution)/shard_map/ppermute | solution.py:977
  216.6 27.8 %collective-permute-start.24 = (bf16[1,96,1536]{2,1,0:T(8,128)(2,1)S(1)}, bf16[1,96,1536]{2,1,0:T(8,128)(2,1)S(1)}, u32[]{:S(2)}, u32[]{:S(2)}) collective-permute-start(bf16[1,96,1536]{2,1,0:T(8,128)(2,1)S(1)} %get-tuple-element.192), channel_id=1, source_target_pairs={{0,4},{1,5},{2,6},{3,7},{4,0},{5,1},{6,2},{7,3},{8,12},{9,13},{10,... | collective-permute-start | bytes 884744 | tf_op jit(solution)/shard_map/ppermute | solution.py:977
  252.8 30.1 %collective-permute-start.30 = (bf16[4,64,1536]{2,1,0:T(8,128)(2,1)}, bf16[4,64,1536]{2,1,0:T(8,128)(2,1)}, u32[]{:S(2)}, u32[]{:S(2)}) collective-permute-start(bf16[4,64,1536]{2,1,0:T(8,128)(2,1)} %get-tuple-element.204), channel_id=1, source_target_pairs={{0,1},{1,0},{2,3},{3,2},{4,5},{5,4},{6,7},{7,6},{8,9},{9,8},{10,11... | collective-permute-start | bytes 2359304 | tf_op jit(solution)/shard_map/ppermute | solution.py:977
  255.0 28.0 %collective-permute-start.29 = (bf16[4,48,1536]{2,1,0:T(8,128)(2,1)}, bf16[4,48,1536]{2,1,0:T(8,128)(2,1)}, u32[]{:S(2)}, u32[]{:S(2)}) collective-permute-start(bf16[4,48,1536]{2,1,0:T(8,128)(2,1)} %get-tuple-element.202), channel_id=1, source_target_pairs={{0,2},{1,3},{2,0},{3,1},{4,6},{5,7},{6,4},{7,5},{8,10},{9,11},{10,... | collective-permute-start | bytes 1769480 | tf_op jit(solution)/shard_map/ppermute | solution.py:977
  258.2 38.6 %all-to-all-start.2 = ((bf16[8,256,384]{2,1,0:T(8,128)(2,1)}), bf16[8,256,384]{2,1,0:T(8,128)(2,1)S(1)}, u32[]{:S(2)}, u32[]{:S(2)}) async-start(bf16[8,256,384]{2,1,0:T(8,128)(2,1)} %bitcast.24), calls=%async_computation.2 | async-start | bytes 3145728 | tf_op jit(solution)/shard_map/all_to_all | solution.py:1083
  266.6 35.5 %collective-permute-start.33 = (bf16[8,48,1536]{2,1,0:T(8,128)(2,1)}, bf16[8,48,1536]{2,1,0:T(8,128)(2,1)}, u32[]{:S(2)}, u32[]{:S(2)}) collective-permute-start(bf16[8,48,1536]{2,1,0:T(8,128)(2,1)} %get-tuple-element.209), channel_id=1, source_target_pairs={{0,16},{1,17},{2,18},{3,19},{4,20},{5,21},{6,22},{7,23},{8,24},{9,... | collective-permute-start | bytes 3538952 | tf_op jit(solution)/shard_map/ppermute | solution.py:977
  306.1 17.9 %collective-permute-start.41 = (bf16[2,48,1536]{2,1,0:T(8,128)(2,1)S(1)}, bf16[2,48,1536]{2,1,0:T(8,128)(2,1)S(1)}, u32[]{:S(2)}, u32[]{:S(2)}) collective-permute-start(bf16[2,48,1536]{2,1,0:T(8,128)(2,1)S(1)} %get-tuple-element.221), channel_id=1, source_target_pairs={{0,1},{1,0},{2,3},{3,2},{4,5},{5,4},{6,7},{7,6},{8,9},{9,8},{10,11... | collective-permute-start | bytes 884744 | tf_op jit(solution)/shard_map/ppermute | solution.py:977
  306.6 19.6 %collective-permute-start.42 = (bf16[2,48,1536]{2,1,0:T(8,128)(2,1)S(1)}, bf16[2,48,1536]{2,1,0:T(8,128)(2,1)S(1)}, u32[]{:S(2)}, u32[]{:S(2)}) collective-permute-start(bf16[2,48,1536]{2,1,0:T(8,128)(2,1)S(1)} %get-tuple-element.222), channel_id=1, source_target_pairs={{0,3},{1,2},{2,1},{3,0},{4,7},{5,6},{6,5},{7,4},{8,11},{9,10},{10,... | collective-permute-start | bytes 884744 | tf_op jit(solution)/shard_map/ppermute | solution.py:977
  307.7 20.3 %collective-permute-start.38 = (bf16[1,160,1536]{2,1,0:T(8,128)(2,1)S(1)}, bf16[1,160,1536]{2,1,0:T(8,128)(2,1)S(1)}, u32[]{:S(2)}, u32[]{:S(2)}) collective-permute-start(bf16[1,160,1536]{2,1,0:T(8,128)(2,1)S(1)} %get-tuple-element.218), channel_id=1, source_target_pairs={{0,4},{1,5},{2,6},{3,7},{4,0},{5,1},{6,2},{7,3},{8,12},{9,13},{10,... | collective-permute-start | bytes 1474568 | tf_op jit(solution)/shard_map/ppermute | solution.py:977
  315.2 19.4 %collective-permute-start.37 = (bf16[960,384]{1,0:T(8,128)(2,1)S(1)}, bf16[960,384]{1,0:T(8,128)(2,1)S(1)}, u32[]{:S(2)}, u32[]{:S(2)}) collective-permute-start(bf16[960,384]{1,0:T(8,128)(2,1)S(1)} %bitcast.41), channel_id=1, source_target_pairs={{0,8},{1,9},{2,10},{3,11},{4,12},{5,13},{6,14},{7,15},{8,0},{9,1},... | collective-permute-start | bytes 2211848 | tf_op jit(solution)/shard_map/ppermute | solution.py:977
  (88 other events, 850.8 us)

commit v7 on v6

--- a/solution.py
+++ b/solution.py
@@ -164,7 +164,7 @@
                 lse_ref[pl.ds(2 * j + h, 1), :] = top + jnp.log(total)
             return carry
 
-        lax.fori_loop(0, HEADS // 2, pair_step, 0)
+        lax.fori_loop(0, HEADS // 2, pair_step, 0, unroll=2)
         emit("ctxt", ctxt, ctxt_ref)
         loads[4 * layer + 1].wait()
         attended = dot(ctxt[...], wout[layer], ROWS) + shifts[base + 2 : base + 3]
@@ -344,7 +344,7 @@
         dmix[:, vcols] = grad_v.astype(LOW)
         return carry
 
-    lax.fori_loop(0, HEADS // 2, pair_step, 0)
+    lax.fori_loop(0, HEADS // 2, pair_step, 0, unroll=2)
 
 
 def chunk_loads(sems, at, pairs, chunk=512):
@@ -1282,9 +1282,8 @@
     mark = step([table, two1], after=(mark,))
     early = Bucket(cube, (), (cube.along(two1.parts[0], ("y",)),))
     early.keep()
-    mark = step([mix0], after=(mark,), cost=LONG)
+    mark = step([mix0, mix1, early], after=(mark,), cost=LONG)
     mix0.start()
-    mark = step([mix1, early], after=(mark,))
     later = Bucket(cube, (), (cube.along(mix1.parts[0], ("y",)),))
     later.keep()
     table_own = table.parts[0].reshape(local_rows, half)

time: 363 us -> 357 us (0.983)
    pallas_call x21 -> x20, Pallas kernels: 169 us -> 166 us  [run(): pl.pallas_call(body, out_shape=out_shape, in_specs=list(in_specs) + [ANY]...]
  transfers between devices with their start and end apart: 55 -> 55, of which waited for: 21 -> 19; matrix products, arithmetic and copies ran while one was open for 1% -> 1% of each run, Pallas kernels for 32% -> 32%
where the time goes in v7:
time: 357 us; the launch traced here: 350 us
  Pallas kernels  166 us (46%)
  waiting for transfers between devices  104 us (29%)
  starting transfers between devices  50.9 us (14%)
  local copies, waits for them, and re-layouts  19.4 us (5%)
  other arithmetic  4.87 us (1%)
    pallas_call x20, Pallas kernels, run(): pl.pallas_call(body, out_shape=out_shape, in_specs=list(in_specs) + [ANY]...  166 us
    ppermute x52, waiting for transfers between devices, permute(): return lax.ppermute(value, AXES, pairs)  59.3 us
    all_to_all x2, waiting for transfers between devices, exchange_rows(): lax.all_to_all(outgoing.reshape(owners, -1, shape[1]), 'vocab', split_axi...  38.3 us
    ppermute x52, starting transfers between devices, permute(): return lax.ppermute(value, AXES, pairs)  36.3 us
    unnamed x114, local copies, waits for them, and re-layouts  15.5 us
    all_to_all x2, starting transfers between devices, exchange_rows(): lax.all_to_all(outgoing.reshape(owners, -1, shape[1]), 'vocab', split_axi...  7.29 us
    all_to_all x1, starting transfers between devices, on_device(): lax.all_to_all(jnp.broadcast_to(token_ids, (owners, tokens)), 'vocab', sp...  7.25 us
  transfers between devices with their start and end apart: 55, of which 19 were waited for; matrix products, arithmetic and copies ran while one was open for 1% of the time, Pallas kernels for 32%

profile of v7, /device:TPU:0, one launch (start us, length us, event | category | flops | bytes accessed | tf_op | source)
XLA Modules:
  0.0 350.4 jit_solution(2268129931571617876)
XLA Ops:
  2.1 7.3 %all-to-all-start = ((s32[8,1,512]{2,1,0:T(1,128)}), s32[8,1,512]{2,1,0:T(1,128)S(1)}, u32[]{:S(2)}, u32[]{:S(2)}) async-start(s32[8,1,512]{2,1,0:T(1,128)} %broadcast_in_dim.36), calls=%async_computation | async-start | bytes 32768 | tf_op jit(solution)/shard_map/all_to_all | solution.py:1046
  9.3 6.6 %all-to-all-done = s32[8,1,512]{2,1,0:T(1,128)S(1)} async-done(((s32[8,1,512]{2,1,0:T(1,128)}), s32[8,1,512]{2,1,0:T(1,128)S(1)}, u32[]{:S(2)}, u32[]{:S(2)}) %all-to-all-start) | async-done | bytes 16416 | tf_op jit(solution)/shard_map/all_to_all | solution.py:1046
  18.3 3.1 fusion.2
  21.4 3.7 %all-to-all-start.1 = ((bf16[8,128,768]{2,1,0:T(8,128)(2,1)}), bf16[8,128,768]{2,1,0:T(8,128)(2,1)S(1)}, u32[]{:S(2)}, u32[]{:S(2)}) async-start(bf16[8,128,768]{2,1,0:T(8,128)(2,1)} %bitcast.47), calls=%async_computation.1 | async-start | bytes 3145728 | tf_op jit(solution)/shard_map/all_to_all | solution.py:1083
  29.3 31.8 %all-to-all-done.1 = bf16[8,128,768]{2,1,0:T(8,128)(2,1)S(1)} async-done(((bf16[8,128,768]{2,1,0:T(8,128)(2,1)}), bf16[8,128,768]{2,1,0:T(8,128)(2,1)S(1)}, u32[]{:S(2)}, u32[]{:S(2)}) %all-to-all-start.1) | async-done | bytes 1572896 | tf_op jit(solution)/shard_map/all_to_all | solution.py:1083
  62.2 49.3 %forward.1 = (f32[512,768]{1,0:T(8,128)}, f32[512,128]{1,0:T(8,128)}, bf16[512,768]{1,0:T(8,128)(2,1)}, f32[512,768]{1,0:T(8,128)}, bf16[512,768]{1,0:T(8,128)(2...) custom-call(s32[6]{0:T(128)} %stack.27.refs_0_, ...), custom_call_target="tpu_custom_call" | custom-call | flops 1 | bytes 1 | tf_op jit(solution)/shard_map/forward/pallas_call | solution.py:31
  113.1 15.9 %feed.1 = (bf16[512,1536]{1,0:T(8,128)(2,1)}, bf16[512,1536]{1,0:T(8,128)(2,1)}, f32[1,3072]{1,0:T(1,128)S(1)}, f32[512,768]{1,0:T(8,128)}, bf16[512,768]{1,0:T(...) custom-call(s32[6]{0:T(128)S(1)} %copy-done.18, ...), custom_call_target="tpu_custom_call" | custom-call | flops 1 | bytes 1 | tf_op jit(solution)/shard_map/feed/pallas_call | solution.py:31
  129.6 3.1 collective-permute-done.1.refs_2_
  136.2 9.2 %weights.2 = (bf16[4,48,1536]{2,1,0:T(8,128)(2,1)S(1)}, bf16[4,48,1536]{2,1,0:T(8,128)(2,1)}, bf16[4,48,1536]{2,1,0:T(8,128)(2,1)}, bf16[4,48,1536]{2,1,0:T(8,12...) custom-call(s32[6]{0:T(128)S(1)} %copy-done.18, bf16[512,384]{1,0:T(8,128)(2,1)S(1)} %copy-done.11, ...), custom_call_target="tpu_custom_call" | custom-call | flops 1 | bytes 1 | tf_op jit(solution)/shard_map/weights/pallas_call | solution.py:31
  150.0 28.7 %between.1 = (bf16[512,1152]{1,0:T(8,128)(2,1)}, bf16[512,1152]{1,0:T(8,128)(2,1)}, bf16[512,1536]{1,0:T(8,128)(2,1)}, bf16[512,1536]{1,0:T(8,128)(2,1)}, f32[2,...) custom-call(s32[6]{0:T(128)} %stack.27.refs_0_, ...), custom_call_target="tpu_custom_call" | custom-call | flops 1 | bytes 1 | tf_op jit(solution)/shard_map/between/pallas_call | solution.py:31
  192.1 18.3 %weights.3 = (bf16[8,48,1536]{2,1,0:T(8,128)(2,1)}, bf16[8,48,1536]{2,1,0:T(8,128)(2,1)}, bf16[8,64,1536]{2,1,0:T(8,128)(2,1)}, bf16[8,64,1536]{2,1,0:T(8,128)(2...) custom-call(s32[6]{0:T(128)S(1)} %copy-done.19, bf16[512,384]{1,0:T(8,128)(2,1)S(1)} %copy-done.12, ...), custom_call_target="tpu_custom_call" | custom-call | flops 1 | bytes 1 | tf_op jit(solution)/shard_map/weights/pallas_call | solution.py:31
  216.8 22.4 %last.1 = (bf16[1024,384]{1,0:T(8,128)(2,1)S(1)}, bf16[1024,384]{1,0:T(8,128)(2,1)}, bf16[16,48,1536]{2,1,0:T(8,128)(2,1)}, bf16[16,48,1536]{2,1,0:T(8,128)(2,1)}) custom-call(s32[6]{0:T(128)S(1)} %copy-done.19, s32[1]{0:T(128)S(6)} %copy.38.refs_1_, bf16[512,2304]{1,0:T(8,128)(2,1)} %get-tuple-element.127.refs_2_, f32[12,512]{1,0:T(8,128)S(1)} %copy-done.21, ...), custom_call_target="tpu_custom_call" | custom-call | flops 1 | bytes 1 | tf_op jit(solution)/shard_map/last/pallas_call | solution.py:31
  239.2 3.2 collective-permute-done.24.refs_1_
  256.3 3.6 %all-to-all-start.2 = ((bf16[8,256,384]{2,1,0:T(8,128)(2,1)}), bf16[8,256,384]{2,1,0:T(8,128)(2,1)S(1)}, u32[]{:S(2)}, u32[]{:S(2)}) async-start(bf16[8,256,384]{2,1,0:T(8,128)(2,1)} %bitcast.24), calls=%async_computation.2 | async-start | bytes 3145728 | tf_op jit(solution)/shard_map/all_to_all | solution.py:1083
  261.6 3.1 combine.14
  267.0 14.1 %collective-permute-done.29.refs_3_ = bf16[4,48,1536]{2,1,0:T(8,128)(2,1)} collective-permute-done((bf16[4,48,1536]{2,1,0:T(8,128)(2,1)}, bf16[4,48,1536]{2,1,0:T(8,128)(2,1)}, u32[]{:S(2)}, u32[]{:S(2)}) %collective-permute-start.29) | collective-permute-done | bytes 589856 | tf_op jit(solution)/shard_map/ppermute | solution.py:977
  288.4 6.5 %all-to-all-done.2 = bf16[8,256,384]{2,1,0:T(8,128)(2,1)S(1)} async-done(((bf16[8,256,384]{2,1,0:T(8,128)(2,1)}), bf16[8,256,384]{2,1,0:T(8,128)(2,1)S(1)}, u32[]{:S(2)}, u32[]{:S(2)}) %all-to-all-start.2) | async-done | bytes 1572896 | tf_op jit(solution)/shard_map/all_to_all | solution.py:1083
  294.9 2.9 table_back.1.refs_8_
  307.4 6.8 %collective-permute-done.32.refs_1_ = bf16[20,48,384]{2,1,0:T(8,128)(2,1)S(1)} collective-permute-done((bf16[20,48,384]{2,1,0:T(8,128)(2,1)S(1)}, bf16[20,48,384]{2,1,0:T(8,128)(2,1)S(1)}, u32[]{:S(2)}, u32[]{:S(2)}) %collective-permute-start.32) | collective-permute-done | bytes 737312 | tf_op jit(solution)/shard_map/ppermute | solution.py:977
  315.5 4.1 %collective-permute-done.38.refs_1_ = bf16[2,48,1536]{2,1,0:T(8,128)(2,1)S(1)} collective-permute-done((bf16[2,48,1536]{2,1,0:T(8,128)(2,1)S(1)}, bf16[2,48,1536]{2,1,0:T(8,128)(2,1)S(1)}, u32[]{:S(2)}, u32[]{:S(2)}) %collective-permute-start.38) | collective-permute-done | bytes 294944 | tf_op jit(solution)/shard_map/ppermute | solution.py:977
  319.6 6.4 %collective-permute-done.40.refs_3_ = bf16[2,48,1536]{2,1,0:T(8,128)(2,1)S(1)} collective-permute-done((bf16[2,48,1536]{2,1,0:T(8,128)(2,1)S(1)}, bf16[2,48,1536]{2,1,0:T(8,128)(2,1)S(1)}, u32[]{:S(2)}, u32[]{:S(2)}) %collective-permute-start.40) | collective-permute-done | bytes 294944 | tf_op jit(solution)/shard_map/ppermute | solution.py:977
  331.4 5.7 %collective-permute-done.44.refs_1_ = bf16[1,48,1536]{2,1,0:T(8,128)(2,1)S(1)} collective-permute-done((bf16[1,48,1536]{2,1,0:T(8,128)(2,1)S(1)}, bf16[1,48,1536]{2,1,0:T(8,128)(2,1)S(1)}, u32[]{:S(2)}, u32[]{:S(2)}) %collective-permute-start.44) | collective-permute-done | bytes 147488 | tf_op jit(solution)/shard_map/ppermute | solution.py:977
  338.6 4.5 %collective-permute-done.47.refs_0_ = bf16[1,48,1536]{2,1,0:T(8,128)(2,1)S(1)} collective-permute-done((bf16[1,48,1536]{2,1,0:T(8,128)(2,1)S(1)}, bf16[1,48,1536]{2,1,0:T(8,128)(2,1)S(1)}, u32[]{:S(2)}, u32[]{:S(2)}) %collective-permute-start.47) | collective-permute-done | bytes 147488 | tf_op jit(solution)/shard_map/ppermute | solution.py:977
  345.5 4.5 %finish.1 = (f32[2,96,2304]{2,1,0:T(8,128)}, f32[2,96,768]{2,1,0:T(8,128)}, f32[2,96,3072]{2,1,0:T(8,128)}, f32[2,384,768]{2,1,0:T(8,128)}, f32[64,768]{1,0:T(8,...) custom-call(s32[6]{0:T(128)S(1)} %copy-done.20, ...), custom_call_target="tpu_custom_call" | custom-call | flops 1 | bytes 1 | tf_op jit(solution)/shard_map/finish/pallas_call | solution.py:31
  (244 shorter events, 83.5 us)
Async XLA Ops:
  21.4 39.7 %all-to-all-start.1 = ((bf16[8,128,768]{2,1,0:T(8,128)(2,1)}), bf16[8,128,768]{2,1,0:T(8,128)(2,1)S(1)}, u32[]{:S(2)}, u32[]{:S(2)}) async-start(bf16[8,128,768]{2,1,0:T(8,128)(2,1)} %bitcast.47), calls=%async_computation.1 | async-start | bytes 3145728 | tf_op jit(solution)/shard_map/all_to_all | solution.py:1083
  111.5 23.1 %collective-permute-start.2 = (bf16[512,3072]{1,0:T(8,128)(2,1)}, bf16[512,3072]{1,0:T(8,128)(2,1)S(1)}, u32[]{:S(2)}, u32[]{:S(2)}) collective-permute-start(bf16[512,3072]{1,0:T(8,128)(2,1)} %get-tuple-element.145.refs_3_), channel_id=1, source_target_pairs={{0,8},{1,9},{2,10},{3,11},{4,12},{5,13},{6,14},{7,15},{8,0},{9,1},... | collective-permute-start | bytes 9437192 | tf_op jit(solution)/shard_map/ppermute | solution.py:977
  111.6 38.3 %collective-permute-start.5 = (bf16[512,3072]{1,0:T(8,128)(2,1)}, bf16[512,3072]{1,0:T(8,128)(2,1)}, u32[]{:S(2)}, u32[]{:S(2)}) collective-permute-start(bf16[512,3072]{1,0:T(8,128)(2,1)} %get-tuple-element.150.refs_3_), channel_id=1, source_target_pairs={{0,8},{1,9},{2,10},{3,11},{4,12},{5,13},{6,14},{7,15},{8,0},{9,1},... | collective-permute-start | bytes 9437192 | tf_op jit(solution)/shard_map/ppermute | solution.py:977
  146.3 33.5 %collective-permute-start.13 = (bf16[8,48,1536]{2,1,0:T(8,128)(2,1)}, bf16[8,48,1536]{2,1,0:T(8,128)(2,1)S(1)}, u32[]{:S(2)}, u32[]{:S(2)}) collective-permute-start(bf16[8,48,1536]{2,1,0:T(8,128)(2,1)} %get-tuple-element.171), channel_id=1, source_target_pairs={{0,2},{1,3},{2,0},{3,1},{4,6},{5,7},{6,4},{7,5},{8,10},{9,11},{10,... | collective-permute-start | bytes 3538952 | tf_op jit(solution)/shard_map/ppermute | solution.py:977
  146.3 32.4 %collective-permute-start.10 = (bf16[4,48,1536]{2,1,0:T(8,128)(2,1)}, bf16[4,48,1536]{2,1,0:T(8,128)(2,1)S(1)}, u32[]{:S(2)}, u32[]{:S(2)}) collective-permute-start(bf16[4,48,1536]{2,1,0:T(8,128)(2,1)} %get-tuple-element.167), channel_id=1, source_target_pairs={{0,16},{1,17},{2,18},{3,19},{4,20},{5,21},{6,22},{7,23},{8,24},{9,... | collective-permute-start | bytes 1769480 | tf_op jit(solution)/shard_map/ppermute | solution.py:977
  147.9 31.3 %collective-permute-start.11 = (bf16[4,48,1536]{2,1,0:T(8,128)(2,1)}, bf16[4,48,1536]{2,1,0:T(8,128)(2,1)}, u32[]{:S(2)}, u32[]{:S(2)}) collective-permute-start(bf16[4,48,1536]{2,1,0:T(8,128)(2,1)} %get-tuple-element.168), channel_id=1, source_target_pairs={{0,1},{1,0},{2,3},{3,2},{4,5},{5,4},{6,7},{7,6},{8,9},{9,8},{10,11... | collective-permute-start | bytes 1769480 | tf_op jit(solution)/shard_map/ppermute | solution.py:977
  149.1 30.2 %collective-permute-start.12 = (bf16[4,48,1536]{2,1,0:T(8,128)(2,1)}, bf16[4,48,1536]{2,1,0:T(8,128)(2,1)}, u32[]{:S(2)}, u32[]{:S(2)}) collective-permute-start(bf16[4,48,1536]{2,1,0:T(8,128)(2,1)} %get-tuple-element.169), channel_id=1, source_target_pairs={{0,17},{1,16},{2,19},{3,18},{4,21},{5,20},{6,23},{7,22},{8,25},{9,... | collective-permute-start | bytes 1769480 | tf_op jit(solution)/shard_map/ppermute | solution.py:977
  149.9 35.3 %collective-permute-start.21 = (bf16[512,384]{1,0:T(8,128)(2,1)}, bf16[512,384]{1,0:T(8,128)(2,1)S(1)}, u32[]{:S(2)}, u32[]{:S(2)}) collective-permute-start(bf16[512,384]{1,0:T(8,128)(2,1)} %get-tuple-element.185), channel_id=1, source_target_pairs={{0,8},{1,9},{2,10},{3,11},{4,12},{5,13},{6,14},{7,15},{8,0},{9,1},... | collective-permute-start | bytes 1179656 | tf_op jit(solution)/shard_map/ppermute | solution.py:977
  185.2 25.5 %collective-permute-start.14 = (bf16[2,48,1536]{2,1,0:T(8,128)(2,1)S(1)}, bf16[2,48,1536]{2,1,0:T(8,128)(2,1)S(1)}, u32[]{:S(2)}, u32[]{:S(2)}) collective-permute-start(bf16[2,48,1536]{2,1,0:T(8,128)(2,1)S(1)} %get-tuple-element.173), channel_id=1, source_target_pairs={{0,2},{1,3},{2,0},{3,1},{4,6},{5,7},{6,4},{7,5},{8,10},{9,11},{10,... | collective-permute-start | bytes 884744 | tf_op jit(solution)/shard_map/ppermute | solution.py:977
  187.2 24.4 %collective-permute-start.15 = (bf16[2,48,1536]{2,1,0:T(8,128)(2,1)S(1)}, bf16[2,48,1536]{2,1,0:T(8,128)(2,1)S(1)}, u32[]{:S(2)}, u32[]{:S(2)}) collective-permute-start(bf16[2,48,1536]{2,1,0:T(8,128)(2,1)S(1)} %get-tuple-element.175), channel_id=1, source_target_pairs={{0,16},{1,17},{2,18},{3,19},{4,20},{5,21},{6,22},{7,23},{8,24},{9,... | collective-permute-start | bytes 884744 | tf_op jit(solution)/shard_map/ppermute | solution.py:977
  188.7 24.4 %collective-permute-start.16 = (bf16[2,48,1536]{2,1,0:T(8,128)(2,1)S(1)}, bf16[2,48,1536]{2,1,0:T(8,128)(2,1)S(1)}, u32[]{:S(2)}, u32[]{:S(2)}) collective-permute-start(bf16[2,48,1536]{2,1,0:T(8,128)(2,1)S(1)} %get-tuple-element.176), channel_id=1, source_target_pairs={{0,1},{1,0},{2,3},{3,2},{4,5},{5,4},{6,7},{7,6},{8,9},{9,8},{10,11... | collective-permute-start | bytes 884744 | tf_op jit(solution)/shard_map/ppermute | solution.py:977
  189.9 23.2 %collective-permute-start.17 = (bf16[2,48,1536]{2,1,0:T(8,128)(2,1)S(1)}, bf16[2,48,1536]{2,1,0:T(8,128)(2,1)S(1)}, u32[]{:S(2)}, u32[]{:S(2)}) collective-permute-start(bf16[2,48,1536]{2,1,0:T(8,128)(2,1)S(1)} %get-tuple-element.177), channel_id=1, source_target_pairs={{0,17},{1,16},{2,19},{3,18},{4,21},{5,20},{6,23},{7,22},{8,25},{9,... | collective-permute-start | bytes 884744 | tf_op jit(solution)/shard_map/ppermute | solution.py:977
  210.5 34.1 %collective-permute-start.25 = (bf16[8,48,1536]{2,1,0:T(8,128)(2,1)}, bf16[8,48,1536]{2,1,0:T(8,128)(2,1)S(1)}, u32[]{:S(2)}, u32[]{:S(2)}) collective-permute-start(bf16[8,48,1536]{2,1,0:T(8,128)(2,1)} %get-tuple-element.194), channel_id=1, source_target_pairs={{0,2},{1,3},{2,0},{3,1},{4,6},{5,7},{6,4},{7,5},{8,10},{9,11},{10,... | collective-permute-start | bytes 3538952 | tf_op jit(solution)/shard_map/ppermute | solution.py:977
  210.6 33.9 %collective-permute-start.26 = (bf16[8,48,1536]{2,1,0:T(8,128)(2,1)}, bf16[8,48,1536]{2,1,0:T(8,128)(2,1)S(1)}, u32[]{:S(2)}, u32[]{:S(2)}) collective-permute-start(bf16[8,48,1536]{2,1,0:T(8,128)(2,1)} %get-tuple-element.195), channel_id=1, source_target_pairs={{0,1},{1,0},{2,3},{3,2},{4,5},{5,4},{6,7},{7,6},{8,9},{9,8},{10,11... | collective-permute-start | bytes 3538952 | tf_op jit(solution)/shard_map/ppermute | solution.py:977
  211.6 35.7 %collective-permute-start.27 = (bf16[8,64,1536]{2,1,0:T(8,128)(2,1)}, bf16[8,64,1536]{2,1,0:T(8,128)(2,1)S(1)}, u32[]{:S(2)}, u32[]{:S(2)}) collective-permute-start(bf16[8,64,1536]{2,1,0:T(8,128)(2,1)} %get-tuple-element.197), channel_id=1, source_target_pairs={{0,16},{1,17},{2,18},{3,19},{4,20},{5,21},{6,22},{7,23},{8,24},{9,... | collective-permute-start | bytes 4718600 | tf_op jit(solution)/shard_map/ppermute | solution.py:977
  214.7 27.7 %collective-permute-start.24 = (bf16[1,96,1536]{2,1,0:T(8,128)(2,1)S(1)}, bf16[1,96,1536]{2,1,0:T(8,128)(2,1)S(1)}, u32[]{:S(2)}, u32[]{:S(2)}) collective-permute-start(bf16[1,96,1536]{2,1,0:T(8,128)(2,1)S(1)} %get-tuple-element.192), channel_id=1, source_target_pairs={{0,4},{1,5},{2,6},{3,7},{4,0},{5,1},{6,2},{7,3},{8,12},{9,13},{10,... | collective-permute-start | bytes 884744 | tf_op jit(solution)/shard_map/ppermute | solution.py:977
  242.4 17.5 %collective-permute-start.31 = (bf16[16,48,1536]{2,1,0:T(8,128)(2,1)}, bf16[16,48,1536]{2,1,0:T(8,128)(2,1)}, u32[]{:S(2)}, u32[]{:S(2)}) collective-permute-start(bf16[16,48,1536]{2,1,0:T(8,128)(2,1)} %get-tuple-element.205), channel_id=1, source_target_pairs={{0,8},{1,9},{2,10},{3,11},{4,12},{5,13},{6,14},{7,15},{8,0},{9,1},... | collective-permute-start | bytes 7077896 | tf_op jit(solution)/shard_map/ppermute | solution.py:977
  250.9 30.1 %collective-permute-start.30 = (bf16[4,64,1536]{2,1,0:T(8,128)(2,1)}, bf16[4,64,1536]{2,1,0:T(8,128)(2,1)}, u32[]{:S(2)}, u32[]{:S(2)}) collective-permute-start(bf16[4,64,1536]{2,1,0:T(8,128)(2,1)} %get-tuple-element.204), channel_id=1, source_target_pairs={{0,1},{1,0},{2,3},{3,2},{4,5},{5,4},{6,7},{7,6},{8,9},{9,8},{10,11... | collective-permute-start | bytes 2359304 | tf_op jit(solution)/shard_map/ppermute | solution.py:977
  253.1 27.9 %collective-permute-start.29 = (bf16[4,48,1536]{2,1,0:T(8,128)(2,1)}, bf16[4,48,1536]{2,1,0:T(8,128)(2,1)}, u32[]{:S(2)}, u32[]{:S(2)}) collective-permute-start(bf16[4,48,1536]{2,1,0:T(8,128)(2,1)} %get-tuple-element.202), channel_id=1, source_target_pairs={{0,2},{1,3},{2,0},{3,1},{4,6},{5,7},{6,4},{7,5},{8,10},{9,11},{10,... | collective-permute-start | bytes 1769480 | tf_op jit(solution)/shard_map/ppermute | solution.py:977
  256.3 38.6 %all-to-all-start.2 = ((bf16[8,256,384]{2,1,0:T(8,128)(2,1)}), bf16[8,256,384]{2,1,0:T(8,128)(2,1)S(1)}, u32[]{:S(2)}, u32[]{:S(2)}) async-start(bf16[8,256,384]{2,1,0:T(8,128)(2,1)} %bitcast.24), calls=%async_computation.2 | async-start | bytes 3145728 | tf_op jit(solution)/shard_map/all_to_all | solution.py:1083
  264.7 35.6 %collective-permute-start.33 = (bf16[8,48,1536]{2,1,0:T(8,128)(2,1)}, bf16[8,48,1536]{2,1,0:T(8,128)(2,1)}, u32[]{:S(2)}, u32[]{:S(2)}) collective-permute-start(bf16[8,48,1536]{2,1,0:T(8,128)(2,1)} %get-tuple-element.209), channel_id=1, source_target_pairs={{0,16},{1,17},{2,18},{3,19},{4,20},{5,21},{6,22},{7,23},{8,24},{9,... | collective-permute-start | bytes 3538952 | tf_op jit(solution)/shard_map/ppermute | solution.py:977
  302.3 23.7 %collective-permute-start.41 = (bf16[1,160,1536]{2,1,0:T(8,128)(2,1)S(1)}, bf16[1,160,1536]{2,1,0:T(8,128)(2,1)S(1)}, u32[]{:S(2)}, u32[]{:S(2)}) collective-permute-start(bf16[1,160,1536]{2,1,0:T(8,128)(2,1)S(1)} %get-tuple-element.221), channel_id=1, source_target_pairs={{0,4},{1,5},{2,6},{3,7},{4,0},{5,1},{6,2},{7,3},{8,12},{9,13},{10,... | collective-permute-start | bytes 1474568 | tf_op jit(solution)/shard_map/ppermute | solution.py:977
  306.9 19.1 %collective-permute-start.40 = (bf16[2,48,1536]{2,1,0:T(8,128)(2,1)S(1)}, bf16[2,48,1536]{2,1,0:T(8,128)(2,1)S(1)}, u32[]{:S(2)}, u32[]{:S(2)}) collective-permute-start(bf16[2,48,1536]{2,1,0:T(8,128)(2,1)S(1)} %get-tuple-element.219), channel_id=1, source_target_pairs={{0,3},{1,2},{2,1},{3,0},{4,7},{5,6},{6,5},{7,4},{8,11},{9,10},{10,... | collective-permute-start | bytes 884744 | tf_op jit(solution)/shard_map/ppermute | solution.py:977
  326.3 16.8 %collective-permute-start.43 = (bf16[1,160,1536]{2,1,0:T(8,128)(2,1)S(1)}, bf16[1,160,1536]{2,1,0:T(8,128)(2,1)S(1)}, u32[]{:S(2)}, u32[]{:S(2)}) collective-permute-start(bf16[1,160,1536]{2,1,0:T(8,128)(2,1)S(1)} %get-tuple-element.225.refs_1_), channel_id=1, source_target_pairs={{0,16},{1,17},{2,18},{3,19},{4,20},{5,21},{6,22},{7,23},{8,24},{9,... | collective-permute-start | bytes 1474568 | tf_op jit(solution)/shard_map/ppermute | solution.py:977
  (88 other events, 825.2 us)

commit v8 on v7

--- a/solution.py
+++ b/solution.py
@@ -238,7 +238,7 @@
             v((tokens, width), F32), v((tokens, width), F32), pltpu.SemaphoreType.DMA((1 + NL * (6 + 2 * chunks),)),
         ],
         cost_estimate=CHEAP,
-        vmem=60,
+        vmem=57,
         name="forward",
     )
     return outs[:3], outs[3:8], [outs[8 + 11 * layer : 19 + 11 * layer] for layer in range(NL)]

time: 357 us -> 357 us (level)
  no operation moved by 1% of the time
where the time goes in v8:
time: 357 us; the launch traced here: 350 us
  Pallas kernels  166 us (46%)
  waiting for transfers between devices  104 us (29%)
  starting transfers between devices  50.9 us (14%)
  local copies, waits for them, and re-layouts  19.4 us (5%)
  other arithmetic  4.87 us (1%)
    pallas_call x20, Pallas kernels, run(): pl.pallas_call(body, out_shape=out_shape, in_specs=list(in_specs) + [ANY]...  166 us
    ppermute x52, waiting for transfers between devices, permute(): return lax.ppermute(value, AXES, pairs)  59.3 us
    all_to_all x2, waiting for transfers between devices, exchange_rows(): lax.all_to_all(outgoing.reshape(owners, -1, shape[1]), 'vocab', split_axi...  38.3 us
    ppermute x52, starting transfers between devices, permute(): return lax.ppermute(value, AXES, pairs)  36.3 us
    unnamed x114, local copies, waits for them, and re-layouts  15.5 us
    all_to_all x2, starting transfers between devices, exchange_rows(): lax.all_to_all(outgoing.reshape(owners, -1, shape[1]), 'vocab', split_axi...  7.29 us
    all_to_all x1, starting transfers between devices, on_device(): lax.all_to_all(jnp.broadcast_to(token_ids, (owners, tokens)), 'vocab', sp...  7.25 us
  transfers between devices with their start and end apart: 55, of which 19 were waited for; matrix products, arithmetic and copies ran while one was open for 1% of the time, Pallas kernels for 32%

profile of v8, /device:TPU:0, one launch (start us, length us, event | category | flops | bytes accessed | tf_op | source)
XLA Modules:
  0.0 350.4 jit_solution(2268129931571617876)
XLA Ops:
  2.1 7.3 %all-to-all-start = ((s32[8,1,512]{2,1,0:T(1,128)}), s32[8,1,512]{2,1,0:T(1,128)S(1)}, u32[]{:S(2)}, u32[]{:S(2)}) async-start(s32[8,1,512]{2,1,0:T(1,128)} %broadcast_in_dim.36), calls=%async_computation | async-start | bytes 32768 | tf_op jit(solution)/shard_map/all_to_all | solution.py:1046
  9.3 6.6 %all-to-all-done = s32[8,1,512]{2,1,0:T(1,128)S(1)} async-done(((s32[8,1,512]{2,1,0:T(1,128)}), s32[8,1,512]{2,1,0:T(1,128)S(1)}, u32[]{:S(2)}, u32[]{:S(2)}) %all-to-all-start) | async-done | bytes 16416 | tf_op jit(solution)/shard_map/all_to_all | solution.py:1046
  18.3 3.1 fusion.2
  21.4 3.7 %all-to-all-start.1 = ((bf16[8,128,768]{2,1,0:T(8,128)(2,1)}), bf16[8,128,768]{2,1,0:T(8,128)(2,1)S(1)}, u32[]{:S(2)}, u32[]{:S(2)}) async-start(bf16[8,128,768]{2,1,0:T(8,128)(2,1)} %bitcast.47), calls=%async_computation.1 | async-start | bytes 3145728 | tf_op jit(solution)/shard_map/all_to_all | solution.py:1083
  29.3 31.8 %all-to-all-done.1 = bf16[8,128,768]{2,1,0:T(8,128)(2,1)S(1)} async-done(((bf16[8,128,768]{2,1,0:T(8,128)(2,1)}), bf16[8,128,768]{2,1,0:T(8,128)(2,1)S(1)}, u32[]{:S(2)}, u32[]{:S(2)}) %all-to-all-start.1) | async-done | bytes 1572896 | tf_op jit(solution)/shard_map/all_to_all | solution.py:1083
  62.2 49.3 %forward.1 = (f32[512,768]{1,0:T(8,128)}, f32[512,128]{1,0:T(8,128)}, bf16[512,768]{1,0:T(8,128)(2,1)}, f32[512,768]{1,0:T(8,128)}, bf16[512,768]{1,0:T(8,128)(2...) custom-call(s32[6]{0:T(128)} %stack.27.refs_0_, ...), custom_call_target="tpu_custom_call" | custom-call | flops 1 | bytes 1 | tf_op jit(solution)/shard_map/forward/pallas_call | solution.py:31
  113.1 15.9 %feed.1 = (bf16[512,1536]{1,0:T(8,128)(2,1)}, bf16[512,1536]{1,0:T(8,128)(2,1)}, f32[1,3072]{1,0:T(1,128)S(1)}, f32[512,768]{1,0:T(8,128)}, bf16[512,768]{1,0:T(...) custom-call(s32[6]{0:T(128)S(1)} %copy-done.18, ...), custom_call_target="tpu_custom_call" | custom-call | flops 1 | bytes 1 | tf_op jit(solution)/shard_map/feed/pallas_call | solution.py:31
  129.6 3.1 collective-permute-done.1.refs_2_
  136.2 9.2 %weights.2 = (bf16[4,48,1536]{2,1,0:T(8,128)(2,1)S(1)}, bf16[4,48,1536]{2,1,0:T(8,128)(2,1)}, bf16[4,48,1536]{2,1,0:T(8,128)(2,1)}, bf16[4,48,1536]{2,1,0:T(8,12...) custom-call(s32[6]{0:T(128)S(1)} %copy-done.18, bf16[512,384]{1,0:T(8,128)(2,1)S(1)} %copy-done.11, ...), custom_call_target="tpu_custom_call" | custom-call | flops 1 | bytes 1 | tf_op jit(solution)/shard_map/weights/pallas_call | solution.py:31
  150.0 28.7 %between.1 = (bf16[512,1152]{1,0:T(8,128)(2,1)}, bf16[512,1152]{1,0:T(8,128)(2,1)}, bf16[512,1536]{1,0:T(8,128)(2,1)}, bf16[512,1536]{1,0:T(8,128)(2,1)}, f32[2,...) custom-call(s32[6]{0:T(128)} %stack.27.refs_0_, ...), custom_call_target="tpu_custom_call" | custom-call | flops 1 | bytes 1 | tf_op jit(solution)/shard_map/between/pallas_call | solution.py:31
  192.1 18.3 %weights.3 = (bf16[8,48,1536]{2,1,0:T(8,128)(2,1)}, bf16[8,48,1536]{2,1,0:T(8,128)(2,1)}, bf16[8,64,1536]{2,1,0:T(8,128)(2,1)}, bf16[8,64,1536]{2,1,0:T(8,128)(2...) custom-call(s32[6]{0:T(128)S(1)} %copy-done.19, bf16[512,384]{1,0:T(8,128)(2,1)S(1)} %copy-done.12, ...), custom_call_target="tpu_custom_call" | custom-call | flops 1 | bytes 1 | tf_op jit(solution)/shard_map/weights/pallas_call | solution.py:31
  216.8 22.4 %last.1 = (bf16[1024,384]{1,0:T(8,128)(2,1)S(1)}, bf16[1024,384]{1,0:T(8,128)(2,1)}, bf16[16,48,1536]{2,1,0:T(8,128)(2,1)}, bf16[16,48,1536]{2,1,0:T(8,128)(2,1)}) custom-call(s32[6]{0:T(128)S(1)} %copy-done.19, s32[1]{0:T(128)S(6)} %copy.38.refs_1_, bf16[512,2304]{1,0:T(8,128)(2,1)} %get-tuple-element.127.refs_2_, f32[12,512]{1,0:T(8,128)S(1)} %copy-done.21, ...), custom_call_target="tpu_custom_call" | custom-call | flops 1 | bytes 1 | tf_op jit(solution)/shard_map/last/pallas_call | solution.py:31
  239.2 3.2 collective-permute-done.24.refs_1_
  256.3 3.6 %all-to-all-start.2 = ((bf16[8,256,384]{2,1,0:T(8,128)(2,1)}), bf16[8,256,384]{2,1,0:T(8,128)(2,1)S(1)}, u32[]{:S(2)}, u32[]{:S(2)}) async-start(bf16[8,256,384]{2,1,0:T(8,128)(2,1)} %bitcast.24), calls=%async_computation.2 | async-start | bytes 3145728 | tf_op jit(solution)/shard_map/all_to_all | solution.py:1083
  261.6 3.1 combine.14
  267.0 14.1 %collective-permute-done.29.refs_3_ = bf16[4,48,1536]{2,1,0:T(8,128)(2,1)} collective-permute-done((bf16[4,48,1536]{2,1,0:T(8,128)(2,1)}, bf16[4,48,1536]{2,1,0:T(8,128)(2,1)}, u32[]{:S(2)}, u32[]{:S(2)}) %collective-permute-start.29) | collective-permute-done | bytes 589856 | tf_op jit(solution)/shard_map/ppermute | solution.py:977
  288.4 6.5 %all-to-all-done.2 = bf16[8,256,384]{2,1,0:T(8,128)(2,1)S(1)} async-done(((bf16[8,256,384]{2,1,0:T(8,128)(2,1)}), bf16[8,256,384]{2,1,0:T(8,128)(2,1)S(1)}, u32[]{:S(2)}, u32[]{:S(2)}) %all-to-all-start.2) | async-done | bytes 1572896 | tf_op jit(solution)/shard_map/all_to_all | solution.py:1083
  294.9 2.9 table_back.1.refs_8_
  307.4 6.8 %collective-permute-done.32.refs_1_ = bf16[20,48,384]{2,1,0:T(8,128)(2,1)S(1)} collective-permute-done((bf16[20,48,384]{2,1,0:T(8,128)(2,1)S(1)}, bf16[20,48,384]{2,1,0:T(8,128)(2,1)S(1)}, u32[]{:S(2)}, u32[]{:S(2)}) %collective-permute-start.32) | collective-permute-done | bytes 737312 | tf_op jit(solution)/shard_map/ppermute | solution.py:977
  315.5 4.1 %collective-permute-done.38.refs_1_ = bf16[2,48,1536]{2,1,0:T(8,128)(2,1)S(1)} collective-permute-done((bf16[2,48,1536]{2,1,0:T(8,128)(2,1)S(1)}, bf16[2,48,1536]{2,1,0:T(8,128)(2,1)S(1)}, u32[]{:S(2)}, u32[]{:S(2)}) %collective-permute-start.38) | collective-permute-done | bytes 294944 | tf_op jit(solution)/shard_map/ppermute | solution.py:977
  319.6 6.4 %collective-permute-done.40.refs_3_ = bf16[2,48,1536]{2,1,0:T(8,128)(2,1)S(1)} collective-permute-done((bf16[2,48,1536]{2,1,0:T(8,128)(2,1)S(1)}, bf16[2,48,1536]{2,1,0:T(8,128)(2,1)S(1)}, u32[]{:S(2)}, u32[]{:S(2)}) %collective-permute-start.40) | collective-permute-done | bytes 294944 | tf_op jit(solution)/shard_map/ppermute | solution.py:977
  331.4 5.7 %collective-permute-done.44.refs_1_ = bf16[1,48,1536]{2,1,0:T(8,128)(2,1)S(1)} collective-permute-done((bf16[1,48,1536]{2,1,0:T(8,128)(2,1)S(1)}, bf16[1,48,1536]{2,1,0:T(8,128)(2,1)S(1)}, u32[]{:S(2)}, u32[]{:S(2)}) %collective-permute-start.44) | collective-permute-done | bytes 147488 | tf_op jit(solution)/shard_map/ppermute | solution.py:977
  338.6 4.5 %collective-permute-done.47.refs_0_ = bf16[1,48,1536]{2,1,0:T(8,128)(2,1)S(1)} collective-permute-done((bf16[1,48,1536]{2,1,0:T(8,128)(2,1)S(1)}, bf16[1,48,1536]{2,1,0:T(8,128)(2,1)S(1)}, u32[]{:S(2)}, u32[]{:S(2)}) %collective-permute-start.47) | collective-permute-done | bytes 147488 | tf_op jit(solution)/shard_map/ppermute | solution.py:977
  345.5 4.5 %finish.1 = (f32[2,96,2304]{2,1,0:T(8,128)}, f32[2,96,768]{2,1,0:T(8,128)}, f32[2,96,3072]{2,1,0:T(8,128)}, f32[2,384,768]{2,1,0:T(8,128)}, f32[64,768]{1,0:T(8,...) custom-call(s32[6]{0:T(128)S(1)} %copy-done.20, ...), custom_call_target="tpu_custom_call" | custom-call | flops 1 | bytes 1 | tf_op jit(solution)/shard_map/finish/pallas_call | solution.py:31
  (244 shorter events, 83.5 us)
Async XLA Ops:
  21.4 39.7 %all-to-all-start.1 = ((bf16[8,128,768]{2,1,0:T(8,128)(2,1)}), bf16[8,128,768]{2,1,0:T(8,128)(2,1)S(1)}, u32[]{:S(2)}, u32[]{:S(2)}) async-start(bf16[8,128,768]{2,1,0:T(8,128)(2,1)} %bitcast.47), calls=%async_computation.1 | async-start | bytes 3145728 | tf_op jit(solution)/shard_map/all_to_all | solution.py:1083
  111.5 23.1 %collective-permute-start.2 = (bf16[512,3072]{1,0:T(8,128)(2,1)}, bf16[512,3072]{1,0:T(8,128)(2,1)S(1)}, u32[]{:S(2)}, u32[]{:S(2)}) collective-permute-start(bf16[512,3072]{1,0:T(8,128)(2,1)} %get-tuple-element.145.refs_3_), channel_id=1, source_target_pairs={{0,8},{1,9},{2,10},{3,11},{4,12},{5,13},{6,14},{7,15},{8,0},{9,1},... | collective-permute-start | bytes 9437192 | tf_op jit(solution)/shard_map/ppermute | solution.py:977
  111.6 38.3 %collective-permute-start.5 = (bf16[512,3072]{1,0:T(8,128)(2,1)}, bf16[512,3072]{1,0:T(8,128)(2,1)}, u32[]{:S(2)}, u32[]{:S(2)}) collective-permute-start(bf16[512,3072]{1,0:T(8,128)(2,1)} %get-tuple-element.150.refs_3_), channel_id=1, source_target_pairs={{0,8},{1,9},{2,10},{3,11},{4,12},{5,13},{6,14},{7,15},{8,0},{9,1},... | collective-permute-start | bytes 9437192 | tf_op jit(solution)/shard_map/ppermute | solution.py:977
  146.3 33.5 %collective-permute-start.13 = (bf16[8,48,1536]{2,1,0:T(8,128)(2,1)}, bf16[8,48,1536]{2,1,0:T(8,128)(2,1)S(1)}, u32[]{:S(2)}, u32[]{:S(2)}) collective-permute-start(bf16[8,48,1536]{2,1,0:T(8,128)(2,1)} %get-tuple-element.171), channel_id=1, source_target_pairs={{0,2},{1,3},{2,0},{3,1},{4,6},{5,7},{6,4},{7,5},{8,10},{9,11},{10,... | collective-permute-start | bytes 3538952 | tf_op jit(solution)/shard_map/ppermute | solution.py:977
  146.3 32.4 %collective-permute-start.10 = (bf16[4,48,1536]{2,1,0:T(8,128)(2,1)}, bf16[4,48,1536]{2,1,0:T(8,128)(2,1)S(1)}, u32[]{:S(2)}, u32[]{:S(2)}) collective-permute-start(bf16[4,48,1536]{2,1,0:T(8,128)(2,1)} %get-tuple-element.167), channel_id=1, source_target_pairs={{0,16},{1,17},{2,18},{3,19},{4,20},{5,21},{6,22},{7,23},{8,24},{9,... | collective-permute-start | bytes 1769480 | tf_op jit(solution)/shard_map/ppermute | solution.py:977
  147.9 31.3 %collective-permute-start.11 = (bf16[4,48,1536]{2,1,0:T(8,128)(2,1)}, bf16[4,48,1536]{2,1,0:T(8,128)(2,1)}, u32[]{:S(2)}, u32[]{:S(2)}) collective-permute-start(bf16[4,48,1536]{2,1,0:T(8,128)(2,1)} %get-tuple-element.168), channel_id=1, source_target_pairs={{0,1},{1,0},{2,3},{3,2},{4,5},{5,4},{6,7},{7,6},{8,9},{9,8},{10,11... | collective-permute-start | bytes 1769480 | tf_op jit(solution)/shard_map/ppermute | solution.py:977
  149.1 30.2 %collective-permute-start.12 = (bf16[4,48,1536]{2,1,0:T(8,128)(2,1)}, bf16[4,48,1536]{2,1,0:T(8,128)(2,1)}, u32[]{:S(2)}, u32[]{:S(2)}) collective-permute-start(bf16[4,48,1536]{2,1,0:T(8,128)(2,1)} %get-tuple-element.169), channel_id=1, source_target_pairs={{0,17},{1,16},{2,19},{3,18},{4,21},{5,20},{6,23},{7,22},{8,25},{9,... | collective-permute-start | bytes 1769480 | tf_op jit(solution)/shard_map/ppermute | solution.py:977
  149.9 35.3 %collective-permute-start.21 = (bf16[512,384]{1,0:T(8,128)(2,1)}, bf16[512,384]{1,0:T(8,128)(2,1)S(1)}, u32[]{:S(2)}, u32[]{:S(2)}) collective-permute-start(bf16[512,384]{1,0:T(8,128)(2,1)} %get-tuple-element.185), channel_id=1, source_target_pairs={{0,8},{1,9},{2,10},{3,11},{4,12},{5,13},{6,14},{7,15},{8,0},{9,1},... | collective-permute-start | bytes 1179656 | tf_op jit(solution)/shard_map/ppermute | solution.py:977
  185.2 25.5 %collective-permute-start.14 = (bf16[2,48,1536]{2,1,0:T(8,128)(2,1)S(1)}, bf16[2,48,1536]{2,1,0:T(8,128)(2,1)S(1)}, u32[]{:S(2)}, u32[]{:S(2)}) collective-permute-start(bf16[2,48,1536]{2,1,0:T(8,128)(2,1)S(1)} %get-tuple-element.173), channel_id=1, source_target_pairs={{0,2},{1,3},{2,0},{3,1},{4,6},{5,7},{6,4},{7,5},{8,10},{9,11},{10,... | collective-permute-start | bytes 884744 | tf_op jit(solution)/shard_map/ppermute | solution.py:977
  187.2 24.4 %collective-permute-start.15 = (bf16[2,48,1536]{2,1,0:T(8,128)(2,1)S(1)}, bf16[2,48,1536]{2,1,0:T(8,128)(2,1)S(1)}, u32[]{:S(2)}, u32[]{:S(2)}) collective-permute-start(bf16[2,48,1536]{2,1,0:T(8,128)(2,1)S(1)} %get-tuple-element.175), channel_id=1, source_target_pairs={{0,16},{1,17},{2,18},{3,19},{4,20},{5,21},{6,22},{7,23},{8,24},{9,... | collective-permute-start | bytes 884744 | tf_op jit(solution)/shard_map/ppermute | solution.py:977
  188.7 24.4 %collective-permute-start.16 = (bf16[2,48,1536]{2,1,0:T(8,128)(2,1)S(1)}, bf16[2,48,1536]{2,1,0:T(8,128)(2,1)S(1)}, u32[]{:S(2)}, u32[]{:S(2)}) collective-permute-start(bf16[2,48,1536]{2,1,0:T(8,128)(2,1)S(1)} %get-tuple-element.176), channel_id=1, source_target_pairs={{0,1},{1,0},{2,3},{3,2},{4,5},{5,4},{6,7},{7,6},{8,9},{9,8},{10,11... | collective-permute-start | bytes 884744 | tf_op jit(solution)/shard_map/ppermute | solution.py:977
  189.9 23.2 %collective-permute-start.17 = (bf16[2,48,1536]{2,1,0:T(8,128)(2,1)S(1)}, bf16[2,48,1536]{2,1,0:T(8,128)(2,1)S(1)}, u32[]{:S(2)}, u32[]{:S(2)}) collective-permute-start(bf16[2,48,1536]{2,1,0:T(8,128)(2,1)S(1)} %get-tuple-element.177), channel_id=1, source_target_pairs={{0,17},{1,16},{2,19},{3,18},{4,21},{5,20},{6,23},{7,22},{8,25},{9,... | collective-permute-start | bytes 884744 | tf_op jit(solution)/shard_map/ppermute | solution.py:977
  210.5 34.1 %collective-permute-start.25 = (bf16[8,48,1536]{2,1,0:T(8,128)(2,1)}, bf16[8,48,1536]{2,1,0:T(8,128)(2,1)S(1)}, u32[]{:S(2)}, u32[]{:S(2)}) collective-permute-start(bf16[8,48,1536]{2,1,0:T(8,128)(2,1)} %get-tuple-element.194), channel_id=1, source_target_pairs={{0,2},{1,3},{2,0},{3,1},{4,6},{5,7},{6,4},{7,5},{8,10},{9,11},{10,... | collective-permute-start | bytes 3538952 | tf_op jit(solution)/shard_map/ppermute | solution.py:977
  210.6 33.9 %collective-permute-start.26 = (bf16[8,48,1536]{2,1,0:T(8,128)(2,1)}, bf16[8,48,1536]{2,1,0:T(8,128)(2,1)S(1)}, u32[]{:S(2)}, u32[]{:S(2)}) collective-permute-start(bf16[8,48,1536]{2,1,0:T(8,128)(2,1)} %get-tuple-element.195), channel_id=1, source_target_pairs={{0,1},{1,0},{2,3},{3,2},{4,5},{5,4},{6,7},{7,6},{8,9},{9,8},{10,11... | collective-permute-start | bytes 3538952 | tf_op jit(solution)/shard_map/ppermute | solution.py:977
  211.6 35.7 %collective-permute-start.27 = (bf16[8,64,1536]{2,1,0:T(8,128)(2,1)}, bf16[8,64,1536]{2,1,0:T(8,128)(2,1)S(1)}, u32[]{:S(2)}, u32[]{:S(2)}) collective-permute-start(bf16[8,64,1536]{2,1,0:T(8,128)(2,1)} %get-tuple-element.197), channel_id=1, source_target_pairs={{0,16},{1,17},{2,18},{3,19},{4,20},{5,21},{6,22},{7,23},{8,24},{9,... | collective-permute-start | bytes 4718600 | tf_op jit(solution)/shard_map/ppermute | solution.py:977
  214.7 27.7 %collective-permute-start.24 = (bf16[1,96,1536]{2,1,0:T(8,128)(2,1)S(1)}, bf16[1,96,1536]{2,1,0:T(8,128)(2,1)S(1)}, u32[]{:S(2)}, u32[]{:S(2)}) collective-permute-start(bf16[1,96,1536]{2,1,0:T(8,128)(2,1)S(1)} %get-tuple-element.192), channel_id=1, source_target_pairs={{0,4},{1,5},{2,6},{3,7},{4,0},{5,1},{6,2},{7,3},{8,12},{9,13},{10,... | collective-permute-start | bytes 884744 | tf_op jit(solution)/shard_map/ppermute | solution.py:977
  242.4 17.5 %collective-permute-start.31 = (bf16[16,48,1536]{2,1,0:T(8,128)(2,1)}, bf16[16,48,1536]{2,1,0:T(8,128)(2,1)}, u32[]{:S(2)}, u32[]{:S(2)}) collective-permute-start(bf16[16,48,1536]{2,1,0:T(8,128)(2,1)} %get-tuple-element.205), channel_id=1, source_target_pairs={{0,8},{1,9},{2,10},{3,11},{4,12},{5,13},{6,14},{7,15},{8,0},{9,1},... | collective-permute-start | bytes 7077896 | tf_op jit(solution)/shard_map/ppermute | solution.py:977
  250.9 30.1 %collective-permute-start.30 = (bf16[4,64,1536]{2,1,0:T(8,128)(2,1)}, bf16[4,64,1536]{2,1,0:T(8,128)(2,1)}, u32[]{:S(2)}, u32[]{:S(2)}) collective-permute-start(bf16[4,64,1536]{2,1,0:T(8,128)(2,1)} %get-tuple-element.204), channel_id=1, source_target_pairs={{0,1},{1,0},{2,3},{3,2},{4,5},{5,4},{6,7},{7,6},{8,9},{9,8},{10,11... | collective-permute-start | bytes 2359304 | tf_op jit(solution)/shard_map/ppermute | solution.py:977
  253.1 27.9 %collective-permute-start.29 = (bf16[4,48,1536]{2,1,0:T(8,128)(2,1)}, bf16[4,48,1536]{2,1,0:T(8,128)(2,1)}, u32[]{:S(2)}, u32[]{:S(2)}) collective-permute-start(bf16[4,48,1536]{2,1,0:T(8,128)(2,1)} %get-tuple-element.202), channel_id=1, source_target_pairs={{0,2},{1,3},{2,0},{3,1},{4,6},{5,7},{6,4},{7,5},{8,10},{9,11},{10,... | collective-permute-start | bytes 1769480 | tf_op jit(solution)/shard_map/ppermute | solution.py:977
  256.3 38.6 %all-to-all-start.2 = ((bf16[8,256,384]{2,1,0:T(8,128)(2,1)}), bf16[8,256,384]{2,1,0:T(8,128)(2,1)S(1)}, u32[]{:S(2)}, u32[]{:S(2)}) async-start(bf16[8,256,384]{2,1,0:T(8,128)(2,1)} %bitcast.24), calls=%async_computation.2 | async-start | bytes 3145728 | tf_op jit(solution)/shard_map/all_to_all | solution.py:1083
  264.7 35.6 %collective-permute-start.33 = (bf16[8,48,1536]{2,1,0:T(8,128)(2,1)}, bf16[8,48,1536]{2,1,0:T(8,128)(2,1)}, u32[]{:S(2)}, u32[]{:S(2)}) collective-permute-start(bf16[8,48,1536]{2,1,0:T(8,128)(2,1)} %get-tuple-element.209), channel_id=1, source_target_pairs={{0,16},{1,17},{2,18},{3,19},{4,20},{5,21},{6,22},{7,23},{8,24},{9,... | collective-permute-start | bytes 3538952 | tf_op jit(solution)/shard_map/ppermute | solution.py:977
  302.3 23.7 %collective-permute-start.41 = (bf16[1,160,1536]{2,1,0:T(8,128)(2,1)S(1)}, bf16[1,160,1536]{2,1,0:T(8,128)(2,1)S(1)}, u32[]{:S(2)}, u32[]{:S(2)}) collective-permute-start(bf16[1,160,1536]{2,1,0:T(8,128)(2,1)S(1)} %get-tuple-element.221), channel_id=1, source_target_pairs={{0,4},{1,5},{2,6},{3,7},{4,0},{5,1},{6,2},{7,3},{8,12},{9,13},{10,... | collective-permute-start | bytes 1474568 | tf_op jit(solution)/shard_map/ppermute | solution.py:977
  306.9 19.1 %collective-permute-start.40 = (bf16[2,48,1536]{2,1,0:T(8,128)(2,1)S(1)}, bf16[2,48,1536]{2,1,0:T(8,128)(2,1)S(1)}, u32[]{:S(2)}, u32[]{:S(2)}) collective-permute-start(bf16[2,48,1536]{2,1,0:T(8,128)(2,1)S(1)} %get-tuple-element.219), channel_id=1, source_target_pairs={{0,3},{1,2},{2,1},{3,0},{4,7},{5,6},{6,5},{7,4},{8,11},{9,10},{10,... | collective-permute-start | bytes 884744 | tf_op jit(solution)/shard_map/ppermute | solution.py:977
  326.3 16.8 %collective-permute-start.43 = (bf16[1,160,1536]{2,1,0:T(8,128)(2,1)S(1)}, bf16[1,160,1536]{2,1,0:T(8,128)(2,1)S(1)}, u32[]{:S(2)}, u32[]{:S(2)}) collective-permute-start(bf16[1,160,1536]{2,1,0:T(8,128)(2,1)S(1)} %get-tuple-element.225.refs_1_), channel_id=1, source_target_pairs={{0,16},{1,17},{2,18},{3,19},{4,20},{5,21},{6,22},{7,23},{8,24},{9,... | collective-permute-start | bytes 1474568 | tf_op jit(solution)/shard_map/ppermute | solution.py:977
  (88 other events, 825.2 us)
